TPU v7x, 32 devices: a whole 2x2x4 slice. The times are simulated.
32 devices in a mesh: seq: 8 (over y, x, core), head: 4 (over z).
Axes of the slice: x: 2, y: 2, z: 4, core: 2. Of those that a mesh axis runs over, the one named last changes fastest.
Arguments:
- queries: bfloat16 [1024, 512], P('seq', 'head'), may hold values from -108 to 108
- key_rows: bfloat16 [1024, 512], P('seq', 'head'), may hold values from -4.5 to 4.5
- value_rows: bfloat16 [1024, 512], P('seq', 'head'), may hold values from -6 to 6
- out_weight: bfloat16 [512, 2048], P('head'), may hold values from -4 to 4
- strided_index: int32 [8, 8], P('seq'), may hold values from 0 to 1
- cotangent: bfloat16 [1024, 2048], P('seq'), may hold values from -6 to 6
Outputs:
- mixed_output: bfloat16 [1024, 2048], P('seq', 'head')
- grad_queries: bfloat16 [1024, 512], P('seq', 'head')
- grad_keys: bfloat16 [1024, 512], P('seq', 'head')
- grad_values: bfloat16 [1024, 512], P('seq', 'head')
All inputs are finite; a program needn't handle non-finite values.
Results may differ from a plain program's by a relative error of at most 0.023.
Values may be sent and summed in bfloat16 or wider, within the bound.
No kernel may reach another device: no remote copies, remote signals or barrier semaphores. Data moves between devices by JAX's collectives and lax.ppermute only.
A program may use at most 64 MiB of HBM per device.

v0:
```python
import jax
import jax.numpy as jnp
from jax import lax
from jax.sharding import PartitionSpec as P

HD = 128
BLK = 128
STRIDE_ROWS = 32


def padded(cells, sides, width):
    for axis, dim in sides:
        count = lax.axis_size(axis)
        head = lax.slice_in_dim(cells, 0, width, axis=dim)
        tail = lax.slice_in_dim(cells, cells.shape[dim] - width, cells.shape[dim], axis=dim)
        cells = jnp.concatenate(
            [
                lax.ppermute(tail, axis, [(i, (i + 1) % count) for i in range(count)]),
                cells,
                lax.ppermute(head, axis, [((i + 1) % count, i) for i in range(count)]),
            ],
            axis=dim,
        )
    return cells


def split_heads(array, head_size):
    return array.reshape(array.shape[:-1] + (array.shape[-1] // head_size, head_size))


def gather_lists(extended, strided_blocks, index_rows, group_size, block_rows):
    paired_width = extended.shape[1]
    window_rows = extended
    window_rows = window_rows.reshape(group_size + 2, block_rows, paired_width)
    window = jnp.stack([window_rows[:-2], window_rows[1:-1], window_rows[2:]], axis=1)
    picked = strided_blocks[index_rows]
    return jnp.concatenate([window, picked], axis=1).reshape(group_size, -1, paired_width)


def shards(queries, key_rows, value_rows, out_weight, strided_index, cotangent):
    tokens, feature_width = queries.shape
    block_rows = BLK
    per_device = tokens // block_rows
    group_size = min(per_device, max(1, 512 // block_rows))
    rounds = per_device // group_size
    score_scale = HD ** (-0.5)
    paired = jnp.concatenate([key_rows, value_rows], axis=1)
    extended = padded(paired, (("seq", 0),), block_rows)
    strided_local = lax.all_gather(paired[:STRIDE_ROWS], "seq", axis=0, tiled=True)
    side_count = strided_local.shape[0] // block_rows
    strided_blocks = strided_local.reshape(side_count, block_rows, 2 * feature_width)
    query_groups = queries.reshape(rounds, group_size, block_rows, feature_width)
    index_groups = strided_index.reshape(rounds, group_size, -1)
    numbers = jnp.arange(rounds, dtype=jnp.int32)

    def scores_for(query_group, key_list):
        query_heads = split_heads(query_group, HD)
        key_heads = split_heads(key_list[..., :feature_width], HD)
        return (
            jnp.einsum(
                "gqhd,gkhd->ghqk", query_heads, key_heads, preferred_element_type=jnp.float32
            )
            * score_scale
        )

    def forward(inputs):
        position, query_group, index_rows = inputs
        key_list = gather_lists(extended, strided_blocks, index_rows, group_size, block_rows)
        scores = scores_for(query_group, key_list)
        row_top = jnp.max(scores, axis=-1, keepdims=True)
        logsum = row_top + jnp.log(jnp.sum(jnp.exp(scores - row_top), axis=-1, keepdims=True))
        weights = jnp.exp(scores - logsum).astype(jnp.bfloat16)
        value_heads = split_heads(key_list[..., feature_width:], HD)
        output = jnp.einsum(
            "ghqk,gkhd->gqhd", weights, value_heads, preferred_element_type=jnp.float32
        )
        return (
            output.astype(jnp.bfloat16).reshape(group_size * block_rows, feature_width),
            logsum[..., 0],
        )

    attention_parts, logsums = lax.map(forward, (numbers, query_groups, index_groups))
    attention = attention_parts.reshape(tokens, feature_width)
    partial_terms = jnp.dot(attention, out_weight, preferred_element_type=jnp.float32)
    mixed_output = lax.psum_scatter(
        partial_terms.astype(jnp.bfloat16), "head", scatter_dimension=1, tiled=True
    )
    grad_attention = jnp.einsum(
        "td,fd->tf", cotangent, out_weight, preferred_element_type=jnp.float32
    ).astype(jnp.bfloat16)
    grad_groups = grad_attention.reshape(rounds, group_size, block_rows, feature_width)
    paired_width = 2 * feature_width
    side_numbers = jnp.arange(side_count, dtype=jnp.int32)

    def backward(state_pair, inputs):
        extended_sum, strided_sum = state_pair
        position, query_group, index_rows, grad_group, logsum = inputs
        key_list = gather_lists(extended, strided_blocks, index_rows, group_size, block_rows)
        scores = scores_for(query_group, key_list)
        probability = jnp.exp(scores - logsum[..., None])
        weights = probability.astype(jnp.bfloat16)
        query_heads = split_heads(query_group, HD)
        grad_heads = split_heads(grad_group, HD)
        key_heads = split_heads(key_list[..., :feature_width], HD)
        value_heads = split_heads(key_list[..., feature_width:], HD)
        grad_weights = jnp.einsum(
            "gqhd,gkhd->ghqk", grad_heads, value_heads, preferred_element_type=jnp.float32
        )
        row_delta = jnp.sum(probability * grad_weights, axis=-1, keepdims=True)
        grad_scores = (probability * (grad_weights - row_delta) * score_scale).astype(jnp.bfloat16)
        grad_query = jnp.einsum(
            "ghqk,gkhd->gqhd", grad_scores, key_heads, preferred_element_type=jnp.float32
        )
        grad_query = grad_query.astype(jnp.bfloat16).reshape(group_size * block_rows, feature_width)
        key_terms = jnp.einsum(
            "ghqk,gqhd->gkhd", grad_scores, query_heads, preferred_element_type=jnp.float32
        )
        value_terms = jnp.einsum(
            "ghqk,gqhd->gkhd", weights, grad_heads, preferred_element_type=jnp.float32
        )
        slot_terms = jnp.concatenate(
            [
                key_terms.reshape(group_size, -1, feature_width),
                value_terms.reshape(group_size, -1, feature_width),
            ],
            axis=2,
        )
        window = slot_terms[:, : 3 * block_rows].reshape(group_size, 3, block_rows, paired_width)
        window_sum = (
            jnp.pad(window[:, 0], ((0, 2), (0, 0), (0, 0)))
            + jnp.pad(window[:, 1], ((1, 1), (0, 0), (0, 0)))
            + jnp.pad(window[:, 2], ((2, 0), (0, 0), (0, 0)))
        )
        current = extended_sum
        extended_sum = current + window_sum.reshape(-1, paired_width)
        picked = slot_terms[:, 3 * block_rows :].reshape(-1, block_rows * paired_width)
        selector = (side_numbers[:, None] == index_rows).astype(jnp.float32)
        strided_sum = strided_sum + jnp.dot(
            selector, picked, precision=lax.Precision.HIGHEST, preferred_element_type=jnp.float32
        )
        return ((extended_sum, strided_sum), grad_query)

    start_state = (
        jnp.zeros((tokens + 2 * block_rows, paired_width), jnp.float32),
        jnp.zeros((side_count, block_rows * paired_width), jnp.float32),
    )
    final_state, grad_parts = lax.scan(
        backward, start_state, (numbers, query_groups, index_groups, grad_groups, logsums)
    )
    extended_sum, strided_sum = final_state
    rim_rows = jnp.concatenate([extended_sum[:block_rows], extended_sum[-block_rows:]], axis=0)
    returned = padded(rim_rows.astype(jnp.bfloat16), (("seq", 0),), block_rows).astype(
        rim_rows.dtype
    )
    own_grads = extended_sum[block_rows:-block_rows]
    own_grads = own_grads.at[:block_rows].add(returned[:block_rows])
    own_grads = own_grads.at[tokens - block_rows :].add(returned[3 * block_rows :])
    strided_mine = lax.psum_scatter(
        strided_sum.reshape(side_count * block_rows, paired_width),
        "seq",
        scatter_dimension=0,
        tiled=True,
    )
    own_grads = own_grads.at[: strided_mine.shape[0]].add(strided_mine)
    grad_queries = grad_parts.reshape(tokens, feature_width)
    grad_keys = own_grads[:, :feature_width].astype(jnp.bfloat16)
    grad_values = own_grads[:, feature_width:].astype(jnp.bfloat16)
    return (mixed_output, grad_queries, grad_keys, grad_values)


def solution(mesh):
    in_specs = (
        P("seq", "head"),
        P("seq", "head"),
        P("seq", "head"),
        P("head", None),
        P("seq", None),
        P("seq", None),
    )
    out_specs = (P("seq", "head"), P("seq", "head"), P("seq", "head"), P("seq", "head"))
    return jax.shard_map(shards, mesh=mesh, in_specs=in_specs, out_specs=out_specs, check_vma=False)
```

profile of v0, /device:TPU:0, one launch (start us, length us, event | category | flops | bytes accessed | tf_op | source)
XLA Modules:
  0.0 99.1 jit_solution(5179649982151655352)
XLA Ops:
  7.2 0.8 constant_dynamic-update-slice_fusion.1
  8.1 3.4 %collective-permute-start.1 = (bf16[128,256]{1,0:T(8,128)(2,1)S(1)}, bf16[128,256]{1,0:T(8,128)(2,1)S(1)}, u32[]{:S(2)}, u32[]{:S(2)}) collective-permute-start(bf16[128,256]{1,0:T(8,128)(2,1)S(1)} %constant_dynamic-update-slice_fusion), channel_id=1, source_target_pairs={{4,0},{8,4},{12,8},{16,12},{20,16},{24,20},{28,24},{0,28},{5,1},{9... | collective-permute-start | bytes 196616 | tf_op jit(solution)/shard_map/ppermute | solution.py:20
  11.5 1.3 %convolution_convert_fusion.2 = bf16[128,128]{1,0:T(8,128)(2,1)S(1)} fusion(bf16[128,2048]{1,0:T(8,128)(2,1)} %param.21, bf16[128,2048]{1,0:T(8,128)(2,1)S(1)} %copy-done), kind=kOutput, calls=%fused_computation.6 | convolution fusion | flops 67125248 | bytes 1081344 | tf_op jit(solution)/shard_map/td,fd->tf/dot_general | solution.py:88
  12.9 9.2 %all_gather.3 = bf16[256,256]{1,0:T(8,128)(2,1)S(1)} all-gather(bf16[32,256]{1,0:T(8,128)(2,1)S(1)} %slice.155), channel_id=1, replica_groups=mesh['seq'=8,'head'=4] {'seq'}, dimensions={0}, use_global_device_ids=true | all-gather | bytes 147456 | tf_op jit(solution)/shard_map/all_gather | solution.py:49
  22.1 0.6 gather_fusion
  22.7 0.1 pad_maximum_fusion.1
  22.8 0.7 copy-done.3
  23.5 0.4 fusion.15
  23.8 0.2 exponential_reduce_fusion
  24.1 0.4 fusion.2
  24.4 0.3 convolution_bitcast_fusion
  24.7 0.2 fusion.4
  24.9 0.3 convolution_bitcast_fusion.1
  25.2 0.4 copy-done.1
  25.7 0.8 pad_maximum_fusion.2
  26.4 0.1 pad_maximum_fusion
  26.6 1.2 %copy.18 = f32[1,384,256]{2,1,0:T(8,128)S(1)} copy(f32[1,384,256]{1,2,0:T(8,128)} %pad_maximum_fusion.2) | data formatting | bytes 786432 | tf_op jit(solution)/shard_map/while/body/eval_jaxpr/slice | solution.py:128
  27.7 1.3 %copy.19 = f32[1,1024,256]{2,1,0:T(8,128)} copy(f32[1,1024,256]{1,2,0:T(8,128)S(1)} %pad_maximum_fusion) | data formatting | bytes 2097152 | tf_op jit(solution)/shard_map/while/body/eval_jaxpr/slice | solution.py:136
  29.0 1.4 %reshape.261 = f32[8,32768]{1,0:T(8,128)S(1)} reshape(f32[1,1024,256]{2,1,0:T(8,128)} %copy.19) | data formatting | bytes 2097152 | tf_op jit(solution)/shard_map/while/body/eval_jaxpr/reshape | solution.py:136
  30.5 1.3 %fusion.8 = f32[2,32768]{1,0:T(2,128)} fusion(f32[8,32768]{1,0:T(8,128)S(1)} %reshape.261, s32[8]{0:T(128)S(1)} %bitcast.98), kind=kOutput, calls=%fused_computation.42 | convolution fusion | flops 6291472 | bytes 1310752 | tf_op jit(solution)/shard_map/while/body/eval_jaxpr/dot_general | solution.py:138
  31.7 1.9 %reshape.262 = f32[256,256]{1,0:T(8,128)} reshape(f32[2,32768]{1,0:T(2,128)} %fusion.8) | data formatting | bytes 524288 | tf_op jit(solution)/shard_map/reshape | solution.py:159
  33.6 0.0 reduce-scatter.3.cloned.1.call-start
  33.7 1.4 %convolution_convert_fusion = bf16[128,2048]{1,0:T(8,128)(2,1)} fusion(bf16[128,2048]{1,0:T(8,128)(2,1)S(1)} %copy-done, bf16[1,1408,256]{2,1,0:T(8,128)(2,1)S(1)} %bitcast.90, f32[1408,128]{1,0:T(8,128)S(1)} %get-tuple-element.128, f32[128]{0:T(128)S(1)} %log_add_fusion), kind=kOutput, calls=%fused_computation.4 | convolution fusion | flops 113885184 | bytes 2130432 | tf_op jit(solution)/shard_map/dot_general | solution.py:84
  35.2 1.5 %collective-permute-start.3 = (bf16[128,256]{1,0:T(8,128)(2,1)S(1)}, bf16[128,256]{1,0:T(8,128)(2,1)S(1)}, u32[]{:S(2)}, u32[]{:S(2)}) collective-permute-start(bf16[128,256]{1,0:T(8,128)(2,1)S(1)} %get-tuple-element.124), channel_id=1, source_target_pairs={{4,0},{8,4},{12,8},{16,12},{20,16},{24,20},{28,24},{0,28},{5,1},{9... | collective-permute-start | bytes 196616 | tf_op jit(solution)/shard_map/ppermute | solution.py:20
  36.7 0.3 fusion.1
  37.0 0.7 copy.20
  37.7 1.5 %collective-permute-done.3 = bf16[128,256]{1,0:T(8,128)(2,1)S(1)} collective-permute-done((bf16[128,256]{1,0:T(8,128)(2,1)S(1)}, bf16[128,256]{1,0:T(8,128)(2,1)S(1)}, u32[]{:S(2)}, u32[]{:S(2)}) %collective-permute-start.3) | collective-permute-done | bytes 65568 | tf_op jit(solution)/shard_map/ppermute | solution.py:20
  39.2 2.1 %collective-permute-done.2 = bf16[128,256]{1,0:T(8,128)(2,1)S(1)} collective-permute-done((bf16[128,256]{1,0:T(8,128)(2,1)S(1)}, bf16[128,256]{1,0:T(8,128)(2,1)S(1)}, u32[]{:S(2)}, u32[]{:S(2)}) %collective-permute-start.2) | collective-permute-done | bytes 65568 | tf_op jit(solution)/shard_map/ppermute | solution.py:18
  41.3 26.4 %reduce-scatter.5.cloned.1.call-done = f32[32,256]{1,0:T(8,128)} async-done(((f32[256,256]{1,0:T(8,128)}), f32[32,256]{1,0:T(8,128)}) %reduce-scatter.5.cloned.1.call-update) | async-done | bytes 32784 | tf_op jit(solution)/shard_map/reduce_scatter | solution.py:158
  67.7 0.8 fusion.7
  68.5 0.6 fusion.14
  69.1 23.2 %reduce-scatter.3.cloned.1.call-done = bf16[128,512]{1,0:T(8,128)(2,1)} async-done(((bf16[128,2048]{1,0:T(8,128)(2,1)}), bf16[128,512]{1,0:T(8,128)(2,1)}) %reduce-scatter.3.cloned.1.call-update) | async-done | bytes 131088 | tf_op jit(solution)/shard_map/reduce_scatter | solution.py:85
  (27 shorter events, 0.3 us)
Async XLA Ops:
  7.2 4.3 %copy-start = (bf16[128,2048]{1,0:T(8,128)(2,1)S(1)}, bf16[128,2048]{1,0:T(8,128)(2,1)}, u32[]{:S(2)}) copy-start(bf16[128,2048]{1,0:T(8,128)(2,1)} %param.19) | copy-start | bytes 1572868
  7.2 0.9 copy-start.4
  7.2 60.5 %reduce-scatter.5.cloned.1.call-start = ((), (), s32[]{:S(2)}) async-start(), calls=%async_computation.3 | async-start | bytes 294912 | tf_op jit(solution)/shard_map/reduce_scatter | solution.py:158
  8.1 3.4 %copy-start.5 = (s32[1,8]{1,0:T(1,128)S(1)}, s32[1,8]{1,0:T(1,128)}, u32[]{:S(2)}) copy-start(s32[1,8]{1,0:T(1,128)} %param.20) | copy-start | bytes 100
  8.1 14.6 %collective-permute-start.1 = (bf16[128,256]{1,0:T(8,128)(2,1)S(1)}, bf16[128,256]{1,0:T(8,128)(2,1)S(1)}, u32[]{:S(2)}, u32[]{:S(2)}) collective-permute-start(bf16[128,256]{1,0:T(8,128)(2,1)S(1)} %constant_dynamic-update-slice_fusion), channel_id=1, source_target_pairs={{4,0},{8,4},{12,8},{16,12},{20,16},{24,20},{28,24},{0,28},{5,1},{9... | collective-permute-start | bytes 196616 | tf_op jit(solution)/shard_map/ppermute | solution.py:20
  11.5 11.2 %collective-permute-start = (bf16[128,256]{1,0:T(8,128)(2,1)S(1)}, bf16[128,256]{1,0:T(8,128)(2,1)S(1)}, u32[]{:S(2)}, u32[]{:S(2)}) collective-permute-start(bf16[128,256]{1,0:T(8,128)(2,1)S(1)} %constant_dynamic-update-slice_fusion), channel_id=1, source_target_pairs={{0,4},{4,8},{8,12},{12,16},{16,20},{20,24},{24,28},{28,0},{1,5},{5... | collective-permute-start | bytes 196616 | tf_op jit(solution)/shard_map/ppermute | solution.py:18
  22.7 0.8 copy-start.3
  24.9 0.8 copy-start.1
  33.6 58.6 %reduce-scatter.3.cloned.1.call-start = ((), (), s32[]{:S(2)}) async-start(), calls=%async_computation.2 | async-start | bytes 655360 | tf_op jit(solution)/shard_map/reduce_scatter | solution.py:85
  35.2 1.5 %copy-start.2 = (bf16[128,1408]{0,1:T(8,128)(2,1)S(1)}, bf16[128,1408]{0,1:T(8,128)(2,1)}, u32[]{:S(2)}) copy-start(bf16[128,1408]{0,1:T(8,128)(2,1)} %copy-done.1) | copy-start | bytes 1081348
  35.2 3.9 %collective-permute-start.3 = (bf16[128,256]{1,0:T(8,128)(2,1)S(1)}, bf16[128,256]{1,0:T(8,128)(2,1)S(1)}, u32[]{:S(2)}, u32[]{:S(2)}) collective-permute-start(bf16[128,256]{1,0:T(8,128)(2,1)S(1)} %get-tuple-element.124), channel_id=1, source_target_pairs={{4,0},{8,4},{12,8},{16,12},{20,16},{24,20},{28,24},{0,28},{5,1},{9... | collective-permute-start | bytes 196616 | tf_op jit(solution)/shard_map/ppermute | solution.py:20
  36.7 4.6 %collective-permute-start.2 = (bf16[128,256]{1,0:T(8,128)(2,1)S(1)}, bf16[128,256]{1,0:T(8,128)(2,1)S(1)}, u32[]{:S(2)}, u32[]{:S(2)}) collective-permute-start(bf16[128,256]{1,0:T(8,128)(2,1)S(1)} %get-tuple-element.123), channel_id=1, source_target_pairs={{0,4},{4,8},{8,12},{12,16},{16,20},{20,24},{24,28},{28,0},{1,5},{5... | collective-permute-start | bytes 196616 | tf_op jit(solution)/shard_map/ppermute | solution.py:18
Sparse Core Ops, SparseCore 0:
  33.8 33.8 reduce-scatter.4
  70.6 21.5 reduce-scatter.2
where the time goes:
time: 99.6 us; the launch traced here: 99.1 us
  waiting for transfers between devices  53.2 us (53%)
  between operations  14.2 us (14%)
  local copies, waits for them, and re-layouts  9.69 us (10%)
  blocking collectives  9.25 us (9%)
  matrix products  5.65 us (6%)
  starting transfers between devices  4.93 us (5%)
  other arithmetic  2.19 us (2%)
    reduce_scatter x1, waiting for transfers between devices, shards(): lax.psum_scatter(strided_sum.reshape(side_count * block_rows, paired_widt...  26.4 us
    reduce_scatter x1, waiting for transfers between devices, shards(): lax.psum_scatter(partial_terms.astype(jnp.bfloat16), 'head', scatter_dime...  23.2 us
    all_gather x1, blocking collectives, shards(): lax.all_gather(paired[:STRIDE_ROWS], 'seq', axis=0, tiled=True)  9.25 us
    ppermute x2, starting transfers between devices, padded(): lax.ppermute(head, axis, [((i + 1) % count, i) for i in range(count)])  4.84 us
    unnamed x14, local copies, waits for them, and re-layouts  2.67 us
    ppermute x2, waiting for transfers between devices, padded(): lax.ppermute(tail, axis, [(i, (i + 1) % count) for i in range(count)])  2.11 us
  transfers between devices with their start and end apart: 6, of which 4 were waited for; matrix products, arithmetic and copies ran while one was open for 6% of the time, Pallas kernels for 0%

commit v1 on v0

v1 whole, which is shorter than its diff:
```python
import jax
import jax.numpy as jnp
from jax import lax
from jax.experimental import pallas as pl
from jax.experimental.pallas import tpu as pltpu
from jax.sharding import PartitionSpec as P

HD = 128
BLK = 128
STRIDE_ROWS = 32
SCALE = HD ** (-0.5)
LOG2E = 1.4426950408889634
ABSENT = -1e30
VMEM = pl.BlockSpec(memory_space=pltpu.VMEM)
SMEM = pl.BlockSpec(memory_space=pltpu.SMEM)


def shift(array, axis, step):
    count = lax.axis_size(axis)
    return lax.ppermute(array, axis, [(i, (i + step) % count) for i in range(count)])


def dot_nt(a, b):
    return lax.dot_general(a, b, (((1,), (1,)), ((), ())), preferred_element_type=jnp.float32)


def dot_nn(a, b):
    return lax.dot_general(a, b, (((1,), (0,)), ((), ())), preferred_element_type=jnp.float32)


def dot_tn(a, b):
    return lax.dot_general(a, b, (((0,), (0,)), ((), ())), preferred_element_type=jnp.float32)


def attend_kernel(index_ref, q_ref, own_ref, left_ref, right_ref, side_ref, grad_ref,
                  att_ref, dq_ref, own_sum_ref, to_left_ref, to_right_ref, to_side_ref):
    side_count = side_ref.shape[0] // BLK
    slots = index_ref.shape[1]
    picks = [index_ref[0, i] for i in range(slots)]
    counts = []
    for j in range(side_count):
        total = jnp.int32(0)
        for pick in picks:
            total = total + jnp.where(pick == j, 1, 0)
        counts.append(total)
    parts = [(own_ref, 0, None), (left_ref, 0, None), (right_ref, 0, None)]
    parts += [(side_ref, j * BLK, counts[j]) for j in range(side_count)]
    keys = [ref[r:r + BLK, :HD] for ref, r, _ in parts]
    values = [ref[r:r + BLK, HD:] for ref, r, _ in parts]
    q = q_ref[...]
    grad = grad_ref[...]

    raw = []
    for k, (_, _, count) in zip(keys, parts):
        s = dot_nt(q, k)
        if count is not None:
            s = s + jnp.where(count > 0, 0.0, ABSENT)
        raw.append(s)
    top = raw[0]
    for s in raw[1:]:
        top = jnp.maximum(top, s)
    top = jnp.max(top, axis=1, keepdims=True)
    terms = []
    total = None
    for s, (_, _, count) in zip(raw, parts):
        e = jnp.exp2((s - top) * (SCALE * LOG2E))
        if count is not None:
            e = e * count.astype(jnp.float32)
        terms.append(e)
        total = e if total is None else total + e
    inverse = 1.0 / jnp.sum(total, axis=1, keepdims=True)
    probability = [e * inverse for e in terms]
    weights = [p.astype(jnp.bfloat16) for p in probability]
    att = None
    for w, v in zip(weights, values):
        term = dot_nn(w, v)
        att = term if att is None else att + term
    att_ref[...] = att.astype(jnp.bfloat16)

    grad_weights = [dot_nt(grad, v) for v in values]
    delta = None
    for p, g in zip(probability, grad_weights):
        delta = p * g if delta is None else delta + p * g
    delta = jnp.sum(delta, axis=1, keepdims=True)
    grad_scores = [(p * (g - delta) * SCALE).astype(jnp.bfloat16)
                   for p, g in zip(probability, grad_weights)]
    dq = None
    for g, k in zip(grad_scores, keys):
        term = dot_nn(g, k)
        dq = term if dq is None else dq + term
    dq_ref[...] = dq.astype(jnp.bfloat16)

    outs = [(own_sum_ref, 0), (to_left_ref, 0), (to_right_ref, 0)]
    outs += [(to_side_ref, j * BLK) for j in range(side_count)]
    for (ref, r), g, w in zip(outs, grad_scores, weights):
        ref[r:r + BLK, :HD] = dot_tn(g, q).astype(ref.dtype)
        ref[r:r + BLK, HD:] = dot_tn(w, grad).astype(ref.dtype)


def attend(index, q, own, left, right, side, grad):
    bf16 = jnp.bfloat16
    return pl.pallas_call(
        attend_kernel,
        out_shape=(
            jax.ShapeDtypeStruct((BLK, HD), bf16),
            jax.ShapeDtypeStruct((BLK, HD), bf16),
            jax.ShapeDtypeStruct((BLK, 2 * HD), jnp.float32),
            jax.ShapeDtypeStruct((BLK, 2 * HD), bf16),
            jax.ShapeDtypeStruct((BLK, 2 * HD), bf16),
            jax.ShapeDtypeStruct(side.shape, bf16),
        ),
        in_specs=[SMEM] + [VMEM] * 6,
        out_specs=(VMEM,) * 6,
        compiler_params=pltpu.CompilerParams(vmem_limit_bytes=40 * 1024 * 1024),
        name="attend",
    )(index, q, own, left, right, side, grad)


def prepare_kernel(me_ref, cot_ref, w_ref, grad_ref, *slice_refs):
    grad_ref[...] = dot_nt(cot_ref[...], w_ref[...]).astype(grad_ref.dtype)
    heads = len(slice_refs)
    width = slice_refs[0].shape[1]
    me = me_ref[0]
    for s, ref in enumerate(slice_refs):
        target = lax.rem(me + s, heads)
        start = pl.multiple_of(target * width, width)
        ref[...] = w_ref[:, pl.ds(start, width)]


def prepare(cotangent, out_weight, heads):
    me = lax.axis_index("head").astype(jnp.int32).reshape(1)
    width = out_weight.shape[1] // heads
    return pl.pallas_call(
        prepare_kernel,
        out_shape=(jax.ShapeDtypeStruct((BLK, HD), jnp.bfloat16),)
        + (jax.ShapeDtypeStruct((HD, width), jnp.bfloat16),) * heads,
        in_specs=[SMEM, VMEM, VMEM],
        out_specs=(VMEM,) * (1 + heads),
        compiler_params=pltpu.CompilerParams(vmem_limit_bytes=40 * 1024 * 1024),
        name="prepare",
    )(me, cotangent, out_weight)


def finish_kernel(heads, *refs):
    att_refs = refs[:heads]
    w_refs = refs[heads:2 * heads]
    own_ref, left_ref, right_ref, side_ref, mixed_ref, dk_ref, dv_ref = refs[2 * heads:]
    mixed = None
    for a, w in zip(att_refs, w_refs):
        term = dot_nn(a[...], w[...])
        mixed = term if mixed is None else mixed + term
    mixed_ref[...] = mixed.astype(mixed_ref.dtype)
    total = own_ref[...] + left_ref[...].astype(jnp.float32) + right_ref[...].astype(jnp.float32)
    lead = total[:STRIDE_ROWS]
    for i in range(side_ref.shape[0] // STRIDE_ROWS):
        lead = lead + side_ref[i * STRIDE_ROWS:(i + 1) * STRIDE_ROWS].astype(jnp.float32)
    for ref, c in ((dk_ref, 0), (dv_ref, HD)):
        ref[:STRIDE_ROWS] = lead[:, c:c + HD].astype(ref.dtype)
        ref[STRIDE_ROWS:] = total[STRIDE_ROWS:, c:c + HD].astype(ref.dtype)


def finish(attentions, slices, own, left, right, side):
    heads = len(attentions)
    width = slices[0].shape[1]

    def body(*refs):
        finish_kernel(heads, *refs)

    return pl.pallas_call(
        body,
        out_shape=(
            jax.ShapeDtypeStruct((BLK, width), jnp.bfloat16),
            jax.ShapeDtypeStruct((BLK, HD), jnp.bfloat16),
            jax.ShapeDtypeStruct((BLK, HD), jnp.bfloat16),
        ),
        in_specs=[VMEM] * (2 * heads + 4),
        out_specs=(VMEM,) * 3,
        compiler_params=pltpu.CompilerParams(vmem_limit_bytes=40 * 1024 * 1024),
        name="finish",
    )(*attentions, *slices, own, left, right, side)


def shards(queries, key_rows, value_rows, out_weight, strided_index, cotangent):
    seq = lax.axis_size("seq")
    heads = lax.axis_size("head")
    own = jnp.concatenate([key_rows, value_rows], axis=1)
    lead = jnp.broadcast_to(own[None, :STRIDE_ROWS], (seq, STRIDE_ROWS, 2 * HD))
    left = shift(own, "seq", 1)
    right = shift(own, "seq", -1)
    side = lax.all_to_all(lead, "seq", 0, 0).reshape(seq * STRIDE_ROWS, 2 * HD)
    grad, *slices = prepare(cotangent, out_weight, heads)
    slices = [slices[0]] + [shift(slices[s], "head", s) for s in range(1, heads)]
    att, dq, own_sum, to_left, to_right, to_side = attend(
        strided_index, queries, own, left, right, side, grad
    )
    attentions = [att] + [shift(att, "head", s) for s in range(1, heads)]
    from_right = shift(to_left, "seq", -1)
    from_left = shift(to_right, "seq", 1)
    from_side = lax.all_to_all(
        to_side.reshape(seq, STRIDE_ROWS, 2 * HD), "seq", 0, 0
    ).reshape(seq * STRIDE_ROWS, 2 * HD)
    mixed, dk, dv = finish(attentions, slices, own_sum, from_left, from_right, from_side)
    return (mixed, dq, dk, dv)


def solution(mesh):
    in_specs = (
        P("seq", "head"),
        P("seq", "head"),
        P("seq", "head"),
        P("head", None),
        P("seq", None),
        P("seq", None),
    )
    out_specs = (P("seq", "head"), P("seq", "head"), P("seq", "head"), P("seq", "head"))
    return jax.shard_map(shards, mesh=mesh, in_specs=in_specs, out_specs=out_specs, check_vma=False)
```

time: 99.6 us -> 35.2 us (0.35)
  waiting for transfers between devices: 53.2 us -> 4.97 us
  starting transfers between devices: 4.93 us -> 22.4 us
  between operations: 14.2 us -> 0.72 us
  blocking collectives: 9.25 us -> 0 us
  local copies, waits for them, and re-layouts: 9.69 us -> 3.2 us
  matrix products: 5.65 us -> 0 us
  Pallas kernels: 0 us -> 3.51 us
  other arithmetic: 2.19 us -> 0 us
    reduce_scatter x2 -> x0, waiting for transfers between devices: 49.6 us -> none  [the longest x1 26.4 us: shards(): lax.psum_scatter(strided_sum.reshape(side_count * block_rows, paired_widt...]
    all_gather x1 -> x0, blocking collectives: 9.25 us -> none  [shards(): lax.all_gather(paired[:STRIDE_ROWS], 'seq', axis=0, tiled=True)]
    ppermute x4 -> x10, starting transfers between devices: 4.85 us -> 13.9 us  [shift(): lax.ppermute(array, axis, [(i, (i + step) % count) for i in range(count)])]
    all_to_all x0 -> x2, starting transfers between devices: none -> 8.54 us  [the longest x1 5.17 us: shards(): side = lax.all_to_all(lead, 'seq', 0, 0).reshape(seq * STRIDE_ROWS, 2 * HD)]
    dot_general x8 -> x0, matrix products: 5.65 us -> none  [the longest x1 1.4 us: shards(): jnp.dot(attention, out_weight, preferred_element_type=jnp.float32)]
    pallas_call x0 -> x3, Pallas kernels: none -> 3.51 us  [the longest x1 2.27 us: attend(): pl.pallas_call(attend_kernel, out_shape=(jax.ShapeDtypeStruct((BLK, HD),...]
    reshape x2 -> x0, local copies, waits for them, and re-layouts: 3.29 us -> none  [the longest x1 1.87 us: shards(): strided_sum.reshape(side_count * block_rows, paired_width)]
    slice x5 -> x1, local copies, waits for them, and re-layouts: 3.11 us -> 0.01 us  [shards(): lead = jnp.broadcast_to(own[None, :STRIDE_ROWS], (seq, STRIDE_ROWS, 2 * HD))]
  transfers between devices with their start and end apart: 6 -> 12, of which waited for: 4 -> 3; matrix products, arithmetic and copies ran while one was open for 6% -> 0% of each run, Pallas kernels for 0% -> 7%
where the time goes in v1:
time: 35.2 us; the launch traced here: 34.8 us
  starting transfers between devices  22.4 us (64%)
  waiting for transfers between devices  4.97 us (14%)
  Pallas kernels  3.51 us (10%)
  local copies, waits for them, and re-layouts  3.2 us (9%)
  between operations  0.72 us (2%)
    ppermute x10, starting transfers between devices, shift(): lax.ppermute(array, axis, [(i, (i + step) % count) for i in range(count)])  13.9 us
    all_to_all x1, starting transfers between devices, shards(): side = lax.all_to_all(lead, 'seq', 0, 0).reshape(seq * STRIDE_ROWS, 2 * HD)  5.17 us
    ppermute x10, waiting for transfers between devices, shift(): lax.ppermute(array, axis, [(i, (i + step) % count) for i in range(count)])  4.96 us
    all_to_all x1, starting transfers between devices, shards(): lax.all_to_all(to_side.reshape(seq, STRIDE_ROWS, 2 * HD), 'seq', 0, 0)  3.37 us
    unnamed x11, local copies, waits for them, and re-layouts  2.52 us
    pallas_call x1, Pallas kernels, attend(): pl.pallas_call(attend_kernel, out_shape=(jax.ShapeDtypeStruct((BLK, HD),...  2.27 us
    pallas_call x1, Pallas kernels, finish(): pl.pallas_call(body, out_shape=(jax.ShapeDtypeStruct((BLK, width), jnp.bf...  0.95 us
  transfers between devices with their start and end apart: 12, of which 3 were waited for; matrix products, arithmetic and copies ran while one was open for 0% of the time, Pallas kernels for 7%

profile of v1, /device:TPU:0, one launch (start us, length us, event | category | flops | bytes accessed | tf_op | source)
XLA Modules:
  0.0 34.8 jit_solution(8003186797571058397)
XLA Ops:
  0.7 0.8 %constant_dynamic-update-slice_fusion.1 = bf16[128,256]{1,0:T(8,128)(2,1)S(1)} fusion(bf16[128,128]{1,0:T(8,128)(2,1)} %param.7), kind=kLoop, calls=%fused_computation.1 | loop fusion | bytes 65536
  1.5 0.7 %broadcast_in_dim.2 = bf16[8,32,256]{2,1,0:T(8,128)(2,1)} broadcast(bf16[32,256]{1,0:T(8,128)(2,1)S(1)} %slice.4), dimensions={1,2} | broadcast | bytes 147456 | tf_op jit(solution)/shard_map/broadcast_in_dim | solution.py:187
  2.2 5.2 %all-to-all-start = ((bf16[8,32,256]{2,1,0:T(8,128)(2,1)}), bf16[8,32,256]{2,1,0:T(8,128)(2,1)S(1)}, u32[]{:S(2)}, u32[]{:S(2)}) async-start(bf16[8,32,256]{2,1,0:T(8,128)(2,1)} %broadcast_in_dim.2), calls=%async_computation | async-start | bytes 262144 | tf_op jit(solution)/shard_map/all_to_all | solution.py:190
  7.3 2.7 %collective-permute-start.1 = (bf16[128,256]{1,0:T(8,128)(2,1)S(1)}, bf16[128,256]{1,0:T(8,128)(2,1)S(1)}, u32[]{:S(2)}, u32[]{:S(2)}) collective-permute-start(bf16[128,256]{1,0:T(8,128)(2,1)S(1)} %constant_dynamic-update-slice_fusion.own_ref), channel_id=1, source_target_pairs={{0,28},{4,0},{8,4},{12,8},{16,12},{20,16},{24,20},{28,24},{1,29},{... | collective-permute-start | bytes 196616 | tf_op jit(solution)/shard_map/ppermute | solution.py:20
  10.0 0.0 collective-permute-start
  10.0 1.0 %copy-done.1 = bf16[128,2048]{1,0:T(8,128)(2,1)S(1)} copy-done((bf16[128,2048]{1,0:T(8,128)(2,1)S(1)}, bf16[128,2048]{1,0:T(8,128)(2,1)}, u32[]{:S(2)}) %copy-start.1) | copy-done | bytes 524312
  11.1 0.3 prepare.1
  11.4 1.6 %collective-permute-start.5 = (bf16[128,512]{1,0:T(8,128)(2,1)S(1)}, bf16[128,512]{1,0:T(8,128)(2,1)S(1)}, u32[]{:S(2)}, u32[]{:S(2)}) collective-permute-start(bf16[128,512]{1,0:T(8,128)(2,1)S(1)} %get-tuple-element.21), channel_id=1, source_target_pairs={{0,1},{1,2},{2,3},{3,0},{4,5},{5,6},{6,7},{7,4},{8,9},{9,10},{10,1... | collective-permute-start | bytes 393224 | tf_op jit(solution)/shard_map/ppermute | solution.py:20
  13.0 2.6 %collective-permute-start.6 = (bf16[128,512]{1,0:T(8,128)(2,1)S(1)}, bf16[128,512]{1,0:T(8,128)(2,1)S(1)}, u32[]{:S(2)}, u32[]{:S(2)}) collective-permute-start(bf16[128,512]{1,0:T(8,128)(2,1)S(1)} %get-tuple-element.22), channel_id=1, source_target_pairs={{0,2},{1,3},{2,0},{3,1},{4,6},{5,7},{6,4},{7,5},{8,10},{9,11},{10,... | collective-permute-start | bytes 393224 | tf_op jit(solution)/shard_map/ppermute | solution.py:20
  15.6 1.3 %collective-permute-start.7 = (bf16[128,512]{1,0:T(8,128)(2,1)S(1)}, bf16[128,512]{1,0:T(8,128)(2,1)S(1)}, u32[]{:S(2)}, u32[]{:S(2)}) collective-permute-start(bf16[128,512]{1,0:T(8,128)(2,1)S(1)} %get-tuple-element.23), channel_id=1, source_target_pairs={{0,3},{1,0},{2,1},{3,2},{4,7},{5,4},{6,5},{7,6},{8,11},{9,8},{10,9... | collective-permute-start | bytes 393224 | tf_op jit(solution)/shard_map/ppermute | solution.py:20
  16.9 0.0 collective-permute-done.1.right_ref
  16.9 0.0 collective-permute-done.left_ref
  17.0 0.0 all-to-all-done
  17.0 0.0 copy-start.3
  17.0 0.6 %copy-done.3 = s32[1,8]{1,0:T(1,128)S(1)} copy-done((s32[1,8]{1,0:T(1,128)S(1)}, s32[1,8]{1,0:T(1,128)}, u32[]{:S(2)}) %copy-start.3) | copy-done | bytes 56
  17.6 2.3 %attend.1 = (bf16[128,128]{1,0:T(8,128)(2,1)S(1)}, bf16[128,128]{1,0:T(8,128)(2,1)}, f32[128,256]{1,0:T(8,128)S(1)}, bf16[128,256]{1,0:T(8,128)(2,1)S(1)}, bf16[...) custom-call(s32[1,8]{1,0:T(1,128)S(1)} %copy-done.3, bf16[128,128]{1,0:T(8,128)(2,1)S(1)} %copy-done.2, ...), custom_call_target="tpu_custom_call" | custom-call | tf_op jit(solution)/shard_map/attend/pallas_call | solution.py:102
  19.9 3.4 %all-to-all-start.1 = ((bf16[8,32,256]{2,1,0:T(8,128)(2,1)}), bf16[8,32,256]{2,1,0:T(8,128)(2,1)S(1)}, u32[]{:S(2)}, u32[]{:S(2)}) async-start(bf16[8,32,256]{2,1,0:T(8,128)(2,1)} %bitcast.2), calls=%async_computation.1 | async-start | bytes 262144 | tf_op jit(solution)/shard_map/all_to_all | solution.py:199
  23.3 0.4 %collective-permute-start.8 = (bf16[128,256]{1,0:T(8,128)(2,1)S(1)}, bf16[128,256]{1,0:T(8,128)(2,1)S(1)}, u32[]{:S(2)}, u32[]{:S(2)}) collective-permute-start(bf16[128,256]{1,0:T(8,128)(2,1)S(1)} %get-tuple-element.25), channel_id=1, source_target_pairs={{0,4},{4,8},{8,12},{12,16},{16,20},{20,24},{24,28},{28,0},{1,5},{5... | collective-permute-start | bytes 196616 | tf_op jit(solution)/shard_map/ppermute | solution.py:20
  23.7 2.3 %collective-permute-start.9 = (bf16[128,256]{1,0:T(8,128)(2,1)S(1)}, bf16[128,256]{1,0:T(8,128)(2,1)S(1)}, u32[]{:S(2)}, u32[]{:S(2)}) collective-permute-start(bf16[128,256]{1,0:T(8,128)(2,1)S(1)} %get-tuple-element.26), channel_id=1, source_target_pairs={{0,28},{4,0},{8,4},{12,8},{16,12},{20,16},{24,20},{28,24},{1,29},{... | collective-permute-start | bytes 196616 | tf_op jit(solution)/shard_map/ppermute | solution.py:20
  26.0 0.0 collective-permute-done.5.refs_5_
  26.0 1.3 %collective-permute-start.4 = (bf16[128,128]{1,0:T(8,128)(2,1)S(1)}, bf16[128,128]{1,0:T(8,128)(2,1)S(1)}, u32[]{:S(2)}, u32[]{:S(2)}) collective-permute-start(bf16[128,128]{1,0:T(8,128)(2,1)S(1)} %get-tuple-element.19.refs_0_), channel_id=1, source_target_pairs={{0,3},{1,0},{2,1},{3,2},{4,7},{5,4},{6,5},{7,6},{8,11},{9,8},{10,9... | collective-permute-start | bytes 98312 | tf_op jit(solution)/shard_map/ppermute | solution.py:20
  27.2 0.0 collective-permute-done.6.refs_6_
  27.2 0.9 %collective-permute-start.3 = (bf16[128,128]{1,0:T(8,128)(2,1)S(1)}, bf16[128,128]{1,0:T(8,128)(2,1)S(1)}, u32[]{:S(2)}, u32[]{:S(2)}) collective-permute-start(bf16[128,128]{1,0:T(8,128)(2,1)S(1)} %get-tuple-element.19.refs_0_), channel_id=1, source_target_pairs={{0,2},{1,3},{2,0},{3,1},{4,6},{5,7},{6,4},{7,5},{8,10},{9,11},{10,... | collective-permute-start | bytes 98312 | tf_op jit(solution)/shard_map/ppermute | solution.py:20
  28.1 0.0 collective-permute-done.7.refs_7_
  28.1 0.8 %collective-permute-start.2 = (bf16[128,128]{1,0:T(8,128)(2,1)S(1)}, bf16[128,128]{1,0:T(8,128)(2,1)S(1)}, u32[]{:S(2)}, u32[]{:S(2)}) collective-permute-start(bf16[128,128]{1,0:T(8,128)(2,1)S(1)} %get-tuple-element.19.refs_0_), channel_id=1, source_target_pairs={{0,1},{1,2},{2,3},{3,0},{4,5},{5,6},{6,7},{7,4},{8,9},{9,10},{10,1... | collective-permute-start | bytes 98312 | tf_op jit(solution)/shard_map/ppermute | solution.py:20
  28.9 1.1 %collective-permute-done.4.refs_3_ = bf16[128,128]{1,0:T(8,128)(2,1)S(1)} collective-permute-done((bf16[128,128]{1,0:T(8,128)(2,1)S(1)}, bf16[128,128]{1,0:T(8,128)(2,1)S(1)}, u32[]{:S(2)}, u32[]{:S(2)}) %collective-permute-start.4) | collective-permute-done | bytes 32800 | tf_op jit(solution)/shard_map/ppermute | solution.py:20
  30.0 2.4 %collective-permute-done.3.refs_2_ = bf16[128,128]{1,0:T(8,128)(2,1)S(1)} collective-permute-done((bf16[128,128]{1,0:T(8,128)(2,1)S(1)}, bf16[128,128]{1,0:T(8,128)(2,1)S(1)}, u32[]{:S(2)}, u32[]{:S(2)}) %collective-permute-start.3) | collective-permute-done | bytes 32800 | tf_op jit(solution)/shard_map/ppermute | solution.py:20
  32.4 1.4 %collective-permute-done.2.refs_1_ = bf16[128,128]{1,0:T(8,128)(2,1)S(1)} collective-permute-done((bf16[128,128]{1,0:T(8,128)(2,1)S(1)}, bf16[128,128]{1,0:T(8,128)(2,1)S(1)}, u32[]{:S(2)}, u32[]{:S(2)}) %collective-permute-start.2) | collective-permute-done | bytes 32800 | tf_op jit(solution)/shard_map/ppermute | solution.py:20
  33.8 0.0 collective-permute-done.8.refs_9_
  33.8 0.0 collective-permute-done.9.refs_10_
  33.8 0.0 all-to-all-done.1
  33.8 0.9 %finish.1 = (bf16[128,512]{1,0:T(8,128)(2,1)}, bf16[128,128]{1,0:T(8,128)(2,1)}, bf16[128,128]{1,0:T(8,128)(2,1)}) custom-call(bf16[128,128]{1,0:T(8,128)(2,1)S(1)} %get-tuple-element.19.refs_0_, bf16[128,128]{1,0:T(8,128)(2,1)S(1)} %collective-permute-done.2.refs_1_, bf16[128,128]{1,0:T(8,128)(2,1)S(1)} %collective-permute-done.3.refs_2_, ...), custom_call_target="tpu_custom_call" | custom-call | tf_op jit(solution)/shard_map/finish/pallas_call | solution.py:169
  (9 shorter events, 0.0 us)
Async XLA Ops:
  0.6 0.8 %copy-start.4 = (bf16[128,128]{1,0:T(8,128)(2,1)S(1)}, bf16[128,128]{1,0:T(8,128)(2,1)}, u32[]{:S(2)}) copy-start(bf16[128,128]{1,0:T(8,128)(2,1)} %param.8) | copy-start | bytes 98308
  0.6 9.4 %copy-start = (bf16[128,2048]{1,0:T(8,128)(2,1)S(1)}, bf16[128,2048]{1,0:T(8,128)(2,1)}, u32[]{:S(2)}) copy-start(bf16[128,2048]{1,0:T(8,128)(2,1)} %cot_ref.1) | copy-start | bytes 1572868
  2.2 14.8 %all-to-all-start = ((bf16[8,32,256]{2,1,0:T(8,128)(2,1)}), bf16[8,32,256]{2,1,0:T(8,128)(2,1)S(1)}, u32[]{:S(2)}, u32[]{:S(2)}) async-start(bf16[8,32,256]{2,1,0:T(8,128)(2,1)} %broadcast_in_dim.2), calls=%async_computation | async-start | bytes 262144 | tf_op jit(solution)/shard_map/all_to_all | solution.py:190
  7.3 9.6 %collective-permute-start.1 = (bf16[128,256]{1,0:T(8,128)(2,1)S(1)}, bf16[128,256]{1,0:T(8,128)(2,1)S(1)}, u32[]{:S(2)}, u32[]{:S(2)}) collective-permute-start(bf16[128,256]{1,0:T(8,128)(2,1)S(1)} %constant_dynamic-update-slice_fusion.own_ref), channel_id=1, source_target_pairs={{0,28},{4,0},{8,4},{12,8},{16,12},{20,16},{24,20},{28,24},{1,29},{... | collective-permute-start | bytes 196616 | tf_op jit(solution)/shard_map/ppermute | solution.py:20
  10.0 6.9 %collective-permute-start = (bf16[128,256]{1,0:T(8,128)(2,1)S(1)}, bf16[128,256]{1,0:T(8,128)(2,1)S(1)}, u32[]{:S(2)}, u32[]{:S(2)}) collective-permute-start(bf16[128,256]{1,0:T(8,128)(2,1)S(1)} %constant_dynamic-update-slice_fusion.own_ref), channel_id=1, source_target_pairs={{0,4},{4,8},{8,12},{12,16},{16,20},{20,24},{24,28},{28,0},{1,5},{5... | collective-permute-start | bytes 196616 | tf_op jit(solution)/shard_map/ppermute | solution.py:20
  10.0 1.0 %copy-start.1 = (bf16[128,2048]{1,0:T(8,128)(2,1)S(1)}, bf16[128,2048]{1,0:T(8,128)(2,1)}, u32[]{:S(2)}) copy-start(bf16[128,2048]{1,0:T(8,128)(2,1)} %w_ref.1) | copy-start | bytes 1572868
  11.1 5.9 %copy-start.2 = (bf16[128,128]{1,0:T(8,128)(2,1)S(1)}, bf16[128,128]{1,0:T(8,128)(2,1)}, u32[]{:S(2)}) copy-start(bf16[128,128]{1,0:T(8,128)(2,1)} %q_ref.1) | copy-start | bytes 98308
  11.4 14.6 %collective-permute-start.5 = (bf16[128,512]{1,0:T(8,128)(2,1)S(1)}, bf16[128,512]{1,0:T(8,128)(2,1)S(1)}, u32[]{:S(2)}, u32[]{:S(2)}) collective-permute-start(bf16[128,512]{1,0:T(8,128)(2,1)S(1)} %get-tuple-element.21), channel_id=1, source_target_pairs={{0,1},{1,2},{2,3},{3,0},{4,5},{5,6},{6,7},{7,4},{8,9},{9,10},{10,1... | collective-permute-start | bytes 393224 | tf_op jit(solution)/shard_map/ppermute | solution.py:20
  13.0 14.2 %collective-permute-start.6 = (bf16[128,512]{1,0:T(8,128)(2,1)S(1)}, bf16[128,512]{1,0:T(8,128)(2,1)S(1)}, u32[]{:S(2)}, u32[]{:S(2)}) collective-permute-start(bf16[128,512]{1,0:T(8,128)(2,1)S(1)} %get-tuple-element.22), channel_id=1, source_target_pairs={{0,2},{1,3},{2,0},{3,1},{4,6},{5,7},{6,4},{7,5},{8,10},{9,11},{10,... | collective-permute-start | bytes 393224 | tf_op jit(solution)/shard_map/ppermute | solution.py:20
  15.6 12.5 %collective-permute-start.7 = (bf16[128,512]{1,0:T(8,128)(2,1)S(1)}, bf16[128,512]{1,0:T(8,128)(2,1)S(1)}, u32[]{:S(2)}, u32[]{:S(2)}) collective-permute-start(bf16[128,512]{1,0:T(8,128)(2,1)S(1)} %get-tuple-element.23), channel_id=1, source_target_pairs={{0,3},{1,0},{2,1},{3,2},{4,7},{5,4},{6,5},{7,6},{8,11},{9,8},{10,9... | collective-permute-start | bytes 393224 | tf_op jit(solution)/shard_map/ppermute | solution.py:20
  17.0 0.7 %copy-start.3 = (s32[1,8]{1,0:T(1,128)S(1)}, s32[1,8]{1,0:T(1,128)}, u32[]{:S(2)}) copy-start(s32[1,8]{1,0:T(1,128)} %index_ref.1) | copy-start | bytes 100
  19.9 14.0 %all-to-all-start.1 = ((bf16[8,32,256]{2,1,0:T(8,128)(2,1)}), bf16[8,32,256]{2,1,0:T(8,128)(2,1)S(1)}, u32[]{:S(2)}, u32[]{:S(2)}) async-start(bf16[8,32,256]{2,1,0:T(8,128)(2,1)} %bitcast.2), calls=%async_computation.1 | async-start | bytes 262144 | tf_op jit(solution)/shard_map/all_to_all | solution.py:199
  23.3 10.6 %collective-permute-start.8 = (bf16[128,256]{1,0:T(8,128)(2,1)S(1)}, bf16[128,256]{1,0:T(8,128)(2,1)S(1)}, u32[]{:S(2)}, u32[]{:S(2)}) collective-permute-start(bf16[128,256]{1,0:T(8,128)(2,1)S(1)} %get-tuple-element.25), channel_id=1, source_target_pairs={{0,4},{4,8},{8,12},{12,16},{16,20},{20,24},{24,28},{28,0},{1,5},{5... | collective-permute-start | bytes 196616 | tf_op jit(solution)/shard_map/ppermute | solution.py:20
  23.7 10.2 %collective-permute-start.9 = (bf16[128,256]{1,0:T(8,128)(2,1)S(1)}, bf16[128,256]{1,0:T(8,128)(2,1)S(1)}, u32[]{:S(2)}, u32[]{:S(2)}) collective-permute-start(bf16[128,256]{1,0:T(8,128)(2,1)S(1)} %get-tuple-element.26), channel_id=1, source_target_pairs={{0,28},{4,0},{8,4},{12,8},{16,12},{20,16},{24,20},{28,24},{1,29},{... | collective-permute-start | bytes 196616 | tf_op jit(solution)/shard_map/ppermute | solution.py:20
  26.0 4.0 %collective-permute-start.4 = (bf16[128,128]{1,0:T(8,128)(2,1)S(1)}, bf16[128,128]{1,0:T(8,128)(2,1)S(1)}, u32[]{:S(2)}, u32[]{:S(2)}) collective-permute-start(bf16[128,128]{1,0:T(8,128)(2,1)S(1)} %get-tuple-element.19.refs_0_), channel_id=1, source_target_pairs={{0,3},{1,0},{2,1},{3,2},{4,7},{5,4},{6,5},{7,6},{8,11},{9,8},{10,9... | collective-permute-start | bytes 98312 | tf_op jit(solution)/shard_map/ppermute | solution.py:20
  27.2 5.2 %collective-permute-start.3 = (bf16[128,128]{1,0:T(8,128)(2,1)S(1)}, bf16[128,128]{1,0:T(8,128)(2,1)S(1)}, u32[]{:S(2)}, u32[]{:S(2)}) collective-permute-start(bf16[128,128]{1,0:T(8,128)(2,1)S(1)} %get-tuple-element.19.refs_0_), channel_id=1, source_target_pairs={{0,2},{1,3},{2,0},{3,1},{4,6},{5,7},{6,4},{7,5},{8,10},{9,11},{10,... | collective-permute-start | bytes 98312 | tf_op jit(solution)/shard_map/ppermute | solution.py:20
  28.1 5.7 %collective-permute-start.2 = (bf16[128,128]{1,0:T(8,128)(2,1)S(1)}, bf16[128,128]{1,0:T(8,128)(2,1)S(1)}, u32[]{:S(2)}, u32[]{:S(2)}) collective-permute-start(bf16[128,128]{1,0:T(8,128)(2,1)S(1)} %get-tuple-element.19.refs_0_), channel_id=1, source_target_pairs={{0,1},{1,2},{2,3},{3,0},{4,5},{5,6},{6,7},{7,4},{8,9},{9,10},{10,1... | collective-permute-start | bytes 98312 | tf_op jit(solution)/shard_map/ppermute | solution.py:20

commit v2 on v1

v2 whole, which is shorter than its diff:
```python
import jax
import jax.numpy as jnp
from jax import lax
from jax.experimental import pallas as pl
from jax.experimental.pallas import tpu as pltpu
from jax.sharding import PartitionSpec as P

HD = 128
BLK = 128
STRIDE_ROWS = 32
PAIR = 2 * HD
SCALE = HD ** (-0.5)
LOG2E = 1.4426950408889634
ABSENT = -1e30
VMEM = pl.BlockSpec(memory_space=pltpu.VMEM)
SMEM = pl.BlockSpec(memory_space=pltpu.SMEM)
PARAMS = pltpu.CompilerParams(vmem_limit_bytes=40 * 1024 * 1024)
BF16 = jnp.bfloat16
F32 = jnp.float32


def dot_nt(a, b):
    return lax.dot_general(a, b, (((1,), (1,)), ((), ())), preferred_element_type=F32)


def dot_nn(a, b):
    return lax.dot_general(a, b, (((1,), (0,)), ((), ())), preferred_element_type=F32)


def dot_tn(a, b):
    return lax.dot_general(a, b, (((0,), (0,)), ((), ())), preferred_element_type=F32)


def shape(*dims, kind=BF16):
    return jax.ShapeDtypeStruct(dims, kind)


def trade(array, step):
    count = lax.axis_size("seq")
    return lax.ppermute(
        array, "seq", [(i, (i + (step if i % 2 == 0 else -step)) % count) for i in range(count)]
    )


def swap(array, mask):
    count = lax.axis_size("head")
    return lax.ppermute(array, "head", [(i, i ^ mask) for i in range(count)])


def own_counts(picks, group):
    total = jnp.zeros(group.shape, F32)
    for pick in picks:
        total = total + jnp.where(group == pick, 1.0, 0.0)
    return total


def prepare_kernel(ring, me_ref, index_ref, cot_ref, w_ref, grad_ref, mult_ref, *slice_refs):
    per_block = BLK // STRIDE_ROWS
    picks = [index_ref[0, i] for i in range(index_ref.shape[1])]
    rows, columns = mult_ref.shape
    lane = lax.broadcasted_iota(jnp.int32, (rows, columns), 1)
    if ring:
        b = me_ref[0]
        sign = 1 - 2 * lax.rem(b, 2)
        offsets = [(0, 0), (BLK, 1), (2 * BLK, -1), (3 * BLK, 3), (3 * BLK + 32, 2),
                   (3 * BLK + 64, 4), (3 * BLK + 96, -3), (3 * BLK + 128, -2)]
        owner = jnp.full((rows, columns), -per_block, jnp.int32)
        for start, offset in offsets:
            inside = (lane >= start) & (lane < start + STRIDE_ROWS)
            owner = jnp.where(inside, lax.rem(b + 16 + sign * offset, 8), owner)
        group = jnp.where(owner < 0, -1, owner // per_block)
    else:
        group = jnp.where(lane < 3 * BLK, -1, (lane - 3 * BLK) // BLK)
    mult_ref[...] = own_counts(picks, group) + jnp.where(lane < 3 * BLK, 1.0, 0.0)

    grad_ref[...] = dot_nt(cot_ref[...], w_ref[...]).astype(grad_ref.dtype)
    width = slice_refs[0].shape[1]
    head = me_ref[1]
    for r, ref in enumerate(slice_refs):
        start = pl.multiple_of((head ^ r) * width, width)
        ref[...] = w_ref[:, pl.ds(start, width)]


def prepare(ring, me, index, cotangent, out_weight, heads, columns):
    width = out_weight.shape[1] // heads

    def body(*refs):
        prepare_kernel(ring, *refs)

    return pl.pallas_call(
        body,
        out_shape=(shape(BLK, HD), shape(8, columns, kind=F32)) + (shape(HD, width),) * heads,
        in_specs=[SMEM, SMEM, VMEM, VMEM],
        out_specs=(VMEM,) * (2 + heads),
        compiler_params=PARAMS,
        name="prepare",
    )(me, index, cotangent, out_weight)


def attend_kernel(sides, mult_ref, q_ref, grad_ref, *refs):
    block_refs = refs[:3 + sides]
    att_ref, dq_ref = refs[3 + sides:5 + sides]
    sum_refs = refs[5 + sides:8 + 2 * sides]
    keys_ref = refs[-1]
    total_rows = keys_ref.shape[0]
    spans = []
    row = 0
    for ref in block_refs:
        spans.append((row, row + ref.shape[0]))
        keys_ref[row:row + ref.shape[0], :] = ref[...]
        row += ref.shape[0]
    if row < total_rows:
        keys_ref[row:, :] = jnp.zeros((total_rows - row, PAIR), BF16)
    keys = keys_ref[:, :HD]
    values = keys_ref[:, HD:]
    q = q_ref[...]
    grad = grad_ref[...]
    mult = mult_ref[0:1, :]

    scores = dot_nt(q, keys) + jnp.where(mult > 0.0, 0.0, ABSENT)
    top = jnp.max(scores, axis=1, keepdims=True)
    terms = jnp.exp2((scores - top) * (SCALE * LOG2E)) * mult
    probability = terms * (1.0 / jnp.sum(terms, axis=1, keepdims=True))
    weights = probability.astype(BF16)
    att_ref[...] = dot_nn(weights, values).astype(BF16)

    grad_weights = dot_nt(grad, values)
    delta = jnp.sum(probability * grad_weights, axis=1, keepdims=True)
    grad_scores = (probability * (grad_weights - delta) * SCALE).astype(BF16)
    dq_ref[...] = dot_nn(grad_scores, keys).astype(BF16)
    key_terms = dot_tn(grad_scores, q)
    value_terms = dot_tn(weights, grad)
    for (start, end), ref in zip(spans, sum_refs):
        ref[:, :HD] = key_terms[start:end].astype(ref.dtype)
        ref[:, HD:] = value_terms[start:end].astype(ref.dtype)


def attend(mult, q, grad, window, sides):
    def body(*refs):
        attend_kernel(len(sides), *refs)

    return pl.pallas_call(
        body,
        out_shape=(shape(BLK, HD), shape(BLK, HD))
        + (shape(BLK, PAIR, kind=F32),) * 3
        + tuple(shape(*s.shape) for s in sides),
        in_specs=[VMEM] * (6 + len(sides)),
        out_specs=(VMEM,) * (5 + len(sides)),
        scratch_shapes=[pltpu.VMEM((mult.shape[1], PAIR), BF16)],
        compiler_params=PARAMS,
        name="attend",
    )(mult, q, grad, *window, *sides)


def combine_kernel(own_ref, first_ref, second_ref, plus_ref, minus_ref, att_ref, other_ref,
                   own_out, first_out, second_out, att_out):
    plus = plus_ref[...].astype(F32)
    minus = minus_ref[...].astype(F32)
    n = STRIDE_ROWS
    own_out[n:] = own_ref[n:]
    own_out[:n] = own_ref[:n] + plus[:n] + minus[:n]
    first_out[n:] = first_ref[n:].astype(BF16)
    first_out[:n] = (first_ref[:n] + plus[n:2 * n]).astype(BF16)
    second_out[n:] = second_ref[n:].astype(BF16)
    second_out[:n] = (second_ref[:n] + plus[2 * n:] + minus[n:]).astype(BF16)
    att_out[:BLK] = att_ref[...]
    att_out[BLK:] = other_ref[...]


def combine(own, first, second, plus, minus, att, other):
    return pl.pallas_call(
        combine_kernel,
        out_shape=(shape(BLK, PAIR, kind=F32), shape(BLK, PAIR), shape(BLK, PAIR),
                   shape(2 * BLK, HD)),
        in_specs=[VMEM] * 7,
        out_specs=(VMEM,) * 4,
        compiler_params=PARAMS,
        name="combine",
    )(own, first, second, plus, minus, att, other)


def finish_kernel(heads, att_count, extra, *refs):
    att_refs = refs[:att_count]
    w_refs = refs[att_count:att_count + heads]
    rest = refs[att_count + heads:]
    own_ref, first_ref, second_ref = rest[:3]
    mixed_ref, dk_ref, dv_ref = rest[-3:]
    pieces = [(ref, r) for ref in att_refs for r in range(0, ref.shape[0], BLK)]
    mixed = None
    for (ref, r), w in zip(pieces, w_refs):
        term = dot_nn(ref[r:r + BLK], w[...])
        mixed = term if mixed is None else mixed + term
    mixed_ref[...] = mixed.astype(mixed_ref.dtype)
    total = own_ref[...] + first_ref[...].astype(F32) + second_ref[...].astype(F32)
    lead = total[:STRIDE_ROWS]
    if extra:
        side_ref = rest[3]
        for i in range(side_ref.shape[0] // STRIDE_ROWS):
            lead = lead + side_ref[i * STRIDE_ROWS:(i + 1) * STRIDE_ROWS].astype(F32)
    for ref, c in ((dk_ref, 0), (dv_ref, HD)):
        ref[:STRIDE_ROWS] = lead[:, c:c + HD].astype(ref.dtype)
        ref[STRIDE_ROWS:] = total[STRIDE_ROWS:, c:c + HD].astype(ref.dtype)


def finish(attentions, slices, own, first, second, *side):
    heads = len(slices)
    width = slices[0].shape[1]

    def body(*refs):
        finish_kernel(heads, len(attentions), len(side), *refs)

    return pl.pallas_call(
        body,
        out_shape=(shape(BLK, width), shape(BLK, HD), shape(BLK, HD)),
        in_specs=[VMEM] * (len(attentions) + heads + 3 + len(side)),
        out_specs=(VMEM,) * 3,
        compiler_params=PARAMS,
        name="finish",
    )(*attentions, *slices, own, first, second, *side)


def shards(queries, key_rows, value_rows, out_weight, strided_index, cotangent):
    seq = lax.axis_size("seq")
    heads = lax.axis_size("head")
    ring = seq == 8 and heads == 4
    n = STRIDE_ROWS
    me = jnp.stack([lax.axis_index("seq"), lax.axis_index("head")]).astype(jnp.int32)
    own = jnp.concatenate([key_rows, value_rows], axis=1)
    first = trade(own, 1)
    second = trade(own, -1)
    columns = 3 * BLK + (2 * BLK if ring else seq * n)
    grad, mult, *slices = prepare(ring, me, strided_index, cotangent, out_weight, heads, columns)
    slices = [slices[0]] + [swap(slices[r], r) for r in range(1, heads)]
    if ring:
        lead = jnp.concatenate([own[:n], first[:n], second[:n]], axis=0)
        plus = trade(lead, 3)
        minus = trade(jnp.concatenate([own[:n], second[:n]], axis=0), -3)
        att, dq, own_sum, first_sum, second_sum, to_plus, to_minus = attend(
            mult, queries, grad, (own, first, second), (plus, minus)
        )
        own_sum, to_first, to_second, pair = combine(
            own_sum, first_sum, second_sum, trade(to_plus, 3), trade(to_minus, -3),
            att, swap(att, 1),
        )
        mixed, dk, dv = finish(
            (pair, swap(pair, 2)), slices, own_sum, trade(to_first, 1), trade(to_second, -1)
        )
    else:
        spread = jnp.broadcast_to(own[None, :n], (seq, n, PAIR))
        side = lax.all_to_all(spread, "seq", 0, 0).reshape(seq * n, PAIR)
        att, dq, own_sum, first_sum, second_sum, to_side = attend(
            mult, queries, grad, (own, first, second), (side,)
        )
        from_side = lax.all_to_all(to_side.reshape(seq, n, PAIR), "seq", 0, 0)
        mixed, dk, dv = finish(
            [att] + [swap(att, r) for r in range(1, heads)], slices, own_sum,
            trade(first_sum.astype(BF16), 1), trade(second_sum.astype(BF16), -1),
            from_side.reshape(seq * n, PAIR),
        )
    return (mixed, dq, dk, dv)


def solution(mesh):
    in_specs = (
        P("seq", "head"),
        P("seq", "head"),
        P("seq", "head"),
        P("head", None),
        P("seq", None),
        P("seq", None),
    )
    out_specs = (P("seq", "head"), P("seq", "head"), P("seq", "head"), P("seq", "head"))
    return jax.shard_map(shards, mesh=mesh, in_specs=in_specs, out_specs=out_specs, check_vma=False)
```

time: 35.2 us -> 38.7 us (1.099)
  waiting for transfers between devices: 4.97 us -> 14.9 us
  starting transfers between devices: 22.4 us -> 15.9 us
    ppermute x10 -> x13, waiting for transfers between devices: 4.96 us -> 14.9 us  [the longest x5 10.6 us: swap(): return lax.ppermute(array, 'head', [(i, i ^ mask) for i in range(count)])]
    all_to_all x2 -> x0, starting transfers between devices: 8.54 us -> none  [the longest x1 5.17 us: shards(): side = lax.all_to_all(lead, 'seq', 0, 0).reshape(seq * STRIDE_ROWS, 2 * HD)]
    ppermute x10 -> x13, starting transfers between devices: 13.9 us -> 15.9 us  [the longest x8 10.5 us: trade(): lax.ppermute(array, 'seq', [(i, (i + (step if i % 2 == 0 else -step)) % c...]
    unnamed x11, local copies, waits for them, and re-layouts: 2.52 us -> 3.44 us
    broadcast_in_dim x1 -> x0, local copies, waits for them, and re-layouts: 0.66 us -> none  [shards(): lead = jnp.broadcast_to(own[None, :STRIDE_ROWS], (seq, STRIDE_ROWS, 2 * HD))]
    pallas_call x3 -> x4, Pallas kernels: 3.51 us -> 3.38 us  [the longest x1 1.53 us: attend(): pl.pallas_call(body, out_shape=(shape(BLK, HD), shape(BLK, HD)) + (shape(...]
  transfers between devices with their start and end apart: 12 -> 13, of which waited for: 3 -> 4; matrix products, arithmetic and copies ran while one was open for 0% -> 0% of each run, Pallas kernels for 7% -> 6%
where the time goes in v2:
time: 38.7 us; the launch traced here: 38.4 us
  starting transfers between devices  15.9 us (41%)
  waiting for transfers between devices  14.9 us (39%)
  local copies, waits for them, and re-layouts  3.46 us (9%)
  Pallas kernels  3.38 us (9%)
  between operations  0.71 us (2%)
    ppermute x5, waiting for transfers between devices, swap(): return lax.ppermute(array, 'head', [(i, i ^ mask) for i in range(count)])  10.6 us
    ppermute x8, starting transfers between devices, trade(): lax.ppermute(array, 'seq', [(i, (i + (step if i % 2 == 0 else -step)) % c...  10.5 us
    ppermute x5, starting transfers between devices, swap(): return lax.ppermute(array, 'head', [(i, i ^ mask) for i in range(count)])  5.34 us
    ppermute x8, waiting for transfers between devices, trade(): lax.ppermute(array, 'seq', [(i, (i + (step if i % 2 == 0 else -step)) % c...  4.25 us
    unnamed x11, local copies, waits for them, and re-layouts  3.44 us
    pallas_call x1, Pallas kernels, attend(): pl.pallas_call(body, out_shape=(shape(BLK, HD), shape(BLK, HD)) + (shape(...  1.53 us
    pallas_call x1, Pallas kernels, finish(): pl.pallas_call(body, out_shape=(shape(BLK, width), shape(BLK, HD), shape(...  0.95 us
    pallas_call x1, Pallas kernels, prepare(): pl.pallas_call(body, out_shape=(shape(BLK, HD), shape(8, columns, kind=F3...  0.86 us
  transfers between devices with their start and end apart: 13, of which 4 were waited for; matrix products, arithmetic and copies ran while one was open for 0% of the time, Pallas kernels for 6%

profile of v2, /device:TPU:0, one launch (start us, length us, event | category | flops | bytes accessed | tf_op | source)
XLA Modules:
  0.0 38.4 jit_solution(15313885531711758690)
XLA Ops:
  0.6 0.8 %constant_dynamic-update-slice_fusion.1 = bf16[128,256]{1,0:T(8,128)(2,1)S(1)} fusion(bf16[128,128]{1,0:T(8,128)(2,1)} %param.7), kind=kLoop, calls=%fused_computation.3 | loop fusion | bytes 65536
  1.4 3.4 %collective-permute-start.1 = (bf16[128,256]{1,0:T(8,128)(2,1)S(1)}, bf16[128,256]{1,0:T(8,128)(2,1)S(1)}, u32[]{:S(2)}, u32[]{:S(2)}) collective-permute-start(bf16[128,256]{1,0:T(8,128)(2,1)S(1)} %constant_dynamic-update-slice_fusion.refs_3_), channel_id=1, source_target_pairs={{0,28},{4,8},{8,4},{12,16},{16,12},{20,24},{24,20},{28,0},{1,29},{... | collective-permute-start | bytes 196616 | tf_op jit(solution)/shard_map/ppermute | solution.py:40
  4.8 0.0 collective-permute-start
  4.8 0.1 pad_add_fusion.refs_0_
  4.9 0.6 %copy-done.3 = s32[1,8]{1,0:T(1,128)S(1)} copy-done((s32[1,8]{1,0:T(1,128)S(1)}, s32[1,8]{1,0:T(1,128)}, u32[]{:S(2)}) %copy-start.3) | copy-done | bytes 56
  5.5 1.0 %copy-done = bf16[128,2048]{1,0:T(8,128)(2,1)S(1)} copy-done((bf16[128,2048]{1,0:T(8,128)(2,1)S(1)}, bf16[128,2048]{1,0:T(8,128)(2,1)}, u32[]{:S(2)}) %copy-start) | copy-done | bytes 524312
  6.5 1.0 %copy-done.1 = bf16[128,2048]{1,0:T(8,128)(2,1)S(1)} copy-done((bf16[128,2048]{1,0:T(8,128)(2,1)S(1)}, bf16[128,2048]{1,0:T(8,128)(2,1)}, u32[]{:S(2)}) %copy-start.1) | copy-done | bytes 524312
  7.6 0.9 %prepare.1 = (bf16[128,128]{1,0:T(8,128)(2,1)S(1)}, f32[8,640]{1,0:T(8,128)S(1)}, bf16[128,512]{1,0:T(8,128)(2,1)S(1)}, bf16[128,512]{1,0:T(8,128)(2,1)S(1)}, bf...) custom-call(s32[2]{0:T(128)S(1)} %pad_add_fusion.refs_0_, s32[1,8]{1,0:T(1,128)S(1)} %copy-done.3, ...), custom_call_target="tpu_custom_call" | custom-call | tf_op jit(solution)/shard_map/prepare/pallas_call | solution.py:90
  8.4 1.6 %collective-permute-start.8 = (bf16[128,512]{1,0:T(8,128)(2,1)S(1)}, bf16[128,512]{1,0:T(8,128)(2,1)S(1)}, u32[]{:S(2)}, u32[]{:S(2)}) collective-permute-start(bf16[128,512]{1,0:T(8,128)(2,1)S(1)} %get-tuple-element.34), channel_id=1, source_target_pairs={{0,1},{1,0},{2,3},{3,2},{4,5},{5,4},{6,7},{7,6},{8,9},{9,8},{10,11... | collective-permute-start | bytes 393224 | tf_op jit(solution)/shard_map/ppermute | solution.py:47
  10.1 0.0 collective-permute-done.1.refs_5_
  10.1 0.0 collective-permute-done.refs_4_
  10.1 0.0 copy-start.2
  10.1 0.6 %collective-permute-start.2 = (bf16[96,256]{1,0:T(8,128)(2,1)S(1)}, bf16[96,256]{1,0:T(8,128)(2,1)S(1)}, u32[]{:S(2)}, u32[]{:S(2)}) collective-permute-start(bf16[96,256]{1,0:T(8,128)(2,1)S(1)} %pad_maximum_fusion), channel_id=1, source_target_pairs={{0,12},{4,24},{8,20},{12,0},{16,28},{20,8},{24,4},{28,16},{1,13},{... | collective-permute-start | bytes 147464 | tf_op jit(solution)/shard_map/ppermute | solution.py:40
  10.8 1.9 %collective-permute-start.3 = (bf16[64,256]{1,0:T(8,128)(2,1)S(1)}, bf16[64,256]{1,0:T(8,128)(2,1)S(1)}, u32[]{:S(2)}, u32[]{:S(2)}) collective-permute-start(bf16[64,256]{1,0:T(8,128)(2,1)S(1)} %pad_maximum_fusion.1), channel_id=1, source_target_pairs={{0,20},{4,16},{8,28},{12,24},{16,4},{20,0},{24,12},{28,8},{1,21},{... | collective-permute-start | bytes 98312 | tf_op jit(solution)/shard_map/ppermute | solution.py:40
  12.6 1.6 %collective-permute-done.3.refs_7_ = bf16[64,256]{1,0:T(8,128)(2,1)S(1)} collective-permute-done((bf16[64,256]{1,0:T(8,128)(2,1)S(1)}, bf16[64,256]{1,0:T(8,128)(2,1)S(1)}, u32[]{:S(2)}, u32[]{:S(2)}) %collective-permute-start.3) | collective-permute-done | bytes 32800 | tf_op jit(solution)/shard_map/ppermute | solution.py:40
  14.2 1.5 %attend.1 = (bf16[128,128]{1,0:T(8,128)(2,1)S(1)}, bf16[128,128]{1,0:T(8,128)(2,1)}, f32[128,256]{1,0:T(8,128)S(1)}, f32[128,256]{1,0:T(8,128)S(1)}, f32[128,256...) custom-call(f32[8,640]{1,0:T(8,128)S(1)} %get-tuple-element.24.refs_0_, ...), custom_call_target="tpu_custom_call" | custom-call | tf_op jit(solution)/shard_map/attend/pallas_call | solution.py:142
  15.7 1.7 %collective-permute-start.5 = (bf16[64,256]{1,0:T(8,128)(2,1)S(1)}, bf16[64,256]{1,0:T(8,128)(2,1)S(1)}, u32[]{:S(2)}, u32[]{:S(2)}) collective-permute-start(bf16[64,256]{1,0:T(8,128)(2,1)S(1)} %get-tuple-element.30), channel_id=1, source_target_pairs={{0,20},{4,16},{8,28},{12,24},{16,4},{20,0},{24,12},{28,8},{1,21},{... | collective-permute-start | bytes 98312 | tf_op jit(solution)/shard_map/ppermute | solution.py:40
  17.5 2.6 %collective-permute-start.9 = (bf16[128,512]{1,0:T(8,128)(2,1)S(1)}, bf16[128,512]{1,0:T(8,128)(2,1)S(1)}, u32[]{:S(2)}, u32[]{:S(2)}) collective-permute-start(bf16[128,512]{1,0:T(8,128)(2,1)S(1)} %get-tuple-element.35), channel_id=1, source_target_pairs={{0,2},{1,3},{2,0},{3,1},{4,6},{5,7},{6,4},{7,5},{8,10},{9,11},{10,... | collective-permute-start | bytes 393224 | tf_op jit(solution)/shard_map/ppermute | solution.py:47
  20.1 0.3 collective-permute-start.10
  20.3 0.5 %collective-permute-start.4 = (bf16[96,256]{1,0:T(8,128)(2,1)S(1)}, bf16[96,256]{1,0:T(8,128)(2,1)S(1)}, u32[]{:S(2)}, u32[]{:S(2)}) collective-permute-start(bf16[96,256]{1,0:T(8,128)(2,1)S(1)} %get-tuple-element.29), channel_id=1, source_target_pairs={{0,12},{4,24},{8,20},{12,0},{16,28},{20,8},{24,4},{28,16},{1,13},{... | collective-permute-start | bytes 147464 | tf_op jit(solution)/shard_map/ppermute | solution.py:40
  20.9 0.6 %collective-permute-start.6 = (bf16[128,128]{1,0:T(8,128)(2,1)S(1)}, bf16[128,128]{1,0:T(8,128)(2,1)S(1)}, u32[]{:S(2)}, u32[]{:S(2)}) collective-permute-start(bf16[128,128]{1,0:T(8,128)(2,1)S(1)} %get-tuple-element.31.att_ref), channel_id=1, source_target_pairs={{0,1},{1,0},{2,3},{3,2},{4,5},{5,4},{6,7},{7,6},{8,9},{9,8},{10,11... | collective-permute-start | bytes 98312 | tf_op jit(solution)/shard_map/ppermute | solution.py:47
  21.5 7.9 %collective-permute-done.6.other_ref = bf16[128,128]{1,0:T(8,128)(2,1)S(1)} collective-permute-done((bf16[128,128]{1,0:T(8,128)(2,1)S(1)}, bf16[128,128]{1,0:T(8,128)(2,1)S(1)}, u32[]{:S(2)}, u32[]{:S(2)}) %collective-permute-start.6) | collective-permute-done | bytes 32800 | tf_op jit(solution)/shard_map/ppermute | solution.py:47
  29.4 0.0 collective-permute-done.4.plus_ref
  29.4 0.2 collective-permute-start.11
  29.6 2.2 %collective-permute-start.12 = (bf16[128,256]{1,0:T(8,128)(2,1)S(1)}, bf16[128,256]{1,0:T(8,128)(2,1)S(1)}, u32[]{:S(2)}, u32[]{:S(2)}) collective-permute-start(bf16[128,256]{1,0:T(8,128)(2,1)S(1)} %get-tuple-element.39), channel_id=1, source_target_pairs={{0,28},{4,8},{8,4},{12,16},{16,12},{20,24},{24,20},{28,0},{1,29},{... | collective-permute-start | bytes 196616 | tf_op jit(solution)/shard_map/ppermute | solution.py:40
  31.8 0.0 collective-permute-done.8.refs_3_
  31.8 0.2 collective-permute-start.7
  32.0 0.0 collective-permute-done.9.refs_4_
  32.0 0.0 collective-permute-done.10.refs_5_
  32.0 2.6 %collective-permute-done.12.refs_8_ = bf16[128,256]{1,0:T(8,128)(2,1)S(1)} collective-permute-done((bf16[128,256]{1,0:T(8,128)(2,1)S(1)}, bf16[128,256]{1,0:T(8,128)(2,1)S(1)}, u32[]{:S(2)}, u32[]{:S(2)}) %collective-permute-start.12) | collective-permute-done | bytes 65568 | tf_op jit(solution)/shard_map/ppermute | solution.py:40
  34.7 2.7 %collective-permute-done.7.refs_1_ = bf16[256,128]{1,0:T(8,128)(2,1)S(1)} collective-permute-done((bf16[256,128]{1,0:T(8,128)(2,1)S(1)}, bf16[256,128]{1,0:T(8,128)(2,1)S(1)}, u32[]{:S(2)}, u32[]{:S(2)}) %collective-permute-start.7) | collective-permute-done | bytes 65568 | tf_op jit(solution)/shard_map/ppermute | solution.py:47
  37.4 1.0 %finish.1 = (bf16[128,512]{1,0:T(8,128)(2,1)}, bf16[128,128]{1,0:T(8,128)(2,1)}, bf16[128,128]{1,0:T(8,128)(2,1)}) custom-call(bf16[256,128]{1,0:T(8,128)(2,1)S(1)} %get-tuple-element.32.refs_0_, bf16[256,128]{1,0:T(8,128)(2,1)S(1)} %collective-permute-done.7.refs_1_, bf16[128,512]{1,0:T(8,128)(2,1)S(1)} %get-tuple-element.33.refs_2_, ...), custom_call_target="tpu_custom_call" | custom-call | tf_op jit(solution)/shard_map/finish/pallas_call | solution.py:212
  (16 shorter events, 0.1 us)
Async XLA Ops:
  0.6 0.8 %copy-start.4 = (bf16[128,128]{1,0:T(8,128)(2,1)S(1)}, bf16[128,128]{1,0:T(8,128)(2,1)}, u32[]{:S(2)}) copy-start(bf16[128,128]{1,0:T(8,128)(2,1)} %param.8) | copy-start | bytes 98308
  1.4 8.7 %collective-permute-start.1 = (bf16[128,256]{1,0:T(8,128)(2,1)S(1)}, bf16[128,256]{1,0:T(8,128)(2,1)S(1)}, u32[]{:S(2)}, u32[]{:S(2)}) collective-permute-start(bf16[128,256]{1,0:T(8,128)(2,1)S(1)} %constant_dynamic-update-slice_fusion.refs_3_), channel_id=1, source_target_pairs={{0,28},{4,8},{8,4},{12,16},{16,12},{20,24},{24,20},{28,0},{1,29},{... | collective-permute-start | bytes 196616 | tf_op jit(solution)/shard_map/ppermute | solution.py:40
  4.8 5.3 %collective-permute-start = (bf16[128,256]{1,0:T(8,128)(2,1)S(1)}, bf16[128,256]{1,0:T(8,128)(2,1)S(1)}, u32[]{:S(2)}, u32[]{:S(2)}) collective-permute-start(bf16[128,256]{1,0:T(8,128)(2,1)S(1)} %constant_dynamic-update-slice_fusion.refs_3_), channel_id=1, source_target_pairs={{0,4},{4,0},{8,12},{12,8},{16,20},{20,16},{24,28},{28,24},{1,5},{5... | collective-permute-start | bytes 196616 | tf_op jit(solution)/shard_map/ppermute | solution.py:40
  4.8 0.7 %copy-start.3 = (s32[1,8]{1,0:T(1,128)S(1)}, s32[1,8]{1,0:T(1,128)}, u32[]{:S(2)}) copy-start(s32[1,8]{1,0:T(1,128)} %refs_1_.2) | copy-start | bytes 100
  5.5 1.0 %copy-start = (bf16[128,2048]{1,0:T(8,128)(2,1)S(1)}, bf16[128,2048]{1,0:T(8,128)(2,1)}, u32[]{:S(2)}) copy-start(bf16[128,2048]{1,0:T(8,128)(2,1)} %refs_2_.1) | copy-start | bytes 1572868
  6.5 1.0 %copy-start.1 = (bf16[128,2048]{1,0:T(8,128)(2,1)S(1)}, bf16[128,2048]{1,0:T(8,128)(2,1)}, u32[]{:S(2)}) copy-start(bf16[128,2048]{1,0:T(8,128)(2,1)} %refs_3_.1) | copy-start | bytes 1572868
  8.4 23.4 %collective-permute-start.8 = (bf16[128,512]{1,0:T(8,128)(2,1)S(1)}, bf16[128,512]{1,0:T(8,128)(2,1)S(1)}, u32[]{:S(2)}, u32[]{:S(2)}) collective-permute-start(bf16[128,512]{1,0:T(8,128)(2,1)S(1)} %get-tuple-element.34), channel_id=1, source_target_pairs={{0,1},{1,0},{2,3},{3,2},{4,5},{5,4},{6,7},{7,6},{8,9},{9,8},{10,11... | collective-permute-start | bytes 393224 | tf_op jit(solution)/shard_map/ppermute | solution.py:47
  10.1 4.1 %copy-start.2 = (bf16[128,128]{1,0:T(8,128)(2,1)S(1)}, bf16[128,128]{1,0:T(8,128)(2,1)}, u32[]{:S(2)}) copy-start(bf16[128,128]{1,0:T(8,128)(2,1)} %refs_1_.3) | copy-start | bytes 98308
  10.1 4.1 %collective-permute-start.2 = (bf16[96,256]{1,0:T(8,128)(2,1)S(1)}, bf16[96,256]{1,0:T(8,128)(2,1)S(1)}, u32[]{:S(2)}, u32[]{:S(2)}) collective-permute-start(bf16[96,256]{1,0:T(8,128)(2,1)S(1)} %pad_maximum_fusion), channel_id=1, source_target_pairs={{0,12},{4,24},{8,20},{12,0},{16,28},{20,8},{24,4},{28,16},{1,13},{... | collective-permute-start | bytes 147464 | tf_op jit(solution)/shard_map/ppermute | solution.py:40
  10.8 3.5 %collective-permute-start.3 = (bf16[64,256]{1,0:T(8,128)(2,1)S(1)}, bf16[64,256]{1,0:T(8,128)(2,1)S(1)}, u32[]{:S(2)}, u32[]{:S(2)}) collective-permute-start(bf16[64,256]{1,0:T(8,128)(2,1)S(1)} %pad_maximum_fusion.1), channel_id=1, source_target_pairs={{0,20},{4,16},{8,28},{12,24},{16,4},{20,0},{24,12},{28,8},{1,21},{... | collective-permute-start | bytes 98312 | tf_op jit(solution)/shard_map/ppermute | solution.py:40
  15.7 5.1 %collective-permute-start.5 = (bf16[64,256]{1,0:T(8,128)(2,1)S(1)}, bf16[64,256]{1,0:T(8,128)(2,1)S(1)}, u32[]{:S(2)}, u32[]{:S(2)}) collective-permute-start(bf16[64,256]{1,0:T(8,128)(2,1)S(1)} %get-tuple-element.30), channel_id=1, source_target_pairs={{0,20},{4,16},{8,28},{12,24},{16,4},{20,0},{24,12},{28,8},{1,21},{... | collective-permute-start | bytes 98312 | tf_op jit(solution)/shard_map/ppermute | solution.py:40
  17.5 14.5 %collective-permute-start.9 = (bf16[128,512]{1,0:T(8,128)(2,1)S(1)}, bf16[128,512]{1,0:T(8,128)(2,1)S(1)}, u32[]{:S(2)}, u32[]{:S(2)}) collective-permute-start(bf16[128,512]{1,0:T(8,128)(2,1)S(1)} %get-tuple-element.35), channel_id=1, source_target_pairs={{0,2},{1,3},{2,0},{3,1},{4,6},{5,7},{6,4},{7,5},{8,10},{9,11},{10,... | collective-permute-start | bytes 393224 | tf_op jit(solution)/shard_map/ppermute | solution.py:47
  20.1 12.0 %collective-permute-start.10 = (bf16[128,512]{1,0:T(8,128)(2,1)S(1)}, bf16[128,512]{1,0:T(8,128)(2,1)S(1)}, u32[]{:S(2)}, u32[]{:S(2)}) collective-permute-start(bf16[128,512]{1,0:T(8,128)(2,1)S(1)} %get-tuple-element.36), channel_id=1, source_target_pairs={{0,3},{1,2},{2,1},{3,0},{4,7},{5,6},{6,5},{7,4},{8,11},{9,10},{10,... | collective-permute-start | bytes 393224 | tf_op jit(solution)/shard_map/ppermute | solution.py:47
  20.3 9.0 %collective-permute-start.4 = (bf16[96,256]{1,0:T(8,128)(2,1)S(1)}, bf16[96,256]{1,0:T(8,128)(2,1)S(1)}, u32[]{:S(2)}, u32[]{:S(2)}) collective-permute-start(bf16[96,256]{1,0:T(8,128)(2,1)S(1)} %get-tuple-element.29), channel_id=1, source_target_pairs={{0,12},{4,24},{8,20},{12,0},{16,28},{20,8},{24,4},{28,16},{1,13},{... | collective-permute-start | bytes 147464 | tf_op jit(solution)/shard_map/ppermute | solution.py:40
  20.9 8.5 %collective-permute-start.6 = (bf16[128,128]{1,0:T(8,128)(2,1)S(1)}, bf16[128,128]{1,0:T(8,128)(2,1)S(1)}, u32[]{:S(2)}, u32[]{:S(2)}) collective-permute-start(bf16[128,128]{1,0:T(8,128)(2,1)S(1)} %get-tuple-element.31.att_ref), channel_id=1, source_target_pairs={{0,1},{1,0},{2,3},{3,2},{4,5},{5,4},{6,7},{7,6},{8,9},{9,8},{10,11... | collective-permute-start | bytes 98312 | tf_op jit(solution)/shard_map/ppermute | solution.py:47
  29.4 2.6 %collective-permute-start.11 = (bf16[128,256]{1,0:T(8,128)(2,1)S(1)}, bf16[128,256]{1,0:T(8,128)(2,1)S(1)}, u32[]{:S(2)}, u32[]{:S(2)}) collective-permute-start(bf16[128,256]{1,0:T(8,128)(2,1)S(1)} %get-tuple-element.38), channel_id=1, source_target_pairs={{0,4},{4,0},{8,12},{12,8},{16,20},{20,16},{24,28},{28,24},{1,5},{5... | collective-permute-start | bytes 196616 | tf_op jit(solution)/shard_map/ppermute | solution.py:40
  29.6 5.1 %collective-permute-start.12 = (bf16[128,256]{1,0:T(8,128)(2,1)S(1)}, bf16[128,256]{1,0:T(8,128)(2,1)S(1)}, u32[]{:S(2)}, u32[]{:S(2)}) collective-permute-start(bf16[128,256]{1,0:T(8,128)(2,1)S(1)} %get-tuple-element.39), channel_id=1, source_target_pairs={{0,28},{4,8},{8,4},{12,16},{16,12},{20,24},{24,20},{28,0},{1,29},{... | collective-permute-start | bytes 196616 | tf_op jit(solution)/shard_map/ppermute | solution.py:40
  31.8 5.6 %collective-permute-start.7 = (bf16[256,128]{1,0:T(8,128)(2,1)S(1)}, bf16[256,128]{1,0:T(8,128)(2,1)S(1)}, u32[]{:S(2)}, u32[]{:S(2)}) collective-permute-start(bf16[256,128]{1,0:T(8,128)(2,1)S(1)} %get-tuple-element.32.refs_0_), channel_id=1, source_target_pairs={{0,2},{1,3},{2,0},{3,1},{4,6},{5,7},{6,4},{7,5},{8,10},{9,11},{10,... | collective-permute-start | bytes 196616 | tf_op jit(solution)/shard_map/ppermute | solution.py:47

commit v3 on v2

--- a/solution.py
+++ b/solution.py
@@ -13,8 +13,9 @@
 LOG2E = 1.4426950408889634
 ABSENT = -1e30
 VMEM = pl.BlockSpec(memory_space=pltpu.VMEM)
-SMEM = pl.BlockSpec(memory_space=pltpu.SMEM)
+HBM = pl.BlockSpec(memory_space=pltpu.HBM)
 PARAMS = pltpu.CompilerParams(vmem_limit_bytes=40 * 1024 * 1024)
+FULL = pltpu.CompilerParams(vmem_limit_bytes=int(53.3 * 1024 * 1024))
 BF16 = jnp.bfloat16
 F32 = jnp.float32
 
@@ -47,54 +48,107 @@
     return lax.ppermute(array, "head", [(i, i ^ mask) for i in range(count)])
 
 
-def own_counts(picks, group):
-    total = jnp.zeros(group.shape, F32)
+def count_of(picks, group):
+    total = jnp.int32(0)
     for pick in picks:
-        total = total + jnp.where(group == pick, 1.0, 0.0)
-    return total
-
-
-def prepare_kernel(ring, me_ref, index_ref, cot_ref, w_ref, grad_ref, mult_ref, *slice_refs):
+        total = total + jnp.where(pick == group, 1, 0)
+    return total.astype(F32)
+
+
+def fill_multiplicity(ring, index_ref, mult_ref):
     per_block = BLK // STRIDE_ROWS
     picks = [index_ref[0, i] for i in range(index_ref.shape[1])]
-    rows, columns = mult_ref.shape
-    lane = lax.broadcasted_iota(jnp.int32, (rows, columns), 1)
+    shape_of = mult_ref.shape
+    lane = lax.broadcasted_iota(jnp.int32, shape_of, 1)
+    mult = jnp.where(lane < 3 * BLK, 1.0, 0.0)
     if ring:
-        b = me_ref[0]
-        sign = 1 - 2 * lax.rem(b, 2)
+        b = lax.axis_index("seq")
+        sign = 1 - 2 * (b & 1)
+        counts = [count_of(picks, j) for j in range(2)]
         offsets = [(0, 0), (BLK, 1), (2 * BLK, -1), (3 * BLK, 3), (3 * BLK + 32, 2),
                    (3 * BLK + 64, 4), (3 * BLK + 96, -3), (3 * BLK + 128, -2)]
-        owner = jnp.full((rows, columns), -per_block, jnp.int32)
         for start, offset in offsets:
+            owner = (b + 16 + sign * offset) & 7
+            count = jnp.where(owner < per_block, counts[0], counts[1])
             inside = (lane >= start) & (lane < start + STRIDE_ROWS)
-            owner = jnp.where(inside, lax.rem(b + 16 + sign * offset, 8), owner)
-        group = jnp.where(owner < 0, -1, owner // per_block)
+            mult = mult + jnp.where(inside, count, 0.0)
     else:
-        group = jnp.where(lane < 3 * BLK, -1, (lane - 3 * BLK) // BLK)
-    mult_ref[...] = own_counts(picks, group) + jnp.where(lane < 3 * BLK, 1.0, 0.0)
-
-    grad_ref[...] = dot_nt(cot_ref[...], w_ref[...]).astype(grad_ref.dtype)
+        for j in range((shape_of[1] - 3 * BLK) // BLK):
+            start = (3 + j) * BLK
+            inside = (lane >= start) & (lane < start + BLK)
+            mult = mult + jnp.where(inside, count_of(picks, j), 0.0)
+    mult_ref[...] = mult
+
+
+CHUNKS = 4
+
+
+def prepare_kernel(ring, index_hbm, cot_hbm, w_hbm, grad_ref, mult_ref, *refs):
+    index_ref, cot_ref, w_ref, sems = refs[-4:]
+    slice_refs = refs[:-4]
     width = slice_refs[0].shape[1]
-    head = me_ref[1]
-    for r, ref in enumerate(slice_refs):
-        start = pl.multiple_of((head ^ r) * width, width)
-        ref[...] = w_ref[:, pl.ds(start, width)]
-
-
-def prepare(ring, me, index, cotangent, out_weight, heads, columns):
+    head = lax.axis_index("head")
+    core = lax.axis_index("seq") & 1
+
+    def columns(h):
+        return pl.ds(pl.multiple_of(h * width, width), width)
+
+    if ring:
+        half = HD // 2
+        sources = [
+            w_hbm.at[:, columns(head)],
+            w_hbm.at[:, columns(head ^ (1 + core))],
+            w_hbm.at[pl.ds(pl.multiple_of(core * half, half), half), columns(head ^ 3)],
+        ]
+    else:
+        sources = [w_hbm.at[:, columns(head ^ r)] for r in range(len(slice_refs))]
+    copies = [(index_hbm, index_ref)]
+    copies += list(zip(sources, slice_refs))
+    depth = cot_ref.shape[1] // CHUNKS
+    for i in range(CHUNKS):
+        span = pl.ds(i * depth, depth)
+        copies.append((cot_hbm.at[:, span], cot_ref.at[:, span]))
+        copies.append((w_hbm.at[:, span], w_ref.at[:, span]))
+    copies = [pltpu.make_async_copy(src, dst, sems.at[i]) for i, (src, dst) in enumerate(copies)]
+    for copy in copies:
+        copy.start()
+    copies[0].wait()
+    fill_multiplicity(ring, index_ref, mult_ref)
+    fixed = 1 + len(slice_refs)
+    total = None
+    for i in range(CHUNKS):
+        copies[fixed + 2 * i].wait()
+        copies[fixed + 2 * i + 1].wait()
+        span = slice(i * depth, (i + 1) * depth)
+        term = dot_nt(cot_ref[:, span], w_ref[:, span])
+        total = term if total is None else total + term
+    grad_ref[...] = total.astype(grad_ref.dtype)
+    for copy in copies[1:fixed]:
+        copy.wait()
+
+
+def prepare(ring, index, cotangent, out_weight, heads, columns):
     width = out_weight.shape[1] // heads
+    rows = (HD, HD, HD // 2) if ring else (HD,) * heads
 
     def body(*refs):
         prepare_kernel(ring, *refs)
 
     return pl.pallas_call(
         body,
-        out_shape=(shape(BLK, HD), shape(8, columns, kind=F32)) + (shape(HD, width),) * heads,
-        in_specs=[SMEM, SMEM, VMEM, VMEM],
-        out_specs=(VMEM,) * (2 + heads),
-        compiler_params=PARAMS,
+        out_shape=(shape(BLK, HD), shape(8, columns, kind=F32))
+        + tuple(shape(r, width) for r in rows),
+        in_specs=[HBM] * 3,
+        out_specs=(VMEM,) * (2 + len(rows)),
+        scratch_shapes=[
+            pltpu.SMEM(index.shape, jnp.int32),
+            pltpu.VMEM(cotangent.shape, BF16),
+            pltpu.VMEM(out_weight.shape, BF16),
+            pltpu.SemaphoreType.DMA((1 + len(rows) + 2 * CHUNKS,)),
+        ],
+        compiler_params=FULL,
         name="prepare",
-    )(me, index, cotangent, out_weight)
+    )(index, cotangent, out_weight)
 
 
 def attend_kernel(sides, mult_ref, q_ref, grad_ref, *refs):
@@ -152,8 +206,9 @@
     )(mult, q, grad, *window, *sides)
 
 
-def combine_kernel(own_ref, first_ref, second_ref, plus_ref, minus_ref, att_ref, other_ref,
-                   own_out, first_out, second_out, att_out):
+def combine_kernel(own_ref, first_ref, second_ref, plus_ref, minus_ref,
+                   mine_ref, whole_ref, half_ref, other_whole_ref, other_half_ref,
+                   own_out, first_out, second_out, w_out):
     plus = plus_ref[...].astype(F32)
     minus = minus_ref[...].astype(F32)
     n = STRIDE_ROWS
@@ -163,32 +218,37 @@
     first_out[:n] = (first_ref[:n] + plus[n:2 * n]).astype(BF16)
     second_out[n:] = second_ref[n:].astype(BF16)
     second_out[:n] = (second_ref[:n] + plus[2 * n:] + minus[n:]).astype(BF16)
-    att_out[:BLK] = att_ref[...]
-    att_out[BLK:] = other_ref[...]
-
-
-def combine(own, first, second, plus, minus, att, other):
+    core = lax.axis_index("seq") & 1
+    half = HD // 2
+    w_out[:HD] = mine_ref[...]
+    w_out[pl.ds(pl.multiple_of(HD + core * HD, HD), HD)] = whole_ref[...]
+    w_out[pl.ds(pl.multiple_of(2 * HD - core * HD, HD), HD)] = other_whole_ref[...]
+    w_out[pl.ds(pl.multiple_of(3 * HD + core * half, half), half)] = half_ref[...]
+    w_out[pl.ds(pl.multiple_of(3 * HD + half - core * half, half), half)] = other_half_ref[...]
+
+
+def combine(own, first, second, plus, minus, *slices):
     return pl.pallas_call(
         combine_kernel,
         out_shape=(shape(BLK, PAIR, kind=F32), shape(BLK, PAIR), shape(BLK, PAIR),
-                   shape(2 * BLK, HD)),
-        in_specs=[VMEM] * 7,
+                   shape(4 * HD, slices[0].shape[1])),
+        in_specs=[VMEM] * 10,
         out_specs=(VMEM,) * 4,
         compiler_params=PARAMS,
         name="combine",
-    )(own, first, second, plus, minus, att, other)
-
-
-def finish_kernel(heads, att_count, extra, *refs):
-    att_refs = refs[:att_count]
-    w_refs = refs[att_count:att_count + heads]
-    rest = refs[att_count + heads:]
+    )(own, first, second, plus, minus, *slices)
+
+
+def finish_kernel(heads, slices, extra, *refs):
+    att_refs = refs[:heads]
+    w_refs = refs[heads:heads + slices]
+    rest = refs[heads + slices:]
     own_ref, first_ref, second_ref = rest[:3]
     mixed_ref, dk_ref, dv_ref = rest[-3:]
-    pieces = [(ref, r) for ref in att_refs for r in range(0, ref.shape[0], BLK)]
+    pieces = [ref[r:r + HD] for ref in w_refs for r in range(0, ref.shape[0], HD)]
     mixed = None
-    for (ref, r), w in zip(pieces, w_refs):
-        term = dot_nn(ref[r:r + BLK], w[...])
+    for ref, w in zip(att_refs, pieces):
+        term = dot_nn(ref[...], w)
         mixed = term if mixed is None else mixed + term
     mixed_ref[...] = mixed.astype(mixed_ref.dtype)
     total = own_ref[...] + first_ref[...].astype(F32) + second_ref[...].astype(F32)
@@ -203,20 +263,27 @@
 
 
 def finish(attentions, slices, own, first, second, *side):
-    heads = len(slices)
     width = slices[0].shape[1]
 
     def body(*refs):
-        finish_kernel(heads, len(attentions), len(side), *refs)
+        finish_kernel(len(attentions), len(slices), len(side), *refs)
 
     return pl.pallas_call(
         body,
         out_shape=(shape(BLK, width), shape(BLK, HD), shape(BLK, HD)),
-        in_specs=[VMEM] * (len(attentions) + heads + 3 + len(side)),
+        in_specs=[VMEM] * (len(attentions) + len(slices) + 3 + len(side)),
         out_specs=(VMEM,) * 3,
         compiler_params=PARAMS,
         name="finish",
     )(*attentions, *slices, own, first, second, *side)
+
+
+def spread_slice(array):
+    seq = lax.axis_size("seq")
+    heads = lax.axis_size("head")
+    pairs = [(b * heads + h, b * heads + (h ^ (1 + b % 2))) for b in range(seq)
+             for h in range(heads)]
+    return lax.ppermute(array, ("seq", "head"), pairs)
 
 
 def shards(queries, key_rows, value_rows, out_weight, strided_index, cotangent):
@@ -224,28 +291,33 @@
     heads = lax.axis_size("head")
     ring = seq == 8 and heads == 4
     n = STRIDE_ROWS
-    me = jnp.stack([lax.axis_index("seq"), lax.axis_index("head")]).astype(jnp.int32)
     own = jnp.concatenate([key_rows, value_rows], axis=1)
     first = trade(own, 1)
     second = trade(own, -1)
     columns = 3 * BLK + (2 * BLK if ring else seq * n)
-    grad, mult, *slices = prepare(ring, me, strided_index, cotangent, out_weight, heads, columns)
-    slices = [slices[0]] + [swap(slices[r], r) for r in range(1, heads)]
+    grad, mult, *slices = prepare(ring, strided_index, cotangent, out_weight, heads, columns)
     if ring:
+        mine, whole, half = slices
+        whole = spread_slice(whole)
+        half = swap(half, 3)
         lead = jnp.concatenate([own[:n], first[:n], second[:n]], axis=0)
         plus = trade(lead, 3)
         minus = trade(jnp.concatenate([own[:n], second[:n]], axis=0), -3)
+        other_whole = trade(whole, 1)
+        other_half = trade(half, 1)
         att, dq, own_sum, first_sum, second_sum, to_plus, to_minus = attend(
             mult, queries, grad, (own, first, second), (plus, minus)
         )
-        own_sum, to_first, to_second, pair = combine(
+        attentions = [att] + [swap(att, r) for r in range(1, heads)]
+        own_sum, to_first, to_second, weight = combine(
             own_sum, first_sum, second_sum, trade(to_plus, 3), trade(to_minus, -3),
-            att, swap(att, 1),
+            mine, whole, half, other_whole, other_half,
         )
         mixed, dk, dv = finish(
-            (pair, swap(pair, 2)), slices, own_sum, trade(to_first, 1), trade(to_second, -1)
+            attentions, [weight], own_sum, trade(to_first, 1), trade(to_second, -1)
         )
     else:
+        slices = [slices[0]] + [swap(slices[r], r) for r in range(1, heads)]
         spread = jnp.broadcast_to(own[None, :n], (seq, n, PAIR))
         side = lax.all_to_all(spread, "seq", 0, 0).reshape(seq * n, PAIR)
         att, dq, own_sum, first_sum, second_sum, to_side = attend(

time: 38.7 us -> 38 us (0.982)
  starting transfers between devices: 15.9 us -> 19.3 us
  local copies, waits for them, and re-layouts: 3.46 us -> 0.81 us
  waiting for transfers between devices: 14.9 us -> 12.4 us
  Pallas kernels: 3.38 us -> 4.5 us
    ppermute x5 -> x4, starting transfers between devices: 5.34 us -> 8.5 us  [swap(): return lax.ppermute(array, 'head', [(i, i ^ mask) for i in range(count)])]
    ppermute x5 -> x4, waiting for transfers between devices: 10.6 us -> 7.48 us  [swap(): return lax.ppermute(array, 'head', [(i, i ^ mask) for i in range(count)])]
    unnamed x11 -> x7, local copies, waits for them, and re-layouts: 3.44 us -> 0.79 us
    ppermute x0 -> x1, waiting for transfers between devices: none -> 1.84 us  [spread_slice(): return lax.ppermute(array, ('seq', 'head'), pairs)]
    ppermute x0 -> x1, starting transfers between devices: none -> 1.64 us  [spread_slice(): return lax.ppermute(array, ('seq', 'head'), pairs)]
    ppermute x8 -> x10, starting transfers between devices: 10.5 us -> 9.12 us  [trade(): lax.ppermute(array, 'seq', [(i, (i + (step if i % 2 == 0 else -step)) % c...]
    ppermute x8 -> x10, waiting for transfers between devices: 4.25 us -> 3.13 us  [trade(): lax.ppermute(array, 'seq', [(i, (i + (step if i % 2 == 0 else -step)) % c...]
    pallas_call x1, Pallas kernels: 0.86 us -> 1.96 us  [prepare(): pl.pallas_call(body, out_shape=(shape(BLK, HD), shape(8, columns, kind=F3...]
  transfers between devices with their start and end apart: 13 -> 15, of which waited for: 4 -> 6; matrix products, arithmetic and copies ran while one was open for 0% -> 0% of each run, Pallas kernels for 6% -> 9%
where the time goes in v3:
time: 38 us; the launch traced here: 37.8 us
  starting transfers between devices  19.3 us (51%)
  waiting for transfers between devices  12.4 us (33%)
  Pallas kernels  4.5 us (12%)
  local copies, waits for them, and re-layouts  0.81 us (2%)
  between operations  0.72 us (2%)
    ppermute x10, starting transfers between devices, trade(): lax.ppermute(array, 'seq', [(i, (i + (step if i % 2 == 0 else -step)) % c...  9.12 us
    ppermute x4, starting transfers between devices, swap(): return lax.ppermute(array, 'head', [(i, i ^ mask) for i in range(count)])  8.5 us
    ppermute x4, waiting for transfers between devices, swap(): return lax.ppermute(array, 'head', [(i, i ^ mask) for i in range(count)])  7.48 us
    ppermute x10, waiting for transfers between devices, trade(): lax.ppermute(array, 'seq', [(i, (i + (step if i % 2 == 0 else -step)) % c...  3.13 us
    pallas_call x1, Pallas kernels, prepare(): pl.pallas_call(body, out_shape=(shape(BLK, HD), shape(8, columns, kind=F3...  1.96 us
    ppermute x1, waiting for transfers between devices, spread_slice(): return lax.ppermute(array, ('seq', 'head'), pairs)  1.84 us
    ppermute x1, starting transfers between devices, spread_slice(): return lax.ppermute(array, ('seq', 'head'), pairs)  1.64 us
    pallas_call x1, Pallas kernels, attend(): pl.pallas_call(body, out_shape=(shape(BLK, HD), shape(BLK, HD)) + (shape(...  1.53 us
  transfers between devices with their start and end apart: 15, of which 6 were waited for; matrix products, arithmetic and copies ran while one was open for 0% of the time, Pallas kernels for 9%

profile of v3, /device:TPU:0, one launch (start us, length us, event | category | flops | bytes accessed | tf_op | source)
XLA Modules:
  0.0 37.8 jit_solution(5449410015713561543)
XLA Ops:
  0.6 0.8 %constant_dynamic-update-slice_fusion.1 = bf16[128,256]{1,0:T(8,128)(2,1)S(1)} fusion(bf16[128,128]{1,0:T(8,128)(2,1)} %param.7), kind=kLoop, calls=%fused_computation.3 | loop fusion | bytes 65536
  1.4 0.0 copy-start.1
  1.4 3.4 %collective-permute-start.1 = (bf16[128,256]{1,0:T(8,128)(2,1)S(1)}, bf16[128,256]{1,0:T(8,128)(2,1)S(1)}, u32[]{:S(2)}, u32[]{:S(2)}) collective-permute-start(bf16[128,256]{1,0:T(8,128)(2,1)S(1)} %constant_dynamic-update-slice_fusion.refs_3_), channel_id=1, source_target_pairs={{0,28},{4,8},{8,4},{12,16},{16,12},{20,24},{24,20},{28,0},{1,29},{... | collective-permute-start | bytes 196616 | tf_op jit(solution)/shard_map/ppermute | solution.py:41
  4.9 2.0 %prepare.1 = (bf16[128,128]{1,0:T(8,128)(2,1)S(1)}, f32[8,640]{1,0:T(8,128)S(1)}, bf16[128,512]{1,0:T(8,128)(2,1)S(1)}, bf16[128,512]{1,0:T(8,128)(2,1)S(1)}, bf16[64,512]{1,0:T(8,128)(2,1)S(1)}) custom-call(s32[1,8]{1,0:T(1,128)S(1)} %copy-done.1, bf16[128,2048]{1,0:T(8,128)(2,1)} %refs_1_.2, bf16[128,2048]{1,0:T(8,128)(2,1)} %refs_2_.1), custom_call_target="tpu_custom_call" | custom-call | tf_op jit(solution)/shard_map/prepare/pallas_call | solution.py:137
  6.8 1.6 %collective-permute-start.9 = (bf16[128,512]{1,0:T(8,128)(2,1)S(1)}, bf16[128,512]{1,0:T(8,128)(2,1)S(1)}, u32[]{:S(2)}, u32[]{:S(2)}) collective-permute-start(bf16[128,512]{1,0:T(8,128)(2,1)S(1)} %get-tuple-element.32), channel_id=1, source_target_pairs={{0,1},{1,0},{2,3},{3,2},{4,6},{5,7},{6,4},{7,5},{8,9},{9,8},{10,11... | collective-permute-start | bytes 393224 | tf_op jit(solution)/shard_map/ppermute | solution.py:286
  8.5 2.5 %collective-permute-start.10 = (bf16[64,512]{1,0:T(8,128)(2,1)S(1)}, bf16[64,512]{1,0:T(8,128)(2,1)S(1)}, u32[]{:S(2)}, u32[]{:S(2)}) collective-permute-start(bf16[64,512]{1,0:T(8,128)(2,1)S(1)} %get-tuple-element.33), channel_id=1, source_target_pairs={{0,3},{1,2},{2,1},{3,0},{4,7},{5,6},{6,5},{7,4},{8,11},{9,10},{10,... | collective-permute-start | bytes 196616 | tf_op jit(solution)/shard_map/ppermute | solution.py:48
  10.9 0.0 collective-permute-done.1.refs_5_
  10.9 0.0 collective-permute-done.refs_4_
  11.0 0.0 copy-start
  11.0 0.2 collective-permute-start.2
  11.2 1.8 %collective-permute-done.9.whole_ref = bf16[128,512]{1,0:T(8,128)(2,1)S(1)} collective-permute-done((bf16[128,512]{1,0:T(8,128)(2,1)S(1)}, bf16[128,512]{1,0:T(8,128)(2,1)S(1)}, u32[]{:S(2)}, u32[]{:S(2)}) %collective-permute-start.9) | collective-permute-done | bytes 131104 | tf_op jit(solution)/shard_map/ppermute | solution.py:286
  13.1 0.6 %collective-permute-start.11 = (bf16[128,512]{1,0:T(8,128)(2,1)S(1)}, bf16[128,512]{1,0:T(8,128)(2,1)S(1)}, u32[]{:S(2)}, u32[]{:S(2)}) collective-permute-start(bf16[128,512]{1,0:T(8,128)(2,1)S(1)} %collective-permute-done.9.whole_ref), channel_id=1, source_target_pairs={{0,4},{4,0},{8,12},{12,8},{16,20},{20,16},{24,28},{28,24},{1,5},{5... | collective-permute-start | bytes 393224 | tf_op jit(solution)/shard_map/ppermute | solution.py:41
  13.6 0.8 %collective-permute-start.3 = (bf16[64,256]{1,0:T(8,128)(2,1)S(1)}, bf16[64,256]{1,0:T(8,128)(2,1)S(1)}, u32[]{:S(2)}, u32[]{:S(2)}) collective-permute-start(bf16[64,256]{1,0:T(8,128)(2,1)S(1)} %pad_maximum_fusion.1), channel_id=1, source_target_pairs={{0,20},{4,16},{8,28},{12,24},{16,4},{20,0},{24,12},{28,8},{1,21},{... | collective-permute-start | bytes 98312 | tf_op jit(solution)/shard_map/ppermute | solution.py:41
  14.4 1.8 %collective-permute-done.10.half_ref = bf16[64,512]{1,0:T(8,128)(2,1)S(1)} collective-permute-done((bf16[64,512]{1,0:T(8,128)(2,1)S(1)}, bf16[64,512]{1,0:T(8,128)(2,1)S(1)}, u32[]{:S(2)}, u32[]{:S(2)}) %collective-permute-start.10) | collective-permute-done | bytes 65568 | tf_op jit(solution)/shard_map/ppermute | solution.py:48
  16.2 0.0 collective-permute-start.12
  16.2 1.0 %collective-permute-done.3.refs_7_ = bf16[64,256]{1,0:T(8,128)(2,1)S(1)} collective-permute-done((bf16[64,256]{1,0:T(8,128)(2,1)S(1)}, bf16[64,256]{1,0:T(8,128)(2,1)S(1)}, u32[]{:S(2)}, u32[]{:S(2)}) %collective-permute-start.3) | collective-permute-done | bytes 32800 | tf_op jit(solution)/shard_map/ppermute | solution.py:41
  17.2 1.5 %attend.1 = (bf16[128,128]{1,0:T(8,128)(2,1)S(1)}, bf16[128,128]{1,0:T(8,128)(2,1)}, f32[128,256]{1,0:T(8,128)S(1)}, f32[128,256]{1,0:T(8,128)S(1)}, f32[128,256...) custom-call(f32[8,640]{1,0:T(8,128)S(1)} %get-tuple-element.23.refs_0_, ...), custom_call_target="tpu_custom_call" | custom-call | tf_op jit(solution)/shard_map/attend/pallas_call | solution.py:196
  18.7 0.6 %collective-permute-start.7 = (bf16[96,256]{1,0:T(8,128)(2,1)S(1)}, bf16[96,256]{1,0:T(8,128)(2,1)S(1)}, u32[]{:S(2)}, u32[]{:S(2)}) collective-permute-start(bf16[96,256]{1,0:T(8,128)(2,1)S(1)} %get-tuple-element.29), channel_id=1, source_target_pairs={{0,12},{4,24},{8,20},{12,0},{16,28},{20,8},{24,4},{28,16},{1,13},{... | collective-permute-start | bytes 147464 | tf_op jit(solution)/shard_map/ppermute | solution.py:41
  19.2 1.3 %collective-permute-start.8 = (bf16[64,256]{1,0:T(8,128)(2,1)S(1)}, bf16[64,256]{1,0:T(8,128)(2,1)S(1)}, u32[]{:S(2)}, u32[]{:S(2)}) collective-permute-start(bf16[64,256]{1,0:T(8,128)(2,1)S(1)} %get-tuple-element.30), channel_id=1, source_target_pairs={{0,20},{4,16},{8,28},{12,24},{16,4},{20,0},{24,12},{28,8},{1,21},{... | collective-permute-start | bytes 98312 | tf_op jit(solution)/shard_map/ppermute | solution.py:41
  20.5 0.0 collective-permute-done.12.other_half_ref
  20.5 2.1 %collective-permute-done.8.minus_ref = bf16[64,256]{1,0:T(8,128)(2,1)S(1)} collective-permute-done((bf16[64,256]{1,0:T(8,128)(2,1)S(1)}, bf16[64,256]{1,0:T(8,128)(2,1)S(1)}, u32[]{:S(2)}, u32[]{:S(2)}) %collective-permute-start.8) | collective-permute-done | bytes 32800 | tf_op jit(solution)/shard_map/ppermute | solution.py:41
  22.6 0.0 collective-permute-done.7.plus_ref
  22.6 0.0 collective-permute-done.11.other_whole_ref
  22.6 0.1 combine.1
  22.7 0.7 %collective-permute-start.13 = (bf16[128,256]{1,0:T(8,128)(2,1)S(1)}, bf16[128,256]{1,0:T(8,128)(2,1)S(1)}, u32[]{:S(2)}, u32[]{:S(2)}) collective-permute-start(bf16[128,256]{1,0:T(8,128)(2,1)S(1)} %get-tuple-element.36), channel_id=1, source_target_pairs={{0,4},{4,0},{8,12},{12,8},{16,20},{20,16},{24,28},{28,24},{1,5},{5... | collective-permute-start | bytes 196616 | tf_op jit(solution)/shard_map/ppermute | solution.py:41
  23.4 1.6 %collective-permute-start.14 = (bf16[128,256]{1,0:T(8,128)(2,1)S(1)}, bf16[128,256]{1,0:T(8,128)(2,1)S(1)}, u32[]{:S(2)}, u32[]{:S(2)}) collective-permute-start(bf16[128,256]{1,0:T(8,128)(2,1)S(1)} %get-tuple-element.37), channel_id=1, source_target_pairs={{0,28},{4,8},{8,4},{12,16},{16,12},{20,24},{24,20},{28,0},{1,29},{... | collective-permute-start | bytes 196616 | tf_op jit(solution)/shard_map/ppermute | solution.py:41
  25.1 2.8 %collective-permute-start.4 = (bf16[128,128]{1,0:T(8,128)(2,1)S(1)}, bf16[128,128]{1,0:T(8,128)(2,1)S(1)}, u32[]{:S(2)}, u32[]{:S(2)}) collective-permute-start(bf16[128,128]{1,0:T(8,128)(2,1)S(1)} %get-tuple-element.25.refs_0_), channel_id=1, source_target_pairs={{0,1},{1,0},{2,3},{3,2},{4,5},{5,4},{6,7},{7,6},{8,9},{9,8},{10,11... | collective-permute-start | bytes 98312 | tf_op jit(solution)/shard_map/ppermute | solution.py:48
  27.9 3.2 %collective-permute-start.5 = (bf16[128,128]{1,0:T(8,128)(2,1)S(1)}, bf16[128,128]{1,0:T(8,128)(2,1)S(1)}, u32[]{:S(2)}, u32[]{:S(2)}) collective-permute-start(bf16[128,128]{1,0:T(8,128)(2,1)S(1)} %get-tuple-element.25.refs_0_), channel_id=1, source_target_pairs={{0,2},{1,3},{2,0},{3,1},{4,6},{5,7},{6,4},{7,5},{8,10},{9,11},{10,... | collective-permute-start | bytes 98312 | tf_op jit(solution)/shard_map/ppermute | solution.py:48
  31.1 0.0 collective-permute-start.6
  31.1 2.3 %collective-permute-done.5.refs_2_ = bf16[128,128]{1,0:T(8,128)(2,1)S(1)} collective-permute-done((bf16[128,128]{1,0:T(8,128)(2,1)S(1)}, bf16[128,128]{1,0:T(8,128)(2,1)S(1)}, u32[]{:S(2)}, u32[]{:S(2)}) %collective-permute-start.5) | collective-permute-done | bytes 32800 | tf_op jit(solution)/shard_map/ppermute | solution.py:48
  33.4 3.4 %collective-permute-done.6.refs_3_ = bf16[128,128]{1,0:T(8,128)(2,1)S(1)} collective-permute-done((bf16[128,128]{1,0:T(8,128)(2,1)S(1)}, bf16[128,128]{1,0:T(8,128)(2,1)S(1)}, u32[]{:S(2)}, u32[]{:S(2)}) %collective-permute-start.6) | collective-permute-done | bytes 32800 | tf_op jit(solution)/shard_map/ppermute | solution.py:48
  36.8 0.9 %finish.1 = (bf16[128,512]{1,0:T(8,128)(2,1)}, bf16[128,128]{1,0:T(8,128)(2,1)}, bf16[128,128]{1,0:T(8,128)(2,1)}) custom-call(bf16[128,128]{1,0:T(8,128)(2,1)S(1)} %get-tuple-element.25.refs_0_, bf16[128,128]{1,0:T(8,128)(2,1)S(1)} %collective-permute-done.4.refs_1_, bf16[128,128]{1,0:T(8,128)(2,1)S(1)} %collective-permute-done.5.refs_2_, ...), custom_call_target="tpu_custom_call" | custom-call | tf_op jit(solution)/shard_map/finish/pallas_call | solution.py:271
  (15 shorter events, 0.1 us)
Async XLA Ops:
  0.6 0.8 %copy-start.2 = (bf16[128,128]{1,0:T(8,128)(2,1)S(1)}, bf16[128,128]{1,0:T(8,128)(2,1)}, u32[]{:S(2)}) copy-start(bf16[128,128]{1,0:T(8,128)(2,1)} %param.8) | copy-start | bytes 98308
  1.4 3.4 %copy-start.1 = (s32[1,8]{1,0:T(1,128)S(1)}, s32[1,8]{1,0:T(1,128)}, u32[]{:S(2)}) copy-start(s32[1,8]{1,0:T(1,128)} %refs_0_.1) | copy-start | bytes 100
  1.4 9.5 %collective-permute-start.1 = (bf16[128,256]{1,0:T(8,128)(2,1)S(1)}, bf16[128,256]{1,0:T(8,128)(2,1)S(1)}, u32[]{:S(2)}, u32[]{:S(2)}) collective-permute-start(bf16[128,256]{1,0:T(8,128)(2,1)S(1)} %constant_dynamic-update-slice_fusion.refs_3_), channel_id=1, source_target_pairs={{0,28},{4,8},{8,4},{12,16},{16,12},{20,24},{24,20},{28,0},{1,29},{... | collective-permute-start | bytes 196616 | tf_op jit(solution)/shard_map/ppermute | solution.py:41
  4.8 6.1 %collective-permute-start = (bf16[128,256]{1,0:T(8,128)(2,1)S(1)}, bf16[128,256]{1,0:T(8,128)(2,1)S(1)}, u32[]{:S(2)}, u32[]{:S(2)}) collective-permute-start(bf16[128,256]{1,0:T(8,128)(2,1)S(1)} %constant_dynamic-update-slice_fusion.refs_3_), channel_id=1, source_target_pairs={{0,4},{4,0},{8,12},{12,8},{16,20},{20,16},{24,28},{28,24},{1,5},{5... | collective-permute-start | bytes 196616 | tf_op jit(solution)/shard_map/ppermute | solution.py:41
  6.8 6.2 %collective-permute-start.9 = (bf16[128,512]{1,0:T(8,128)(2,1)S(1)}, bf16[128,512]{1,0:T(8,128)(2,1)S(1)}, u32[]{:S(2)}, u32[]{:S(2)}) collective-permute-start(bf16[128,512]{1,0:T(8,128)(2,1)S(1)} %get-tuple-element.32), channel_id=1, source_target_pairs={{0,1},{1,0},{2,3},{3,2},{4,6},{5,7},{6,4},{7,5},{8,9},{9,8},{10,11... | collective-permute-start | bytes 393224 | tf_op jit(solution)/shard_map/ppermute | solution.py:286
  8.5 7.7 %collective-permute-start.10 = (bf16[64,512]{1,0:T(8,128)(2,1)S(1)}, bf16[64,512]{1,0:T(8,128)(2,1)S(1)}, u32[]{:S(2)}, u32[]{:S(2)}) collective-permute-start(bf16[64,512]{1,0:T(8,128)(2,1)S(1)} %get-tuple-element.33), channel_id=1, source_target_pairs={{0,3},{1,2},{2,1},{3,0},{4,7},{5,6},{6,5},{7,4},{8,11},{9,10},{10,... | collective-permute-start | bytes 196616 | tf_op jit(solution)/shard_map/ppermute | solution.py:48
  11.0 6.2 %copy-start = (bf16[128,128]{1,0:T(8,128)(2,1)S(1)}, bf16[128,128]{1,0:T(8,128)(2,1)}, u32[]{:S(2)}) copy-start(bf16[128,128]{1,0:T(8,128)(2,1)} %refs_1_.3) | copy-start | bytes 98308
  11.0 6.2 %collective-permute-start.2 = (bf16[96,256]{1,0:T(8,128)(2,1)S(1)}, bf16[96,256]{1,0:T(8,128)(2,1)S(1)}, u32[]{:S(2)}, u32[]{:S(2)}) collective-permute-start(bf16[96,256]{1,0:T(8,128)(2,1)S(1)} %pad_maximum_fusion), channel_id=1, source_target_pairs={{0,12},{4,24},{8,20},{12,0},{16,28},{20,8},{24,4},{28,16},{1,13},{... | collective-permute-start | bytes 147464 | tf_op jit(solution)/shard_map/ppermute | solution.py:41
  13.1 9.6 %collective-permute-start.11 = (bf16[128,512]{1,0:T(8,128)(2,1)S(1)}, bf16[128,512]{1,0:T(8,128)(2,1)S(1)}, u32[]{:S(2)}, u32[]{:S(2)}) collective-permute-start(bf16[128,512]{1,0:T(8,128)(2,1)S(1)} %collective-permute-done.9.whole_ref), channel_id=1, source_target_pairs={{0,4},{4,0},{8,12},{12,8},{16,20},{20,16},{24,28},{28,24},{1,5},{5... | collective-permute-start | bytes 393224 | tf_op jit(solution)/shard_map/ppermute | solution.py:41
  13.6 3.5 %collective-permute-start.3 = (bf16[64,256]{1,0:T(8,128)(2,1)S(1)}, bf16[64,256]{1,0:T(8,128)(2,1)S(1)}, u32[]{:S(2)}, u32[]{:S(2)}) collective-permute-start(bf16[64,256]{1,0:T(8,128)(2,1)S(1)} %pad_maximum_fusion.1), channel_id=1, source_target_pairs={{0,20},{4,16},{8,28},{12,24},{16,4},{20,0},{24,12},{28,8},{1,21},{... | collective-permute-start | bytes 98312 | tf_op jit(solution)/shard_map/ppermute | solution.py:41
  16.2 4.3 %collective-permute-start.12 = (bf16[64,512]{1,0:T(8,128)(2,1)S(1)}, bf16[64,512]{1,0:T(8,128)(2,1)S(1)}, u32[]{:S(2)}, u32[]{:S(2)}) collective-permute-start(bf16[64,512]{1,0:T(8,128)(2,1)S(1)} %collective-permute-done.10.half_ref), channel_id=1, source_target_pairs={{0,4},{4,0},{8,12},{12,8},{16,20},{20,16},{24,28},{28,24},{1,5},{5... | collective-permute-start | bytes 196616 | tf_op jit(solution)/shard_map/ppermute | solution.py:41
  18.7 4.0 %collective-permute-start.7 = (bf16[96,256]{1,0:T(8,128)(2,1)S(1)}, bf16[96,256]{1,0:T(8,128)(2,1)S(1)}, u32[]{:S(2)}, u32[]{:S(2)}) collective-permute-start(bf16[96,256]{1,0:T(8,128)(2,1)S(1)} %get-tuple-element.29), channel_id=1, source_target_pairs={{0,12},{4,24},{8,20},{12,0},{16,28},{20,8},{24,4},{28,16},{1,13},{... | collective-permute-start | bytes 147464 | tf_op jit(solution)/shard_map/ppermute | solution.py:41
  19.2 3.4 %collective-permute-start.8 = (bf16[64,256]{1,0:T(8,128)(2,1)S(1)}, bf16[64,256]{1,0:T(8,128)(2,1)S(1)}, u32[]{:S(2)}, u32[]{:S(2)}) collective-permute-start(bf16[64,256]{1,0:T(8,128)(2,1)S(1)} %get-tuple-element.30), channel_id=1, source_target_pairs={{0,20},{4,16},{8,28},{12,24},{16,4},{20,0},{24,12},{28,8},{1,21},{... | collective-permute-start | bytes 98312 | tf_op jit(solution)/shard_map/ppermute | solution.py:41
  22.7 14.1 %collective-permute-start.13 = (bf16[128,256]{1,0:T(8,128)(2,1)S(1)}, bf16[128,256]{1,0:T(8,128)(2,1)S(1)}, u32[]{:S(2)}, u32[]{:S(2)}) collective-permute-start(bf16[128,256]{1,0:T(8,128)(2,1)S(1)} %get-tuple-element.36), channel_id=1, source_target_pairs={{0,4},{4,0},{8,12},{12,8},{16,20},{20,16},{24,28},{28,24},{1,5},{5... | collective-permute-start | bytes 196616 | tf_op jit(solution)/shard_map/ppermute | solution.py:41
  23.4 13.4 %collective-permute-start.14 = (bf16[128,256]{1,0:T(8,128)(2,1)S(1)}, bf16[128,256]{1,0:T(8,128)(2,1)S(1)}, u32[]{:S(2)}, u32[]{:S(2)}) collective-permute-start(bf16[128,256]{1,0:T(8,128)(2,1)S(1)} %get-tuple-element.37), channel_id=1, source_target_pairs={{0,28},{4,8},{8,4},{12,16},{16,12},{20,24},{24,20},{28,0},{1,29},{... | collective-permute-start | bytes 196616 | tf_op jit(solution)/shard_map/ppermute | solution.py:41
  25.1 6.0 %collective-permute-start.4 = (bf16[128,128]{1,0:T(8,128)(2,1)S(1)}, bf16[128,128]{1,0:T(8,128)(2,1)S(1)}, u32[]{:S(2)}, u32[]{:S(2)}) collective-permute-start(bf16[128,128]{1,0:T(8,128)(2,1)S(1)} %get-tuple-element.25.refs_0_), channel_id=1, source_target_pairs={{0,1},{1,0},{2,3},{3,2},{4,5},{5,4},{6,7},{7,6},{8,9},{9,8},{10,11... | collective-permute-start | bytes 98312 | tf_op jit(solution)/shard_map/ppermute | solution.py:48
  27.9 5.4 %collective-permute-start.5 = (bf16[128,128]{1,0:T(8,128)(2,1)S(1)}, bf16[128,128]{1,0:T(8,128)(2,1)S(1)}, u32[]{:S(2)}, u32[]{:S(2)}) collective-permute-start(bf16[128,128]{1,0:T(8,128)(2,1)S(1)} %get-tuple-element.25.refs_0_), channel_id=1, source_target_pairs={{0,2},{1,3},{2,0},{3,1},{4,6},{5,7},{6,4},{7,5},{8,10},{9,11},{10,... | collective-permute-start | bytes 98312 | tf_op jit(solution)/shard_map/ppermute | solution.py:48
  31.1 5.7 %collective-permute-start.6 = (bf16[128,128]{1,0:T(8,128)(2,1)S(1)}, bf16[128,128]{1,0:T(8,128)(2,1)S(1)}, u32[]{:S(2)}, u32[]{:S(2)}) collective-permute-start(bf16[128,128]{1,0:T(8,128)(2,1)S(1)} %get-tuple-element.25.refs_0_), channel_id=1, source_target_pairs={{0,3},{1,2},{2,1},{3,0},{4,7},{5,6},{6,5},{7,4},{8,11},{9,10},{10,... | collective-permute-start | bytes 98312 | tf_op jit(solution)/shard_map/ppermute | solution.py:48

commit v4 on v3

v4 whole, which is shorter than its diff:
```python
import jax
import jax.numpy as jnp
from jax import lax
from jax.experimental import pallas as pl
from jax.experimental.pallas import tpu as pltpu
from jax.sharding import PartitionSpec as P

HD = 128
BLK = 128
STRIDE_ROWS = 32
PAIR = 2 * HD
SCALE = HD ** (-0.5)
LOG2E = 1.4426950408889634
ABSENT = -1e30
VMEM = pl.BlockSpec(memory_space=pltpu.VMEM)
HBM = pl.BlockSpec(memory_space=pltpu.HBM)
PARAMS = pltpu.CompilerParams(vmem_limit_bytes=40 * 1024 * 1024)
FULL = pltpu.CompilerParams(vmem_limit_bytes=int(53.3 * 1024 * 1024))
BF16 = jnp.bfloat16
PREPARE_COST = 10**10
ATTEND_COST = 10**9
COLLECT_COST = 10**10
F32 = jnp.float32


def dot_nt(a, b):
    return lax.dot_general(a, b, (((1,), (1,)), ((), ())), preferred_element_type=F32)


def dot_nn(a, b):
    return lax.dot_general(a, b, (((1,), (0,)), ((), ())), preferred_element_type=F32)


def dot_tn(a, b):
    return lax.dot_general(a, b, (((0,), (0,)), ((), ())), preferred_element_type=F32)


def shape(*dims, kind=BF16):
    return jax.ShapeDtypeStruct(dims, kind)


def trade(array, step):
    count = lax.axis_size("seq")
    return lax.ppermute(
        array, "seq", [(i, (i + (step if i % 2 == 0 else -step)) % count) for i in range(count)]
    )


def swap(array, mask):
    count = lax.axis_size("head")
    return lax.ppermute(array, "head", [(i, i ^ mask) for i in range(count)])


def count_of(picks, group):
    total = jnp.int32(0)
    for pick in picks:
        total = total + jnp.where(pick == group, 1, 0)
    return total.astype(F32)


def fill_multiplicity(ring, index_ref, mult_ref):
    per_block = BLK // STRIDE_ROWS
    picks = [index_ref[0, i] for i in range(index_ref.shape[1])]
    shape_of = mult_ref.shape
    lane = lax.broadcasted_iota(jnp.int32, shape_of, 1)
    mult = jnp.where(lane < 3 * BLK, 1.0, 0.0)
    if ring:
        b = lax.axis_index("seq")
        sign = 1 - 2 * (b & 1)
        counts = [count_of(picks, j) for j in range(2)]
        offsets = [(0, 0), (BLK, 1), (2 * BLK, -1), (3 * BLK, 3), (3 * BLK + 32, 2),
                   (3 * BLK + 64, 4), (3 * BLK + 96, -3), (3 * BLK + 128, -2)]
        for start, offset in offsets:
            owner = (b + 16 + sign * offset) & 7
            count = jnp.where(owner < per_block, counts[0], counts[1])
            inside = (lane >= start) & (lane < start + STRIDE_ROWS)
            mult = mult + jnp.where(inside, count, 0.0)
    else:
        for j in range((shape_of[1] - 3 * BLK) // BLK):
            start = (3 + j) * BLK
            inside = (lane >= start) & (lane < start + BLK)
            mult = mult + jnp.where(inside, count_of(picks, j), 0.0)
    mult_ref[...] = mult


def cost(flops):
    return pl.CostEstimate(flops=flops, bytes_accessed=0, transcendentals=0)


def slices_kernel(ring, w_hbm, *refs):
    slice_refs = refs[:-1]
    sems = refs[-1]
    width = slice_refs[0].shape[1]
    head = lax.axis_index("head")
    core = lax.axis_index("seq") & 1

    def columns(h):
        return pl.ds(pl.multiple_of(h * width, width), width)

    if ring:
        half = HD // 2
        sources = [
            w_hbm.at[:, columns(head)],
            w_hbm.at[:, columns(head ^ (1 + core))],
            w_hbm.at[pl.ds(pl.multiple_of(core * half, half), half), columns(head ^ 3)],
        ]
    else:
        sources = [w_hbm.at[:, columns(head ^ r)] for r in range(len(slice_refs))]
    copies = [pltpu.make_async_copy(src, dst, sems.at[i])
              for i, (src, dst) in enumerate(zip(sources, slice_refs))]
    for copy in copies:
        copy.start()
    for copy in copies:
        copy.wait()


def weight_slices(ring, out_weight, heads):
    width = out_weight.shape[1] // heads
    rows = (HD, HD, HD // 2) if ring else (HD,) * heads

    def body(*refs):
        slices_kernel(ring, *refs)

    return pl.pallas_call(
        body,
        out_shape=tuple(shape(r, width) for r in rows),
        in_specs=[HBM],
        out_specs=(VMEM,) * len(rows),
        scratch_shapes=[pltpu.SemaphoreType.DMA((len(rows),))],
        compiler_params=FULL,
        name="slices",
    )(out_weight)


CHUNKS = 4


def prepare_kernel(ring, index_hbm, cot_hbm, w_hbm, after_ref, grad_ref, mult_ref,
                   index_ref, cot_ref, w_ref, sems):
    del after_ref
    copies = [(index_hbm, index_ref)]
    depth = cot_ref.shape[1] // CHUNKS
    for i in range(CHUNKS):
        span = pl.ds(i * depth, depth)
        copies.append((cot_hbm.at[:, span], cot_ref.at[:, span]))
        copies.append((w_hbm.at[:, span], w_ref.at[:, span]))
    copies = [pltpu.make_async_copy(src, dst, sems.at[i]) for i, (src, dst) in enumerate(copies)]
    for copy in copies:
        copy.start()
    copies[0].wait()
    fill_multiplicity(ring, index_ref, mult_ref)
    total = None
    for i in range(CHUNKS):
        copies[1 + 2 * i].wait()
        copies[2 + 2 * i].wait()
        span = slice(i * depth, (i + 1) * depth)
        term = dot_nt(cot_ref[:, span], w_ref[:, span])
        total = term if total is None else total + term
    grad_ref[...] = total.astype(grad_ref.dtype)


def prepare(ring, index, cotangent, out_weight, columns, after):
    def body(*refs):
        prepare_kernel(ring, *refs)

    return pl.pallas_call(
        body,
        out_shape=(shape(BLK, HD), shape(8, columns, kind=F32)),
        in_specs=[HBM] * 3 + [VMEM],
        out_specs=(VMEM,) * 2,
        scratch_shapes=[
            pltpu.SMEM(index.shape, jnp.int32),
            pltpu.VMEM(cotangent.shape, BF16),
            pltpu.VMEM(out_weight.shape, BF16),
            pltpu.SemaphoreType.DMA((1 + 2 * CHUNKS,)),
        ],
        compiler_params=FULL,
        cost_estimate=cost(PREPARE_COST),
        name="prepare",
    )(index, cotangent, out_weight, after)


def lead_kernel(own_ref, first_ref, second_ref, plus_ref, minus_ref):
    n = STRIDE_ROWS
    plus_ref[:n] = own_ref[:n]
    plus_ref[n:2 * n] = first_ref[:n]
    plus_ref[2 * n:] = second_ref[:n]
    minus_ref[:n] = own_ref[:n]
    minus_ref[n:] = second_ref[:n]


def leads(own, first, second):
    n = STRIDE_ROWS
    return pl.pallas_call(
        lead_kernel,
        out_shape=(shape(3 * n, PAIR), shape(2 * n, PAIR)),
        in_specs=[VMEM] * 3,
        out_specs=(VMEM,) * 2,
        compiler_params=PARAMS,
        name="leads",
    )(own, first, second)


def attend_kernel(sides, mult_ref, q_ref, grad_ref, *refs):
    block_refs = refs[:3 + sides]
    att_ref, dq_ref = refs[3 + sides:5 + sides]
    sum_refs = refs[5 + sides:9 + sides]
    keys_ref = refs[-1]
    total_rows = keys_ref.shape[0]
    spans = []
    row = 0
    for ref in block_refs:
        spans.append((row, row + ref.shape[0]))
        keys_ref[row:row + ref.shape[0], :] = ref[...]
        row += ref.shape[0]
    if row < total_rows:
        keys_ref[row:, :] = jnp.zeros((total_rows - row, PAIR), BF16)
    keys = keys_ref[:, :HD]
    values = keys_ref[:, HD:]
    q = q_ref[...]
    grad = grad_ref[...]
    mult = mult_ref[0:1, :]

    scores = dot_nt(q, keys) + jnp.where(mult > 0.0, 0.0, ABSENT)
    top = jnp.max(scores, axis=1, keepdims=True)
    terms = jnp.exp2((scores - top) * (SCALE * LOG2E)) * mult
    probability = terms * (1.0 / jnp.sum(terms, axis=1, keepdims=True))
    weights = probability.astype(BF16)
    att_ref[...] = dot_nn(weights, values).astype(BF16)

    grad_weights = dot_nt(grad, values)
    delta = jnp.sum(probability * grad_weights, axis=1, keepdims=True)
    grad_scores = (probability * (grad_weights - delta) * SCALE).astype(BF16)
    dq_ref[...] = dot_nn(grad_scores, keys).astype(BF16)
    key_terms = dot_tn(grad_scores, q)
    value_terms = dot_tn(weights, grad)
    for (start, end), ref in zip(spans, sum_refs[:3]):
        ref[:, :HD] = key_terms[start:end].astype(ref.dtype)
        ref[:, HD:] = value_terms[start:end].astype(ref.dtype)
    side_ref = sum_refs[3]
    if sides == 1:
        side_ref[:, :HD] = key_terms[3 * BLK:].astype(BF16)
        side_ref[:, HD:] = value_terms[3 * BLK:].astype(BF16)
    else:
        b = lax.axis_index("seq")
        sign = 1 - 2 * (b & 1)
        side_ref[...] = jnp.zeros(side_ref.shape, BF16)
        for i, offset in enumerate((3, 2, 4, -3, -2)):
            owner = (b + 16 + sign * offset) & 7
            start = 3 * BLK + i * STRIDE_ROWS
            rows = pl.ds(pl.multiple_of(owner * STRIDE_ROWS, STRIDE_ROWS), STRIDE_ROWS)
            side_ref[rows, :HD] = key_terms[start:start + STRIDE_ROWS].astype(BF16)
            side_ref[rows, HD:] = value_terms[start:start + STRIDE_ROWS].astype(BF16)


def attend(mult, q, grad, window, sides, side_rows):
    def body(*refs):
        attend_kernel(len(sides), *refs)

    return pl.pallas_call(
        body,
        out_shape=(shape(BLK, HD), shape(BLK, HD), shape(BLK, PAIR, kind=F32),
                   shape(BLK, PAIR), shape(BLK, PAIR), shape(side_rows, PAIR)),
        in_specs=[VMEM] * (6 + len(sides)),
        out_specs=(VMEM,) * 6,
        scratch_shapes=[pltpu.VMEM((mult.shape[1], PAIR), BF16)],
        compiler_params=PARAMS,
        cost_estimate=cost(ATTEND_COST),
        name="attend",
    )(mult, q, grad, *window, *sides)


def join_kernel(whole_ref, half_ref, after_ref, out_ref):
    del after_ref
    out_ref[:HD] = whole_ref[...]
    out_ref[HD:] = half_ref[...]


def join(whole, half, after):
    return pl.pallas_call(
        join_kernel,
        out_shape=shape(HD + HD // 2, whole.shape[1]),
        in_specs=[VMEM] * 3,
        out_specs=VMEM,
        compiler_params=PARAMS,
        name="join",
    )(whole, half, after)


def collect_kernel(mine_ref, here_ref, there_ref, own_ref, first_ref, second_ref, *refs):
    att_refs = refs[:-3]
    att_out, w_out, sum_out = refs[-3:]
    for r, ref in enumerate(att_refs):
        att_out[:, r * HD:(r + 1) * HD] = ref[...]
    core = lax.axis_index("seq") & 1
    half = HD // 2
    w_out[:HD] = mine_ref[...]
    w_out[pl.ds(pl.multiple_of(HD + core * HD, HD), HD)] = here_ref[:HD]
    w_out[pl.ds(pl.multiple_of(2 * HD - core * HD, HD), HD)] = there_ref[:HD]
    w_out[pl.ds(pl.multiple_of(3 * HD + core * half, half), half)] = here_ref[HD:]
    w_out[pl.ds(pl.multiple_of(3 * HD + half - core * half, half), half)] = there_ref[HD:]
    sum_out[...] = own_ref[...] + first_ref[...].astype(F32) + second_ref[...].astype(F32)


def collect(mine, here, there, own, first, second, attentions):
    return pl.pallas_call(
        collect_kernel,
        out_shape=(shape(BLK, 4 * HD), shape(4 * HD, mine.shape[1]), shape(BLK, PAIR, kind=F32)),
        in_specs=[VMEM] * (6 + len(attentions)),
        out_specs=(VMEM,) * 3,
        compiler_params=PARAMS,
        cost_estimate=cost(COLLECT_COST),
        name="collect",
    )(mine, here, there, own, first, second, *attentions)


def finish_kernel(count, *refs):
    att_refs = refs[:count]
    w_refs = refs[count:2 * count]
    sum_refs = refs[2 * count:-4]
    side_ref, mixed_ref, dk_ref, dv_ref = refs[-4:]
    mixed = None
    for ref, w in zip(att_refs, w_refs):
        term = dot_nn(ref[...], w[...])
        mixed = term if mixed is None else mixed + term
    mixed_ref[...] = mixed.astype(mixed_ref.dtype)
    total = sum_refs[0][...]
    for ref in sum_refs[1:]:
        total = total + ref[...].astype(F32)
    lead = total[:STRIDE_ROWS]
    for i in range(side_ref.shape[0] // STRIDE_ROWS):
        lead = lead + side_ref[i * STRIDE_ROWS:(i + 1) * STRIDE_ROWS].astype(F32)
    for ref, c in ((dk_ref, 0), (dv_ref, HD)):
        ref[:STRIDE_ROWS] = lead[:, c:c + HD].astype(ref.dtype)
        ref[STRIDE_ROWS:] = total[STRIDE_ROWS:, c:c + HD].astype(ref.dtype)


def finish(attentions, slices, sums, side):
    width = slices[0].shape[1]
    count = len(attentions)

    def body(*refs):
        finish_kernel(count, *refs)

    return pl.pallas_call(
        body,
        out_shape=(shape(BLK, width), shape(BLK, HD), shape(BLK, HD)),
        in_specs=[VMEM] * (2 * count + len(sums) + 1),
        out_specs=(VMEM,) * 3,
        compiler_params=PARAMS,
        name="finish",
    )(*attentions, *slices, *sums, side)


def spread_slice(array):
    seq = lax.axis_size("seq")
    heads = lax.axis_size("head")
    pairs = [(b * heads + h, b * heads + (h ^ (1 + b % 2))) for b in range(seq)
             for h in range(heads)]
    return lax.ppermute(array, ("seq", "head"), pairs)


def shards(queries, key_rows, value_rows, out_weight, strided_index, cotangent):
    seq = lax.axis_size("seq")
    heads = lax.axis_size("head")
    ring = seq == 8 and heads == 4
    n = STRIDE_ROWS
    side_rows = seq * n
    columns = 3 * BLK + side_rows
    own = jnp.concatenate([key_rows, value_rows], axis=1)
    first = trade(own, 1)
    second = trade(own, -1)
    slices = weight_slices(ring, out_weight, heads)
    if ring:
        mine, whole, half = slices
        whole = spread_slice(whole)
        half = swap(half, 3)
        plus, minus = leads(own, first, second)
        grad, mult = prepare(ring, strided_index, cotangent, out_weight, columns, minus)
        sides = (trade(plus, 3), trade(minus, -3))
    else:
        slices = [slices[0]] + [swap(slices[r], r) for r in range(1, heads)]
        grad, mult = prepare(ring, strided_index, cotangent, out_weight, columns, own)
        spread = jnp.broadcast_to(own[None, :n], (seq, n, PAIR))
        sides = (lax.all_to_all(spread, "seq", 0, 0).reshape(side_rows, PAIR),)
    att, dq, own_sum, to_first, to_second, to_side = attend(
        mult, queries, grad, (own, first, second), sides, side_rows
    )
    attentions = [att] + [swap(att, r) for r in range(1, heads)]
    sums = (own_sum, trade(to_first, 1), trade(to_second, -1))
    from_side = lax.all_to_all(to_side.reshape(seq, n, PAIR), "seq", 0, 0)
    from_side = from_side.reshape(side_rows, PAIR)
    if ring:
        here = join(whole, half, att)
        gathered, weight, total = collect(mine, here, trade(here, 1), *sums, attentions)
        mixed, dk, dv = finish([gathered], [weight], [total], from_side)
    else:
        mixed, dk, dv = finish(attentions, slices, sums, from_side)
    return (mixed, dq, dk, dv)


def solution(mesh):
    in_specs = (
        P("seq", "head"),
        P("seq", "head"),
        P("seq", "head"),
        P("head", None),
        P("seq", None),
        P("seq", None),
    )
    out_specs = (P("seq", "head"), P("seq", "head"), P("seq", "head"), P("seq", "head"))
    return jax.shard_map(shards, mesh=mesh, in_specs=in_specs, out_specs=out_specs, check_vma=False)
```

time: 38 us -> 33.2 us (0.87)
  waiting for transfers between devices: 12.4 us -> 8.41 us
  starting transfers between devices: 19.3 us -> 17.5 us
  Pallas kernels: 4.5 us -> 5.35 us
    ppermute x4, waiting for transfers between devices: 7.48 us -> 1.91 us  [swap(): return lax.ppermute(array, 'head', [(i, i ^ mask) for i in range(count)])]
    all_to_all x0 -> x1, waiting for transfers between devices: none -> 5.04 us  [shards(): from_side = lax.all_to_all(to_side.reshape(seq, n, PAIR), 'seq', 0, 0)]
    all_to_all x0 -> x1, starting transfers between devices: none -> 3.37 us  [shards(): from_side = lax.all_to_all(to_side.reshape(seq, n, PAIR), 'seq', 0, 0)]
    ppermute x4, starting transfers between devices: 8.5 us -> 5.89 us  [swap(): return lax.ppermute(array, 'head', [(i, i ^ mask) for i in range(count)])]
    ppermute x10 -> x7, waiting for transfers between devices: 3.13 us -> 0.97 us  [trade(): lax.ppermute(array, 'seq', [(i, (i + (step if i % 2 == 0 else -step)) % c...]
    ppermute x1, starting transfers between devices: 1.64 us -> 0.01 us  [spread_slice(): return lax.ppermute(array, ('seq', 'head'), pairs)]
    ppermute x1, waiting for transfers between devices: 1.84 us -> 0.49 us  [spread_slice(): return lax.ppermute(array, ('seq', 'head'), pairs)]
    pallas_call x2 -> x5, Pallas kernels: 1.6 us -> 2.78 us  [the longest x1 1.68 us: attend(): pl.pallas_call(body, out_shape=(shape(BLK, HD), shape(BLK, HD), shape(BLK...]
  transfers between devices with their start and end apart: 15 -> 13, of which waited for: 6 -> 6; matrix products, arithmetic and copies ran while one was open for 0% -> 0% of each run, Pallas kernels for 9% -> 14%
where the time goes in v4:
time: 33.2 us; the launch traced here: 32.9 us
  starting transfers between devices  17.5 us (53%)
  waiting for transfers between devices  8.41 us (25%)
  Pallas kernels  5.35 us (16%)
  local copies, waits for them, and re-layouts  0.86 us (3%)
  between operations  0.74 us (2%)
    ppermute x7, starting transfers between devices, trade(): lax.ppermute(array, 'seq', [(i, (i + (step if i % 2 == 0 else -step)) % c...  8.28 us
    ppermute x4, starting transfers between devices, swap(): return lax.ppermute(array, 'head', [(i, i ^ mask) for i in range(count)])  5.89 us
    all_to_all x1, waiting for transfers between devices, shards(): from_side = lax.all_to_all(to_side.reshape(seq, n, PAIR), 'seq', 0, 0)  5.04 us
    all_to_all x1, starting transfers between devices, shards(): from_side = lax.all_to_all(to_side.reshape(seq, n, PAIR), 'seq', 0, 0)  3.37 us
    ppermute x4, waiting for transfers between devices, swap(): return lax.ppermute(array, 'head', [(i, i ^ mask) for i in range(count)])  1.91 us
    pallas_call x1, Pallas kernels, attend(): pl.pallas_call(body, out_shape=(shape(BLK, HD), shape(BLK, HD), shape(BLK...  1.68 us
    pallas_call x1, Pallas kernels, prepare(): pl.pallas_call(body, out_shape=(shape(BLK, HD), shape(8, columns, kind=F3...  1.68 us
    pallas_call x1, Pallas kernels, weight_slices(): pl.pallas_call(body, out_shape=tuple((shape(r, width) for r in rows)), in...  1 us
  transfers between devices with their start and end apart: 13, of which 6 were waited for; matrix products, arithmetic and copies ran while one was open for 0% of the time, Pallas kernels for 14%

profile of v4, /device:TPU:0, one launch (start us, length us, event | category | flops | bytes accessed | tf_op | source)
XLA Modules:
  0.0 32.9 jit_solution(9435715247014543388)
XLA Ops:
  0.7 0.8 %constant_dynamic-update-slice_fusion.1 = bf16[128,256]{1,0:T(8,128)(2,1)S(1)} fusion(bf16[128,128]{1,0:T(8,128)(2,1)} %param.7), kind=kLoop, calls=%fused_computation.1 | loop fusion | bytes 65536
  1.5 3.4 %collective-permute-start.3 = (bf16[128,256]{1,0:T(8,128)(2,1)S(1)}, bf16[128,256]{1,0:T(8,128)(2,1)S(1)}, u32[]{:S(2)}, u32[]{:S(2)}) collective-permute-start(bf16[128,256]{1,0:T(8,128)(2,1)S(1)} %constant_dynamic-update-slice_fusion.own_ref.refs_3_), channel_id=1, source_target_pairs={{0,28},{4,8},{8,4},{12,16},{16,12},{20,24},{24,20},{28,0},{1,29},{... | collective-permute-start | bytes 196616 | tf_op jit(solution)/shard_map/ppermute | solution.py:44
  4.9 0.0 collective-permute-start.2
  4.9 1.0 %slices.1 = (bf16[128,512]{1,0:T(8,128)(2,1)S(1)}, bf16[128,512]{1,0:T(8,128)(2,1)S(1)}, bf16[64,512]{1,0:T(8,128)(2,1)S(1)}) custom-call(bf16[128,2048]{1,0:T(8,128)(2,1)} %refs_2_.1), custom_call_target="tpu_custom_call" | custom-call | tf_op jit(solution)/shard_map/slices/pallas_call | solution.py:124
  5.9 3.7 %collective-permute-start.1 = (bf16[64,512]{1,0:T(8,128)(2,1)S(1)}, bf16[64,512]{1,0:T(8,128)(2,1)S(1)}, u32[]{:S(2)}, u32[]{:S(2)}) collective-permute-start(bf16[64,512]{1,0:T(8,128)(2,1)S(1)} %get-tuple-element.25), channel_id=1, source_target_pairs={{0,3},{1,2},{2,1},{3,0},{4,7},{5,6},{6,5},{7,4},{8,11},{9,10},{10,... | collective-permute-start | bytes 196616 | tf_op jit(solution)/shard_map/ppermute | solution.py:51
  9.6 0.0 collective-permute-start
  9.6 0.0 collective-permute-done.3.second_ref.refs_5_
  9.6 0.0 collective-permute-done.2.first_ref.refs_4_
  9.6 0.0 copy-start.2
  9.6 0.6 %collective-permute-start.5 = (bf16[64,256]{1,0:T(8,128)(2,1)S(1)}, bf16[64,256]{1,0:T(8,128)(2,1)S(1)}, u32[]{:S(2)}, u32[]{:S(2)}) collective-permute-start(bf16[64,256]{1,0:T(8,128)(2,1)S(1)} %get-tuple-element.26.refs_3_), channel_id=1, source_target_pairs={{0,20},{4,16},{8,28},{12,24},{16,4},{20,0},{24,12},{28,8},{1,21},{... | collective-permute-start | bytes 98312 | tf_op jit(solution)/shard_map/ppermute | solution.py:44
  10.2 0.9 %collective-permute-start.4 = (bf16[96,256]{1,0:T(8,128)(2,1)S(1)}, bf16[96,256]{1,0:T(8,128)(2,1)S(1)}, u32[]{:S(2)}, u32[]{:S(2)}) collective-permute-start(bf16[96,256]{1,0:T(8,128)(2,1)S(1)} %get-tuple-element.29), channel_id=1, source_target_pairs={{0,12},{4,24},{8,20},{12,0},{16,28},{20,8},{24,4},{28,16},{1,13},{... | collective-permute-start | bytes 147464 | tf_op jit(solution)/shard_map/ppermute | solution.py:44
  11.1 1.7 %prepare.1 = (bf16[128,128]{1,0:T(8,128)(2,1)S(1)}, f32[8,640]{1,0:T(8,128)S(1)}) custom-call(s32[1,8]{1,0:T(1,128)S(1)} %copy-done.2, bf16[128,2048]{1,0:T(8,128)(2,1)S(1)} %copy-done, bf16[128,2048]{1,0:T(8,128)(2,1)} %refs_2_.1, bf16[64,256]{1,0:T(8,128)(2,1)S(1)} %get-tuple-element.26.refs_3_), custom_call_target="tpu_custom_call" | custom-call | flops 10000000000 | tf_op jit(solution)/shard_map/prepare/pallas_call | solution.py:166
  12.8 0.2 collective-permute-done.5.refs_7_
  13.0 0.7 %collective-permute-done.4.refs_6_ = bf16[96,256]{1,0:T(8,128)(2,1)S(1)} collective-permute-done((bf16[96,256]{1,0:T(8,128)(2,1)S(1)}, bf16[96,256]{1,0:T(8,128)(2,1)S(1)}, u32[]{:S(2)}, u32[]{:S(2)}) %collective-permute-start.4) | collective-permute-done | bytes 49184 | tf_op jit(solution)/shard_map/ppermute | solution.py:44
  13.8 1.7 %attend.1 = (bf16[128,128]{1,0:T(8,128)(2,1)S(1)}, bf16[128,128]{1,0:T(8,128)(2,1)}, f32[128,256]{1,0:T(8,128)S(1)}, bf16[128,256]{1,0:T(8,128)(2,1)S(1)}, bf16[...) custom-call(f32[8,640]{1,0:T(8,128)S(1)} %get-tuple-element.27.refs_0_, bf16[128,128]{1,0:T(8,128)(2,1)S(1)} %copy-done.1, ...), custom_call_target="tpu_custom_call" | custom-call | flops 1000000000 | tf_op jit(solution)/shard_map/attend/pallas_call | solution.py:260
  15.4 0.0 collective-permute-done.1.half_ref
  15.4 0.5 %collective-permute-done.whole_ref = bf16[128,512]{1,0:T(8,128)(2,1)S(1)} collective-permute-done((bf16[128,512]{1,0:T(8,128)(2,1)S(1)}, bf16[128,512]{1,0:T(8,128)(2,1)S(1)}, u32[]{:S(2)}, u32[]{:S(2)}) %collective-permute-start) | collective-permute-done | bytes 131104 | tf_op jit(solution)/shard_map/ppermute | solution.py:360
  16.0 1.3 %collective-permute-start.6 = (bf16[192,512]{1,0:T(8,128)(2,1)S(1)}, bf16[192,512]{1,0:T(8,128)(2,1)S(1)}, u32[]{:S(2)}, u32[]{:S(2)}) collective-permute-start(bf16[192,512]{1,0:T(8,128)(2,1)S(1)} %join.1.here_ref), channel_id=1, source_target_pairs={{0,4},{4,0},{8,12},{12,8},{16,20},{20,16},{24,28},{28,24},{1,5},{5... | collective-permute-start | bytes 589832 | tf_op jit(solution)/shard_map/ppermute | solution.py:44
  17.2 1.9 %collective-permute-start.11 = (bf16[128,128]{1,0:T(8,128)(2,1)S(1)}, bf16[128,128]{1,0:T(8,128)(2,1)S(1)}, u32[]{:S(2)}, u32[]{:S(2)}) collective-permute-start(bf16[128,128]{1,0:T(8,128)(2,1)S(1)} %get-tuple-element.30.after_ref.refs_0_), channel_id=1, source_target_pairs={{0,3},{1,2},{2,1},{3,0},{4,7},{5,6},{6,5},{7,4},{8,11},{9,10},{10,... | collective-permute-start | bytes 98312 | tf_op jit(solution)/shard_map/ppermute | solution.py:51
  19.1 0.0 collective-permute-start.7
  19.1 2.1 %collective-permute-start.8 = (bf16[128,256]{1,0:T(8,128)(2,1)S(1)}, bf16[128,256]{1,0:T(8,128)(2,1)S(1)}, u32[]{:S(2)}, u32[]{:S(2)}) collective-permute-start(bf16[128,256]{1,0:T(8,128)(2,1)S(1)} %get-tuple-element.33), channel_id=1, source_target_pairs={{0,28},{4,8},{8,4},{12,16},{16,12},{20,24},{24,20},{28,0},{1,29},{... | collective-permute-start | bytes 196616 | tf_op jit(solution)/shard_map/ppermute | solution.py:44
  21.2 0.1 collective-permute-start.10
  21.4 1.6 %collective-permute-done.11.refs_3_ = bf16[128,128]{1,0:T(8,128)(2,1)S(1)} collective-permute-done((bf16[128,128]{1,0:T(8,128)(2,1)S(1)}, bf16[128,128]{1,0:T(8,128)(2,1)S(1)}, u32[]{:S(2)}, u32[]{:S(2)}) %collective-permute-start.11) | collective-permute-done | bytes 32800 | tf_op jit(solution)/shard_map/ppermute | solution.py:51
  22.9 0.2 collective-permute-start.9
  23.2 3.4 %all-to-all-start = ((bf16[8,32,256]{2,1,0:T(8,128)(2,1)}), bf16[8,32,256]{2,1,0:T(8,128)(2,1)S(1)}, u32[]{:S(2)}, u32[]{:S(2)}) async-start(bf16[8,32,256]{2,1,0:T(8,128)(2,1)} %bitcast), calls=%async_computation | async-start | bytes 262144 | tf_op jit(solution)/shard_map/all_to_all | solution.py:391
  26.5 0.0 collective-permute-done.10.refs_2_
  26.5 0.3 collective-permute-done.9.refs_1_
  26.9 0.0 collective-permute-done.7.first_ref
  26.9 0.0 collective-permute-done.8.second_ref
  26.9 0.1 collect.1
  27.0 5.0 %all-to-all-done = bf16[8,32,256]{2,1,0:T(8,128)(2,1)S(1)} async-done(((bf16[8,32,256]{2,1,0:T(8,128)(2,1)}), bf16[8,32,256]{2,1,0:T(8,128)(2,1)S(1)}, u32[]{:S(2)}, u32[]{:S(2)}) %all-to-all-start) | async-done | bytes 131104 | tf_op jit(solution)/shard_map/all_to_all | solution.py:391
  32.0 0.9 %finish.1 = (bf16[128,512]{1,0:T(8,128)(2,1)}, bf16[128,128]{1,0:T(8,128)(2,1)}, bf16[128,128]{1,0:T(8,128)(2,1)}) custom-call(bf16[128,512]{1,0:T(8,128)(2,1)S(1)} %get-tuple-element.34.refs_0_, bf16[512,512]{1,0:T(8,128)(2,1)S(1)} %get-tuple-element.35.refs_1_, f32[128,256]{1,0:T(8,128)S(1)} %get-tuple-element.36.refs_2_, bf16[256,256]{1,0:T(8,128)(2,1)S(1)} %bitcast.2), custom_call_target="tpu_custom_call" | custom-call | tf_op jit(solution)/shard_map/finish/pallas_call | solution.py:345
  (11 shorter events, 0.1 us)
Async XLA Ops:
  0.6 0.8 %copy-start.3 = (bf16[128,128]{1,0:T(8,128)(2,1)S(1)}, bf16[128,128]{1,0:T(8,128)(2,1)}, u32[]{:S(2)}) copy-start(bf16[128,128]{1,0:T(8,128)(2,1)} %param.8) | copy-start | bytes 98308
  0.6 10.5 %copy-start = (bf16[128,2048]{1,0:T(8,128)(2,1)S(1)}, bf16[128,2048]{1,0:T(8,128)(2,1)}, u32[]{:S(2)}) copy-start(bf16[128,2048]{1,0:T(8,128)(2,1)} %refs_1_.2) | copy-start | bytes 1572868
  1.5 8.1 %collective-permute-start.3 = (bf16[128,256]{1,0:T(8,128)(2,1)S(1)}, bf16[128,256]{1,0:T(8,128)(2,1)S(1)}, u32[]{:S(2)}, u32[]{:S(2)}) collective-permute-start(bf16[128,256]{1,0:T(8,128)(2,1)S(1)} %constant_dynamic-update-slice_fusion.own_ref.refs_3_), channel_id=1, source_target_pairs={{0,28},{4,8},{8,4},{12,16},{16,12},{20,24},{24,20},{28,0},{1,29},{... | collective-permute-start | bytes 196616 | tf_op jit(solution)/shard_map/ppermute | solution.py:44
  4.9 4.7 %collective-permute-start.2 = (bf16[128,256]{1,0:T(8,128)(2,1)S(1)}, bf16[128,256]{1,0:T(8,128)(2,1)S(1)}, u32[]{:S(2)}, u32[]{:S(2)}) collective-permute-start(bf16[128,256]{1,0:T(8,128)(2,1)S(1)} %constant_dynamic-update-slice_fusion.own_ref.refs_3_), channel_id=1, source_target_pairs={{0,4},{4,0},{8,12},{12,8},{16,20},{20,16},{24,28},{28,24},{1,5},{5... | collective-permute-start | bytes 196616 | tf_op jit(solution)/shard_map/ppermute | solution.py:44
  5.9 9.5 %collective-permute-start.1 = (bf16[64,512]{1,0:T(8,128)(2,1)S(1)}, bf16[64,512]{1,0:T(8,128)(2,1)S(1)}, u32[]{:S(2)}, u32[]{:S(2)}) collective-permute-start(bf16[64,512]{1,0:T(8,128)(2,1)S(1)} %get-tuple-element.25), channel_id=1, source_target_pairs={{0,3},{1,2},{2,1},{3,0},{4,7},{5,6},{6,5},{7,4},{8,11},{9,10},{10,... | collective-permute-start | bytes 196616 | tf_op jit(solution)/shard_map/ppermute | solution.py:51
  9.6 6.4 %collective-permute-start = (bf16[128,512]{1,0:T(8,128)(2,1)S(1)}, bf16[128,512]{1,0:T(8,128)(2,1)S(1)}, u32[]{:S(2)}, u32[]{:S(2)}) collective-permute-start(bf16[128,512]{1,0:T(8,128)(2,1)S(1)} %get-tuple-element.24), channel_id=1, source_target_pairs={{0,1},{1,0},{2,3},{3,2},{4,6},{5,7},{6,4},{7,5},{8,9},{9,8},{10,11... | collective-permute-start | bytes 393224 | tf_op jit(solution)/shard_map/ppermute | solution.py:360
  9.6 1.5 %copy-start.2 = (s32[1,8]{1,0:T(1,128)S(1)}, s32[1,8]{1,0:T(1,128)}, u32[]{:S(2)}) copy-start(s32[1,8]{1,0:T(1,128)} %refs_0_.3) | copy-start | bytes 100
  9.6 3.4 %collective-permute-start.5 = (bf16[64,256]{1,0:T(8,128)(2,1)S(1)}, bf16[64,256]{1,0:T(8,128)(2,1)S(1)}, u32[]{:S(2)}, u32[]{:S(2)}) collective-permute-start(bf16[64,256]{1,0:T(8,128)(2,1)S(1)} %get-tuple-element.26.refs_3_), channel_id=1, source_target_pairs={{0,20},{4,16},{8,28},{12,24},{16,4},{20,0},{24,12},{28,8},{1,21},{... | collective-permute-start | bytes 98312 | tf_op jit(solution)/shard_map/ppermute | solution.py:44
  10.2 3.5 %copy-start.1 = (bf16[128,128]{1,0:T(8,128)(2,1)S(1)}, bf16[128,128]{1,0:T(8,128)(2,1)}, u32[]{:S(2)}) copy-start(bf16[128,128]{1,0:T(8,128)(2,1)} %refs_1_.3) | copy-start | bytes 98308
  10.2 3.5 %collective-permute-start.4 = (bf16[96,256]{1,0:T(8,128)(2,1)S(1)}, bf16[96,256]{1,0:T(8,128)(2,1)S(1)}, u32[]{:S(2)}, u32[]{:S(2)}) collective-permute-start(bf16[96,256]{1,0:T(8,128)(2,1)S(1)} %get-tuple-element.29), channel_id=1, source_target_pairs={{0,12},{4,24},{8,20},{12,0},{16,28},{20,8},{24,4},{28,16},{1,13},{... | collective-permute-start | bytes 147464 | tf_op jit(solution)/shard_map/ppermute | solution.py:44
  16.0 10.9 %collective-permute-start.6 = (bf16[192,512]{1,0:T(8,128)(2,1)S(1)}, bf16[192,512]{1,0:T(8,128)(2,1)S(1)}, u32[]{:S(2)}, u32[]{:S(2)}) collective-permute-start(bf16[192,512]{1,0:T(8,128)(2,1)S(1)} %join.1.here_ref), channel_id=1, source_target_pairs={{0,4},{4,0},{8,12},{12,8},{16,20},{20,16},{24,28},{28,24},{1,5},{5... | collective-permute-start | bytes 589832 | tf_op jit(solution)/shard_map/ppermute | solution.py:44
  17.2 5.7 %collective-permute-start.11 = (bf16[128,128]{1,0:T(8,128)(2,1)S(1)}, bf16[128,128]{1,0:T(8,128)(2,1)S(1)}, u32[]{:S(2)}, u32[]{:S(2)}) collective-permute-start(bf16[128,128]{1,0:T(8,128)(2,1)S(1)} %get-tuple-element.30.after_ref.refs_0_), channel_id=1, source_target_pairs={{0,3},{1,2},{2,1},{3,0},{4,7},{5,6},{6,5},{7,4},{8,11},{9,10},{10,... | collective-permute-start | bytes 98312 | tf_op jit(solution)/shard_map/ppermute | solution.py:51
  19.1 7.7 %collective-permute-start.7 = (bf16[128,256]{1,0:T(8,128)(2,1)S(1)}, bf16[128,256]{1,0:T(8,128)(2,1)S(1)}, u32[]{:S(2)}, u32[]{:S(2)}) collective-permute-start(bf16[128,256]{1,0:T(8,128)(2,1)S(1)} %get-tuple-element.32), channel_id=1, source_target_pairs={{0,4},{4,0},{8,12},{12,8},{16,20},{20,16},{24,28},{28,24},{1,5},{5... | collective-permute-start | bytes 196616 | tf_op jit(solution)/shard_map/ppermute | solution.py:44
  19.1 7.7 %collective-permute-start.8 = (bf16[128,256]{1,0:T(8,128)(2,1)S(1)}, bf16[128,256]{1,0:T(8,128)(2,1)S(1)}, u32[]{:S(2)}, u32[]{:S(2)}) collective-permute-start(bf16[128,256]{1,0:T(8,128)(2,1)S(1)} %get-tuple-element.33), channel_id=1, source_target_pairs={{0,28},{4,8},{8,4},{12,16},{16,12},{20,24},{24,20},{28,0},{1,29},{... | collective-permute-start | bytes 196616 | tf_op jit(solution)/shard_map/ppermute | solution.py:44
  21.2 5.3 %collective-permute-start.10 = (bf16[128,128]{1,0:T(8,128)(2,1)S(1)}, bf16[128,128]{1,0:T(8,128)(2,1)S(1)}, u32[]{:S(2)}, u32[]{:S(2)}) collective-permute-start(bf16[128,128]{1,0:T(8,128)(2,1)S(1)} %get-tuple-element.30.after_ref.refs_0_), channel_id=1, source_target_pairs={{0,2},{1,3},{2,0},{3,1},{4,6},{5,7},{6,4},{7,5},{8,10},{9,11},{10,... | collective-permute-start | bytes 98312 | tf_op jit(solution)/shard_map/ppermute | solution.py:51
  22.9 3.9 %collective-permute-start.9 = (bf16[128,128]{1,0:T(8,128)(2,1)S(1)}, bf16[128,128]{1,0:T(8,128)(2,1)S(1)}, u32[]{:S(2)}, u32[]{:S(2)}) collective-permute-start(bf16[128,128]{1,0:T(8,128)(2,1)S(1)} %get-tuple-element.30.after_ref.refs_0_), channel_id=1, source_target_pairs={{0,1},{1,0},{2,3},{3,2},{4,5},{5,4},{6,7},{7,6},{8,9},{9,8},{10,11... | collective-permute-start | bytes 98312 | tf_op jit(solution)/shard_map/ppermute | solution.py:51
  23.2 8.8 %all-to-all-start = ((bf16[8,32,256]{2,1,0:T(8,128)(2,1)}), bf16[8,32,256]{2,1,0:T(8,128)(2,1)S(1)}, u32[]{:S(2)}, u32[]{:S(2)}) async-start(bf16[8,32,256]{2,1,0:T(8,128)(2,1)} %bitcast), calls=%async_computation | async-start | bytes 262144 | tf_op jit(solution)/shard_map/all_to_all | solution.py:391

commit v5 on v3

--- a/solution.py
+++ b/solution.py
@@ -17,6 +17,10 @@
 PARAMS = pltpu.CompilerParams(vmem_limit_bytes=40 * 1024 * 1024)
 FULL = pltpu.CompilerParams(vmem_limit_bytes=int(53.3 * 1024 * 1024))
 BF16 = jnp.bfloat16
+PREPARE_COST = 10**10
+ATTEND_COST = 10**9
+COMBINE_COST = 10**10
+GATHER_COST = 10**10
 F32 = jnp.float32
 
 
@@ -80,54 +84,57 @@
     mult_ref[...] = mult
 
 
+def cost(flops):
+    return pl.CostEstimate(flops=flops, bytes_accessed=0, transcendentals=0)
+
+
 CHUNKS = 4
 
 
-def prepare_kernel(ring, index_hbm, cot_hbm, w_hbm, grad_ref, mult_ref, *refs):
+def prepare_kernel(ring, index_hbm, cot_hbm, w_hbm, after_ref, grad_ref, mult_ref, *refs):
+    del after_ref
     index_ref, cot_ref, w_ref, sems = refs[-4:]
     slice_refs = refs[:-4]
-    width = slice_refs[0].shape[1]
-    head = lax.axis_index("head")
-    core = lax.axis_index("seq") & 1
-
-    def columns(h):
-        return pl.ds(pl.multiple_of(h * width, width), width)
-
-    if ring:
-        half = HD // 2
-        sources = [
-            w_hbm.at[:, columns(head)],
-            w_hbm.at[:, columns(head ^ (1 + core))],
-            w_hbm.at[pl.ds(pl.multiple_of(core * half, half), half), columns(head ^ 3)],
-        ]
-    else:
-        sources = [w_hbm.at[:, columns(head ^ r)] for r in range(len(slice_refs))]
     copies = [(index_hbm, index_ref)]
-    copies += list(zip(sources, slice_refs))
     depth = cot_ref.shape[1] // CHUNKS
     for i in range(CHUNKS):
         span = pl.ds(i * depth, depth)
+        copies.append((w_hbm.at[:, span], w_ref.at[:, span]))
         copies.append((cot_hbm.at[:, span], cot_ref.at[:, span]))
-        copies.append((w_hbm.at[:, span], w_ref.at[:, span]))
     copies = [pltpu.make_async_copy(src, dst, sems.at[i]) for i, (src, dst) in enumerate(copies)]
     for copy in copies:
         copy.start()
     copies[0].wait()
     fill_multiplicity(ring, index_ref, mult_ref)
-    fixed = 1 + len(slice_refs)
     total = None
     for i in range(CHUNKS):
-        copies[fixed + 2 * i].wait()
-        copies[fixed + 2 * i + 1].wait()
+        copies[1 + 2 * i].wait()
+        copies[2 + 2 * i].wait()
         span = slice(i * depth, (i + 1) * depth)
         term = dot_nt(cot_ref[:, span], w_ref[:, span])
         total = term if total is None else total + term
     grad_ref[...] = total.astype(grad_ref.dtype)
-    for copy in copies[1:fixed]:
-        copy.wait()
-
-
-def prepare(ring, index, cotangent, out_weight, heads, columns):
+
+    width = slice_refs[0].shape[1]
+    head = lax.axis_index("head")
+
+    def columns(h):
+        return pl.ds(pl.multiple_of(h * width, width), width)
+
+    if ring:
+        core = lax.axis_index("seq") & 1
+        half = HD // 2
+        mine_ref, whole_ref, half_ref = slice_refs
+        mine_ref[...] = w_ref[:, columns(head)]
+        whole_ref[...] = w_ref[:, columns(head ^ (1 + core))]
+        rows = pl.ds(pl.multiple_of(core * half, half), half)
+        half_ref[...] = w_ref[rows, columns(head ^ 3)]
+    else:
+        for r, ref in enumerate(slice_refs):
+            ref[...] = w_ref[:, columns(head ^ r)]
+
+
+def prepare(ring, index, cotangent, out_weight, heads, columns, after):
     width = out_weight.shape[1] // heads
     rows = (HD, HD, HD // 2) if ring else (HD,) * heads
 
@@ -138,17 +145,42 @@
         body,
         out_shape=(shape(BLK, HD), shape(8, columns, kind=F32))
         + tuple(shape(r, width) for r in rows),
-        in_specs=[HBM] * 3,
+        in_specs=[HBM] * 3 + [VMEM],
         out_specs=(VMEM,) * (2 + len(rows)),
         scratch_shapes=[
             pltpu.SMEM(index.shape, jnp.int32),
             pltpu.VMEM(cotangent.shape, BF16),
             pltpu.VMEM(out_weight.shape, BF16),
-            pltpu.SemaphoreType.DMA((1 + len(rows) + 2 * CHUNKS,)),
+            pltpu.SemaphoreType.DMA((1 + 2 * CHUNKS,)),
         ],
         compiler_params=FULL,
+        cost_estimate=cost(PREPARE_COST),
         name="prepare",
-    )(index, cotangent, out_weight)
+    )(index, cotangent, out_weight, after)
+
+
+def lead_kernel(own_ref, first_ref, second_ref, mult_ref, whole_ref,
+                plus_ref, minus_ref, whole_out):
+    del mult_ref
+    n = STRIDE_ROWS
+    plus_ref[:n] = own_ref[:n]
+    plus_ref[n:2 * n] = first_ref[:n]
+    plus_ref[2 * n:] = second_ref[:n]
+    minus_ref[:n] = own_ref[:n]
+    minus_ref[n:] = second_ref[:n]
+    whole_out[...] = whole_ref[...]
+
+
+def leads(own, first, second, mult, whole):
+    n = STRIDE_ROWS
+    return pl.pallas_call(
+        lead_kernel,
+        out_shape=(shape(3 * n, PAIR), shape(2 * n, PAIR), shape(*whole.shape)),
+        in_specs=[VMEM] * 5,
+        out_specs=(VMEM,) * 3,
+        compiler_params=PARAMS,
+        name="leads",
+    )(own, first, second, mult, whole)
 
 
 def attend_kernel(sides, mult_ref, q_ref, grad_ref, *refs):
@@ -202,80 +234,130 @@
         out_specs=(VMEM,) * (5 + len(sides)),
         scratch_shapes=[pltpu.VMEM((mult.shape[1], PAIR), BF16)],
         compiler_params=PARAMS,
+        cost_estimate=cost(ATTEND_COST),
         name="attend",
     )(mult, q, grad, *window, *sides)
 
 
-def combine_kernel(own_ref, first_ref, second_ref, plus_ref, minus_ref,
-                   mine_ref, whole_ref, half_ref, other_whole_ref, other_half_ref,
-                   own_out, first_out, second_out, w_out):
+def combine_kernel(own_ref, first_ref, second_ref, plus_ref, minus_ref, whole_ref, half_ref,
+                   own_out, first_out, second_out):
     plus = plus_ref[...].astype(F32)
     minus = minus_ref[...].astype(F32)
     n = STRIDE_ROWS
     own_out[n:] = own_ref[n:]
     own_out[:n] = own_ref[:n] + plus[:n] + minus[:n]
-    first_out[n:] = first_ref[n:].astype(BF16)
-    first_out[:n] = (first_ref[:n] + plus[n:2 * n]).astype(BF16)
     second_out[n:] = second_ref[n:].astype(BF16)
     second_out[:n] = (second_ref[:n] + plus[2 * n:] + minus[n:]).astype(BF16)
+    first_out[n:BLK] = first_ref[n:].astype(BF16)
+    first_out[:n] = (first_ref[:n] + plus[n:2 * n]).astype(BF16)
+    row = BLK
+    for ref in (whole_ref, half_ref):
+        for c in range(0, ref.shape[1], PAIR):
+            first_out[row:row + ref.shape[0]] = ref[:, c:c + PAIR]
+            row += ref.shape[0]
+
+
+def combine(own, first, second, plus, minus, whole, half):
+    extra = (whole.size + half.size) // PAIR
+    return pl.pallas_call(
+        combine_kernel,
+        out_shape=(shape(BLK, PAIR, kind=F32), shape(BLK + extra, PAIR), shape(BLK, PAIR)),
+        in_specs=[VMEM] * 7,
+        out_specs=(VMEM,) * 3,
+        compiler_params=PARAMS,
+        cost_estimate=cost(COMBINE_COST),
+        name="combine",
+    )(own, first, second, plus, minus, whole, half)
+
+
+def gather_kernel(*refs):
+    for r, ref in enumerate(refs[:-1]):
+        refs[-1][:, r * HD:(r + 1) * HD] = ref[...]
+
+
+def gather(attentions):
+    return pl.pallas_call(
+        gather_kernel,
+        out_shape=shape(BLK, len(attentions) * HD),
+        in_specs=[VMEM] * len(attentions),
+        out_specs=VMEM,
+        compiler_params=PARAMS,
+        cost_estimate=cost(GATHER_COST),
+        name="gather",
+    )(*attentions)
+
+
+def settle(total, lead, dk_ref, dv_ref):
+    for ref, c in ((dk_ref, 0), (dv_ref, HD)):
+        ref[:STRIDE_ROWS] = lead[:, c:c + HD].astype(ref.dtype)
+        ref[STRIDE_ROWS:] = total[STRIDE_ROWS:, c:c + HD].astype(ref.dtype)
+
+
+def finish_ring_kernel(att_ref, mine_ref, whole_ref, half_ref, first_ref, own_ref, second_ref,
+                       mixed_ref, dk_ref, dv_ref):
     core = lax.axis_index("seq") & 1
     half = HD // 2
-    w_out[:HD] = mine_ref[...]
-    w_out[pl.ds(pl.multiple_of(HD + core * HD, HD), HD)] = whole_ref[...]
-    w_out[pl.ds(pl.multiple_of(2 * HD - core * HD, HD), HD)] = other_whole_ref[...]
-    w_out[pl.ds(pl.multiple_of(3 * HD + core * half, half), half)] = half_ref[...]
-    w_out[pl.ds(pl.multiple_of(3 * HD + half - core * half, half), half)] = other_half_ref[...]
-
-
-def combine(own, first, second, plus, minus, *slices):
-    return pl.pallas_call(
-        combine_kernel,
-        out_shape=(shape(BLK, PAIR, kind=F32), shape(BLK, PAIR), shape(BLK, PAIR),
-                   shape(4 * HD, slices[0].shape[1])),
-        in_specs=[VMEM] * 10,
-        out_specs=(VMEM,) * 4,
-        compiler_params=PARAMS,
-        name="combine",
-    )(own, first, second, plus, minus, *slices)
-
-
-def finish_kernel(heads, slices, extra, *refs):
-    att_refs = refs[:heads]
-    w_refs = refs[heads:heads + slices]
-    rest = refs[heads + slices:]
-    own_ref, first_ref, second_ref = rest[:3]
-    mixed_ref, dk_ref, dv_ref = rest[-3:]
-    pieces = [ref[r:r + HD] for ref in w_refs for r in range(0, ref.shape[0], HD)]
+    att = [att_ref[:, r * HD:(r + 1) * HD] for r in range(4)]
+    here = jnp.where(core == 0, att[1], att[2])
+    there = jnp.where(core == 0, att[2], att[1])
+    here_half = jnp.where(core == 0, att[3][:, :half], att[3][:, half:])
+    there_half = jnp.where(core == 0, att[3][:, half:], att[3][:, :half])
+    whole_row = BLK
+    half_row = BLK + (mine_ref.shape[1] // PAIR) * HD
+    for i, c in enumerate(range(0, mine_ref.shape[1], PAIR)):
+        span = slice(c, c + PAIR)
+        other_whole = first_ref[whole_row + i * HD:whole_row + (i + 1) * HD]
+        other_half = first_ref[half_row + i * half:half_row + (i + 1) * half]
+        mixed = dot_nn(att[0], mine_ref[:, span]) + dot_nn(here, whole_ref[:, span])
+        mixed = mixed + dot_nn(there, other_whole) + dot_nn(here_half, half_ref[:, span])
+        mixed = mixed + dot_nn(there_half, other_half)
+        mixed_ref[:, span] = mixed.astype(mixed_ref.dtype)
+    total = own_ref[...] + first_ref[:BLK].astype(F32) + second_ref[...].astype(F32)
+    settle(total, total[:STRIDE_ROWS], dk_ref, dv_ref)
+
+
+def finish_ring(att, mine, whole, half, first, own, second):
+    return pl.pallas_call(
+        finish_ring_kernel,
+        out_shape=(shape(BLK, mine.shape[1]), shape(BLK, HD), shape(BLK, HD)),
+        in_specs=[VMEM] * 7,
+        out_specs=(VMEM,) * 3,
+        compiler_params=PARAMS,
+        name="finish",
+    )(att, mine, whole, half, first, own, second)
+
+
+def finish_kernel(count, *refs):
+    att_refs = refs[:count]
+    w_refs = refs[count:2 * count]
+    own_ref, first_ref, second_ref, side_ref, mixed_ref, dk_ref, dv_ref = refs[2 * count:]
     mixed = None
-    for ref, w in zip(att_refs, pieces):
-        term = dot_nn(ref[...], w)
+    for ref, w in zip(att_refs, w_refs):
+        term = dot_nn(ref[...], w[...])
         mixed = term if mixed is None else mixed + term
     mixed_ref[...] = mixed.astype(mixed_ref.dtype)
     total = own_ref[...] + first_ref[...].astype(F32) + second_ref[...].astype(F32)
     lead = total[:STRIDE_ROWS]
-    if extra:
-        side_ref = rest[3]
-        for i in range(side_ref.shape[0] // STRIDE_ROWS):
-            lead = lead + side_ref[i * STRIDE_ROWS:(i + 1) * STRIDE_ROWS].astype(F32)
-    for ref, c in ((dk_ref, 0), (dv_ref, HD)):
-        ref[:STRIDE_ROWS] = lead[:, c:c + HD].astype(ref.dtype)
-        ref[STRIDE_ROWS:] = total[STRIDE_ROWS:, c:c + HD].astype(ref.dtype)
-
-
-def finish(attentions, slices, own, first, second, *side):
+    for i in range(side_ref.shape[0] // STRIDE_ROWS):
+        lead = lead + side_ref[i * STRIDE_ROWS:(i + 1) * STRIDE_ROWS].astype(F32)
+    settle(total, lead, dk_ref, dv_ref)
+
+
+def finish(attentions, slices, own, first, second, side):
     width = slices[0].shape[1]
+    count = len(attentions)
 
     def body(*refs):
-        finish_kernel(len(attentions), len(slices), len(side), *refs)
+        finish_kernel(count, *refs)
 
     return pl.pallas_call(
         body,
         out_shape=(shape(BLK, width), shape(BLK, HD), shape(BLK, HD)),
-        in_specs=[VMEM] * (len(attentions) + len(slices) + 3 + len(side)),
+        in_specs=[VMEM] * (2 * count + 4),
         out_specs=(VMEM,) * 3,
         compiler_params=PARAMS,
         name="finish",
-    )(*attentions, *slices, own, first, second, *side)
+    )(*attentions, *slices, own, first, second, side)
 
 
 def spread_slice(array):
@@ -291,35 +373,34 @@
     heads = lax.axis_size("head")
     ring = seq == 8 and heads == 4
     n = STRIDE_ROWS
+    side_rows = seq * n
+    columns = 3 * BLK + side_rows
     own = jnp.concatenate([key_rows, value_rows], axis=1)
     first = trade(own, 1)
     second = trade(own, -1)
-    columns = 3 * BLK + (2 * BLK if ring else seq * n)
-    grad, mult, *slices = prepare(ring, strided_index, cotangent, out_weight, heads, columns)
+    grad, mult, *slices = prepare(
+        ring, strided_index, cotangent, out_weight, heads, columns, own
+    )
     if ring:
         mine, whole, half = slices
+        half = swap(half, 3)
+        plus, minus, whole = leads(own, first, second, mult, whole)
         whole = spread_slice(whole)
-        half = swap(half, 3)
-        lead = jnp.concatenate([own[:n], first[:n], second[:n]], axis=0)
-        plus = trade(lead, 3)
-        minus = trade(jnp.concatenate([own[:n], second[:n]], axis=0), -3)
-        other_whole = trade(whole, 1)
-        other_half = trade(half, 1)
         att, dq, own_sum, first_sum, second_sum, to_plus, to_minus = attend(
-            mult, queries, grad, (own, first, second), (plus, minus)
+            mult, queries, grad, (own, first, second), (trade(plus, 3), trade(minus, -3))
         )
         attentions = [att] + [swap(att, r) for r in range(1, heads)]
-        own_sum, to_first, to_second, weight = combine(
-            own_sum, first_sum, second_sum, trade(to_plus, 3), trade(to_minus, -3),
-            mine, whole, half, other_whole, other_half,
+        own_sum, to_first, to_second = combine(
+            own_sum, first_sum, second_sum, trade(to_plus, 3), trade(to_minus, -3), whole, half
         )
-        mixed, dk, dv = finish(
-            attentions, [weight], own_sum, trade(to_first, 1), trade(to_second, -1)
+        mixed, dk, dv = finish_ring(
+            gather(attentions), mine, whole, half, trade(to_first, 1), own_sum,
+            trade(to_second, -1),
         )
     else:
         slices = [slices[0]] + [swap(slices[r], r) for r in range(1, heads)]
         spread = jnp.broadcast_to(own[None, :n], (seq, n, PAIR))
-        side = lax.all_to_all(spread, "seq", 0, 0).reshape(seq * n, PAIR)
+        side = lax.all_to_all(spread, "seq", 0, 0).reshape(side_rows, PAIR)
         att, dq, own_sum, first_sum, second_sum, to_side = attend(
             mult, queries, grad, (own, first, second), (side,)
         )
@@ -327,7 +408,7 @@
         mixed, dk, dv = finish(
             [att] + [swap(att, r) for r in range(1, heads)], slices, own_sum,
             trade(first_sum.astype(BF16), 1), trade(second_sum.astype(BF16), -1),
-            from_side.reshape(seq * n, PAIR),
+            from_side.reshape(side_rows, PAIR),
         )
     return (mixed, dq, dk, dv)
 

time: 38 us -> 29.2 us (0.77)
  waiting for transfers between devices: 12.4 us -> 3.06 us
  starting transfers between devices: 19.3 us -> 20 us
    ppermute x4, waiting for transfers between devices: 7.48 us -> 1.35 us  [swap(): return lax.ppermute(array, 'head', [(i, i ^ mask) for i in range(count)])]
    ppermute x10 -> x8, starting transfers between devices: 9.12 us -> 12 us  [trade(): lax.ppermute(array, 'seq', [(i, (i + (step if i % 2 == 0 else -step)) % c...]
    ppermute x1, waiting for transfers between devices: 1.84 us -> 0.01 us  [spread_slice(): return lax.ppermute(array, ('seq', 'head'), pairs)]
    ppermute x1, starting transfers between devices: 1.64 us -> 0.01 us  [spread_slice(): return lax.ppermute(array, ('seq', 'head'), pairs)]
    ppermute x10 -> x8, waiting for transfers between devices: 3.13 us -> 1.71 us  [trade(): lax.ppermute(array, 'seq', [(i, (i + (step if i % 2 == 0 else -step)) % c...]
    ppermute x4, starting transfers between devices: 8.5 us -> 7.99 us  [swap(): return lax.ppermute(array, 'head', [(i, i ^ mask) for i in range(count)])]
    pallas_call x1 -> x3, Pallas kernels: 0.95 us -> 1.02 us  [the longest x1 0.98 us: finish_ring(): pl.pallas_call(finish_ring_kernel, out_shape=(shape(BLK, mine.shape[1]),...]
  transfers between devices with their start and end apart: 15 -> 13, of which waited for: 6 -> 3; matrix products, arithmetic and copies ran while one was open for 0% -> 0% of each run, Pallas kernels for 9% -> 12%
where the time goes in v5:
time: 29.2 us; the launch traced here: 29 us
  starting transfers between devices  20 us (68%)
  Pallas kernels  4.41 us (15%)
  waiting for transfers between devices  3.06 us (10%)
  local copies, waits for them, and re-layouts  0.8 us (3%)
  between operations  0.71 us (2%)
    ppermute x8, starting transfers between devices, trade(): lax.ppermute(array, 'seq', [(i, (i + (step if i % 2 == 0 else -step)) % c...  12 us
    ppermute x4, starting transfers between devices, swap(): return lax.ppermute(array, 'head', [(i, i ^ mask) for i in range(count)])  7.99 us
    pallas_call x1, Pallas kernels, prepare(): pl.pallas_call(body, out_shape=(shape(BLK, HD), shape(8, columns, kind=F3...  1.81 us
    ppermute x8, waiting for transfers between devices, trade(): lax.ppermute(array, 'seq', [(i, (i + (step if i % 2 == 0 else -step)) % c...  1.71 us
    pallas_call x1, Pallas kernels, attend(): pl.pallas_call(body, out_shape=(shape(BLK, HD), shape(BLK, HD)) + (shape(...  1.54 us
    ppermute x4, waiting for transfers between devices, swap(): return lax.ppermute(array, 'head', [(i, i ^ mask) for i in range(count)])  1.35 us
    pallas_call x1, Pallas kernels, finish_ring(): pl.pallas_call(finish_ring_kernel, out_shape=(shape(BLK, mine.shape[1]),...  0.98 us
    unnamed x7, local copies, waits for them, and re-layouts  0.78 us
  transfers between devices with their start and end apart: 13, of which 3 were waited for; matrix products, arithmetic and copies ran while one was open for 0% of the time, Pallas kernels for 12%

profile of v5, /device:TPU:0, one launch (start us, length us, event | category | flops | bytes accessed | tf_op | source)
XLA Modules:
  0.0 29.0 jit_solution(12836889493285916402)
XLA Ops:
  0.6 0.8 %constant_dynamic-update-slice_fusion.1 = bf16[128,256]{1,0:T(8,128)(2,1)S(1)} fusion(bf16[128,128]{1,0:T(8,128)(2,1)} %param.7), kind=kLoop, calls=%fused_computation.1 | loop fusion | bytes 65536
  1.4 0.0 copy-done.2
  1.4 0.0 copy-start.1
  1.4 0.5 %collective-permute-start = (bf16[128,256]{1,0:T(8,128)(2,1)S(1)}, bf16[128,256]{1,0:T(8,128)(2,1)S(1)}, u32[]{:S(2)}, u32[]{:S(2)}) collective-permute-start(bf16[128,256]{1,0:T(8,128)(2,1)S(1)} %constant_dynamic-update-slice_fusion.refs_3_.own_ref), channel_id=1, source_target_pairs={{0,4},{4,0},{8,12},{12,8},{16,20},{20,16},{24,28},{28,24},{1,5},{5... | collective-permute-start | bytes 196616 | tf_op jit(solution)/shard_map/ppermute | solution.py:45
  2.0 3.6 %collective-permute-start.1 = (bf16[128,256]{1,0:T(8,128)(2,1)S(1)}, bf16[128,256]{1,0:T(8,128)(2,1)S(1)}, u32[]{:S(2)}, u32[]{:S(2)}) collective-permute-start(bf16[128,256]{1,0:T(8,128)(2,1)S(1)} %constant_dynamic-update-slice_fusion.refs_3_.own_ref), channel_id=1, source_target_pairs={{0,28},{4,8},{8,4},{12,16},{16,12},{20,24},{24,20},{28,0},{1,29},{... | collective-permute-start | bytes 196616 | tf_op jit(solution)/shard_map/ppermute | solution.py:45
  5.5 1.8 %prepare.1 = (bf16[128,128]{1,0:T(8,128)(2,1)S(1)}, f32[8,640]{1,0:T(8,128)S(1)}, bf16[128,512]{1,0:T(8,128)(2,1)S(1)}, bf16[128,512]{1,0:T(8,128)(2,1)S(1)}, bf16[64,512]{1,0:T(8,128)(2,1)S(1)}) custom-call(s32[1,8]{1,0:T(1,128)S(1)} %copy-done.1, bf16[128,2048]{1,0:T(8,128)(2,1)} %refs_1_.2, bf16[128,2048]{1,0:T(8,128)(2,1)} %refs_2_.1, ...), custom_call_target="tpu_custom_call" | custom-call | flops 10000000000 | tf_op jit(solution)/shard_map/prepare/pallas_call | solution.py:144
  7.3 0.0 collective-permute-done.first_ref.refs_4_
  7.3 0.1 collective-permute-done.1.second_ref.refs_5_
  7.5 1.9 %collective-permute-start.2 = (bf16[96,256]{1,0:T(8,128)(2,1)S(1)}, bf16[96,256]{1,0:T(8,128)(2,1)S(1)}, u32[]{:S(2)}, u32[]{:S(2)}) collective-permute-start(bf16[96,256]{1,0:T(8,128)(2,1)S(1)} %get-tuple-element.28), channel_id=1, source_target_pairs={{0,12},{4,24},{8,20},{12,0},{16,28},{20,8},{24,4},{28,16},{1,13},{... | collective-permute-start | bytes 147464 | tf_op jit(solution)/shard_map/ppermute | solution.py:45
  9.4 0.1 collective-permute-start.3
  9.5 3.6 %collective-permute-start.8 = (bf16[64,512]{1,0:T(8,128)(2,1)S(1)}, bf16[64,512]{1,0:T(8,128)(2,1)S(1)}, u32[]{:S(2)}, u32[]{:S(2)}) collective-permute-start(bf16[64,512]{1,0:T(8,128)(2,1)S(1)} %get-tuple-element.33), channel_id=1, source_target_pairs={{0,3},{1,2},{2,1},{3,0},{4,7},{5,6},{6,5},{7,4},{8,11},{9,10},{10,... | collective-permute-start | bytes 196616 | tf_op jit(solution)/shard_map/ppermute | solution.py:52
  13.1 0.0 collective-permute-start.7
  13.1 0.0 collective-permute-done.3.refs_7_
  13.1 0.0 collective-permute-done.2.refs_6_
  13.1 1.5 %attend.1 = (bf16[128,128]{1,0:T(8,128)(2,1)S(1)}, bf16[128,128]{1,0:T(8,128)(2,1)}, f32[128,256]{1,0:T(8,128)S(1)}, f32[128,256]{1,0:T(8,128)S(1)}, f32[128,256...) custom-call(f32[8,640]{1,0:T(8,128)S(1)} %get-tuple-element.25.mult_ref.refs_0_, ...), custom_call_target="tpu_custom_call" | custom-call | flops 1000000000 | tf_op jit(solution)/shard_map/attend/pallas_call | solution.py:228
  14.7 0.9 %collective-permute-start.9 = (bf16[96,256]{1,0:T(8,128)(2,1)S(1)}, bf16[96,256]{1,0:T(8,128)(2,1)S(1)}, u32[]{:S(2)}, u32[]{:S(2)}) collective-permute-start(bf16[96,256]{1,0:T(8,128)(2,1)S(1)} %get-tuple-element.37), channel_id=1, source_target_pairs={{0,12},{4,24},{8,20},{12,0},{16,28},{20,8},{24,4},{28,16},{1,13},{... | collective-permute-start | bytes 147464 | tf_op jit(solution)/shard_map/ppermute | solution.py:45
  15.6 2.1 %collective-permute-start.10 = (bf16[64,256]{1,0:T(8,128)(2,1)S(1)}, bf16[64,256]{1,0:T(8,128)(2,1)S(1)}, u32[]{:S(2)}, u32[]{:S(2)}) collective-permute-start(bf16[64,256]{1,0:T(8,128)(2,1)S(1)} %get-tuple-element.38), channel_id=1, source_target_pairs={{0,20},{4,16},{8,28},{12,24},{16,4},{20,0},{24,12},{28,8},{1,21},{... | collective-permute-start | bytes 98312 | tf_op jit(solution)/shard_map/ppermute | solution.py:45
  17.7 2.0 %collective-permute-start.4 = (bf16[128,128]{1,0:T(8,128)(2,1)S(1)}, bf16[128,128]{1,0:T(8,128)(2,1)S(1)}, u32[]{:S(2)}, u32[]{:S(2)}) collective-permute-start(bf16[128,128]{1,0:T(8,128)(2,1)S(1)} %get-tuple-element.30.refs_0_), channel_id=1, source_target_pairs={{0,1},{1,0},{2,3},{3,2},{4,5},{5,4},{6,7},{7,6},{8,9},{9,8},{10,11... | collective-permute-start | bytes 98312 | tf_op jit(solution)/shard_map/ppermute | solution.py:52
  19.7 0.0 collective-permute-done.8.half_ref
  19.7 1.0 %collective-permute-start.5 = (bf16[128,128]{1,0:T(8,128)(2,1)S(1)}, bf16[128,128]{1,0:T(8,128)(2,1)S(1)}, u32[]{:S(2)}, u32[]{:S(2)}) collective-permute-start(bf16[128,128]{1,0:T(8,128)(2,1)S(1)} %get-tuple-element.30.refs_0_), channel_id=1, source_target_pairs={{0,2},{1,3},{2,0},{3,1},{4,6},{5,7},{6,4},{7,5},{8,10},{9,11},{10,... | collective-permute-start | bytes 98312 | tf_op jit(solution)/shard_map/ppermute | solution.py:52
  20.7 0.0 collective-permute-done.10.minus_ref
  20.7 1.4 %collective-permute-start.6 = (bf16[128,128]{1,0:T(8,128)(2,1)S(1)}, bf16[128,128]{1,0:T(8,128)(2,1)S(1)}, u32[]{:S(2)}, u32[]{:S(2)}) collective-permute-start(bf16[128,128]{1,0:T(8,128)(2,1)S(1)} %get-tuple-element.30.refs_0_), channel_id=1, source_target_pairs={{0,3},{1,2},{2,1},{3,0},{4,7},{5,6},{6,5},{7,4},{8,11},{9,10},{10,... | collective-permute-start | bytes 98312 | tf_op jit(solution)/shard_map/ppermute | solution.py:52
  22.1 0.0 collective-permute-done.9.plus_ref
  22.1 0.0 collective-permute-done.7.whole_ref
  22.1 1.1 %collective-permute-start.11 = (bf16[512,256]{1,0:T(8,128)(2,1)S(1)}, bf16[512,256]{1,0:T(8,128)(2,1)S(1)}, u32[]{:S(2)}, u32[]{:S(2)}) collective-permute-start(bf16[512,256]{1,0:T(8,128)(2,1)S(1)} %get-tuple-element.39), channel_id=1, source_target_pairs={{0,4},{4,0},{8,12},{12,8},{16,20},{20,16},{24,28},{28,24},{1,5},{5... | collective-permute-start | bytes 786440 | tf_op jit(solution)/shard_map/ppermute | solution.py:45
  23.2 1.9 %collective-permute-start.12 = (bf16[128,256]{1,0:T(8,128)(2,1)S(1)}, bf16[128,256]{1,0:T(8,128)(2,1)S(1)}, u32[]{:S(2)}, u32[]{:S(2)}) collective-permute-start(bf16[128,256]{1,0:T(8,128)(2,1)S(1)} %get-tuple-element.41), channel_id=1, source_target_pairs={{0,28},{4,8},{8,4},{12,16},{16,12},{20,24},{24,20},{28,0},{1,29},{... | collective-permute-start | bytes 196616 | tf_op jit(solution)/shard_map/ppermute | solution.py:45
  25.1 0.0 collective-permute-done.4.refs_1_
  25.1 0.0 collective-permute-done.5.refs_2_
  25.1 1.3 %collective-permute-done.6.refs_3_ = bf16[128,128]{1,0:T(8,128)(2,1)S(1)} collective-permute-done((bf16[128,128]{1,0:T(8,128)(2,1)S(1)}, bf16[128,128]{1,0:T(8,128)(2,1)S(1)}, u32[]{:S(2)}, u32[]{:S(2)}) %collective-permute-start.6) | collective-permute-done | bytes 32800 | tf_op jit(solution)/shard_map/ppermute | solution.py:52
  26.5 1.6 %collective-permute-done.12.second_ref = bf16[128,256]{1,0:T(8,128)(2,1)S(1)} collective-permute-done((bf16[128,256]{1,0:T(8,128)(2,1)S(1)}, bf16[128,256]{1,0:T(8,128)(2,1)S(1)}, u32[]{:S(2)}, u32[]{:S(2)}) %collective-permute-start.12) | collective-permute-done | bytes 65568 | tf_op jit(solution)/shard_map/ppermute | solution.py:45
  28.0 0.0 collective-permute-done.11.first_ref
  28.0 1.0 %finish.1 = (bf16[128,512]{1,0:T(8,128)(2,1)}, bf16[128,128]{1,0:T(8,128)(2,1)}, bf16[128,128]{1,0:T(8,128)(2,1)}) custom-call(bf16[128,512]{1,0:T(8,128)(2,1)S(1)} %gather.1.att_ref, bf16[128,512]{1,0:T(8,128)(2,1)S(1)} %get-tuple-element.31.mine_ref, bf16[128,512]{1,0:T(8,128)(2,1)S(1)} %collective-permute-done.7.whole_ref, ...), custom_call_target="tpu_custom_call" | custom-call | tf_op jit(solution)/shard_map/finish/pallas_call | solution.py:320
  (8 shorter events, 0.1 us)
Async XLA Ops:
  0.6 0.8 %copy-start.2 = (bf16[128,128]{1,0:T(8,128)(2,1)S(1)}, bf16[128,128]{1,0:T(8,128)(2,1)}, u32[]{:S(2)}) copy-start(bf16[128,128]{1,0:T(8,128)(2,1)} %param.8) | copy-start | bytes 98308
  1.4 4.1 %copy-start.1 = (s32[1,8]{1,0:T(1,128)S(1)}, s32[1,8]{1,0:T(1,128)}, u32[]{:S(2)}) copy-start(s32[1,8]{1,0:T(1,128)} %refs_0_.1) | copy-start | bytes 100
  1.4 5.9 %collective-permute-start = (bf16[128,256]{1,0:T(8,128)(2,1)S(1)}, bf16[128,256]{1,0:T(8,128)(2,1)S(1)}, u32[]{:S(2)}, u32[]{:S(2)}) collective-permute-start(bf16[128,256]{1,0:T(8,128)(2,1)S(1)} %constant_dynamic-update-slice_fusion.refs_3_.own_ref), channel_id=1, source_target_pairs={{0,4},{4,0},{8,12},{12,8},{16,20},{20,16},{24,28},{28,24},{1,5},{5... | collective-permute-start | bytes 196616 | tf_op jit(solution)/shard_map/ppermute | solution.py:45
  2.0 5.5 %collective-permute-start.1 = (bf16[128,256]{1,0:T(8,128)(2,1)S(1)}, bf16[128,256]{1,0:T(8,128)(2,1)S(1)}, u32[]{:S(2)}, u32[]{:S(2)}) collective-permute-start(bf16[128,256]{1,0:T(8,128)(2,1)S(1)} %constant_dynamic-update-slice_fusion.refs_3_.own_ref), channel_id=1, source_target_pairs={{0,28},{4,8},{8,4},{12,16},{16,12},{20,24},{24,20},{28,0},{1,29},{... | collective-permute-start | bytes 196616 | tf_op jit(solution)/shard_map/ppermute | solution.py:45
  7.5 5.6 %copy-start = (bf16[128,128]{1,0:T(8,128)(2,1)S(1)}, bf16[128,128]{1,0:T(8,128)(2,1)}, u32[]{:S(2)}) copy-start(bf16[128,128]{1,0:T(8,128)(2,1)} %refs_1_.3) | copy-start | bytes 98308
  7.5 5.6 %collective-permute-start.2 = (bf16[96,256]{1,0:T(8,128)(2,1)S(1)}, bf16[96,256]{1,0:T(8,128)(2,1)S(1)}, u32[]{:S(2)}, u32[]{:S(2)}) collective-permute-start(bf16[96,256]{1,0:T(8,128)(2,1)S(1)} %get-tuple-element.28), channel_id=1, source_target_pairs={{0,12},{4,24},{8,20},{12,0},{16,28},{20,8},{24,4},{28,16},{1,13},{... | collective-permute-start | bytes 147464 | tf_op jit(solution)/shard_map/ppermute | solution.py:45
  9.4 3.7 %collective-permute-start.3 = (bf16[64,256]{1,0:T(8,128)(2,1)S(1)}, bf16[64,256]{1,0:T(8,128)(2,1)S(1)}, u32[]{:S(2)}, u32[]{:S(2)}) collective-permute-start(bf16[64,256]{1,0:T(8,128)(2,1)S(1)} %get-tuple-element.29), channel_id=1, source_target_pairs={{0,20},{4,16},{8,28},{12,24},{16,4},{20,0},{24,12},{28,8},{1,21},{... | collective-permute-start | bytes 98312 | tf_op jit(solution)/shard_map/ppermute | solution.py:45
  9.5 10.2 %collective-permute-start.8 = (bf16[64,512]{1,0:T(8,128)(2,1)S(1)}, bf16[64,512]{1,0:T(8,128)(2,1)S(1)}, u32[]{:S(2)}, u32[]{:S(2)}) collective-permute-start(bf16[64,512]{1,0:T(8,128)(2,1)S(1)} %get-tuple-element.33), channel_id=1, source_target_pairs={{0,3},{1,2},{2,1},{3,0},{4,7},{5,6},{6,5},{7,4},{8,11},{9,10},{10,... | collective-permute-start | bytes 196616 | tf_op jit(solution)/shard_map/ppermute | solution.py:52
  13.1 9.0 %collective-permute-start.7 = (bf16[128,512]{1,0:T(8,128)(2,1)S(1)}, bf16[128,512]{1,0:T(8,128)(2,1)S(1)}, u32[]{:S(2)}, u32[]{:S(2)}) collective-permute-start(bf16[128,512]{1,0:T(8,128)(2,1)S(1)} %get-tuple-element.32), channel_id=1, source_target_pairs={{0,1},{1,0},{2,3},{3,2},{4,6},{5,7},{6,4},{7,5},{8,9},{9,8},{10,11... | collective-permute-start | bytes 393224 | tf_op jit(solution)/shard_map/ppermute | solution.py:368
  14.7 7.4 %collective-permute-start.9 = (bf16[96,256]{1,0:T(8,128)(2,1)S(1)}, bf16[96,256]{1,0:T(8,128)(2,1)S(1)}, u32[]{:S(2)}, u32[]{:S(2)}) collective-permute-start(bf16[96,256]{1,0:T(8,128)(2,1)S(1)} %get-tuple-element.37), channel_id=1, source_target_pairs={{0,12},{4,24},{8,20},{12,0},{16,28},{20,8},{24,4},{28,16},{1,13},{... | collective-permute-start | bytes 147464 | tf_op jit(solution)/shard_map/ppermute | solution.py:45
  15.6 5.1 %collective-permute-start.10 = (bf16[64,256]{1,0:T(8,128)(2,1)S(1)}, bf16[64,256]{1,0:T(8,128)(2,1)S(1)}, u32[]{:S(2)}, u32[]{:S(2)}) collective-permute-start(bf16[64,256]{1,0:T(8,128)(2,1)S(1)} %get-tuple-element.38), channel_id=1, source_target_pairs={{0,20},{4,16},{8,28},{12,24},{16,4},{20,0},{24,12},{28,8},{1,21},{... | collective-permute-start | bytes 98312 | tf_op jit(solution)/shard_map/ppermute | solution.py:45
  17.7 7.4 %collective-permute-start.4 = (bf16[128,128]{1,0:T(8,128)(2,1)S(1)}, bf16[128,128]{1,0:T(8,128)(2,1)S(1)}, u32[]{:S(2)}, u32[]{:S(2)}) collective-permute-start(bf16[128,128]{1,0:T(8,128)(2,1)S(1)} %get-tuple-element.30.refs_0_), channel_id=1, source_target_pairs={{0,1},{1,0},{2,3},{3,2},{4,5},{5,4},{6,7},{7,6},{8,9},{9,8},{10,11... | collective-permute-start | bytes 98312 | tf_op jit(solution)/shard_map/ppermute | solution.py:52
  19.7 5.4 %collective-permute-start.5 = (bf16[128,128]{1,0:T(8,128)(2,1)S(1)}, bf16[128,128]{1,0:T(8,128)(2,1)S(1)}, u32[]{:S(2)}, u32[]{:S(2)}) collective-permute-start(bf16[128,128]{1,0:T(8,128)(2,1)S(1)} %get-tuple-element.30.refs_0_), channel_id=1, source_target_pairs={{0,2},{1,3},{2,0},{3,1},{4,6},{5,7},{6,4},{7,5},{8,10},{9,11},{10,... | collective-permute-start | bytes 98312 | tf_op jit(solution)/shard_map/ppermute | solution.py:52
  20.7 5.7 %collective-permute-start.6 = (bf16[128,128]{1,0:T(8,128)(2,1)S(1)}, bf16[128,128]{1,0:T(8,128)(2,1)S(1)}, u32[]{:S(2)}, u32[]{:S(2)}) collective-permute-start(bf16[128,128]{1,0:T(8,128)(2,1)S(1)} %get-tuple-element.30.refs_0_), channel_id=1, source_target_pairs={{0,3},{1,2},{2,1},{3,0},{4,7},{5,6},{6,5},{7,4},{8,11},{9,10},{10,... | collective-permute-start | bytes 98312 | tf_op jit(solution)/shard_map/ppermute | solution.py:52
  22.1 5.9 %collective-permute-start.11 = (bf16[512,256]{1,0:T(8,128)(2,1)S(1)}, bf16[512,256]{1,0:T(8,128)(2,1)S(1)}, u32[]{:S(2)}, u32[]{:S(2)}) collective-permute-start(bf16[512,256]{1,0:T(8,128)(2,1)S(1)} %get-tuple-element.39), channel_id=1, source_target_pairs={{0,4},{4,0},{8,12},{12,8},{16,20},{20,16},{24,28},{28,24},{1,5},{5... | collective-permute-start | bytes 786440 | tf_op jit(solution)/shard_map/ppermute | solution.py:45
  23.2 4.8 %collective-permute-start.12 = (bf16[128,256]{1,0:T(8,128)(2,1)S(1)}, bf16[128,256]{1,0:T(8,128)(2,1)S(1)}, u32[]{:S(2)}, u32[]{:S(2)}) collective-permute-start(bf16[128,256]{1,0:T(8,128)(2,1)S(1)} %get-tuple-element.41), channel_id=1, source_target_pairs={{0,28},{4,8},{8,4},{12,16},{16,12},{20,24},{24,20},{28,0},{1,29},{... | collective-permute-start | bytes 196616 | tf_op jit(solution)/shard_map/ppermute | solution.py:45

commit v6 on v5

--- a/solution.py
+++ b/solution.py
@@ -159,7 +159,7 @@
     )(index, cotangent, out_weight, after)
 
 
-def lead_kernel(own_ref, first_ref, second_ref, mult_ref, whole_ref,
+def lead_kernel(own_ref, second_ref, first_ref, mult_ref, whole_ref,
                 plus_ref, minus_ref, whole_out):
     del mult_ref
     n = STRIDE_ROWS
@@ -180,7 +180,7 @@
         out_specs=(VMEM,) * 3,
         compiler_params=PARAMS,
         name="leads",
-    )(own, first, second, mult, whole)
+    )(own, second, first, mult, whole)
 
 
 def attend_kernel(sides, mult_ref, q_ref, grad_ref, *refs):
@@ -240,7 +240,7 @@
 
 
 def combine_kernel(own_ref, first_ref, second_ref, plus_ref, minus_ref, whole_ref, half_ref,
-                   own_out, first_out, second_out):
+                   att_ref, own_out, first_out, second_out, att_out):
     plus = plus_ref[...].astype(F32)
     minus = minus_ref[...].astype(F32)
     n = STRIDE_ROWS
@@ -250,6 +250,7 @@
     second_out[:n] = (second_ref[:n] + plus[2 * n:] + minus[n:]).astype(BF16)
     first_out[n:BLK] = first_ref[n:].astype(BF16)
     first_out[:n] = (first_ref[:n] + plus[n:2 * n]).astype(BF16)
+    att_out[...] = att_ref[...]
     row = BLK
     for ref in (whole_ref, half_ref):
         for c in range(0, ref.shape[1], PAIR):
@@ -257,17 +258,18 @@
             row += ref.shape[0]
 
 
-def combine(own, first, second, plus, minus, whole, half):
+def combine(own, first, second, plus, minus, whole, half, att):
     extra = (whole.size + half.size) // PAIR
     return pl.pallas_call(
         combine_kernel,
-        out_shape=(shape(BLK, PAIR, kind=F32), shape(BLK + extra, PAIR), shape(BLK, PAIR)),
-        in_specs=[VMEM] * 7,
-        out_specs=(VMEM,) * 3,
+        out_shape=(shape(BLK, PAIR, kind=F32), shape(BLK + extra, PAIR), shape(BLK, PAIR),
+                   shape(BLK, HD)),
+        in_specs=[VMEM] * 8,
+        out_specs=(VMEM,) * 4,
         compiler_params=PARAMS,
         cost_estimate=cost(COMBINE_COST),
         name="combine",
-    )(own, first, second, plus, minus, whole, half)
+    )(own, first, second, plus, minus, whole, half, att)
 
 
 def gather_kernel(*refs):
@@ -293,11 +295,13 @@
         ref[STRIDE_ROWS:] = total[STRIDE_ROWS:, c:c + HD].astype(ref.dtype)
 
 
-def finish_ring_kernel(att_ref, mine_ref, whole_ref, half_ref, first_ref, own_ref, second_ref,
-                       mixed_ref, dk_ref, dv_ref):
+def finish_ring_kernel(*refs):
+    att_ref, near_ref, far_ref = refs[:3]
+    att = [att_ref[...], near_ref[...], far_ref[:, :HD], far_ref[:, HD:]]
+    mine_ref, whole_ref, half_ref, first_ref, own_ref, second_ref = refs[3:9]
+    mixed_ref, dk_ref, dv_ref = refs[9:]
     core = lax.axis_index("seq") & 1
     half = HD // 2
-    att = [att_ref[:, r * HD:(r + 1) * HD] for r in range(4)]
     here = jnp.where(core == 0, att[1], att[2])
     there = jnp.where(core == 0, att[2], att[1])
     here_half = jnp.where(core == 0, att[3][:, :half], att[3][:, half:])
@@ -316,15 +320,15 @@
     settle(total, total[:STRIDE_ROWS], dk_ref, dv_ref)
 
 
-def finish_ring(att, mine, whole, half, first, own, second):
+def finish_ring(attentions, mine, whole, half, first, own, second):
     return pl.pallas_call(
         finish_ring_kernel,
         out_shape=(shape(BLK, mine.shape[1]), shape(BLK, HD), shape(BLK, HD)),
-        in_specs=[VMEM] * 7,
+        in_specs=[VMEM] * 9,
         out_specs=(VMEM,) * 3,
         compiler_params=PARAMS,
         name="finish",
-    )(att, mine, whole, half, first, own, second)
+    )(*attentions, mine, whole, half, first, own, second)
 
 
 def finish_kernel(count, *refs):
@@ -376,8 +380,8 @@
     side_rows = seq * n
     columns = 3 * BLK + side_rows
     own = jnp.concatenate([key_rows, value_rows], axis=1)
+    second = trade(own, -1)
     first = trade(own, 1)
-    second = trade(own, -1)
     grad, mult, *slices = prepare(
         ring, strided_index, cotangent, out_weight, heads, columns, own
     )
@@ -389,12 +393,13 @@
         att, dq, own_sum, first_sum, second_sum, to_plus, to_minus = attend(
             mult, queries, grad, (own, first, second), (trade(plus, 3), trade(minus, -3))
         )
-        attentions = [att] + [swap(att, r) for r in range(1, heads)]
-        own_sum, to_first, to_second = combine(
-            own_sum, first_sum, second_sum, trade(to_plus, 3), trade(to_minus, -3), whole, half
+        far = gather([swap(att, 2), swap(att, 3)])
+        own_sum, to_first, to_second, last = combine(
+            own_sum, first_sum, second_sum, trade(to_plus, 3), trade(to_minus, -3), whole, half,
+            att,
         )
         mixed, dk, dv = finish_ring(
-            gather(attentions), mine, whole, half, trade(to_first, 1), own_sum,
+            [att, swap(last, 1), far], mine, whole, half, trade(to_first, 1), own_sum,
             trade(to_second, -1),
         )
     else:

time: 29.2 us -> 27.3 us (0.935)
  starting transfers between devices: 20 us -> 18.4 us
  waiting for transfers between devices: 3.06 us -> 2.75 us
    ppermute x8, starting transfers between devices: 12 us -> 9.94 us  [trade(): lax.ppermute(array, 'seq', [(i, (i + (step if i % 2 == 0 else -step)) % c...]
    ppermute x8, waiting for transfers between devices: 1.71 us -> 0.19 us  [trade(): lax.ppermute(array, 'seq', [(i, (i + (step if i % 2 == 0 else -step)) % c...]
    ppermute x4, waiting for transfers between devices: 1.35 us -> 2.55 us  [swap(): return lax.ppermute(array, 'head', [(i, i ^ mask) for i in range(count)])]
    ppermute x4, starting transfers between devices: 7.99 us -> 8.43 us  [swap(): return lax.ppermute(array, 'head', [(i, i ^ mask) for i in range(count)])]
  transfers between devices with their start and end apart: 13 -> 13, of which waited for: 3 -> 5; matrix products, arithmetic and copies ran while one was open for 0% -> 0% of each run, Pallas kernels for 12% -> 13%
where the time goes in v6:
time: 27.3 us; the launch traced here: 27 us
  starting transfers between devices  18.4 us (67%)
  Pallas kernels  4.41 us (16%)
  waiting for transfers between devices  2.75 us (10%)
  local copies, waits for them, and re-layouts  0.8 us (3%)
  between operations  0.72 us (3%)
    ppermute x8, starting transfers between devices, trade(): lax.ppermute(array, 'seq', [(i, (i + (step if i % 2 == 0 else -step)) % c...  9.94 us
    ppermute x4, starting transfers between devices, swap(): return lax.ppermute(array, 'head', [(i, i ^ mask) for i in range(count)])  8.43 us
    ppermute x4, waiting for transfers between devices, swap(): return lax.ppermute(array, 'head', [(i, i ^ mask) for i in range(count)])  2.55 us
    pallas_call x1, Pallas kernels, prepare(): pl.pallas_call(body, out_shape=(shape(BLK, HD), shape(8, columns, kind=F3...  1.81 us
    pallas_call x1, Pallas kernels, attend(): pl.pallas_call(body, out_shape=(shape(BLK, HD), shape(BLK, HD)) + (shape(...  1.54 us
    pallas_call x1, Pallas kernels, finish_ring(): pl.pallas_call(finish_ring_kernel, out_shape=(shape(BLK, mine.shape[1]),...  0.99 us
    unnamed x7, local copies, waits for them, and re-layouts  0.78 us
  transfers between devices with their start and end apart: 13, of which 5 were waited for; matrix products, arithmetic and copies ran while one was open for 0% of the time, Pallas kernels for 13%

profile of v6, /device:TPU:0, one launch (start us, length us, event | category | flops | bytes accessed | tf_op | source)
XLA Modules:
  0.0 27.0 jit_solution(2448861551916164389)
XLA Ops:
  0.6 0.8 %constant_dynamic-update-slice_fusion.1 = bf16[128,256]{1,0:T(8,128)(2,1)S(1)} fusion(bf16[128,128]{1,0:T(8,128)(2,1)} %param.7), kind=kLoop, calls=%fused_computation.1 | loop fusion | bytes 65536
  1.4 0.0 copy-done.2
  1.4 0.0 copy-start.1
  1.4 0.5 %collective-permute-start = (bf16[128,256]{1,0:T(8,128)(2,1)S(1)}, bf16[128,256]{1,0:T(8,128)(2,1)S(1)}, u32[]{:S(2)}, u32[]{:S(2)}) collective-permute-start(bf16[128,256]{1,0:T(8,128)(2,1)S(1)} %constant_dynamic-update-slice_fusion.refs_3_.own_ref), channel_id=1, source_target_pairs={{0,4},{4,0},{8,12},{12,8},{16,20},{20,16},{24,28},{28,24},{1,5},{5... | collective-permute-start | bytes 196616 | tf_op jit(solution)/shard_map/ppermute | solution.py:45
  2.0 3.6 %collective-permute-start.1 = (bf16[128,256]{1,0:T(8,128)(2,1)S(1)}, bf16[128,256]{1,0:T(8,128)(2,1)S(1)}, u32[]{:S(2)}, u32[]{:S(2)}) collective-permute-start(bf16[128,256]{1,0:T(8,128)(2,1)S(1)} %constant_dynamic-update-slice_fusion.refs_3_.own_ref), channel_id=1, source_target_pairs={{0,28},{4,8},{8,4},{12,16},{16,12},{20,24},{24,20},{28,0},{1,29},{... | collective-permute-start | bytes 196616 | tf_op jit(solution)/shard_map/ppermute | solution.py:45
  5.5 1.8 %prepare.1 = (bf16[128,128]{1,0:T(8,128)(2,1)S(1)}, f32[8,640]{1,0:T(8,128)S(1)}, bf16[128,512]{1,0:T(8,128)(2,1)S(1)}, bf16[128,512]{1,0:T(8,128)(2,1)S(1)}, bf16[64,512]{1,0:T(8,128)(2,1)S(1)}) custom-call(s32[1,8]{1,0:T(1,128)S(1)} %copy-done.1, bf16[128,2048]{1,0:T(8,128)(2,1)} %refs_1_.2, bf16[128,2048]{1,0:T(8,128)(2,1)} %refs_2_.1, ...), custom_call_target="tpu_custom_call" | custom-call | flops 10000000000 | tf_op jit(solution)/shard_map/prepare/pallas_call | solution.py:144
  7.3 0.0 collective-permute-done.first_ref.refs_4_
  7.3 0.1 collective-permute-done.1.second_ref.refs_5_
  7.5 1.9 %collective-permute-start.2 = (bf16[96,256]{1,0:T(8,128)(2,1)S(1)}, bf16[96,256]{1,0:T(8,128)(2,1)S(1)}, u32[]{:S(2)}, u32[]{:S(2)}) collective-permute-start(bf16[96,256]{1,0:T(8,128)(2,1)S(1)} %get-tuple-element.29), channel_id=1, source_target_pairs={{0,12},{4,24},{8,20},{12,0},{16,28},{20,8},{24,4},{28,16},{1,13},{... | collective-permute-start | bytes 147464 | tf_op jit(solution)/shard_map/ppermute | solution.py:45
  9.4 0.1 collective-permute-start.3
  9.5 3.6 %collective-permute-start.7 = (bf16[64,512]{1,0:T(8,128)(2,1)S(1)}, bf16[64,512]{1,0:T(8,128)(2,1)S(1)}, u32[]{:S(2)}, u32[]{:S(2)}) collective-permute-start(bf16[64,512]{1,0:T(8,128)(2,1)S(1)} %get-tuple-element.38), channel_id=1, source_target_pairs={{0,3},{1,2},{2,1},{3,0},{4,7},{5,6},{6,5},{7,4},{8,11},{9,10},{10,... | collective-permute-start | bytes 196616 | tf_op jit(solution)/shard_map/ppermute | solution.py:52
  13.1 0.0 collective-permute-start.6
  13.1 0.0 collective-permute-done.3.refs_7_
  13.1 0.0 collective-permute-done.2.refs_6_
  13.1 1.5 %attend.1 = (bf16[128,128]{1,0:T(8,128)(2,1)S(1)}, bf16[128,128]{1,0:T(8,128)(2,1)}, f32[128,256]{1,0:T(8,128)S(1)}, f32[128,256]{1,0:T(8,128)S(1)}, f32[128,256...) custom-call(f32[8,640]{1,0:T(8,128)S(1)} %get-tuple-element.26.mult_ref.refs_0_, ...), custom_call_target="tpu_custom_call" | custom-call | flops 1000000000 | tf_op jit(solution)/shard_map/attend/pallas_call | solution.py:228
  14.7 0.9 %collective-permute-start.4 = (bf16[96,256]{1,0:T(8,128)(2,1)S(1)}, bf16[96,256]{1,0:T(8,128)(2,1)S(1)}, u32[]{:S(2)}, u32[]{:S(2)}) collective-permute-start(bf16[96,256]{1,0:T(8,128)(2,1)S(1)} %get-tuple-element.35), channel_id=1, source_target_pairs={{0,12},{4,24},{8,20},{12,0},{16,28},{20,8},{24,4},{28,16},{1,13},{... | collective-permute-start | bytes 147464 | tf_op jit(solution)/shard_map/ppermute | solution.py:45
  15.6 2.1 %collective-permute-start.5 = (bf16[64,256]{1,0:T(8,128)(2,1)S(1)}, bf16[64,256]{1,0:T(8,128)(2,1)S(1)}, u32[]{:S(2)}, u32[]{:S(2)}) collective-permute-start(bf16[64,256]{1,0:T(8,128)(2,1)S(1)} %get-tuple-element.36), channel_id=1, source_target_pairs={{0,20},{4,16},{8,28},{12,24},{16,4},{20,0},{24,12},{28,8},{1,21},{... | collective-permute-start | bytes 98312 | tf_op jit(solution)/shard_map/ppermute | solution.py:45
  17.7 2.5 %collective-permute-start.10 = (bf16[128,128]{1,0:T(8,128)(2,1)S(1)}, bf16[128,128]{1,0:T(8,128)(2,1)S(1)}, u32[]{:S(2)}, u32[]{:S(2)}) collective-permute-start(bf16[128,128]{1,0:T(8,128)(2,1)S(1)} %get-tuple-element.31.att_ref.refs_0_), channel_id=1, source_target_pairs={{0,3},{1,2},{2,1},{3,0},{4,7},{5,6},{6,5},{7,4},{8,11},{9,10},{10,... | collective-permute-start | bytes 98312 | tf_op jit(solution)/shard_map/ppermute | solution.py:52
  20.1 0.0 collective-permute-done.7.half_ref.refs_5_
  20.1 1.0 %collective-permute-start.9 = (bf16[128,128]{1,0:T(8,128)(2,1)S(1)}, bf16[128,128]{1,0:T(8,128)(2,1)S(1)}, u32[]{:S(2)}, u32[]{:S(2)}) collective-permute-start(bf16[128,128]{1,0:T(8,128)(2,1)S(1)} %get-tuple-element.31.att_ref.refs_0_), channel_id=1, source_target_pairs={{0,2},{1,3},{2,0},{3,1},{4,6},{5,7},{6,4},{7,5},{8,10},{9,11},{10,... | collective-permute-start | bytes 98312 | tf_op jit(solution)/shard_map/ppermute | solution.py:52
  21.2 0.0 collective-permute-done.5.minus_ref
  21.2 0.0 collective-permute-done.4.plus_ref
  21.2 0.0 collective-permute-done.6.whole_ref.refs_4_
  21.2 0.1 collective-permute-start.11
  21.3 0.8 %collective-permute-start.12 = (bf16[128,256]{1,0:T(8,128)(2,1)S(1)}, bf16[128,256]{1,0:T(8,128)(2,1)S(1)}, u32[]{:S(2)}, u32[]{:S(2)}) collective-permute-start(bf16[128,256]{1,0:T(8,128)(2,1)S(1)} %get-tuple-element.43), channel_id=1, source_target_pairs={{0,28},{4,8},{8,4},{12,16},{16,12},{20,24},{24,20},{28,0},{1,29},{... | collective-permute-start | bytes 196616 | tf_op jit(solution)/shard_map/ppermute | solution.py:45
  22.1 1.3 %collective-permute-start.8 = (bf16[128,128]{1,0:T(8,128)(2,1)S(1)}, bf16[128,128]{1,0:T(8,128)(2,1)S(1)}, u32[]{:S(2)}, u32[]{:S(2)}) collective-permute-start(bf16[128,128]{1,0:T(8,128)(2,1)S(1)} %get-tuple-element.39), channel_id=1, source_target_pairs={{0,1},{1,0},{2,3},{3,2},{4,5},{5,4},{6,7},{7,6},{8,9},{9,8},{10,11... | collective-permute-start | bytes 98312 | tf_op jit(solution)/shard_map/ppermute | solution.py:52
  23.4 0.2 collective-permute-done.10.refs_1_
  23.6 1.4 %collective-permute-done.9.refs_0_ = bf16[128,128]{1,0:T(8,128)(2,1)S(1)} collective-permute-done((bf16[128,128]{1,0:T(8,128)(2,1)S(1)}, bf16[128,128]{1,0:T(8,128)(2,1)S(1)}, u32[]{:S(2)}, u32[]{:S(2)}) %collective-permute-start.9) | collective-permute-done | bytes 32800 | tf_op jit(solution)/shard_map/ppermute | solution.py:52
  25.0 1.0 %collective-permute-done.8.refs_1_ = bf16[128,128]{1,0:T(8,128)(2,1)S(1)} collective-permute-done((bf16[128,128]{1,0:T(8,128)(2,1)S(1)}, bf16[128,128]{1,0:T(8,128)(2,1)S(1)}, u32[]{:S(2)}, u32[]{:S(2)}) %collective-permute-start.8) | collective-permute-done | bytes 32800 | tf_op jit(solution)/shard_map/ppermute | solution.py:52
  26.0 0.1 collective-permute-done.12.refs_8_
  26.1 0.0 collective-permute-done.11.refs_6_
  26.1 1.0 %finish.1 = (bf16[128,512]{1,0:T(8,128)(2,1)}, bf16[128,128]{1,0:T(8,128)(2,1)}, bf16[128,128]{1,0:T(8,128)(2,1)}) custom-call(bf16[128,128]{1,0:T(8,128)(2,1)S(1)} %get-tuple-element.31.att_ref.refs_0_, bf16[128,128]{1,0:T(8,128)(2,1)S(1)} %collective-permute-done.8.refs_1_, bf16[128,256]{1,0:T(8,128)(2,1)S(1)} %gather.1.refs_2_, ...), custom_call_target="tpu_custom_call" | custom-call | tf_op jit(solution)/shard_map/finish/pallas_call | solution.py:324
  (8 shorter events, 0.1 us)
Async XLA Ops:
  0.6 0.8 %copy-start.2 = (bf16[128,128]{1,0:T(8,128)(2,1)S(1)}, bf16[128,128]{1,0:T(8,128)(2,1)}, u32[]{:S(2)}) copy-start(bf16[128,128]{1,0:T(8,128)(2,1)} %param.8) | copy-start | bytes 98308
  1.4 4.1 %copy-start.1 = (s32[1,8]{1,0:T(1,128)S(1)}, s32[1,8]{1,0:T(1,128)}, u32[]{:S(2)}) copy-start(s32[1,8]{1,0:T(1,128)} %refs_0_.1) | copy-start | bytes 100
  1.4 5.9 %collective-permute-start = (bf16[128,256]{1,0:T(8,128)(2,1)S(1)}, bf16[128,256]{1,0:T(8,128)(2,1)S(1)}, u32[]{:S(2)}, u32[]{:S(2)}) collective-permute-start(bf16[128,256]{1,0:T(8,128)(2,1)S(1)} %constant_dynamic-update-slice_fusion.refs_3_.own_ref), channel_id=1, source_target_pairs={{0,4},{4,0},{8,12},{12,8},{16,20},{20,16},{24,28},{28,24},{1,5},{5... | collective-permute-start | bytes 196616 | tf_op jit(solution)/shard_map/ppermute | solution.py:45
  2.0 5.5 %collective-permute-start.1 = (bf16[128,256]{1,0:T(8,128)(2,1)S(1)}, bf16[128,256]{1,0:T(8,128)(2,1)S(1)}, u32[]{:S(2)}, u32[]{:S(2)}) collective-permute-start(bf16[128,256]{1,0:T(8,128)(2,1)S(1)} %constant_dynamic-update-slice_fusion.refs_3_.own_ref), channel_id=1, source_target_pairs={{0,28},{4,8},{8,4},{12,16},{16,12},{20,24},{24,20},{28,0},{1,29},{... | collective-permute-start | bytes 196616 | tf_op jit(solution)/shard_map/ppermute | solution.py:45
  7.5 5.6 %copy-start = (bf16[128,128]{1,0:T(8,128)(2,1)S(1)}, bf16[128,128]{1,0:T(8,128)(2,1)}, u32[]{:S(2)}) copy-start(bf16[128,128]{1,0:T(8,128)(2,1)} %refs_1_.3) | copy-start | bytes 98308
  7.5 5.6 %collective-permute-start.2 = (bf16[96,256]{1,0:T(8,128)(2,1)S(1)}, bf16[96,256]{1,0:T(8,128)(2,1)S(1)}, u32[]{:S(2)}, u32[]{:S(2)}) collective-permute-start(bf16[96,256]{1,0:T(8,128)(2,1)S(1)} %get-tuple-element.29), channel_id=1, source_target_pairs={{0,12},{4,24},{8,20},{12,0},{16,28},{20,8},{24,4},{28,16},{1,13},{... | collective-permute-start | bytes 147464 | tf_op jit(solution)/shard_map/ppermute | solution.py:45
  9.4 3.7 %collective-permute-start.3 = (bf16[64,256]{1,0:T(8,128)(2,1)S(1)}, bf16[64,256]{1,0:T(8,128)(2,1)S(1)}, u32[]{:S(2)}, u32[]{:S(2)}) collective-permute-start(bf16[64,256]{1,0:T(8,128)(2,1)S(1)} %get-tuple-element.30), channel_id=1, source_target_pairs={{0,20},{4,16},{8,28},{12,24},{16,4},{20,0},{24,12},{28,8},{1,21},{... | collective-permute-start | bytes 98312 | tf_op jit(solution)/shard_map/ppermute | solution.py:45
  9.5 10.7 %collective-permute-start.7 = (bf16[64,512]{1,0:T(8,128)(2,1)S(1)}, bf16[64,512]{1,0:T(8,128)(2,1)S(1)}, u32[]{:S(2)}, u32[]{:S(2)}) collective-permute-start(bf16[64,512]{1,0:T(8,128)(2,1)S(1)} %get-tuple-element.38), channel_id=1, source_target_pairs={{0,3},{1,2},{2,1},{3,0},{4,7},{5,6},{6,5},{7,4},{8,11},{9,10},{10,... | collective-permute-start | bytes 196616 | tf_op jit(solution)/shard_map/ppermute | solution.py:52
  13.1 8.1 %collective-permute-start.6 = (bf16[128,512]{1,0:T(8,128)(2,1)S(1)}, bf16[128,512]{1,0:T(8,128)(2,1)S(1)}, u32[]{:S(2)}, u32[]{:S(2)}) collective-permute-start(bf16[128,512]{1,0:T(8,128)(2,1)S(1)} %get-tuple-element.37), channel_id=1, source_target_pairs={{0,1},{1,0},{2,3},{3,2},{4,6},{5,7},{6,4},{7,5},{8,9},{9,8},{10,11... | collective-permute-start | bytes 393224 | tf_op jit(solution)/shard_map/ppermute | solution.py:372
  14.7 6.5 %collective-permute-start.4 = (bf16[96,256]{1,0:T(8,128)(2,1)S(1)}, bf16[96,256]{1,0:T(8,128)(2,1)S(1)}, u32[]{:S(2)}, u32[]{:S(2)}) collective-permute-start(bf16[96,256]{1,0:T(8,128)(2,1)S(1)} %get-tuple-element.35), channel_id=1, source_target_pairs={{0,12},{4,24},{8,20},{12,0},{16,28},{20,8},{24,4},{28,16},{1,13},{... | collective-permute-start | bytes 147464 | tf_op jit(solution)/shard_map/ppermute | solution.py:45
  15.6 5.6 %collective-permute-start.5 = (bf16[64,256]{1,0:T(8,128)(2,1)S(1)}, bf16[64,256]{1,0:T(8,128)(2,1)S(1)}, u32[]{:S(2)}, u32[]{:S(2)}) collective-permute-start(bf16[64,256]{1,0:T(8,128)(2,1)S(1)} %get-tuple-element.36), channel_id=1, source_target_pairs={{0,20},{4,16},{8,28},{12,24},{16,4},{20,0},{24,12},{28,8},{1,21},{... | collective-permute-start | bytes 98312 | tf_op jit(solution)/shard_map/ppermute | solution.py:45
  17.7 5.9 %collective-permute-start.10 = (bf16[128,128]{1,0:T(8,128)(2,1)S(1)}, bf16[128,128]{1,0:T(8,128)(2,1)S(1)}, u32[]{:S(2)}, u32[]{:S(2)}) collective-permute-start(bf16[128,128]{1,0:T(8,128)(2,1)S(1)} %get-tuple-element.31.att_ref.refs_0_), channel_id=1, source_target_pairs={{0,3},{1,2},{2,1},{3,0},{4,7},{5,6},{6,5},{7,4},{8,11},{9,10},{10,... | collective-permute-start | bytes 98312 | tf_op jit(solution)/shard_map/ppermute | solution.py:52
  20.1 4.8 %collective-permute-start.9 = (bf16[128,128]{1,0:T(8,128)(2,1)S(1)}, bf16[128,128]{1,0:T(8,128)(2,1)S(1)}, u32[]{:S(2)}, u32[]{:S(2)}) collective-permute-start(bf16[128,128]{1,0:T(8,128)(2,1)S(1)} %get-tuple-element.31.att_ref.refs_0_), channel_id=1, source_target_pairs={{0,2},{1,3},{2,0},{3,1},{4,6},{5,7},{6,4},{7,5},{8,10},{9,11},{10,... | collective-permute-start | bytes 98312 | tf_op jit(solution)/shard_map/ppermute | solution.py:52
  21.2 4.8 %collective-permute-start.11 = (bf16[512,256]{1,0:T(8,128)(2,1)S(1)}, bf16[512,256]{1,0:T(8,128)(2,1)S(1)}, u32[]{:S(2)}, u32[]{:S(2)}) collective-permute-start(bf16[512,256]{1,0:T(8,128)(2,1)S(1)} %get-tuple-element.41), channel_id=1, source_target_pairs={{0,4},{4,0},{8,12},{12,8},{16,20},{20,16},{24,28},{28,24},{1,5},{5... | collective-permute-start | bytes 786440 | tf_op jit(solution)/shard_map/ppermute | solution.py:45
  21.3 4.7 %collective-permute-start.12 = (bf16[128,256]{1,0:T(8,128)(2,1)S(1)}, bf16[128,256]{1,0:T(8,128)(2,1)S(1)}, u32[]{:S(2)}, u32[]{:S(2)}) collective-permute-start(bf16[128,256]{1,0:T(8,128)(2,1)S(1)} %get-tuple-element.43), channel_id=1, source_target_pairs={{0,28},{4,8},{8,4},{12,16},{16,12},{20,24},{24,20},{28,0},{1,29},{... | collective-permute-start | bytes 196616 | tf_op jit(solution)/shard_map/ppermute | solution.py:45
  22.1 3.9 %collective-permute-start.8 = (bf16[128,128]{1,0:T(8,128)(2,1)S(1)}, bf16[128,128]{1,0:T(8,128)(2,1)S(1)}, u32[]{:S(2)}, u32[]{:S(2)}) collective-permute-start(bf16[128,128]{1,0:T(8,128)(2,1)S(1)} %get-tuple-element.39), channel_id=1, source_target_pairs={{0,1},{1,0},{2,3},{3,2},{4,5},{5,4},{6,7},{7,6},{8,9},{9,8},{10,11... | collective-permute-start | bytes 98312 | tf_op jit(solution)/shard_map/ppermute | solution.py:52

commit v7 on v6

--- a/solution.py
+++ b/solution.py
@@ -296,10 +296,22 @@
 
 
 def finish_ring_kernel(*refs):
-    att_ref, near_ref, far_ref = refs[:3]
+    att_ref, near_ref, far_ref, mine_ref, whole_ref, half_ref = refs[:6]
+    first_ref, own_ref, second_ref, dq_ref = refs[6:10]
+    mixed_hbm, dq_hbm, dk_hbm, dv_hbm, mixed_ref, dk_ref, dv_ref, sems = refs[10:]
+    copies = []
+
+    def send(src, dst):
+        copy = pltpu.make_async_copy(src, dst, sems.at[len(copies)])
+        copy.start()
+        copies.append(copy)
+
+    send(dq_ref, dq_hbm)
+    total = own_ref[...] + first_ref[:BLK].astype(F32) + second_ref[...].astype(F32)
+    settle(total, total[:STRIDE_ROWS], dk_ref, dv_ref)
+    send(dk_ref, dk_hbm)
+    send(dv_ref, dv_hbm)
     att = [att_ref[...], near_ref[...], far_ref[:, :HD], far_ref[:, HD:]]
-    mine_ref, whole_ref, half_ref, first_ref, own_ref, second_ref = refs[3:9]
-    mixed_ref, dk_ref, dv_ref = refs[9:]
     core = lax.axis_index("seq") & 1
     half = HD // 2
     here = jnp.where(core == 0, att[1], att[2])
@@ -316,19 +328,27 @@
         mixed = mixed + dot_nn(there, other_whole) + dot_nn(here_half, half_ref[:, span])
         mixed = mixed + dot_nn(there_half, other_half)
         mixed_ref[:, span] = mixed.astype(mixed_ref.dtype)
-    total = own_ref[...] + first_ref[:BLK].astype(F32) + second_ref[...].astype(F32)
-    settle(total, total[:STRIDE_ROWS], dk_ref, dv_ref)
-
-
-def finish_ring(attentions, mine, whole, half, first, own, second):
+        send(mixed_ref.at[:, pl.ds(c, PAIR)], mixed_hbm.at[:, pl.ds(c, PAIR)])
+    for copy in copies:
+        copy.wait()
+
+
+def finish_ring(attentions, mine, whole, half, first, own, second, dq):
+    width = mine.shape[1]
     return pl.pallas_call(
         finish_ring_kernel,
-        out_shape=(shape(BLK, mine.shape[1]), shape(BLK, HD), shape(BLK, HD)),
-        in_specs=[VMEM] * 9,
-        out_specs=(VMEM,) * 3,
+        out_shape=(shape(BLK, width),) + (shape(BLK, HD),) * 3,
+        in_specs=[VMEM] * 10,
+        out_specs=(HBM,) * 4,
+        scratch_shapes=[
+            pltpu.VMEM((BLK, width), BF16),
+            pltpu.VMEM((BLK, HD), BF16),
+            pltpu.VMEM((BLK, HD), BF16),
+            pltpu.SemaphoreType.DMA((3 + width // PAIR,)),
+        ],
         compiler_params=PARAMS,
         name="finish",
-    )(*attentions, mine, whole, half, first, own, second)
+    )(*attentions, mine, whole, half, first, own, second, dq)
 
 
 def finish_kernel(count, *refs):
@@ -398,9 +418,9 @@
             own_sum, first_sum, second_sum, trade(to_plus, 3), trade(to_minus, -3), whole, half,
             att,
         )
-        mixed, dk, dv = finish_ring(
+        mixed, dq, dk, dv = finish_ring(
             [att, swap(last, 1), far], mine, whole, half, trade(to_first, 1), own_sum,
-            trade(to_second, -1),
+            trade(to_second, -1), dq,
         )
     else:
         slices = [slices[0]] + [swap(slices[r], r) for r in range(1, heads)]

time: 27.3 us -> 27.1 us (level)
  Pallas kernels: 4.41 us -> 3.93 us
    pallas_call x1, Pallas kernels: 1.54 us -> 1.02 us  [attend(): pl.pallas_call(body, out_shape=(shape(BLK, HD), shape(BLK, HD)) + (shape(...]
  transfers between devices with their start and end apart: 13 -> 13, of which waited for: 5 -> 5; matrix products, arithmetic and copies ran while one was open for 0% -> 0% of each run, Pallas kernels for 13% -> 11%
where the time goes in v7:
time: 27.1 us; the launch traced here: 26.9 us
  starting transfers between devices  18.4 us (68%)
  Pallas kernels  3.93 us (15%)
  waiting for transfers between devices  2.98 us (11%)
  local copies, waits for them, and re-layouts  0.8 us (3%)
  between operations  0.72 us (3%)
    ppermute x8, starting transfers between devices, trade(): lax.ppermute(array, 'seq', [(i, (i + (step if i % 2 == 0 else -step)) % c...  10 us
    ppermute x4, starting transfers between devices, swap(): return lax.ppermute(array, 'head', [(i, i ^ mask) for i in range(count)])  8.43 us
    ppermute x4, waiting for transfers between devices, swap(): return lax.ppermute(array, 'head', [(i, i ^ mask) for i in range(count)])  2.55 us
    pallas_call x1, Pallas kernels, prepare(): pl.pallas_call(body, out_shape=(shape(BLK, HD), shape(8, columns, kind=F3...  1.81 us
    pallas_call x1, Pallas kernels, finish_ring(): pl.pallas_call(finish_ring_kernel, out_shape=(shape(BLK, width),) + (shap...  1.02 us
    pallas_call x1, Pallas kernels, attend(): pl.pallas_call(body, out_shape=(shape(BLK, HD), shape(BLK, HD)) + (shape(...  1.02 us
    unnamed x7, local copies, waits for them, and re-layouts  0.78 us
  transfers between devices with their start and end apart: 13, of which 5 were waited for; matrix products, arithmetic and copies ran while one was open for 0% of the time, Pallas kernels for 11%

profile of v7, /device:TPU:0, one launch (start us, length us, event | category | flops | bytes accessed | tf_op | source)
XLA Modules:
  0.0 26.9 jit_solution(7532458166332228046)
XLA Ops:
  0.6 0.8 %constant_dynamic-update-slice_fusion.1 = bf16[128,256]{1,0:T(8,128)(2,1)S(1)} fusion(bf16[128,128]{1,0:T(8,128)(2,1)} %param.7), kind=kLoop, calls=%fused_computation.1 | loop fusion | bytes 65536
  1.4 0.0 copy-start.1
  1.4 0.5 %collective-permute-start = (bf16[128,256]{1,0:T(8,128)(2,1)S(1)}, bf16[128,256]{1,0:T(8,128)(2,1)S(1)}, u32[]{:S(2)}, u32[]{:S(2)}) collective-permute-start(bf16[128,256]{1,0:T(8,128)(2,1)S(1)} %constant_dynamic-update-slice_fusion.refs_3_.own_ref), channel_id=1, source_target_pairs={{0,4},{4,0},{8,12},{12,8},{16,20},{20,16},{24,28},{28,24},{1,5},{5... | collective-permute-start | bytes 196616 | tf_op jit(solution)/shard_map/ppermute | solution.py:45
  2.0 3.6 %collective-permute-start.1 = (bf16[128,256]{1,0:T(8,128)(2,1)S(1)}, bf16[128,256]{1,0:T(8,128)(2,1)S(1)}, u32[]{:S(2)}, u32[]{:S(2)}) collective-permute-start(bf16[128,256]{1,0:T(8,128)(2,1)S(1)} %constant_dynamic-update-slice_fusion.refs_3_.own_ref), channel_id=1, source_target_pairs={{0,28},{4,8},{8,4},{12,16},{16,12},{20,24},{24,20},{28,0},{1,29},{... | collective-permute-start | bytes 196616 | tf_op jit(solution)/shard_map/ppermute | solution.py:45
  5.5 1.8 %prepare.1 = (bf16[128,128]{1,0:T(8,128)(2,1)S(1)}, f32[8,640]{1,0:T(8,128)S(1)}, bf16[128,512]{1,0:T(8,128)(2,1)S(1)}, bf16[128,512]{1,0:T(8,128)(2,1)S(1)}, bf16[64,512]{1,0:T(8,128)(2,1)S(1)}) custom-call(s32[1,8]{1,0:T(1,128)S(1)} %copy-done.1, bf16[128,2048]{1,0:T(8,128)(2,1)} %refs_1_.2, bf16[128,2048]{1,0:T(8,128)(2,1)} %refs_2_.1, ...), custom_call_target="tpu_custom_call" | custom-call | flops 10000000000 | tf_op jit(solution)/shard_map/prepare/pallas_call | solution.py:144
  7.3 0.0 collective-permute-done.first_ref.refs_4_
  7.3 0.1 collective-permute-done.1.second_ref.refs_5_
  7.5 1.9 %collective-permute-start.2 = (bf16[96,256]{1,0:T(8,128)(2,1)S(1)}, bf16[96,256]{1,0:T(8,128)(2,1)S(1)}, u32[]{:S(2)}, u32[]{:S(2)}) collective-permute-start(bf16[96,256]{1,0:T(8,128)(2,1)S(1)} %get-tuple-element.26), channel_id=1, source_target_pairs={{0,12},{4,24},{8,20},{12,0},{16,28},{20,8},{24,4},{28,16},{1,13},{... | collective-permute-start | bytes 147464 | tf_op jit(solution)/shard_map/ppermute | solution.py:45
  9.4 0.1 collective-permute-start.3
  9.5 3.6 %collective-permute-start.7 = (bf16[64,512]{1,0:T(8,128)(2,1)S(1)}, bf16[64,512]{1,0:T(8,128)(2,1)S(1)}, u32[]{:S(2)}, u32[]{:S(2)}) collective-permute-start(bf16[64,512]{1,0:T(8,128)(2,1)S(1)} %get-tuple-element.35), channel_id=1, source_target_pairs={{0,3},{1,2},{2,1},{3,0},{4,7},{5,6},{6,5},{7,4},{8,11},{9,10},{10,... | collective-permute-start | bytes 196616 | tf_op jit(solution)/shard_map/ppermute | solution.py:52
  13.1 0.0 collective-permute-start.6
  13.1 0.0 collective-permute-done.3.refs_7_
  13.1 0.0 collective-permute-done.2.refs_6_
  13.1 1.0 %attend.1 = (bf16[128,128]{1,0:T(8,128)(2,1)S(1)}, bf16[128,128]{1,0:T(8,128)(2,1)S(1)}, f32[128,256]{1,0:T(8,128)S(1)}, f32[128,256]{1,0:T(8,128)S(1)}, f32[128...) custom-call(f32[8,640]{1,0:T(8,128)S(1)} %get-tuple-element.23.mult_ref.refs_0_, ...), custom_call_target="tpu_custom_call" | custom-call | flops 1000000000 | tf_op jit(solution)/shard_map/attend/pallas_call | solution.py:228
  14.1 1.0 %collective-permute-start.4 = (bf16[96,256]{1,0:T(8,128)(2,1)S(1)}, bf16[96,256]{1,0:T(8,128)(2,1)S(1)}, u32[]{:S(2)}, u32[]{:S(2)}) collective-permute-start(bf16[96,256]{1,0:T(8,128)(2,1)S(1)} %get-tuple-element.32), channel_id=1, source_target_pairs={{0,12},{4,24},{8,20},{12,0},{16,28},{20,8},{24,4},{28,16},{1,13},{... | collective-permute-start | bytes 147464 | tf_op jit(solution)/shard_map/ppermute | solution.py:45
  15.2 2.1 %collective-permute-start.5 = (bf16[64,256]{1,0:T(8,128)(2,1)S(1)}, bf16[64,256]{1,0:T(8,128)(2,1)S(1)}, u32[]{:S(2)}, u32[]{:S(2)}) collective-permute-start(bf16[64,256]{1,0:T(8,128)(2,1)S(1)} %get-tuple-element.33), channel_id=1, source_target_pairs={{0,20},{4,16},{8,28},{12,24},{16,4},{20,0},{24,12},{28,8},{1,21},{... | collective-permute-start | bytes 98312 | tf_op jit(solution)/shard_map/ppermute | solution.py:45
  17.2 2.5 %collective-permute-start.10 = (bf16[128,128]{1,0:T(8,128)(2,1)S(1)}, bf16[128,128]{1,0:T(8,128)(2,1)S(1)}, u32[]{:S(2)}, u32[]{:S(2)}) collective-permute-start(bf16[128,128]{1,0:T(8,128)(2,1)S(1)} %get-tuple-element.28.att_ref.refs_0_), channel_id=1, source_target_pairs={{0,3},{1,2},{2,1},{3,0},{4,7},{5,6},{6,5},{7,4},{8,11},{9,10},{10,... | collective-permute-start | bytes 98312 | tf_op jit(solution)/shard_map/ppermute | solution.py:52
  19.7 0.0 collective-permute-done.7.half_ref.refs_5_
  19.7 1.0 %collective-permute-start.9 = (bf16[128,128]{1,0:T(8,128)(2,1)S(1)}, bf16[128,128]{1,0:T(8,128)(2,1)S(1)}, u32[]{:S(2)}, u32[]{:S(2)}) collective-permute-start(bf16[128,128]{1,0:T(8,128)(2,1)S(1)} %get-tuple-element.28.att_ref.refs_0_), channel_id=1, source_target_pairs={{0,2},{1,3},{2,0},{3,1},{4,6},{5,7},{6,4},{7,5},{8,10},{9,11},{10,... | collective-permute-start | bytes 98312 | tf_op jit(solution)/shard_map/ppermute | solution.py:52
  20.7 0.0 collective-permute-done.5.minus_ref
  20.7 0.0 collective-permute-done.4.plus_ref
  20.7 0.0 collective-permute-done.6.whole_ref.refs_4_
  20.7 0.1 combine.1
  20.8 0.1 collective-permute-start.11
  20.9 0.8 %collective-permute-start.12 = (bf16[128,256]{1,0:T(8,128)(2,1)S(1)}, bf16[128,256]{1,0:T(8,128)(2,1)S(1)}, u32[]{:S(2)}, u32[]{:S(2)}) collective-permute-start(bf16[128,256]{1,0:T(8,128)(2,1)S(1)} %get-tuple-element.40), channel_id=1, source_target_pairs={{0,28},{4,8},{8,4},{12,16},{16,12},{20,24},{24,20},{28,0},{1,29},{... | collective-permute-start | bytes 196616 | tf_op jit(solution)/shard_map/ppermute | solution.py:45
  21.6 1.4 %collective-permute-start.8 = (bf16[128,128]{1,0:T(8,128)(2,1)S(1)}, bf16[128,128]{1,0:T(8,128)(2,1)S(1)}, u32[]{:S(2)}, u32[]{:S(2)}) collective-permute-start(bf16[128,128]{1,0:T(8,128)(2,1)S(1)} %get-tuple-element.36), channel_id=1, source_target_pairs={{0,1},{1,0},{2,3},{3,2},{4,5},{5,4},{6,7},{7,6},{8,9},{9,8},{10,11... | collective-permute-start | bytes 98312 | tf_op jit(solution)/shard_map/ppermute | solution.py:52
  23.0 0.2 collective-permute-done.10.refs_1_
  23.1 1.4 %collective-permute-done.9.refs_0_ = bf16[128,128]{1,0:T(8,128)(2,1)S(1)} collective-permute-done((bf16[128,128]{1,0:T(8,128)(2,1)S(1)}, bf16[128,128]{1,0:T(8,128)(2,1)S(1)}, u32[]{:S(2)}, u32[]{:S(2)}) %collective-permute-start.9) | collective-permute-done | bytes 32800 | tf_op jit(solution)/shard_map/ppermute | solution.py:52
  24.5 1.0 %collective-permute-done.8.refs_1_ = bf16[128,128]{1,0:T(8,128)(2,1)S(1)} collective-permute-done((bf16[128,128]{1,0:T(8,128)(2,1)S(1)}, bf16[128,128]{1,0:T(8,128)(2,1)S(1)}, u32[]{:S(2)}, u32[]{:S(2)}) %collective-permute-start.8) | collective-permute-done | bytes 32800 | tf_op jit(solution)/shard_map/ppermute | solution.py:52
  25.5 0.3 %collective-permute-done.12.refs_8_ = bf16[128,256]{1,0:T(8,128)(2,1)S(1)} collective-permute-done((bf16[128,256]{1,0:T(8,128)(2,1)S(1)}, bf16[128,256]{1,0:T(8,128)(2,1)S(1)}, u32[]{:S(2)}, u32[]{:S(2)}) %collective-permute-start.12) | collective-permute-done | bytes 65568 | tf_op jit(solution)/shard_map/ppermute | solution.py:45
  25.8 0.0 collective-permute-done.11.refs_6_
  25.8 1.0 %finish.1 = (bf16[128,512]{1,0:T(8,128)(2,1)}, bf16[128,128]{1,0:T(8,128)(2,1)}, bf16[128,128]{1,0:T(8,128)(2,1)}, bf16[128,128]{1,0:T(8,128)(2,1)}) custom-call(bf16[128,128]{1,0:T(8,128)(2,1)S(1)} %get-tuple-element.28.att_ref.refs_0_, bf16[128,128]{1,0:T(8,128)(2,1)S(1)} %collective-permute-done.8.refs_1_, bf16[128,256]{1,0:T(8,128)(2,1)S(1)} %gather.1.refs_2_, ...), custom_call_target="tpu_custom_call" | custom-call | tf_op jit(solution)/shard_map/finish/pallas_call | solution.py:338
  (8 shorter events, 0.1 us)
Async XLA Ops:
  0.6 0.8 %copy-start.2 = (bf16[128,128]{1,0:T(8,128)(2,1)S(1)}, bf16[128,128]{1,0:T(8,128)(2,1)}, u32[]{:S(2)}) copy-start(bf16[128,128]{1,0:T(8,128)(2,1)} %param.8) | copy-start | bytes 98308
  1.4 4.1 %copy-start.1 = (s32[1,8]{1,0:T(1,128)S(1)}, s32[1,8]{1,0:T(1,128)}, u32[]{:S(2)}) copy-start(s32[1,8]{1,0:T(1,128)} %refs_0_.1) | copy-start | bytes 100
  1.4 5.9 %collective-permute-start = (bf16[128,256]{1,0:T(8,128)(2,1)S(1)}, bf16[128,256]{1,0:T(8,128)(2,1)S(1)}, u32[]{:S(2)}, u32[]{:S(2)}) collective-permute-start(bf16[128,256]{1,0:T(8,128)(2,1)S(1)} %constant_dynamic-update-slice_fusion.refs_3_.own_ref), channel_id=1, source_target_pairs={{0,4},{4,0},{8,12},{12,8},{16,20},{20,16},{24,28},{28,24},{1,5},{5... | collective-permute-start | bytes 196616 | tf_op jit(solution)/shard_map/ppermute | solution.py:45
  2.0 5.5 %collective-permute-start.1 = (bf16[128,256]{1,0:T(8,128)(2,1)S(1)}, bf16[128,256]{1,0:T(8,128)(2,1)S(1)}, u32[]{:S(2)}, u32[]{:S(2)}) collective-permute-start(bf16[128,256]{1,0:T(8,128)(2,1)S(1)} %constant_dynamic-update-slice_fusion.refs_3_.own_ref), channel_id=1, source_target_pairs={{0,28},{4,8},{8,4},{12,16},{16,12},{20,24},{24,20},{28,0},{1,29},{... | collective-permute-start | bytes 196616 | tf_op jit(solution)/shard_map/ppermute | solution.py:45
  7.5 5.6 %copy-start = (bf16[128,128]{1,0:T(8,128)(2,1)S(1)}, bf16[128,128]{1,0:T(8,128)(2,1)}, u32[]{:S(2)}) copy-start(bf16[128,128]{1,0:T(8,128)(2,1)} %refs_1_.3) | copy-start | bytes 98308
  7.5 5.6 %collective-permute-start.2 = (bf16[96,256]{1,0:T(8,128)(2,1)S(1)}, bf16[96,256]{1,0:T(8,128)(2,1)S(1)}, u32[]{:S(2)}, u32[]{:S(2)}) collective-permute-start(bf16[96,256]{1,0:T(8,128)(2,1)S(1)} %get-tuple-element.26), channel_id=1, source_target_pairs={{0,12},{4,24},{8,20},{12,0},{16,28},{20,8},{24,4},{28,16},{1,13},{... | collective-permute-start | bytes 147464 | tf_op jit(solution)/shard_map/ppermute | solution.py:45
  9.4 3.7 %collective-permute-start.3 = (bf16[64,256]{1,0:T(8,128)(2,1)S(1)}, bf16[64,256]{1,0:T(8,128)(2,1)S(1)}, u32[]{:S(2)}, u32[]{:S(2)}) collective-permute-start(bf16[64,256]{1,0:T(8,128)(2,1)S(1)} %get-tuple-element.27), channel_id=1, source_target_pairs={{0,20},{4,16},{8,28},{12,24},{16,4},{20,0},{24,12},{28,8},{1,21},{... | collective-permute-start | bytes 98312 | tf_op jit(solution)/shard_map/ppermute | solution.py:45
  9.5 10.2 %collective-permute-start.7 = (bf16[64,512]{1,0:T(8,128)(2,1)S(1)}, bf16[64,512]{1,0:T(8,128)(2,1)S(1)}, u32[]{:S(2)}, u32[]{:S(2)}) collective-permute-start(bf16[64,512]{1,0:T(8,128)(2,1)S(1)} %get-tuple-element.35), channel_id=1, source_target_pairs={{0,3},{1,2},{2,1},{3,0},{4,7},{5,6},{6,5},{7,4},{8,11},{9,10},{10,... | collective-permute-start | bytes 196616 | tf_op jit(solution)/shard_map/ppermute | solution.py:52
  13.1 7.6 %collective-permute-start.6 = (bf16[128,512]{1,0:T(8,128)(2,1)S(1)}, bf16[128,512]{1,0:T(8,128)(2,1)S(1)}, u32[]{:S(2)}, u32[]{:S(2)}) collective-permute-start(bf16[128,512]{1,0:T(8,128)(2,1)S(1)} %get-tuple-element.34), channel_id=1, source_target_pairs={{0,1},{1,0},{2,3},{3,2},{4,6},{5,7},{6,4},{7,5},{8,9},{9,8},{10,11... | collective-permute-start | bytes 393224 | tf_op jit(solution)/shard_map/ppermute | solution.py:392
  14.1 6.6 %collective-permute-start.4 = (bf16[96,256]{1,0:T(8,128)(2,1)S(1)}, bf16[96,256]{1,0:T(8,128)(2,1)S(1)}, u32[]{:S(2)}, u32[]{:S(2)}) collective-permute-start(bf16[96,256]{1,0:T(8,128)(2,1)S(1)} %get-tuple-element.32), channel_id=1, source_target_pairs={{0,12},{4,24},{8,20},{12,0},{16,28},{20,8},{24,4},{28,16},{1,13},{... | collective-permute-start | bytes 147464 | tf_op jit(solution)/shard_map/ppermute | solution.py:45
  15.2 5.6 %collective-permute-start.5 = (bf16[64,256]{1,0:T(8,128)(2,1)S(1)}, bf16[64,256]{1,0:T(8,128)(2,1)S(1)}, u32[]{:S(2)}, u32[]{:S(2)}) collective-permute-start(bf16[64,256]{1,0:T(8,128)(2,1)S(1)} %get-tuple-element.33), channel_id=1, source_target_pairs={{0,20},{4,16},{8,28},{12,24},{16,4},{20,0},{24,12},{28,8},{1,21},{... | collective-permute-start | bytes 98312 | tf_op jit(solution)/shard_map/ppermute | solution.py:45
  17.2 5.9 %collective-permute-start.10 = (bf16[128,128]{1,0:T(8,128)(2,1)S(1)}, bf16[128,128]{1,0:T(8,128)(2,1)S(1)}, u32[]{:S(2)}, u32[]{:S(2)}) collective-permute-start(bf16[128,128]{1,0:T(8,128)(2,1)S(1)} %get-tuple-element.28.att_ref.refs_0_), channel_id=1, source_target_pairs={{0,3},{1,2},{2,1},{3,0},{4,7},{5,6},{6,5},{7,4},{8,11},{9,10},{10,... | collective-permute-start | bytes 98312 | tf_op jit(solution)/shard_map/ppermute | solution.py:52
  19.7 4.8 %collective-permute-start.9 = (bf16[128,128]{1,0:T(8,128)(2,1)S(1)}, bf16[128,128]{1,0:T(8,128)(2,1)S(1)}, u32[]{:S(2)}, u32[]{:S(2)}) collective-permute-start(bf16[128,128]{1,0:T(8,128)(2,1)S(1)} %get-tuple-element.28.att_ref.refs_0_), channel_id=1, source_target_pairs={{0,2},{1,3},{2,0},{3,1},{4,6},{5,7},{6,4},{7,5},{8,10},{9,11},{10,... | collective-permute-start | bytes 98312 | tf_op jit(solution)/shard_map/ppermute | solution.py:52
  20.8 5.1 %collective-permute-start.11 = (bf16[512,256]{1,0:T(8,128)(2,1)S(1)}, bf16[512,256]{1,0:T(8,128)(2,1)S(1)}, u32[]{:S(2)}, u32[]{:S(2)}) collective-permute-start(bf16[512,256]{1,0:T(8,128)(2,1)S(1)} %get-tuple-element.38), channel_id=1, source_target_pairs={{0,4},{4,0},{8,12},{12,8},{16,20},{20,16},{24,28},{28,24},{1,5},{5... | collective-permute-start | bytes 786440 | tf_op jit(solution)/shard_map/ppermute | solution.py:45
  20.9 5.0 %collective-permute-start.12 = (bf16[128,256]{1,0:T(8,128)(2,1)S(1)}, bf16[128,256]{1,0:T(8,128)(2,1)S(1)}, u32[]{:S(2)}, u32[]{:S(2)}) collective-permute-start(bf16[128,256]{1,0:T(8,128)(2,1)S(1)} %get-tuple-element.40), channel_id=1, source_target_pairs={{0,28},{4,8},{8,4},{12,16},{16,12},{20,24},{24,20},{28,0},{1,29},{... | collective-permute-start | bytes 196616 | tf_op jit(solution)/shard_map/ppermute | solution.py:45
  21.6 3.9 %collective-permute-start.8 = (bf16[128,128]{1,0:T(8,128)(2,1)S(1)}, bf16[128,128]{1,0:T(8,128)(2,1)S(1)}, u32[]{:S(2)}, u32[]{:S(2)}) collective-permute-start(bf16[128,128]{1,0:T(8,128)(2,1)S(1)} %get-tuple-element.36), channel_id=1, source_target_pairs={{0,1},{1,0},{2,3},{3,2},{4,5},{5,4},{6,7},{7,6},{8,9},{9,8},{10,11... | collective-permute-start | bytes 98312 | tf_op jit(solution)/shard_map/ppermute | solution.py:52

commit v8 on v7

--- a/solution.py
+++ b/solution.py
@@ -8,6 +8,7 @@
 HD = 128
 BLK = 128
 STRIDE_ROWS = 32
+MARGIN = 16
 PAIR = 2 * HD
 SCALE = HD ** (-0.5)
 LOG2E = 1.4426950408889634
@@ -18,7 +19,7 @@
 FULL = pltpu.CompilerParams(vmem_limit_bytes=int(53.3 * 1024 * 1024))
 BF16 = jnp.bfloat16
 PREPARE_COST = 10**10
-ATTEND_COST = 10**9
+ATTEND_COST = 10**10
 COMBINE_COST = 10**10
 GATHER_COST = 10**10
 F32 = jnp.float32
@@ -69,9 +70,9 @@
         b = lax.axis_index("seq")
         sign = 1 - 2 * (b & 1)
         counts = [count_of(picks, j) for j in range(2)]
-        offsets = [(0, 0), (BLK, 1), (2 * BLK, -1), (3 * BLK, 3), (3 * BLK + 32, 2),
-                   (3 * BLK + 64, 4), (3 * BLK + 96, -3), (3 * BLK + 128, -2)]
-        for start, offset in offsets:
+        places = [(0, 0), (BLK, 1), (2 * BLK, -1)]
+        places += [(3 * BLK + i * STRIDE_ROWS, o) for i, o in enumerate((-2, 3, 2, 4, 5))]
+        for start, offset in places:
             owner = (b + 16 + sign * offset) & 7
             count = jnp.where(owner < per_block, counts[0], counts[1])
             inside = (lane >= start) & (lane < start + STRIDE_ROWS)
@@ -127,7 +128,7 @@
         mine_ref, whole_ref, half_ref = slice_refs
         mine_ref[...] = w_ref[:, columns(head)]
         whole_ref[...] = w_ref[:, columns(head ^ (1 + core))]
-        rows = pl.ds(pl.multiple_of(core * half, half), half)
+        rows = pl.ds(pl.multiple_of(core * (half - MARGIN), MARGIN), half + MARGIN)
         half_ref[...] = w_ref[rows, columns(head ^ 3)]
     else:
         for r, ref in enumerate(slice_refs):
@@ -136,7 +137,7 @@
 
 def prepare(ring, index, cotangent, out_weight, heads, columns, after):
     width = out_weight.shape[1] // heads
-    rows = (HD, HD, HD // 2) if ring else (HD,) * heads
+    rows = (HD, HD, HD // 2 + MARGIN) if ring else (HD,) * heads
 
     def body(*refs):
         prepare_kernel(ring, *refs)
@@ -159,34 +160,32 @@
     )(index, cotangent, out_weight, after)
 
 
-def lead_kernel(own_ref, second_ref, first_ref, mult_ref, whole_ref,
-                plus_ref, minus_ref, whole_out):
+def lead_kernel(own_ref, first_ref, mult_ref, whole_ref, near_ref, pair_ref, whole_out):
     del mult_ref
     n = STRIDE_ROWS
-    plus_ref[:n] = own_ref[:n]
-    plus_ref[n:2 * n] = first_ref[:n]
-    plus_ref[2 * n:] = second_ref[:n]
-    minus_ref[:n] = own_ref[:n]
-    minus_ref[n:] = second_ref[:n]
+    near_ref[:BLK] = own_ref[...]
+    near_ref[BLK:] = first_ref[:n]
+    pair_ref[:n] = own_ref[:n]
+    pair_ref[n:] = first_ref[:n]
     whole_out[...] = whole_ref[...]
 
 
-def leads(own, first, second, mult, whole):
+def leads(own, first, mult, whole):
     n = STRIDE_ROWS
     return pl.pallas_call(
         lead_kernel,
-        out_shape=(shape(3 * n, PAIR), shape(2 * n, PAIR), shape(*whole.shape)),
-        in_specs=[VMEM] * 5,
+        out_shape=(shape(BLK + n, PAIR), shape(2 * n, PAIR), shape(*whole.shape)),
+        in_specs=[VMEM] * 4,
         out_specs=(VMEM,) * 3,
         compiler_params=PARAMS,
         name="leads",
-    )(own, second, first, mult, whole)
-
-
-def attend_kernel(sides, mult_ref, q_ref, grad_ref, *refs):
-    block_refs = refs[:3 + sides]
-    att_ref, dq_ref = refs[3 + sides:5 + sides]
-    sum_refs = refs[5 + sides:8 + 2 * sides]
+    )(own, first, mult, whole)
+
+
+def attend_kernel(blocks, mult_ref, q_ref, grad_ref, *refs):
+    block_refs = refs[:blocks]
+    att_ref, dq_ref = refs[blocks:blocks + 2]
+    sum_refs = refs[blocks + 2:2 * blocks + 2]
     keys_ref = refs[-1]
     total_rows = keys_ref.shape[0]
     spans = []
@@ -221,55 +220,57 @@
         ref[:, HD:] = value_terms[start:end].astype(ref.dtype)
 
 
-def attend(mult, q, grad, window, sides):
+def attend(mult, q, grad, blocks, wide):
     def body(*refs):
-        attend_kernel(len(sides), *refs)
+        attend_kernel(len(blocks), *refs)
 
     return pl.pallas_call(
         body,
         out_shape=(shape(BLK, HD), shape(BLK, HD))
-        + (shape(BLK, PAIR, kind=F32),) * 3
-        + tuple(shape(*s.shape) for s in sides),
-        in_specs=[VMEM] * (6 + len(sides)),
-        out_specs=(VMEM,) * (5 + len(sides)),
+        + tuple(shape(*b.shape, kind=F32 if i < wide else BF16) for i, b in enumerate(blocks)),
+        in_specs=[VMEM] * (3 + len(blocks)),
+        out_specs=(VMEM,) * (2 + len(blocks)),
         scratch_shapes=[pltpu.VMEM((mult.shape[1], PAIR), BF16)],
         compiler_params=PARAMS,
         cost_estimate=cost(ATTEND_COST),
         name="attend",
-    )(mult, q, grad, *window, *sides)
-
-
-def combine_kernel(own_ref, first_ref, second_ref, plus_ref, minus_ref, whole_ref, half_ref,
-                   att_ref, own_out, first_out, second_out, att_out):
+    )(mult, q, grad, *blocks)
+
+
+def half_rows():
+    core = lax.axis_index("seq") & 1
+    return pl.ds(pl.multiple_of(core * MARGIN, MARGIN), HD // 2)
+
+
+def combine_kernel(own_ref, first_ref, near_ref, plus_ref, across_ref, whole_ref, half_ref,
+                   own_out, first_out):
+    near = near_ref[...].astype(F32)
     plus = plus_ref[...].astype(F32)
-    minus = minus_ref[...].astype(F32)
+    across = across_ref[...].astype(F32)
     n = STRIDE_ROWS
-    own_out[n:] = own_ref[n:]
-    own_out[:n] = own_ref[:n] + plus[:n] + minus[:n]
-    second_out[n:] = second_ref[n:].astype(BF16)
-    second_out[:n] = (second_ref[:n] + plus[2 * n:] + minus[n:]).astype(BF16)
+    own_out[n:] = own_ref[n:] + near[n:BLK]
+    own_out[:n] = own_ref[:n] + near[:n] + plus[:n] + across[:n]
     first_out[n:BLK] = first_ref[n:].astype(BF16)
-    first_out[:n] = (first_ref[:n] + plus[n:2 * n]).astype(BF16)
-    att_out[...] = att_ref[...]
+    first_out[:n] = (first_ref[:n] + near[BLK:] + plus[n:] + across[n:]).astype(BF16)
     row = BLK
-    for ref in (whole_ref, half_ref):
+    for ref, rows in ((whole_ref, slice(0, HD)), (half_ref, half_rows())):
         for c in range(0, ref.shape[1], PAIR):
-            first_out[row:row + ref.shape[0]] = ref[:, c:c + PAIR]
-            row += ref.shape[0]
-
-
-def combine(own, first, second, plus, minus, whole, half, att):
-    extra = (whole.size + half.size) // PAIR
+            piece = ref[rows, c:c + PAIR]
+            first_out[row:row + piece.shape[0]] = piece
+            row += piece.shape[0]
+
+
+def combine(own, first, near, plus, across, whole, half):
+    extra = (HD + HD // 2) * whole.shape[1] // PAIR
     return pl.pallas_call(
         combine_kernel,
-        out_shape=(shape(BLK, PAIR, kind=F32), shape(BLK + extra, PAIR), shape(BLK, PAIR),
-                   shape(BLK, HD)),
-        in_specs=[VMEM] * 8,
-        out_specs=(VMEM,) * 4,
+        out_shape=(shape(BLK, PAIR, kind=F32), shape(BLK + extra, PAIR)),
+        in_specs=[VMEM] * 7,
+        out_specs=(VMEM,) * 2,
         compiler_params=PARAMS,
         cost_estimate=cost(COMBINE_COST),
         name="combine",
-    )(own, first, second, plus, minus, whole, half, att)
+    )(own, first, near, plus, across, whole, half)
 
 
 def gather_kernel(*refs):
@@ -296,9 +297,8 @@
 
 
 def finish_ring_kernel(*refs):
-    att_ref, near_ref, far_ref, mine_ref, whole_ref, half_ref = refs[:6]
-    first_ref, own_ref, second_ref, dq_ref = refs[6:10]
-    mixed_hbm, dq_hbm, dk_hbm, dv_hbm, mixed_ref, dk_ref, dv_ref, sems = refs[10:]
+    att_ref, mine_ref, whole_ref, half_ref, first_ref, own_ref, dq_ref = refs[:7]
+    mixed_hbm, dq_hbm, dk_hbm, dv_hbm, mixed_ref, dk_ref, dv_ref, sems = refs[7:]
     copies = []
 
     def send(src, dst):
@@ -307,11 +307,11 @@
         copies.append(copy)
 
     send(dq_ref, dq_hbm)
-    total = own_ref[...] + first_ref[:BLK].astype(F32) + second_ref[...].astype(F32)
+    total = own_ref[...] + first_ref[:BLK].astype(F32)
     settle(total, total[:STRIDE_ROWS], dk_ref, dv_ref)
     send(dk_ref, dk_hbm)
     send(dv_ref, dv_hbm)
-    att = [att_ref[...], near_ref[...], far_ref[:, :HD], far_ref[:, HD:]]
+    att = [att_ref[:, r * HD:(r + 1) * HD] for r in range(4)]
     core = lax.axis_index("seq") & 1
     half = HD // 2
     here = jnp.where(core == 0, att[1], att[2])
@@ -325,7 +325,7 @@
         other_whole = first_ref[whole_row + i * HD:whole_row + (i + 1) * HD]
         other_half = first_ref[half_row + i * half:half_row + (i + 1) * half]
         mixed = dot_nn(att[0], mine_ref[:, span]) + dot_nn(here, whole_ref[:, span])
-        mixed = mixed + dot_nn(there, other_whole) + dot_nn(here_half, half_ref[:, span])
+        mixed = mixed + dot_nn(there, other_whole) + dot_nn(here_half, half_ref[half_rows(), span])
         mixed = mixed + dot_nn(there_half, other_half)
         mixed_ref[:, span] = mixed.astype(mixed_ref.dtype)
         send(mixed_ref.at[:, pl.ds(c, PAIR)], mixed_hbm.at[:, pl.ds(c, PAIR)])
@@ -333,12 +333,12 @@
         copy.wait()
 
 
-def finish_ring(attentions, mine, whole, half, first, own, second, dq):
+def finish_ring(attentions, mine, whole, half, first, own, dq):
     width = mine.shape[1]
     return pl.pallas_call(
         finish_ring_kernel,
         out_shape=(shape(BLK, width),) + (shape(BLK, HD),) * 3,
-        in_specs=[VMEM] * 10,
+        in_specs=[VMEM] * 7,
         out_specs=(HBM,) * 4,
         scratch_shapes=[
             pltpu.VMEM((BLK, width), BF16),
@@ -348,7 +348,7 @@
         ],
         compiler_params=PARAMS,
         name="finish",
-    )(*attentions, mine, whole, half, first, own, second, dq)
+    )(attentions, mine, whole, half, first, own, dq)
 
 
 def finish_kernel(count, *refs):
@@ -400,7 +400,6 @@
     side_rows = seq * n
     columns = 3 * BLK + side_rows
     own = jnp.concatenate([key_rows, value_rows], axis=1)
-    second = trade(own, -1)
     first = trade(own, 1)
     grad, mult, *slices = prepare(
         ring, strided_index, cotangent, out_weight, heads, columns, own
@@ -408,32 +407,33 @@
     if ring:
         mine, whole, half = slices
         half = swap(half, 3)
-        plus, minus, whole = leads(own, first, second, mult, whole)
+        near, pair, whole = leads(own, first, mult, whole)
         whole = spread_slice(whole)
-        att, dq, own_sum, first_sum, second_sum, to_plus, to_minus = attend(
-            mult, queries, grad, (own, first, second), (trade(plus, 3), trade(minus, -3))
+        near = trade(near, -1)
+        blocks = (own, first, near, trade(pair, 3), trade(pair, 4))
+        att, dq, own_sum, first_sum, to_near, to_plus, to_across = attend(
+            mult, queries, grad, blocks, 2
         )
-        far = gather([swap(att, 2), swap(att, 3)])
-        own_sum, to_first, to_second, last = combine(
-            own_sum, first_sum, second_sum, trade(to_plus, 3), trade(to_minus, -3), whole, half,
-            att,
+        attentions = gather([att] + [swap(att, r) for r in range(1, heads)])
+        own_sum, to_first = combine(
+            own_sum, first_sum, trade(to_near, -1), trade(to_plus, 3), trade(to_across, 4),
+            whole, half,
         )
         mixed, dq, dk, dv = finish_ring(
-            [att, swap(last, 1), far], mine, whole, half, trade(to_first, 1), own_sum,
-            trade(to_second, -1), dq,
+            attentions, mine, whole, half, trade(to_first, 1), own_sum, dq
         )
     else:
+        second = trade(own, -1)
         slices = [slices[0]] + [swap(slices[r], r) for r in range(1, heads)]
         spread = jnp.broadcast_to(own[None, :n], (seq, n, PAIR))
         side = lax.all_to_all(spread, "seq", 0, 0).reshape(side_rows, PAIR)
-        att, dq, own_sum, first_sum, second_sum, to_side = attend(
-            mult, queries, grad, (own, first, second), (side,)
+        att, dq, own_sum, to_first, to_second, to_side = attend(
+            mult, queries, grad, (own, first, second, side), 1
         )
         from_side = lax.all_to_all(to_side.reshape(seq, n, PAIR), "seq", 0, 0)
         mixed, dk, dv = finish(
             [att] + [swap(att, r) for r in range(1, heads)], slices, own_sum,
-            trade(first_sum.astype(BF16), 1), trade(second_sum.astype(BF16), -1),
-            from_side.reshape(side_rows, PAIR),
+            trade(to_first, 1), trade(to_second, -1), from_side.reshape(side_rows, PAIR),
         )
     return (mixed, dq, dk, dv)
 

time: 27.1 us -> 27.9 us (1.030)
  starting transfers between devices: 18.4 us -> 19 us
    ppermute x4, starting transfers between devices: 8.43 us -> 10.4 us  [swap(): return lax.ppermute(array, 'head', [(i, i ^ mask) for i in range(count)])]
    ppermute x8, starting transfers between devices: 10 us -> 8.51 us  [trade(): lax.ppermute(array, 'seq', [(i, (i + (step if i % 2 == 0 else -step)) % c...]
    ppermute x4, waiting for transfers between devices: 2.55 us -> 3.16 us  [swap(): return lax.ppermute(array, 'head', [(i, i ^ mask) for i in range(count)])]
    ppermute x8, waiting for transfers between devices: 0.43 us -> 0.02 us  [trade(): lax.ppermute(array, 'seq', [(i, (i + (step if i % 2 == 0 else -step)) % c...]
  transfers between devices with their start and end apart: 13 -> 13, of which waited for: 5 -> 2; matrix products, arithmetic and copies ran while one was open for 0% -> 0% of each run, Pallas kernels for 11% -> 10%
where the time goes in v8:
time: 27.9 us; the launch traced here: 27.7 us
  starting transfers between devices  19 us (68%)
  Pallas kernels  3.93 us (14%)
  waiting for transfers between devices  3.18 us (11%)
  local copies, waits for them, and re-layouts  0.91 us (3%)
  between operations  0.74 us (3%)
    ppermute x4, starting transfers between devices, swap(): return lax.ppermute(array, 'head', [(i, i ^ mask) for i in range(count)])  10.4 us
    ppermute x8, starting transfers between devices, trade(): lax.ppermute(array, 'seq', [(i, (i + (step if i % 2 == 0 else -step)) % c...  8.51 us
    ppermute x4, waiting for transfers between devices, swap(): return lax.ppermute(array, 'head', [(i, i ^ mask) for i in range(count)])  3.16 us
    pallas_call x1, Pallas kernels, prepare(): pl.pallas_call(body, out_shape=(shape(BLK, HD), shape(8, columns, kind=F3...  1.8 us
    pallas_call x1, Pallas kernels, finish_ring(): pl.pallas_call(finish_ring_kernel, out_shape=(shape(BLK, width),) + (shap...  1.02 us
    pallas_call x1, Pallas kernels, attend(): pl.pallas_call(body, out_shape=(shape(BLK, HD), shape(BLK, HD)) + tuple((...  1.02 us
    unnamed x7, local copies, waits for them, and re-layouts  0.89 us
  transfers between devices with their start and end apart: 13, of which 2 were waited for; matrix products, arithmetic and copies ran while one was open for 0% of the time, Pallas kernels for 10%

profile of v8, /device:TPU:0, one launch (start us, length us, event | category | flops | bytes accessed | tf_op | source)
XLA Modules:
  0.0 27.7 jit_solution(6762552534921817112)
XLA Ops:
  0.6 0.8 %constant_dynamic-update-slice_fusion.1 = bf16[128,256]{1,0:T(8,128)(2,1)S(1)} fusion(bf16[128,128]{1,0:T(8,128)(2,1)} %param.7), kind=kLoop, calls=%fused_computation.1 | loop fusion | bytes 65536
  1.4 0.0 copy-start.1
  1.4 0.5 %collective-permute-start = (bf16[128,256]{1,0:T(8,128)(2,1)S(1)}, bf16[128,256]{1,0:T(8,128)(2,1)S(1)}, u32[]{:S(2)}, u32[]{:S(2)}) collective-permute-start(bf16[128,256]{1,0:T(8,128)(2,1)S(1)} %constant_dynamic-update-slice_fusion.refs_3_.own_ref), channel_id=1, source_target_pairs={{0,4},{4,0},{8,12},{12,8},{16,20},{20,16},{24,28},{28,24},{1,5},{5... | collective-permute-start | bytes 196616 | tf_op jit(solution)/shard_map/ppermute | solution.py:46
  2.0 0.1 copy-done.1
  2.1 1.8 %prepare.1 = (bf16[128,128]{1,0:T(8,128)(2,1)S(1)}, f32[8,640]{1,0:T(8,128)S(1)}, bf16[128,512]{1,0:T(8,128)(2,1)S(1)}, bf16[128,512]{1,0:T(8,128)(2,1)S(1)}, bf16[80,512]{1,0:T(8,128)(2,1)S(1)}) custom-call(s32[1,8]{1,0:T(1,128)S(1)} %copy-done.1, bf16[128,2048]{1,0:T(8,128)(2,1)} %refs_1_.2, bf16[128,2048]{1,0:T(8,128)(2,1)} %refs_2_.1, ...), custom_call_target="tpu_custom_call" | custom-call | flops 10000000000 | tf_op jit(solution)/shard_map/prepare/pallas_call | solution.py:145
  3.9 0.0 collective-permute-done.first_ref.refs_4_
  3.9 0.0 copy-start
  3.9 3.5 %collective-permute-start.1 = (bf16[160,256]{1,0:T(8,128)(2,1)S(1)}, bf16[160,256]{1,0:T(8,128)(2,1)S(1)}, u32[]{:S(2)}, u32[]{:S(2)}) collective-permute-start(bf16[160,256]{1,0:T(8,128)(2,1)S(1)} %get-tuple-element.24), channel_id=1, source_target_pairs={{0,28},{4,8},{8,4},{12,16},{16,12},{20,24},{24,20},{28,0},{1,29},{... | collective-permute-start | bytes 245768 | tf_op jit(solution)/shard_map/ppermute | solution.py:46
  7.5 0.7 %collective-permute-start.2 = (bf16[64,256]{1,0:T(8,128)(2,1)S(1)}, bf16[64,256]{1,0:T(8,128)(2,1)S(1)}, u32[]{:S(2)}, u32[]{:S(2)}) collective-permute-start(bf16[64,256]{1,0:T(8,128)(2,1)S(1)} %get-tuple-element.25), channel_id=1, source_target_pairs={{0,12},{4,24},{8,20},{12,0},{16,28},{20,8},{24,4},{28,16},{1,13},{... | collective-permute-start | bytes 98312 | tf_op jit(solution)/shard_map/ppermute | solution.py:46
  8.2 0.0 collective-permute-start.3
  8.2 4.1 %collective-permute-start.8 = (bf16[80,512]{1,0:T(8,128)(2,1)S(1)}, bf16[80,512]{1,0:T(8,128)(2,1)S(1)}, u32[]{:S(2)}, u32[]{:S(2)}) collective-permute-start(bf16[80,512]{1,0:T(8,128)(2,1)S(1)} %get-tuple-element.29), channel_id=1, source_target_pairs={{0,3},{1,2},{2,1},{3,0},{4,7},{5,6},{6,5},{7,4},{8,11},{9,10},{10,... | collective-permute-start | bytes 245768 | tf_op jit(solution)/shard_map/ppermute | solution.py:53
  12.3 0.0 collective-permute-start.7
  12.3 0.0 collective-permute-done.2.refs_6_
  12.3 0.0 collective-permute-done.3.refs_7_
  12.3 0.0 collective-permute-done.1.refs_5_
  12.3 1.0 %attend.1 = (bf16[128,128]{1,0:T(8,128)(2,1)S(1)}, bf16[128,128]{1,0:T(8,128)(2,1)S(1)}, f32[128,256]{1,0:T(8,128)S(1)}, f32[128,256]{1,0:T(8,128)S(1)}, bf16[16...) custom-call(f32[8,640]{1,0:T(8,128)S(1)} %get-tuple-element.21.mult_ref.refs_0_, ...), custom_call_target="tpu_custom_call" | custom-call | flops 10000000000 | tf_op jit(solution)/shard_map/attend/pallas_call | solution.py:227
  13.3 1.5 %collective-permute-start.9 = (bf16[160,256]{1,0:T(8,128)(2,1)S(1)}, bf16[160,256]{1,0:T(8,128)(2,1)S(1)}, u32[]{:S(2)}, u32[]{:S(2)}) collective-permute-start(bf16[160,256]{1,0:T(8,128)(2,1)S(1)} %get-tuple-element.32), channel_id=1, source_target_pairs={{0,28},{4,8},{8,4},{12,16},{16,12},{20,24},{24,20},{28,0},{1,29},{... | collective-permute-start | bytes 245768 | tf_op jit(solution)/shard_map/ppermute | solution.py:46
  14.8 1.3 %collective-permute-start.10 = (bf16[64,256]{1,0:T(8,128)(2,1)S(1)}, bf16[64,256]{1,0:T(8,128)(2,1)S(1)}, u32[]{:S(2)}, u32[]{:S(2)}) collective-permute-start(bf16[64,256]{1,0:T(8,128)(2,1)S(1)} %get-tuple-element.33), channel_id=1, source_target_pairs={{0,12},{4,24},{8,20},{12,0},{16,28},{20,8},{24,4},{28,16},{1,13},{... | collective-permute-start | bytes 98312 | tf_op jit(solution)/shard_map/ppermute | solution.py:46
  16.1 0.5 %collective-permute-start.11 = (bf16[64,256]{1,0:T(8,128)(2,1)S(1)}, bf16[64,256]{1,0:T(8,128)(2,1)S(1)}, u32[]{:S(2)}, u32[]{:S(2)}) collective-permute-start(bf16[64,256]{1,0:T(8,128)(2,1)S(1)} %get-tuple-element.34), channel_id=1, source_target_pairs={{0,16},{4,20},{8,24},{12,28},{16,0},{20,4},{24,8},{28,12},{1,17},{... | collective-permute-start | bytes 98312 | tf_op jit(solution)/shard_map/ppermute | solution.py:46
  16.6 0.0 collective-permute-done.8.half_ref.refs_3_
  16.6 2.0 %collective-permute-start.4 = (bf16[128,128]{1,0:T(8,128)(2,1)S(1)}, bf16[128,128]{1,0:T(8,128)(2,1)S(1)}, u32[]{:S(2)}, u32[]{:S(2)}) collective-permute-start(bf16[128,128]{1,0:T(8,128)(2,1)S(1)} %get-tuple-element.26.refs_0_), channel_id=1, source_target_pairs={{0,1},{1,0},{2,3},{3,2},{4,5},{5,4},{6,7},{7,6},{8,9},{9,8},{10,11... | collective-permute-start | bytes 98312 | tf_op jit(solution)/shard_map/ppermute | solution.py:53
  18.6 0.0 collective-permute-done.10.plus_ref
  18.6 2.2 %collective-permute-start.5 = (bf16[128,128]{1,0:T(8,128)(2,1)S(1)}, bf16[128,128]{1,0:T(8,128)(2,1)S(1)}, u32[]{:S(2)}, u32[]{:S(2)}) collective-permute-start(bf16[128,128]{1,0:T(8,128)(2,1)S(1)} %get-tuple-element.26.refs_0_), channel_id=1, source_target_pairs={{0,2},{1,3},{2,0},{3,1},{4,6},{5,7},{6,4},{7,5},{8,10},{9,11},{10,... | collective-permute-start | bytes 98312 | tf_op jit(solution)/shard_map/ppermute | solution.py:53
  20.8 0.0 collective-permute-done.11.across_ref
  20.8 2.1 %collective-permute-start.6 = (bf16[128,128]{1,0:T(8,128)(2,1)S(1)}, bf16[128,128]{1,0:T(8,128)(2,1)S(1)}, u32[]{:S(2)}, u32[]{:S(2)}) collective-permute-start(bf16[128,128]{1,0:T(8,128)(2,1)S(1)} %get-tuple-element.26.refs_0_), channel_id=1, source_target_pairs={{0,3},{1,2},{2,1},{3,0},{4,7},{5,6},{6,5},{7,4},{8,11},{9,10},{10,... | collective-permute-start | bytes 98312 | tf_op jit(solution)/shard_map/ppermute | solution.py:53
  22.9 0.0 collective-permute-done.7.whole_ref.refs_2_
  22.9 0.0 collective-permute-done.9.near_ref
  23.0 0.5 %collective-permute-start.12 = (bf16[512,256]{1,0:T(8,128)(2,1)S(1)}, bf16[512,256]{1,0:T(8,128)(2,1)S(1)}, u32[]{:S(2)}, u32[]{:S(2)}) collective-permute-start(bf16[512,256]{1,0:T(8,128)(2,1)S(1)} %get-tuple-element.35), channel_id=1, source_target_pairs={{0,4},{4,0},{8,12},{12,8},{16,20},{20,16},{24,28},{28,24},{1,5},{5... | collective-permute-start | bytes 786440 | tf_op jit(solution)/shard_map/ppermute | solution.py:46
  23.5 0.0 collective-permute-done.4.refs_1_
  23.5 0.3 collective-permute-done.5.refs_2_
  23.8 2.9 %collective-permute-done.6.refs_3_ = bf16[128,128]{1,0:T(8,128)(2,1)S(1)} collective-permute-done((bf16[128,128]{1,0:T(8,128)(2,1)S(1)}, bf16[128,128]{1,0:T(8,128)(2,1)S(1)}, u32[]{:S(2)}, u32[]{:S(2)}) %collective-permute-start.6) | collective-permute-done | bytes 32800 | tf_op jit(solution)/shard_map/ppermute | solution.py:53
  26.7 1.0 %finish.1 = (bf16[128,512]{1,0:T(8,128)(2,1)}, bf16[128,128]{1,0:T(8,128)(2,1)}, bf16[128,128]{1,0:T(8,128)(2,1)}, bf16[128,128]{1,0:T(8,128)(2,1)}) custom-call(bf16[128,512]{1,0:T(8,128)(2,1)S(1)} %gather.1.refs_0_, bf16[128,512]{1,0:T(8,128)(2,1)S(1)} %get-tuple-element.27.refs_1_, bf16[128,512]{1,0:T(8,128)(2,1)S(1)} %collective-permute-done.7.whole_ref.refs_2_, ...), custom_call_target="tpu_custom_call" | custom-call | tf_op jit(solution)/shard_map/finish/pallas_call | solution.py:338
  (8 shorter events, 0.1 us)
Async XLA Ops:
  0.6 0.8 %copy-start.2 = (bf16[128,128]{1,0:T(8,128)(2,1)S(1)}, bf16[128,128]{1,0:T(8,128)(2,1)}, u32[]{:S(2)}) copy-start(bf16[128,128]{1,0:T(8,128)(2,1)} %param.8) | copy-start | bytes 98308
  1.4 0.7 %copy-start.1 = (s32[1,8]{1,0:T(1,128)S(1)}, s32[1,8]{1,0:T(1,128)}, u32[]{:S(2)}) copy-start(s32[1,8]{1,0:T(1,128)} %refs_0_.1) | copy-start | bytes 100
  1.4 2.4 %collective-permute-start = (bf16[128,256]{1,0:T(8,128)(2,1)S(1)}, bf16[128,256]{1,0:T(8,128)(2,1)S(1)}, u32[]{:S(2)}, u32[]{:S(2)}) collective-permute-start(bf16[128,256]{1,0:T(8,128)(2,1)S(1)} %constant_dynamic-update-slice_fusion.refs_3_.own_ref), channel_id=1, source_target_pairs={{0,4},{4,0},{8,12},{12,8},{16,20},{20,16},{24,28},{28,24},{1,5},{5... | collective-permute-start | bytes 196616 | tf_op jit(solution)/shard_map/ppermute | solution.py:46
  3.9 8.4 %copy-start = (bf16[128,128]{1,0:T(8,128)(2,1)S(1)}, bf16[128,128]{1,0:T(8,128)(2,1)}, u32[]{:S(2)}) copy-start(bf16[128,128]{1,0:T(8,128)(2,1)} %refs_1_.3) | copy-start | bytes 98308
  3.9 8.3 %collective-permute-start.1 = (bf16[160,256]{1,0:T(8,128)(2,1)S(1)}, bf16[160,256]{1,0:T(8,128)(2,1)S(1)}, u32[]{:S(2)}, u32[]{:S(2)}) collective-permute-start(bf16[160,256]{1,0:T(8,128)(2,1)S(1)} %get-tuple-element.24), channel_id=1, source_target_pairs={{0,28},{4,8},{8,4},{12,16},{16,12},{20,24},{24,20},{28,0},{1,29},{... | collective-permute-start | bytes 245768 | tf_op jit(solution)/shard_map/ppermute | solution.py:46
  7.5 4.8 %collective-permute-start.2 = (bf16[64,256]{1,0:T(8,128)(2,1)S(1)}, bf16[64,256]{1,0:T(8,128)(2,1)S(1)}, u32[]{:S(2)}, u32[]{:S(2)}) collective-permute-start(bf16[64,256]{1,0:T(8,128)(2,1)S(1)} %get-tuple-element.25), channel_id=1, source_target_pairs={{0,12},{4,24},{8,20},{12,0},{16,28},{20,8},{24,4},{28,16},{1,13},{... | collective-permute-start | bytes 98312 | tf_op jit(solution)/shard_map/ppermute | solution.py:46
  8.2 4.1 %collective-permute-start.3 = (bf16[64,256]{1,0:T(8,128)(2,1)S(1)}, bf16[64,256]{1,0:T(8,128)(2,1)S(1)}, u32[]{:S(2)}, u32[]{:S(2)}) collective-permute-start(bf16[64,256]{1,0:T(8,128)(2,1)S(1)} %get-tuple-element.25), channel_id=1, source_target_pairs={{0,16},{4,20},{8,24},{12,28},{16,0},{20,4},{24,8},{28,12},{1,17},{... | collective-permute-start | bytes 98312 | tf_op jit(solution)/shard_map/ppermute | solution.py:46
  8.2 8.4 %collective-permute-start.8 = (bf16[80,512]{1,0:T(8,128)(2,1)S(1)}, bf16[80,512]{1,0:T(8,128)(2,1)S(1)}, u32[]{:S(2)}, u32[]{:S(2)}) collective-permute-start(bf16[80,512]{1,0:T(8,128)(2,1)S(1)} %get-tuple-element.29), channel_id=1, source_target_pairs={{0,3},{1,2},{2,1},{3,0},{4,7},{5,6},{6,5},{7,4},{8,11},{9,10},{10,... | collective-permute-start | bytes 245768 | tf_op jit(solution)/shard_map/ppermute | solution.py:53
  12.3 10.7 %collective-permute-start.7 = (bf16[128,512]{1,0:T(8,128)(2,1)S(1)}, bf16[128,512]{1,0:T(8,128)(2,1)S(1)}, u32[]{:S(2)}, u32[]{:S(2)}) collective-permute-start(bf16[128,512]{1,0:T(8,128)(2,1)S(1)} %get-tuple-element.28), channel_id=1, source_target_pairs={{0,1},{1,0},{2,3},{3,2},{4,6},{5,7},{6,4},{7,5},{8,9},{9,8},{10,11... | collective-permute-start | bytes 393224 | tf_op jit(solution)/shard_map/ppermute | solution.py:392
  13.3 9.6 %collective-permute-start.9 = (bf16[160,256]{1,0:T(8,128)(2,1)S(1)}, bf16[160,256]{1,0:T(8,128)(2,1)S(1)}, u32[]{:S(2)}, u32[]{:S(2)}) collective-permute-start(bf16[160,256]{1,0:T(8,128)(2,1)S(1)} %get-tuple-element.32), channel_id=1, source_target_pairs={{0,28},{4,8},{8,4},{12,16},{16,12},{20,24},{24,20},{28,0},{1,29},{... | collective-permute-start | bytes 245768 | tf_op jit(solution)/shard_map/ppermute | solution.py:46
  14.8 3.8 %collective-permute-start.10 = (bf16[64,256]{1,0:T(8,128)(2,1)S(1)}, bf16[64,256]{1,0:T(8,128)(2,1)S(1)}, u32[]{:S(2)}, u32[]{:S(2)}) collective-permute-start(bf16[64,256]{1,0:T(8,128)(2,1)S(1)} %get-tuple-element.33), channel_id=1, source_target_pairs={{0,12},{4,24},{8,20},{12,0},{16,28},{20,8},{24,4},{28,16},{1,13},{... | collective-permute-start | bytes 98312 | tf_op jit(solution)/shard_map/ppermute | solution.py:46
  16.1 4.7 %collective-permute-start.11 = (bf16[64,256]{1,0:T(8,128)(2,1)S(1)}, bf16[64,256]{1,0:T(8,128)(2,1)S(1)}, u32[]{:S(2)}, u32[]{:S(2)}) collective-permute-start(bf16[64,256]{1,0:T(8,128)(2,1)S(1)} %get-tuple-element.34), channel_id=1, source_target_pairs={{0,16},{4,20},{8,24},{12,28},{16,0},{20,4},{24,8},{28,12},{1,17},{... | collective-permute-start | bytes 98312 | tf_op jit(solution)/shard_map/ppermute | solution.py:46
  16.6 6.9 %collective-permute-start.4 = (bf16[128,128]{1,0:T(8,128)(2,1)S(1)}, bf16[128,128]{1,0:T(8,128)(2,1)S(1)}, u32[]{:S(2)}, u32[]{:S(2)}) collective-permute-start(bf16[128,128]{1,0:T(8,128)(2,1)S(1)} %get-tuple-element.26.refs_0_), channel_id=1, source_target_pairs={{0,1},{1,0},{2,3},{3,2},{4,5},{5,4},{6,7},{7,6},{8,9},{9,8},{10,11... | collective-permute-start | bytes 98312 | tf_op jit(solution)/shard_map/ppermute | solution.py:53
  18.6 5.1 %collective-permute-start.5 = (bf16[128,128]{1,0:T(8,128)(2,1)S(1)}, bf16[128,128]{1,0:T(8,128)(2,1)S(1)}, u32[]{:S(2)}, u32[]{:S(2)}) collective-permute-start(bf16[128,128]{1,0:T(8,128)(2,1)S(1)} %get-tuple-element.26.refs_0_), channel_id=1, source_target_pairs={{0,2},{1,3},{2,0},{3,1},{4,6},{5,7},{6,4},{7,5},{8,10},{9,11},{10,... | collective-permute-start | bytes 98312 | tf_op jit(solution)/shard_map/ppermute | solution.py:53
  20.8 5.8 %collective-permute-start.6 = (bf16[128,128]{1,0:T(8,128)(2,1)S(1)}, bf16[128,128]{1,0:T(8,128)(2,1)S(1)}, u32[]{:S(2)}, u32[]{:S(2)}) collective-permute-start(bf16[128,128]{1,0:T(8,128)(2,1)S(1)} %get-tuple-element.26.refs_0_), channel_id=1, source_target_pairs={{0,3},{1,2},{2,1},{3,0},{4,7},{5,6},{6,5},{7,4},{8,11},{9,10},{10,... | collective-permute-start | bytes 98312 | tf_op jit(solution)/shard_map/ppermute | solution.py:53
  23.0 3.7 %collective-permute-start.12 = (bf16[512,256]{1,0:T(8,128)(2,1)S(1)}, bf16[512,256]{1,0:T(8,128)(2,1)S(1)}, u32[]{:S(2)}, u32[]{:S(2)}) collective-permute-start(bf16[512,256]{1,0:T(8,128)(2,1)S(1)} %get-tuple-element.35), channel_id=1, source_target_pairs={{0,4},{4,0},{8,12},{12,8},{16,20},{20,16},{24,28},{28,24},{1,5},{5... | collective-permute-start | bytes 786440 | tf_op jit(solution)/shard_map/ppermute | solution.py:46

commit v9 on v8

--- a/solution.py
+++ b/solution.py
@@ -21,7 +21,6 @@
 PREPARE_COST = 10**10
 ATTEND_COST = 10**10
 COMBINE_COST = 10**10
-GATHER_COST = 10**10
 F32 = jnp.float32
 
 
@@ -207,7 +206,9 @@
     terms = jnp.exp2((scores - top) * (SCALE * LOG2E)) * mult
     probability = terms * (1.0 / jnp.sum(terms, axis=1, keepdims=True))
     weights = probability.astype(BF16)
-    att_ref[...] = dot_nn(weights, values).astype(BF16)
+    att = dot_nn(weights, values).astype(BF16)
+    for r in range(0, att_ref.shape[0], BLK):
+        att_ref[r:r + BLK] = att
 
     grad_weights = dot_nt(grad, values)
     delta = jnp.sum(probability * grad_weights, axis=1, keepdims=True)
@@ -220,13 +221,13 @@
         ref[:, HD:] = value_terms[start:end].astype(ref.dtype)
 
 
-def attend(mult, q, grad, blocks, wide):
+def attend(mult, q, grad, blocks, wide, copies):
     def body(*refs):
         attend_kernel(len(blocks), *refs)
 
     return pl.pallas_call(
         body,
-        out_shape=(shape(BLK, HD), shape(BLK, HD))
+        out_shape=(shape(copies * BLK, HD), shape(BLK, HD))
         + tuple(shape(*b.shape, kind=F32 if i < wide else BF16) for i, b in enumerate(blocks)),
         in_specs=[VMEM] * (3 + len(blocks)),
         out_specs=(VMEM,) * (2 + len(blocks)),
@@ -273,23 +274,6 @@
     )(own, first, near, plus, across, whole, half)
 
 
-def gather_kernel(*refs):
-    for r, ref in enumerate(refs[:-1]):
-        refs[-1][:, r * HD:(r + 1) * HD] = ref[...]
-
-
-def gather(attentions):
-    return pl.pallas_call(
-        gather_kernel,
-        out_shape=shape(BLK, len(attentions) * HD),
-        in_specs=[VMEM] * len(attentions),
-        out_specs=VMEM,
-        compiler_params=PARAMS,
-        cost_estimate=cost(GATHER_COST),
-        name="gather",
-    )(*attentions)
-
-
 def settle(total, lead, dk_ref, dv_ref):
     for ref, c in ((dk_ref, 0), (dv_ref, HD)):
         ref[:STRIDE_ROWS] = lead[:, c:c + HD].astype(ref.dtype)
@@ -311,7 +295,8 @@
     settle(total, total[:STRIDE_ROWS], dk_ref, dv_ref)
     send(dk_ref, dk_hbm)
     send(dv_ref, dv_hbm)
-    att = [att_ref[:, r * HD:(r + 1) * HD] for r in range(4)]
+    head = lax.axis_index("head")
+    att = [att_ref[head ^ r] for r in range(4)]
     core = lax.axis_index("seq") & 1
     half = HD // 2
     here = jnp.where(core == 0, att[1], att[2])
@@ -412,9 +397,9 @@
         near = trade(near, -1)
         blocks = (own, first, near, trade(pair, 3), trade(pair, 4))
         att, dq, own_sum, first_sum, to_near, to_plus, to_across = attend(
-            mult, queries, grad, blocks, 2
+            mult, queries, grad, blocks, 2, heads
         )
-        attentions = gather([att] + [swap(att, r) for r in range(1, heads)])
+        attentions = lax.all_to_all(att.reshape(heads, BLK, HD), "head", 0, 0)
         own_sum, to_first = combine(
             own_sum, first_sum, trade(to_near, -1), trade(to_plus, 3), trade(to_across, 4),
             whole, half,
@@ -428,7 +413,7 @@
         spread = jnp.broadcast_to(own[None, :n], (seq, n, PAIR))
         side = lax.all_to_all(spread, "seq", 0, 0).reshape(side_rows, PAIR)
         att, dq, own_sum, to_first, to_second, to_side = attend(
-            mult, queries, grad, (own, first, second, side), 1
+            mult, queries, grad, (own, first, second, side), 1, 1
         )
         from_side = lax.all_to_all(to_side.reshape(seq, n, PAIR), "seq", 0, 0)
         mixed, dk, dv = finish(

time: 27.9 us -> 31.7 us (1.14)
  blocking collectives: 0 us -> 10.5 us
  starting transfers between devices: 19 us -> 11.9 us
  waiting for transfers between devices: 3.18 us -> 3.5 us
    all_to_all x0 -> x1, blocking collectives: none -> 10.5 us  [shards(): attentions = lax.all_to_all(att.reshape(heads, BLK, HD), 'head', 0, 0)]
    ppermute x4 -> x1, starting transfers between devices: 10.4 us -> 3.83 us  [swap(): return lax.ppermute(array, 'head', [(i, i ^ mask) for i in range(count)])]
    ppermute x8, waiting for transfers between devices: 0.02 us -> 3.5 us  [trade(): lax.ppermute(array, 'seq', [(i, (i + (step if i % 2 == 0 else -step)) % c...]
    ppermute x4 -> x1, waiting for transfers between devices: 3.16 us -> 0.01 us  [swap(): return lax.ppermute(array, 'head', [(i, i ^ mask) for i in range(count)])]
    ppermute x8, starting transfers between devices: 8.51 us -> 8.08 us  [trade(): lax.ppermute(array, 'seq', [(i, (i + (step if i % 2 == 0 else -step)) % c...]
    pallas_call x2 -> x1, Pallas kernels: 1.04 us -> 1.02 us  [attend(): pl.pallas_call(body, out_shape=(shape(copies * BLK, HD), shape(BLK, HD))...]
  transfers between devices with their start and end apart: 13 -> 10, of which waited for: 2 -> 2; matrix products, arithmetic and copies ran while one was open for 0% -> 0% of each run, Pallas kernels for 10% -> 9%
where the time goes in v9:
time: 31.7 us; the launch traced here: 31.4 us
  starting transfers between devices  11.9 us (38%)
  blocking collectives  10.5 us (33%)
  Pallas kernels  3.9 us (12%)
  waiting for transfers between devices  3.5 us (11%)
  local copies, waits for them, and re-layouts  0.91 us (3%)
  between operations  0.74 us (2%)
    all_to_all x1, blocking collectives, shards(): attentions = lax.all_to_all(att.reshape(heads, BLK, HD), 'head', 0, 0)  10.5 us
    ppermute x8, starting transfers between devices, trade(): lax.ppermute(array, 'seq', [(i, (i + (step if i % 2 == 0 else -step)) % c...  8.08 us
    ppermute x1, starting transfers between devices, swap(): return lax.ppermute(array, 'head', [(i, i ^ mask) for i in range(count)])  3.83 us
    ppermute x8, waiting for transfers between devices, trade(): lax.ppermute(array, 'seq', [(i, (i + (step if i % 2 == 0 else -step)) % c...  3.5 us
    pallas_call x1, Pallas kernels, prepare(): pl.pallas_call(body, out_shape=(shape(BLK, HD), shape(8, columns, kind=F3...  1.8 us
    pallas_call x1, Pallas kernels, attend(): pl.pallas_call(body, out_shape=(shape(copies * BLK, HD), shape(BLK, HD))...  1.02 us
    pallas_call x1, Pallas kernels, finish_ring(): pl.pallas_call(finish_ring_kernel, out_shape=(shape(BLK, width),) + (shap...  1.02 us
    unnamed x7, local copies, waits for them, and re-layouts  0.89 us
  transfers between devices with their start and end apart: 10, of which 2 were waited for; matrix products, arithmetic and copies ran while one was open for 0% of the time, Pallas kernels for 9%

profile of v9, /device:TPU:0, one launch (start us, length us, event | category | flops | bytes accessed | tf_op | source)
XLA Modules:
  0.0 31.4 jit_solution(5268501866192127942)
XLA Ops:
  0.6 0.0 copy-start.2
  0.6 0.8 %constant_dynamic-update-slice_fusion.1 = bf16[128,256]{1,0:T(8,128)(2,1)S(1)} fusion(bf16[128,128]{1,0:T(8,128)(2,1)} %param.7), kind=kLoop, calls=%fused_computation.1 | loop fusion | bytes 65536
  1.4 0.0 copy-done.2
  1.4 0.0 copy-start.1
  1.4 0.5 %collective-permute-start = (bf16[128,256]{1,0:T(8,128)(2,1)S(1)}, bf16[128,256]{1,0:T(8,128)(2,1)S(1)}, u32[]{:S(2)}, u32[]{:S(2)}) collective-permute-start(bf16[128,256]{1,0:T(8,128)(2,1)S(1)} %constant_dynamic-update-slice_fusion.refs_3_.own_ref), channel_id=1, source_target_pairs={{0,4},{4,0},{8,12},{12,8},{16,20},{20,16},{24,28},{28,24},{1,5},{5... | collective-permute-start | bytes 196616 | tf_op jit(solution)/shard_map/ppermute | solution.py:45
  2.0 0.1 copy-done.1
  2.1 1.8 %prepare.1 = (bf16[128,128]{1,0:T(8,128)(2,1)S(1)}, f32[8,640]{1,0:T(8,128)S(1)}, bf16[128,512]{1,0:T(8,128)(2,1)S(1)}, bf16[128,512]{1,0:T(8,128)(2,1)S(1)}, bf16[80,512]{1,0:T(8,128)(2,1)S(1)}) custom-call(s32[1,8]{1,0:T(1,128)S(1)} %copy-done.1, bf16[128,2048]{1,0:T(8,128)(2,1)} %refs_1_.2, bf16[128,2048]{1,0:T(8,128)(2,1)} %refs_2_.1, ...), custom_call_target="tpu_custom_call" | custom-call | flops 10000000000 | tf_op jit(solution)/shard_map/prepare/pallas_call | solution.py:144
  3.9 0.0 collective-permute-done.first_ref.refs_4_
  3.9 0.0 copy-start
  3.9 3.5 %collective-permute-start.1 = (bf16[160,256]{1,0:T(8,128)(2,1)S(1)}, bf16[160,256]{1,0:T(8,128)(2,1)S(1)}, u32[]{:S(2)}, u32[]{:S(2)}) collective-permute-start(bf16[160,256]{1,0:T(8,128)(2,1)S(1)} %get-tuple-element.24), channel_id=1, source_target_pairs={{0,28},{4,8},{8,4},{12,16},{16,12},{20,24},{24,20},{28,0},{1,29},{... | collective-permute-start | bytes 245768 | tf_op jit(solution)/shard_map/ppermute | solution.py:45
  7.5 0.5 %collective-permute-start.3 = (bf16[64,256]{1,0:T(8,128)(2,1)S(1)}, bf16[64,256]{1,0:T(8,128)(2,1)S(1)}, u32[]{:S(2)}, u32[]{:S(2)}) collective-permute-start(bf16[64,256]{1,0:T(8,128)(2,1)S(1)} %get-tuple-element.25), channel_id=1, source_target_pairs={{0,16},{4,20},{8,24},{12,28},{16,0},{20,4},{24,8},{28,12},{1,17},{... | collective-permute-start | bytes 98312 | tf_op jit(solution)/shard_map/ppermute | solution.py:45
  8.0 0.2 collective-permute-start.2
  8.2 3.8 %collective-permute-start.5 = (bf16[80,512]{1,0:T(8,128)(2,1)S(1)}, bf16[80,512]{1,0:T(8,128)(2,1)S(1)}, u32[]{:S(2)}, u32[]{:S(2)}) collective-permute-start(bf16[80,512]{1,0:T(8,128)(2,1)S(1)} %get-tuple-element.29), channel_id=1, source_target_pairs={{0,3},{1,2},{2,1},{3,0},{4,7},{5,6},{6,5},{7,4},{8,11},{9,10},{10,... | collective-permute-start | bytes 245768 | tf_op jit(solution)/shard_map/ppermute | solution.py:52
  12.0 0.0 collective-permute-start.4
  12.0 0.0 collective-permute-done.3.refs_7_
  12.0 0.0 collective-permute-done.2.refs_6_
  12.0 0.0 collective-permute-done.1.refs_5_
  12.0 0.0 copy-done
  12.0 1.0 %attend.1 = (bf16[512,128]{1,0:T(8,128)(2,1)S(1)}, bf16[128,128]{1,0:T(8,128)(2,1)S(1)}, f32[128,256]{1,0:T(8,128)S(1)}, f32[128,256]{1,0:T(8,128)S(1)}, bf16[16...) custom-call(f32[8,640]{1,0:T(8,128)S(1)} %get-tuple-element.21.mult_ref.refs_0_, ...), custom_call_target="tpu_custom_call" | custom-call | flops 10000000000 | tf_op jit(solution)/shard_map/attend/pallas_call | solution.py:228
  13.0 2.1 %collective-permute-start.6 = (bf16[160,256]{1,0:T(8,128)(2,1)S(1)}, bf16[160,256]{1,0:T(8,128)(2,1)S(1)}, u32[]{:S(2)}, u32[]{:S(2)}) collective-permute-start(bf16[160,256]{1,0:T(8,128)(2,1)S(1)} %get-tuple-element.32), channel_id=1, source_target_pairs={{0,28},{4,8},{8,4},{12,16},{16,12},{20,24},{24,20},{28,0},{1,29},{... | collective-permute-start | bytes 245768 | tf_op jit(solution)/shard_map/ppermute | solution.py:45
  15.1 0.7 %collective-permute-start.7 = (bf16[64,256]{1,0:T(8,128)(2,1)S(1)}, bf16[64,256]{1,0:T(8,128)(2,1)S(1)}, u32[]{:S(2)}, u32[]{:S(2)}) collective-permute-start(bf16[64,256]{1,0:T(8,128)(2,1)S(1)} %get-tuple-element.33), channel_id=1, source_target_pairs={{0,12},{4,24},{8,20},{12,0},{16,28},{20,8},{24,4},{28,16},{1,13},{... | collective-permute-start | bytes 98312 | tf_op jit(solution)/shard_map/ppermute | solution.py:45
  15.8 0.5 %collective-permute-start.8 = (bf16[64,256]{1,0:T(8,128)(2,1)S(1)}, bf16[64,256]{1,0:T(8,128)(2,1)S(1)}, u32[]{:S(2)}, u32[]{:S(2)}) collective-permute-start(bf16[64,256]{1,0:T(8,128)(2,1)S(1)} %get-tuple-element.34), channel_id=1, source_target_pairs={{0,16},{4,20},{8,24},{12,28},{16,0},{20,4},{24,8},{28,12},{1,17},{... | collective-permute-start | bytes 98312 | tf_op jit(solution)/shard_map/ppermute | solution.py:45
  16.3 0.0 collective-permute-done.5.half_ref.refs_3_
  16.3 2.6 %collective-permute-done.7.plus_ref = bf16[64,256]{1,0:T(8,128)(2,1)S(1)} collective-permute-done((bf16[64,256]{1,0:T(8,128)(2,1)S(1)}, bf16[64,256]{1,0:T(8,128)(2,1)S(1)}, u32[]{:S(2)}, u32[]{:S(2)}) %collective-permute-start.7) | collective-permute-done | bytes 32800 | tf_op jit(solution)/shard_map/ppermute | solution.py:45
  18.9 0.9 %collective-permute-done.8.across_ref = bf16[64,256]{1,0:T(8,128)(2,1)S(1)} collective-permute-done((bf16[64,256]{1,0:T(8,128)(2,1)S(1)}, bf16[64,256]{1,0:T(8,128)(2,1)S(1)}, u32[]{:S(2)}, u32[]{:S(2)}) %collective-permute-start.8) | collective-permute-done | bytes 32800 | tf_op jit(solution)/shard_map/ppermute | solution.py:45
  19.8 0.0 collective-permute-done.4.whole_ref.refs_2_
  19.8 0.0 collective-permute-done.6.near_ref
  19.9 0.1 collective-permute-start.9
  19.9 10.5 %all_to_all.5.refs_0_ = bf16[4,128,128]{2,1,0:T(8,128)(2,1)S(1)} all-to-all(bf16[4,128,128]{2,1,0:T(8,128)(2,1)S(1)} %bitcast.1), channel_id=1, replica_groups=mesh['seq'=8,'head'=4] {'head'}, dimensions={0} | all-to-all | bytes 262144 | tf_op jit(solution)/shard_map/all_to_all | solution.py:402
  30.4 0.0 collective-permute-done.9.refs_4_
  30.4 1.0 %finish.1 = (bf16[128,512]{1,0:T(8,128)(2,1)}, bf16[128,128]{1,0:T(8,128)(2,1)}, bf16[128,128]{1,0:T(8,128)(2,1)}, bf16[128,128]{1,0:T(8,128)(2,1)}) custom-call(bf16[4,128,128]{2,1,0:T(8,128)(2,1)S(1)} %all_to_all.5.refs_0_, bf16[128,512]{1,0:T(8,128)(2,1)S(1)} %get-tuple-element.27.refs_1_, bf16[128,512]{1,0:T(8,128)(2,1)S(1)} %collective-permute-done.4.whole_ref.refs_2_, ...), custom_call_target="tpu_custom_call" | custom-call | tf_op jit(solution)/shard_map/finish/pallas_call | solution.py:323
  (3 shorter events, 0.1 us)
Async XLA Ops:
  0.6 0.8 %copy-start.2 = (bf16[128,128]{1,0:T(8,128)(2,1)S(1)}, bf16[128,128]{1,0:T(8,128)(2,1)}, u32[]{:S(2)}) copy-start(bf16[128,128]{1,0:T(8,128)(2,1)} %param.8) | copy-start | bytes 98308
  1.4 0.7 %copy-start.1 = (s32[1,8]{1,0:T(1,128)S(1)}, s32[1,8]{1,0:T(1,128)}, u32[]{:S(2)}) copy-start(s32[1,8]{1,0:T(1,128)} %refs_0_.1) | copy-start | bytes 100
  1.4 2.4 %collective-permute-start = (bf16[128,256]{1,0:T(8,128)(2,1)S(1)}, bf16[128,256]{1,0:T(8,128)(2,1)S(1)}, u32[]{:S(2)}, u32[]{:S(2)}) collective-permute-start(bf16[128,256]{1,0:T(8,128)(2,1)S(1)} %constant_dynamic-update-slice_fusion.refs_3_.own_ref), channel_id=1, source_target_pairs={{0,4},{4,0},{8,12},{12,8},{16,20},{20,16},{24,28},{28,24},{1,5},{5... | collective-permute-start | bytes 196616 | tf_op jit(solution)/shard_map/ppermute | solution.py:45
  3.9 8.1 %copy-start = (bf16[128,128]{1,0:T(8,128)(2,1)S(1)}, bf16[128,128]{1,0:T(8,128)(2,1)}, u32[]{:S(2)}) copy-start(bf16[128,128]{1,0:T(8,128)(2,1)} %refs_1_.3) | copy-start | bytes 98308
  3.9 8.1 %collective-permute-start.1 = (bf16[160,256]{1,0:T(8,128)(2,1)S(1)}, bf16[160,256]{1,0:T(8,128)(2,1)S(1)}, u32[]{:S(2)}, u32[]{:S(2)}) collective-permute-start(bf16[160,256]{1,0:T(8,128)(2,1)S(1)} %get-tuple-element.24), channel_id=1, source_target_pairs={{0,28},{4,8},{8,4},{12,16},{16,12},{20,24},{24,20},{28,0},{1,29},{... | collective-permute-start | bytes 245768 | tf_op jit(solution)/shard_map/ppermute | solution.py:45
  7.5 4.5 %collective-permute-start.3 = (bf16[64,256]{1,0:T(8,128)(2,1)S(1)}, bf16[64,256]{1,0:T(8,128)(2,1)S(1)}, u32[]{:S(2)}, u32[]{:S(2)}) collective-permute-start(bf16[64,256]{1,0:T(8,128)(2,1)S(1)} %get-tuple-element.25), channel_id=1, source_target_pairs={{0,16},{4,20},{8,24},{12,28},{16,0},{20,4},{24,8},{28,12},{1,17},{... | collective-permute-start | bytes 98312 | tf_op jit(solution)/shard_map/ppermute | solution.py:45
  8.0 4.0 %collective-permute-start.2 = (bf16[64,256]{1,0:T(8,128)(2,1)S(1)}, bf16[64,256]{1,0:T(8,128)(2,1)S(1)}, u32[]{:S(2)}, u32[]{:S(2)}) collective-permute-start(bf16[64,256]{1,0:T(8,128)(2,1)S(1)} %get-tuple-element.25), channel_id=1, source_target_pairs={{0,12},{4,24},{8,20},{12,0},{16,28},{20,8},{24,4},{28,16},{1,13},{... | collective-permute-start | bytes 98312 | tf_op jit(solution)/shard_map/ppermute | solution.py:45
  8.2 8.2 %collective-permute-start.5 = (bf16[80,512]{1,0:T(8,128)(2,1)S(1)}, bf16[80,512]{1,0:T(8,128)(2,1)S(1)}, u32[]{:S(2)}, u32[]{:S(2)}) collective-permute-start(bf16[80,512]{1,0:T(8,128)(2,1)S(1)} %get-tuple-element.29), channel_id=1, source_target_pairs={{0,3},{1,2},{2,1},{3,0},{4,7},{5,6},{6,5},{7,4},{8,11},{9,10},{10,... | collective-permute-start | bytes 245768 | tf_op jit(solution)/shard_map/ppermute | solution.py:52
  12.0 7.8 %collective-permute-start.4 = (bf16[128,512]{1,0:T(8,128)(2,1)S(1)}, bf16[128,512]{1,0:T(8,128)(2,1)S(1)}, u32[]{:S(2)}, u32[]{:S(2)}) collective-permute-start(bf16[128,512]{1,0:T(8,128)(2,1)S(1)} %get-tuple-element.28), channel_id=1, source_target_pairs={{0,1},{1,0},{2,3},{3,2},{4,6},{5,7},{6,4},{7,5},{8,9},{9,8},{10,11... | collective-permute-start | bytes 393224 | tf_op jit(solution)/shard_map/ppermute | solution.py:377
  13.0 6.8 %collective-permute-start.6 = (bf16[160,256]{1,0:T(8,128)(2,1)S(1)}, bf16[160,256]{1,0:T(8,128)(2,1)S(1)}, u32[]{:S(2)}, u32[]{:S(2)}) collective-permute-start(bf16[160,256]{1,0:T(8,128)(2,1)S(1)} %get-tuple-element.32), channel_id=1, source_target_pairs={{0,28},{4,8},{8,4},{12,16},{16,12},{20,24},{24,20},{28,0},{1,29},{... | collective-permute-start | bytes 245768 | tf_op jit(solution)/shard_map/ppermute | solution.py:45
  15.1 3.8 %collective-permute-start.7 = (bf16[64,256]{1,0:T(8,128)(2,1)S(1)}, bf16[64,256]{1,0:T(8,128)(2,1)S(1)}, u32[]{:S(2)}, u32[]{:S(2)}) collective-permute-start(bf16[64,256]{1,0:T(8,128)(2,1)S(1)} %get-tuple-element.33), channel_id=1, source_target_pairs={{0,12},{4,24},{8,20},{12,0},{16,28},{20,8},{24,4},{28,16},{1,13},{... | collective-permute-start | bytes 98312 | tf_op jit(solution)/shard_map/ppermute | solution.py:45
  15.8 4.0 %collective-permute-start.8 = (bf16[64,256]{1,0:T(8,128)(2,1)S(1)}, bf16[64,256]{1,0:T(8,128)(2,1)S(1)}, u32[]{:S(2)}, u32[]{:S(2)}) collective-permute-start(bf16[64,256]{1,0:T(8,128)(2,1)S(1)} %get-tuple-element.34), channel_id=1, source_target_pairs={{0,16},{4,20},{8,24},{12,28},{16,0},{20,4},{24,8},{28,12},{1,17},{... | collective-permute-start | bytes 98312 | tf_op jit(solution)/shard_map/ppermute | solution.py:45
  19.9 10.5 %collective-permute-start.9 = (bf16[512,256]{1,0:T(8,128)(2,1)S(1)}, bf16[512,256]{1,0:T(8,128)(2,1)S(1)}, u32[]{:S(2)}, u32[]{:S(2)}) collective-permute-start(bf16[512,256]{1,0:T(8,128)(2,1)S(1)} %get-tuple-element.35), channel_id=1, source_target_pairs={{0,4},{4,0},{8,12},{12,8},{16,20},{20,16},{24,28},{28,24},{1,5},{5... | collective-permute-start | bytes 786440 | tf_op jit(solution)/shard_map/ppermute | solution.py:45

commit v10 on v8

--- a/solution.py
+++ b/solution.py
@@ -243,7 +243,7 @@
 
 
 def combine_kernel(own_ref, first_ref, near_ref, plus_ref, across_ref, whole_ref, half_ref,
-                   own_out, first_out):
+                   att_ref, own_out, first_out, att_out):
     near = near_ref[...].astype(F32)
     plus = plus_ref[...].astype(F32)
     across = across_ref[...].astype(F32)
@@ -252,6 +252,7 @@
     own_out[:n] = own_ref[:n] + near[:n] + plus[:n] + across[:n]
     first_out[n:BLK] = first_ref[n:].astype(BF16)
     first_out[:n] = (first_ref[:n] + near[BLK:] + plus[n:] + across[n:]).astype(BF16)
+    att_out[...] = att_ref[...]
     row = BLK
     for ref, rows in ((whole_ref, slice(0, HD)), (half_ref, half_rows())):
         for c in range(0, ref.shape[1], PAIR):
@@ -260,17 +261,17 @@
             row += piece.shape[0]
 
 
-def combine(own, first, near, plus, across, whole, half):
+def combine(own, first, near, plus, across, whole, half, att):
     extra = (HD + HD // 2) * whole.shape[1] // PAIR
     return pl.pallas_call(
         combine_kernel,
-        out_shape=(shape(BLK, PAIR, kind=F32), shape(BLK + extra, PAIR)),
-        in_specs=[VMEM] * 7,
-        out_specs=(VMEM,) * 2,
+        out_shape=(shape(BLK, PAIR, kind=F32), shape(BLK + extra, PAIR), shape(BLK, HD)),
+        in_specs=[VMEM] * 8,
+        out_specs=(VMEM,) * 3,
         compiler_params=PARAMS,
         cost_estimate=cost(COMBINE_COST),
         name="combine",
-    )(own, first, near, plus, across, whole, half)
+    )(own, first, near, plus, across, whole, half, att)
 
 
 def gather_kernel(*refs):
@@ -297,8 +298,9 @@
 
 
 def finish_ring_kernel(*refs):
-    att_ref, mine_ref, whole_ref, half_ref, first_ref, own_ref, dq_ref = refs[:7]
-    mixed_hbm, dq_hbm, dk_hbm, dv_hbm, mixed_ref, dk_ref, dv_ref, sems = refs[7:]
+    att_ref, beside_ref, far_ref = refs[:3]
+    mine_ref, whole_ref, half_ref, first_ref, own_ref, dq_ref = refs[3:9]
+    mixed_hbm, dq_hbm, dk_hbm, dv_hbm, mixed_ref, dk_ref, dv_ref, sems = refs[9:]
     copies = []
 
     def send(src, dst):
@@ -311,7 +313,7 @@
     settle(total, total[:STRIDE_ROWS], dk_ref, dv_ref)
     send(dk_ref, dk_hbm)
     send(dv_ref, dv_hbm)
-    att = [att_ref[:, r * HD:(r + 1) * HD] for r in range(4)]
+    att = [att_ref[...], beside_ref[...], far_ref[:, :HD], far_ref[:, HD:]]
     core = lax.axis_index("seq") & 1
     half = HD // 2
     here = jnp.where(core == 0, att[1], att[2])
@@ -338,7 +340,7 @@
     return pl.pallas_call(
         finish_ring_kernel,
         out_shape=(shape(BLK, width),) + (shape(BLK, HD),) * 3,
-        in_specs=[VMEM] * 7,
+        in_specs=[VMEM] * 9,
         out_specs=(HBM,) * 4,
         scratch_shapes=[
             pltpu.VMEM((BLK, width), BF16),
@@ -348,7 +350,7 @@
         ],
         compiler_params=PARAMS,
         name="finish",
-    )(attentions, mine, whole, half, first, own, dq)
+    )(*attentions, mine, whole, half, first, own, dq)
 
 
 def finish_kernel(count, *refs):
@@ -414,13 +416,13 @@
         att, dq, own_sum, first_sum, to_near, to_plus, to_across = attend(
             mult, queries, grad, blocks, 2
         )
-        attentions = gather([att] + [swap(att, r) for r in range(1, heads)])
-        own_sum, to_first = combine(
+        far = gather([swap(att, 2), swap(att, 3)])
+        own_sum, to_first, last = combine(
             own_sum, first_sum, trade(to_near, -1), trade(to_plus, 3), trade(to_across, 4),
-            whole, half,
+            whole, half, att,
         )
         mixed, dq, dk, dv = finish_ring(
-            attentions, mine, whole, half, trade(to_first, 1), own_sum, dq
+            (att, swap(last, 1), far), mine, whole, half, trade(to_first, 1), own_sum, dq
         )
     else:
         second = trade(own, -1)

time: 27.9 us -> 27.7 us (level)
  starting transfers between devices: 19 us -> 18 us
  waiting for transfers between devices: 3.18 us -> 3.92 us
    ppermute x4, starting transfers between devices: 10.4 us -> 9.31 us  [swap(): return lax.ppermute(array, 'head', [(i, i ^ mask) for i in range(count)])]
    ppermute x4, waiting for transfers between devices: 3.16 us -> 3.9 us  [swap(): return lax.ppermute(array, 'head', [(i, i ^ mask) for i in range(count)])]
where the time goes in v10:
time: 27.7 us; the launch traced here: 27.5 us
  starting transfers between devices  18 us (65%)
  Pallas kernels  3.93 us (14%)
  waiting for transfers between devices  3.92 us (14%)
  local copies, waits for them, and re-layouts  0.91 us (3%)
  between operations  0.73 us (3%)
    ppermute x4, starting transfers between devices, swap(): return lax.ppermute(array, 'head', [(i, i ^ mask) for i in range(count)])  9.31 us
    ppermute x8, starting transfers between devices, trade(): lax.ppermute(array, 'seq', [(i, (i + (step if i % 2 == 0 else -step)) % c...  8.73 us
    ppermute x4, waiting for transfers between devices, swap(): return lax.ppermute(array, 'head', [(i, i ^ mask) for i in range(count)])  3.9 us
    pallas_call x1, Pallas kernels, prepare(): pl.pallas_call(body, out_shape=(shape(BLK, HD), shape(8, columns, kind=F3...  1.8 us
    pallas_call x1, Pallas kernels, attend(): pl.pallas_call(body, out_shape=(shape(BLK, HD), shape(BLK, HD)) + tuple((...  1.02 us
    pallas_call x1, Pallas kernels, finish_ring(): pl.pallas_call(finish_ring_kernel, out_shape=(shape(BLK, width),) + (shap...  1.02 us
    unnamed x7, local copies, waits for them, and re-layouts  0.89 us
  transfers between devices with their start and end apart: 13, of which 2 were waited for; matrix products, arithmetic and copies ran while one was open for 0% of the time, Pallas kernels for 10%

profile of v10, /device:TPU:0, one launch (start us, length us, event | category | flops | bytes accessed | tf_op | source)
XLA Modules:
  0.0 27.5 jit_solution(17721410447476461586)
XLA Ops:
  0.6 0.8 %constant_dynamic-update-slice_fusion.1 = bf16[128,256]{1,0:T(8,128)(2,1)S(1)} fusion(bf16[128,128]{1,0:T(8,128)(2,1)} %param.7), kind=kLoop, calls=%fused_computation.1 | loop fusion | bytes 65536
  1.4 0.0 copy-start.1
  1.4 0.5 %collective-permute-start = (bf16[128,256]{1,0:T(8,128)(2,1)S(1)}, bf16[128,256]{1,0:T(8,128)(2,1)S(1)}, u32[]{:S(2)}, u32[]{:S(2)}) collective-permute-start(bf16[128,256]{1,0:T(8,128)(2,1)S(1)} %constant_dynamic-update-slice_fusion.refs_3_.own_ref), channel_id=1, source_target_pairs={{0,4},{4,0},{8,12},{12,8},{16,20},{20,16},{24,28},{28,24},{1,5},{5... | collective-permute-start | bytes 196616 | tf_op jit(solution)/shard_map/ppermute | solution.py:46
  2.0 0.1 copy-done.1
  2.1 1.8 %prepare.1 = (bf16[128,128]{1,0:T(8,128)(2,1)S(1)}, f32[8,640]{1,0:T(8,128)S(1)}, bf16[128,512]{1,0:T(8,128)(2,1)S(1)}, bf16[128,512]{1,0:T(8,128)(2,1)S(1)}, bf16[80,512]{1,0:T(8,128)(2,1)S(1)}) custom-call(s32[1,8]{1,0:T(1,128)S(1)} %copy-done.1, bf16[128,2048]{1,0:T(8,128)(2,1)} %refs_1_.2, bf16[128,2048]{1,0:T(8,128)(2,1)} %refs_2_.1, ...), custom_call_target="tpu_custom_call" | custom-call | flops 10000000000 | tf_op jit(solution)/shard_map/prepare/pallas_call | solution.py:145
  3.9 0.0 collective-permute-done.first_ref.refs_4_
  3.9 0.0 copy-start
  3.9 3.5 %collective-permute-start.1 = (bf16[160,256]{1,0:T(8,128)(2,1)S(1)}, bf16[160,256]{1,0:T(8,128)(2,1)S(1)}, u32[]{:S(2)}, u32[]{:S(2)}) collective-permute-start(bf16[160,256]{1,0:T(8,128)(2,1)S(1)} %get-tuple-element.25), channel_id=1, source_target_pairs={{0,28},{4,8},{8,4},{12,16},{16,12},{20,24},{24,20},{28,0},{1,29},{... | collective-permute-start | bytes 245768 | tf_op jit(solution)/shard_map/ppermute | solution.py:46
  7.5 0.7 %collective-permute-start.2 = (bf16[64,256]{1,0:T(8,128)(2,1)S(1)}, bf16[64,256]{1,0:T(8,128)(2,1)S(1)}, u32[]{:S(2)}, u32[]{:S(2)}) collective-permute-start(bf16[64,256]{1,0:T(8,128)(2,1)S(1)} %get-tuple-element.26), channel_id=1, source_target_pairs={{0,12},{4,24},{8,20},{12,0},{16,28},{20,8},{24,4},{28,16},{1,13},{... | collective-permute-start | bytes 98312 | tf_op jit(solution)/shard_map/ppermute | solution.py:46
  8.2 0.0 collective-permute-start.3
  8.2 4.1 %collective-permute-start.8 = (bf16[80,512]{1,0:T(8,128)(2,1)S(1)}, bf16[80,512]{1,0:T(8,128)(2,1)S(1)}, u32[]{:S(2)}, u32[]{:S(2)}) collective-permute-start(bf16[80,512]{1,0:T(8,128)(2,1)S(1)} %get-tuple-element.34), channel_id=1, source_target_pairs={{0,3},{1,2},{2,1},{3,0},{4,7},{5,6},{6,5},{7,4},{8,11},{9,10},{10,... | collective-permute-start | bytes 245768 | tf_op jit(solution)/shard_map/ppermute | solution.py:53
  12.3 0.0 collective-permute-start.7
  12.3 0.0 collective-permute-done.2.refs_6_
  12.3 0.0 collective-permute-done.3.refs_7_
  12.3 0.0 collective-permute-done.1.refs_5_
  12.3 1.0 %attend.1 = (bf16[128,128]{1,0:T(8,128)(2,1)S(1)}, bf16[128,128]{1,0:T(8,128)(2,1)S(1)}, f32[128,256]{1,0:T(8,128)S(1)}, f32[128,256]{1,0:T(8,128)S(1)}, bf16[16...) custom-call(f32[8,640]{1,0:T(8,128)S(1)} %get-tuple-element.22.mult_ref.refs_0_, ...), custom_call_target="tpu_custom_call" | custom-call | flops 10000000000 | tf_op jit(solution)/shard_map/attend/pallas_call | solution.py:227
  13.3 1.5 %collective-permute-start.4 = (bf16[160,256]{1,0:T(8,128)(2,1)S(1)}, bf16[160,256]{1,0:T(8,128)(2,1)S(1)}, u32[]{:S(2)}, u32[]{:S(2)}) collective-permute-start(bf16[160,256]{1,0:T(8,128)(2,1)S(1)} %get-tuple-element.30), channel_id=1, source_target_pairs={{0,28},{4,8},{8,4},{12,16},{16,12},{20,24},{24,20},{28,0},{1,29},{... | collective-permute-start | bytes 245768 | tf_op jit(solution)/shard_map/ppermute | solution.py:46
  14.8 1.3 %collective-permute-start.5 = (bf16[64,256]{1,0:T(8,128)(2,1)S(1)}, bf16[64,256]{1,0:T(8,128)(2,1)S(1)}, u32[]{:S(2)}, u32[]{:S(2)}) collective-permute-start(bf16[64,256]{1,0:T(8,128)(2,1)S(1)} %get-tuple-element.31), channel_id=1, source_target_pairs={{0,12},{4,24},{8,20},{12,0},{16,28},{20,8},{24,4},{28,16},{1,13},{... | collective-permute-start | bytes 98312 | tf_op jit(solution)/shard_map/ppermute | solution.py:46
  16.1 0.5 %collective-permute-start.6 = (bf16[64,256]{1,0:T(8,128)(2,1)S(1)}, bf16[64,256]{1,0:T(8,128)(2,1)S(1)}, u32[]{:S(2)}, u32[]{:S(2)}) collective-permute-start(bf16[64,256]{1,0:T(8,128)(2,1)S(1)} %get-tuple-element.32), channel_id=1, source_target_pairs={{0,16},{4,20},{8,24},{12,28},{16,0},{20,4},{24,8},{28,12},{1,17},{... | collective-permute-start | bytes 98312 | tf_op jit(solution)/shard_map/ppermute | solution.py:46
  16.6 0.0 collective-permute-done.8.half_ref.refs_5_
  16.6 3.1 %collective-permute-start.10 = (bf16[128,128]{1,0:T(8,128)(2,1)S(1)}, bf16[128,128]{1,0:T(8,128)(2,1)S(1)}, u32[]{:S(2)}, u32[]{:S(2)}) collective-permute-start(bf16[128,128]{1,0:T(8,128)(2,1)S(1)} %get-tuple-element.27.att_ref.refs_0_), channel_id=1, source_target_pairs={{0,2},{1,3},{2,0},{3,1},{4,6},{5,7},{6,4},{7,5},{8,10},{9,11},{10,... | collective-permute-start | bytes 98312 | tf_op jit(solution)/shard_map/ppermute | solution.py:53
  19.7 0.0 collective-permute-done.5.plus_ref
  19.7 2.1 %collective-permute-start.11 = (bf16[128,128]{1,0:T(8,128)(2,1)S(1)}, bf16[128,128]{1,0:T(8,128)(2,1)S(1)}, u32[]{:S(2)}, u32[]{:S(2)}) collective-permute-start(bf16[128,128]{1,0:T(8,128)(2,1)S(1)} %get-tuple-element.27.att_ref.refs_0_), channel_id=1, source_target_pairs={{0,3},{1,2},{2,1},{3,0},{4,7},{5,6},{6,5},{7,4},{8,11},{9,10},{10,... | collective-permute-start | bytes 98312 | tf_op jit(solution)/shard_map/ppermute | solution.py:53
  21.8 0.0 collective-permute-done.6.across_ref
  21.8 0.0 collective-permute-done.7.whole_ref.refs_4_
  21.9 0.7 %collective-permute-start.12 = (bf16[512,256]{1,0:T(8,128)(2,1)S(1)}, bf16[512,256]{1,0:T(8,128)(2,1)S(1)}, u32[]{:S(2)}, u32[]{:S(2)}) collective-permute-start(bf16[512,256]{1,0:T(8,128)(2,1)S(1)} %get-tuple-element.37), channel_id=1, source_target_pairs={{0,4},{4,0},{8,12},{12,8},{16,20},{20,16},{24,28},{28,24},{1,5},{5... | collective-permute-start | bytes 786440 | tf_op jit(solution)/shard_map/ppermute | solution.py:46
  22.6 0.0 collective-permute-start.9
  22.6 0.0 collective-permute-done.10.refs_0_
  22.6 3.3 %collective-permute-done.11.refs_1_ = bf16[128,128]{1,0:T(8,128)(2,1)S(1)} collective-permute-done((bf16[128,128]{1,0:T(8,128)(2,1)S(1)}, bf16[128,128]{1,0:T(8,128)(2,1)S(1)}, u32[]{:S(2)}, u32[]{:S(2)}) %collective-permute-start.11) | collective-permute-done | bytes 32800 | tf_op jit(solution)/shard_map/ppermute | solution.py:53
  25.9 0.6 %collective-permute-done.9.refs_1_ = bf16[128,128]{1,0:T(8,128)(2,1)S(1)} collective-permute-done((bf16[128,128]{1,0:T(8,128)(2,1)S(1)}, bf16[128,128]{1,0:T(8,128)(2,1)S(1)}, u32[]{:S(2)}, u32[]{:S(2)}) %collective-permute-start.9) | collective-permute-done | bytes 32800 | tf_op jit(solution)/shard_map/ppermute | solution.py:53
  26.5 0.0 collective-permute-done.12.refs_6_
  26.5 1.0 %finish.1 = (bf16[128,512]{1,0:T(8,128)(2,1)}, bf16[128,128]{1,0:T(8,128)(2,1)}, bf16[128,128]{1,0:T(8,128)(2,1)}, bf16[128,128]{1,0:T(8,128)(2,1)}) custom-call(bf16[128,128]{1,0:T(8,128)(2,1)S(1)} %get-tuple-element.27.att_ref.refs_0_, bf16[128,128]{1,0:T(8,128)(2,1)S(1)} %collective-permute-done.9.refs_1_, bf16[128,256]{1,0:T(8,128)(2,1)S(1)} %gather.1.refs_2_, ...), custom_call_target="tpu_custom_call" | custom-call | tf_op jit(solution)/shard_map/finish/pallas_call | solution.py:340
  (8 shorter events, 0.1 us)
Async XLA Ops:
  0.6 0.8 %copy-start.2 = (bf16[128,128]{1,0:T(8,128)(2,1)S(1)}, bf16[128,128]{1,0:T(8,128)(2,1)}, u32[]{:S(2)}) copy-start(bf16[128,128]{1,0:T(8,128)(2,1)} %param.8) | copy-start | bytes 98308
  1.4 0.7 %copy-start.1 = (s32[1,8]{1,0:T(1,128)S(1)}, s32[1,8]{1,0:T(1,128)}, u32[]{:S(2)}) copy-start(s32[1,8]{1,0:T(1,128)} %refs_0_.1) | copy-start | bytes 100
  1.4 2.4 %collective-permute-start = (bf16[128,256]{1,0:T(8,128)(2,1)S(1)}, bf16[128,256]{1,0:T(8,128)(2,1)S(1)}, u32[]{:S(2)}, u32[]{:S(2)}) collective-permute-start(bf16[128,256]{1,0:T(8,128)(2,1)S(1)} %constant_dynamic-update-slice_fusion.refs_3_.own_ref), channel_id=1, source_target_pairs={{0,4},{4,0},{8,12},{12,8},{16,20},{20,16},{24,28},{28,24},{1,5},{5... | collective-permute-start | bytes 196616 | tf_op jit(solution)/shard_map/ppermute | solution.py:46
  3.9 8.4 %copy-start = (bf16[128,128]{1,0:T(8,128)(2,1)S(1)}, bf16[128,128]{1,0:T(8,128)(2,1)}, u32[]{:S(2)}) copy-start(bf16[128,128]{1,0:T(8,128)(2,1)} %refs_1_.3) | copy-start | bytes 98308
  3.9 8.3 %collective-permute-start.1 = (bf16[160,256]{1,0:T(8,128)(2,1)S(1)}, bf16[160,256]{1,0:T(8,128)(2,1)S(1)}, u32[]{:S(2)}, u32[]{:S(2)}) collective-permute-start(bf16[160,256]{1,0:T(8,128)(2,1)S(1)} %get-tuple-element.25), channel_id=1, source_target_pairs={{0,28},{4,8},{8,4},{12,16},{16,12},{20,24},{24,20},{28,0},{1,29},{... | collective-permute-start | bytes 245768 | tf_op jit(solution)/shard_map/ppermute | solution.py:46
  7.5 4.8 %collective-permute-start.2 = (bf16[64,256]{1,0:T(8,128)(2,1)S(1)}, bf16[64,256]{1,0:T(8,128)(2,1)S(1)}, u32[]{:S(2)}, u32[]{:S(2)}) collective-permute-start(bf16[64,256]{1,0:T(8,128)(2,1)S(1)} %get-tuple-element.26), channel_id=1, source_target_pairs={{0,12},{4,24},{8,20},{12,0},{16,28},{20,8},{24,4},{28,16},{1,13},{... | collective-permute-start | bytes 98312 | tf_op jit(solution)/shard_map/ppermute | solution.py:46
  8.2 4.1 %collective-permute-start.3 = (bf16[64,256]{1,0:T(8,128)(2,1)S(1)}, bf16[64,256]{1,0:T(8,128)(2,1)S(1)}, u32[]{:S(2)}, u32[]{:S(2)}) collective-permute-start(bf16[64,256]{1,0:T(8,128)(2,1)S(1)} %get-tuple-element.26), channel_id=1, source_target_pairs={{0,16},{4,20},{8,24},{12,28},{16,0},{20,4},{24,8},{28,12},{1,17},{... | collective-permute-start | bytes 98312 | tf_op jit(solution)/shard_map/ppermute | solution.py:46
  8.2 8.4 %collective-permute-start.8 = (bf16[80,512]{1,0:T(8,128)(2,1)S(1)}, bf16[80,512]{1,0:T(8,128)(2,1)S(1)}, u32[]{:S(2)}, u32[]{:S(2)}) collective-permute-start(bf16[80,512]{1,0:T(8,128)(2,1)S(1)} %get-tuple-element.34), channel_id=1, source_target_pairs={{0,3},{1,2},{2,1},{3,0},{4,7},{5,6},{6,5},{7,4},{8,11},{9,10},{10,... | collective-permute-start | bytes 245768 | tf_op jit(solution)/shard_map/ppermute | solution.py:53
  12.3 9.5 %collective-permute-start.7 = (bf16[128,512]{1,0:T(8,128)(2,1)S(1)}, bf16[128,512]{1,0:T(8,128)(2,1)S(1)}, u32[]{:S(2)}, u32[]{:S(2)}) collective-permute-start(bf16[128,512]{1,0:T(8,128)(2,1)S(1)} %get-tuple-element.33), channel_id=1, source_target_pairs={{0,1},{1,0},{2,3},{3,2},{4,6},{5,7},{6,4},{7,5},{8,9},{9,8},{10,11... | collective-permute-start | bytes 393224 | tf_op jit(solution)/shard_map/ppermute | solution.py:394
  13.3 8.5 %collective-permute-start.4 = (bf16[160,256]{1,0:T(8,128)(2,1)S(1)}, bf16[160,256]{1,0:T(8,128)(2,1)S(1)}, u32[]{:S(2)}, u32[]{:S(2)}) collective-permute-start(bf16[160,256]{1,0:T(8,128)(2,1)S(1)} %get-tuple-element.30), channel_id=1, source_target_pairs={{0,28},{4,8},{8,4},{12,16},{16,12},{20,24},{24,20},{28,0},{1,29},{... | collective-permute-start | bytes 245768 | tf_op jit(solution)/shard_map/ppermute | solution.py:46
  14.8 4.9 %collective-permute-start.5 = (bf16[64,256]{1,0:T(8,128)(2,1)S(1)}, bf16[64,256]{1,0:T(8,128)(2,1)S(1)}, u32[]{:S(2)}, u32[]{:S(2)}) collective-permute-start(bf16[64,256]{1,0:T(8,128)(2,1)S(1)} %get-tuple-element.31), channel_id=1, source_target_pairs={{0,12},{4,24},{8,20},{12,0},{16,28},{20,8},{24,4},{28,16},{1,13},{... | collective-permute-start | bytes 98312 | tf_op jit(solution)/shard_map/ppermute | solution.py:46
  16.1 5.7 %collective-permute-start.6 = (bf16[64,256]{1,0:T(8,128)(2,1)S(1)}, bf16[64,256]{1,0:T(8,128)(2,1)S(1)}, u32[]{:S(2)}, u32[]{:S(2)}) collective-permute-start(bf16[64,256]{1,0:T(8,128)(2,1)S(1)} %get-tuple-element.32), channel_id=1, source_target_pairs={{0,16},{4,20},{8,24},{12,28},{16,0},{20,4},{24,8},{28,12},{1,17},{... | collective-permute-start | bytes 98312 | tf_op jit(solution)/shard_map/ppermute | solution.py:46
  16.6 6.0 %collective-permute-start.10 = (bf16[128,128]{1,0:T(8,128)(2,1)S(1)}, bf16[128,128]{1,0:T(8,128)(2,1)S(1)}, u32[]{:S(2)}, u32[]{:S(2)}) collective-permute-start(bf16[128,128]{1,0:T(8,128)(2,1)S(1)} %get-tuple-element.27.att_ref.refs_0_), channel_id=1, source_target_pairs={{0,2},{1,3},{2,0},{3,1},{4,6},{5,7},{6,4},{7,5},{8,10},{9,11},{10,... | collective-permute-start | bytes 98312 | tf_op jit(solution)/shard_map/ppermute | solution.py:53
  19.7 6.1 %collective-permute-start.11 = (bf16[128,128]{1,0:T(8,128)(2,1)S(1)}, bf16[128,128]{1,0:T(8,128)(2,1)S(1)}, u32[]{:S(2)}, u32[]{:S(2)}) collective-permute-start(bf16[128,128]{1,0:T(8,128)(2,1)S(1)} %get-tuple-element.27.att_ref.refs_0_), channel_id=1, source_target_pairs={{0,3},{1,2},{2,1},{3,0},{4,7},{5,6},{6,5},{7,4},{8,11},{9,10},{10,... | collective-permute-start | bytes 98312 | tf_op jit(solution)/shard_map/ppermute | solution.py:53
  21.9 4.6 %collective-permute-start.12 = (bf16[512,256]{1,0:T(8,128)(2,1)S(1)}, bf16[512,256]{1,0:T(8,128)(2,1)S(1)}, u32[]{:S(2)}, u32[]{:S(2)}) collective-permute-start(bf16[512,256]{1,0:T(8,128)(2,1)S(1)} %get-tuple-element.37), channel_id=1, source_target_pairs={{0,4},{4,0},{8,12},{12,8},{16,20},{20,16},{24,28},{28,24},{1,5},{5... | collective-permute-start | bytes 786440 | tf_op jit(solution)/shard_map/ppermute | solution.py:46
  22.6 3.9 %collective-permute-start.9 = (bf16[128,128]{1,0:T(8,128)(2,1)S(1)}, bf16[128,128]{1,0:T(8,128)(2,1)S(1)}, u32[]{:S(2)}, u32[]{:S(2)}) collective-permute-start(bf16[128,128]{1,0:T(8,128)(2,1)S(1)} %get-tuple-element.35), channel_id=1, source_target_pairs={{0,1},{1,0},{2,3},{3,2},{4,5},{5,4},{6,7},{7,6},{8,9},{9,8},{10,11... | collective-permute-start | bytes 98312 | tf_op jit(solution)/shard_map/ppermute | solution.py:53

commit v11 on v10

--- a/solution.py
+++ b/solution.py
@@ -182,16 +182,14 @@
     )(own, first, mult, whole)
 
 
-def attend_kernel(blocks, mult_ref, q_ref, grad_ref, *refs):
+def attend_kernel(blocks, pieces, mult_ref, q_ref, grad_ref, *refs):
     block_refs = refs[:blocks]
     att_ref, dq_ref = refs[blocks:blocks + 2]
-    sum_refs = refs[blocks + 2:2 * blocks + 2]
+    sum_refs = refs[blocks + 2:-1]
     keys_ref = refs[-1]
     total_rows = keys_ref.shape[0]
-    spans = []
     row = 0
     for ref in block_refs:
-        spans.append((row, row + ref.shape[0]))
         keys_ref[row:row + ref.shape[0], :] = ref[...]
         row += ref.shape[0]
     if row < total_rows:
@@ -215,21 +213,28 @@
     dq_ref[...] = dot_nn(grad_scores, keys).astype(BF16)
     key_terms = dot_tn(grad_scores, q)
     value_terms = dot_tn(weights, grad)
-    for (start, end), ref in zip(spans, sum_refs):
-        ref[:, :HD] = key_terms[start:end].astype(ref.dtype)
-        ref[:, HD:] = value_terms[start:end].astype(ref.dtype)
-
-
-def attend(mult, q, grad, blocks, wide):
+    for spans, ref in zip(pieces, sum_refs):
+        row = 0
+        for start, end in spans:
+            rows = slice(row, row + end - start)
+            ref[rows, :HD] = key_terms[start:end].astype(ref.dtype)
+            ref[rows, HD:] = value_terms[start:end].astype(ref.dtype)
+            row += end - start
+
+
+def attend(mult, q, grad, blocks, pieces, wide):
     def body(*refs):
-        attend_kernel(len(blocks), *refs)
-
+        attend_kernel(len(blocks), pieces, *refs)
+
+    sums = []
+    for i, spans in enumerate(pieces):
+        rows = sum(end - start for start, end in spans)
+        sums.append(shape(rows, PAIR, kind=F32 if i < wide else BF16))
     return pl.pallas_call(
         body,
-        out_shape=(shape(BLK, HD), shape(BLK, HD))
-        + tuple(shape(*b.shape, kind=F32 if i < wide else BF16) for i, b in enumerate(blocks)),
+        out_shape=(shape(BLK, HD), shape(BLK, HD), *sums),
         in_specs=[VMEM] * (3 + len(blocks)),
-        out_specs=(VMEM,) * (2 + len(blocks)),
+        out_specs=(VMEM,) * (2 + len(sums)),
         scratch_shapes=[pltpu.VMEM((mult.shape[1], PAIR), BF16)],
         compiler_params=PARAMS,
         cost_estimate=cost(ATTEND_COST),
@@ -242,16 +247,17 @@
     return pl.ds(pl.multiple_of(core * MARGIN, MARGIN), HD // 2)
 
 
-def combine_kernel(own_ref, first_ref, near_ref, plus_ref, across_ref, whole_ref, half_ref,
-                   att_ref, own_out, first_out, att_out):
-    near = near_ref[...].astype(F32)
+def combine_kernel(own_ref, first_ref, second_ref, plus_ref, minus_ref, whole_ref, half_ref,
+                   att_ref, own_out, first_out, second_out, att_out):
     plus = plus_ref[...].astype(F32)
-    across = across_ref[...].astype(F32)
+    minus = minus_ref[...].astype(F32)
     n = STRIDE_ROWS
-    own_out[n:] = own_ref[n:] + near[n:BLK]
-    own_out[:n] = own_ref[:n] + near[:n] + plus[:n] + across[:n]
+    own_out[n:] = own_ref[n:]
+    own_out[:n] = own_ref[:n] + plus[:n] + minus[:n]
+    second_out[n:] = second_ref[n:].astype(BF16)
+    second_out[:n] = (second_ref[:n] + plus[2 * n:] + minus[n:]).astype(BF16)
     first_out[n:BLK] = first_ref[n:].astype(BF16)
-    first_out[:n] = (first_ref[:n] + near[BLK:] + plus[n:] + across[n:]).astype(BF16)
+    first_out[:n] = (first_ref[:n] + plus[n:2 * n]).astype(BF16)
     att_out[...] = att_ref[...]
     row = BLK
     for ref, rows in ((whole_ref, slice(0, HD)), (half_ref, half_rows())):
@@ -261,17 +267,18 @@
             row += piece.shape[0]
 
 
-def combine(own, first, near, plus, across, whole, half, att):
+def combine(own, first, second, plus, minus, whole, half, att):
     extra = (HD + HD // 2) * whole.shape[1] // PAIR
     return pl.pallas_call(
         combine_kernel,
-        out_shape=(shape(BLK, PAIR, kind=F32), shape(BLK + extra, PAIR), shape(BLK, HD)),
+        out_shape=(shape(BLK, PAIR, kind=F32), shape(BLK + extra, PAIR), shape(BLK, PAIR),
+                   shape(BLK, HD)),
         in_specs=[VMEM] * 8,
-        out_specs=(VMEM,) * 3,
+        out_specs=(VMEM,) * 4,
         compiler_params=PARAMS,
         cost_estimate=cost(COMBINE_COST),
         name="combine",
-    )(own, first, near, plus, across, whole, half, att)
+    )(own, first, second, plus, minus, whole, half, att)
 
 
 def gather_kernel(*refs):
@@ -298,9 +305,9 @@
 
 
 def finish_ring_kernel(*refs):
-    att_ref, beside_ref, far_ref = refs[:3]
-    mine_ref, whole_ref, half_ref, first_ref, own_ref, dq_ref = refs[3:9]
-    mixed_hbm, dq_hbm, dk_hbm, dv_hbm, mixed_ref, dk_ref, dv_ref, sems = refs[9:]
+    att_ref, near_ref, far_ref, mine_ref, whole_ref, half_ref = refs[:6]
+    first_ref, own_ref, second_ref, dq_ref = refs[6:10]
+    mixed_hbm, dq_hbm, dk_hbm, dv_hbm, mixed_ref, dk_ref, dv_ref, sems = refs[10:]
     copies = []
 
     def send(src, dst):
@@ -309,11 +316,11 @@
         copies.append(copy)
 
     send(dq_ref, dq_hbm)
-    total = own_ref[...] + first_ref[:BLK].astype(F32)
+    total = own_ref[...] + first_ref[:BLK].astype(F32) + second_ref[...].astype(F32)
     settle(total, total[:STRIDE_ROWS], dk_ref, dv_ref)
     send(dk_ref, dk_hbm)
     send(dv_ref, dv_hbm)
-    att = [att_ref[...], beside_ref[...], far_ref[:, :HD], far_ref[:, HD:]]
+    att = [att_ref[...], near_ref[...], far_ref[:, :HD], far_ref[:, HD:]]
     core = lax.axis_index("seq") & 1
     half = HD // 2
     here = jnp.where(core == 0, att[1], att[2])
@@ -335,12 +342,12 @@
         copy.wait()
 
 
-def finish_ring(attentions, mine, whole, half, first, own, dq):
+def finish_ring(attentions, mine, whole, half, first, own, second, dq):
     width = mine.shape[1]
     return pl.pallas_call(
         finish_ring_kernel,
         out_shape=(shape(BLK, width),) + (shape(BLK, HD),) * 3,
-        in_specs=[VMEM] * 9,
+        in_specs=[VMEM] * 10,
         out_specs=(HBM,) * 4,
         scratch_shapes=[
             pltpu.VMEM((BLK, width), BF16),
@@ -350,7 +357,7 @@
         ],
         compiler_params=PARAMS,
         name="finish",
-    )(*attentions, mine, whole, half, first, own, dq)
+    )(*attentions, mine, whole, half, first, own, second, dq)
 
 
 def finish_kernel(count, *refs):
@@ -413,24 +420,30 @@
         whole = spread_slice(whole)
         near = trade(near, -1)
         blocks = (own, first, near, trade(pair, 3), trade(pair, 4))
-        att, dq, own_sum, first_sum, to_near, to_plus, to_across = attend(
-            mult, queries, grad, blocks, 2
+        side = 3 * BLK
+        places = [side + i * n for i in range(6)]
+        pieces = [[(i * BLK, (i + 1) * BLK)] for i in range(3)]
+        pieces += [[(places[1], places[4])], [(places[4], places[5]), (places[0], places[1])]]
+        att, dq, own_sum, first_sum, second_sum, to_plus, to_minus = attend(
+            mult, queries, grad, blocks, pieces, 3
         )
         far = gather([swap(att, 2), swap(att, 3)])
-        own_sum, to_first, last = combine(
-            own_sum, first_sum, trade(to_near, -1), trade(to_plus, 3), trade(to_across, 4),
-            whole, half, att,
+        own_sum, to_first, to_second, last = combine(
+            own_sum, first_sum, second_sum, trade(to_plus, 3), trade(to_minus, -3), whole, half,
+            att,
         )
         mixed, dq, dk, dv = finish_ring(
-            (att, swap(last, 1), far), mine, whole, half, trade(to_first, 1), own_sum, dq
+            [att, swap(last, 1), far], mine, whole, half, trade(to_first, 1), own_sum,
+            trade(to_second, -1), dq,
         )
     else:
         second = trade(own, -1)
         slices = [slices[0]] + [swap(slices[r], r) for r in range(1, heads)]
         spread = jnp.broadcast_to(own[None, :n], (seq, n, PAIR))
         side = lax.all_to_all(spread, "seq", 0, 0).reshape(side_rows, PAIR)
+        pieces = [[(i * BLK, (i + 1) * BLK)] for i in range(3)] + [[(3 * BLK, columns)]]
         att, dq, own_sum, to_first, to_second, to_side = attend(
-            mult, queries, grad, (own, first, second, side), 1
+            mult, queries, grad, (own, first, second, side), pieces, 1
         )
         from_side = lax.all_to_all(to_side.reshape(seq, n, PAIR), "seq", 0, 0)
         mixed, dk, dv = finish(

time: 27.7 us -> 27.6 us (level)
  waiting for transfers between devices: 3.92 us -> 3.61 us
    ppermute x8, starting transfers between devices: 8.73 us -> 10.1 us  [trade(): lax.ppermute(array, 'seq', [(i, (i + (step if i % 2 == 0 else -step)) % c...]
    ppermute x4, starting transfers between devices: 9.31 us -> 8.08 us  [swap(): return lax.ppermute(array, 'head', [(i, i ^ mask) for i in range(count)])]
    ppermute x4, waiting for transfers between devices: 3.9 us -> 3.59 us  [swap(): return lax.ppermute(array, 'head', [(i, i ^ mask) for i in range(count)])]
  transfers between devices with their start and end apart: 13 -> 13, of which waited for: 2 -> 2; matrix products, arithmetic and copies ran while one was open for 0% -> 0% of each run, Pallas kernels for 10% -> 11%
where the time goes in v11:
time: 27.6 us; the launch traced here: 27.4 us
  starting transfers between devices  18.2 us (66%)
  Pallas kernels  3.93 us (14%)
  waiting for transfers between devices  3.61 us (13%)
  local copies, waits for them, and re-layouts  0.91 us (3%)
  between operations  0.74 us (3%)
    ppermute x8, starting transfers between devices, trade(): lax.ppermute(array, 'seq', [(i, (i + (step if i % 2 == 0 else -step)) % c...  10.1 us
    ppermute x4, starting transfers between devices, swap(): return lax.ppermute(array, 'head', [(i, i ^ mask) for i in range(count)])  8.08 us
    ppermute x4, waiting for transfers between devices, swap(): return lax.ppermute(array, 'head', [(i, i ^ mask) for i in range(count)])  3.59 us
    pallas_call x1, Pallas kernels, prepare(): pl.pallas_call(body, out_shape=(shape(BLK, HD), shape(8, columns, kind=F3...  1.8 us
    pallas_call x1, Pallas kernels, finish_ring(): pl.pallas_call(finish_ring_kernel, out_shape=(shape(BLK, width),) + (shap...  1.02 us
    pallas_call x1, Pallas kernels, attend(): pl.pallas_call(body, out_shape=(shape(BLK, HD), shape(BLK, HD), *sums), i...  1.02 us
    unnamed x7, local copies, waits for them, and re-layouts  0.89 us
  transfers between devices with their start and end apart: 13, of which 2 were waited for; matrix products, arithmetic and copies ran while one was open for 0% of the time, Pallas kernels for 11%

profile of v11, /device:TPU:0, one launch (start us, length us, event | category | flops | bytes accessed | tf_op | source)
XLA Modules:
  0.0 27.4 jit_solution(14657679652166939939)
XLA Ops:
  0.6 0.8 %constant_dynamic-update-slice_fusion.1 = bf16[128,256]{1,0:T(8,128)(2,1)S(1)} fusion(bf16[128,128]{1,0:T(8,128)(2,1)} %param.7), kind=kLoop, calls=%fused_computation.1 | loop fusion | bytes 65536
  1.4 0.0 copy-start.1
  1.4 0.5 %collective-permute-start = (bf16[128,256]{1,0:T(8,128)(2,1)S(1)}, bf16[128,256]{1,0:T(8,128)(2,1)S(1)}, u32[]{:S(2)}, u32[]{:S(2)}) collective-permute-start(bf16[128,256]{1,0:T(8,128)(2,1)S(1)} %constant_dynamic-update-slice_fusion.refs_3_.own_ref), channel_id=1, source_target_pairs={{0,4},{4,0},{8,12},{12,8},{16,20},{20,16},{24,28},{28,24},{1,5},{5... | collective-permute-start | bytes 196616 | tf_op jit(solution)/shard_map/ppermute | solution.py:46
  2.0 0.1 copy-done.1
  2.1 1.8 %prepare.1 = (bf16[128,128]{1,0:T(8,128)(2,1)S(1)}, f32[8,640]{1,0:T(8,128)S(1)}, bf16[128,512]{1,0:T(8,128)(2,1)S(1)}, bf16[128,512]{1,0:T(8,128)(2,1)S(1)}, bf16[80,512]{1,0:T(8,128)(2,1)S(1)}) custom-call(s32[1,8]{1,0:T(1,128)S(1)} %copy-done.1, bf16[128,2048]{1,0:T(8,128)(2,1)} %refs_1_.2, bf16[128,2048]{1,0:T(8,128)(2,1)} %refs_2_.1, ...), custom_call_target="tpu_custom_call" | custom-call | flops 10000000000 | tf_op jit(solution)/shard_map/prepare/pallas_call | solution.py:145
  3.9 0.0 collective-permute-done.first_ref.refs_4_
  3.9 0.0 copy-start
  3.9 3.5 %collective-permute-start.1 = (bf16[160,256]{1,0:T(8,128)(2,1)S(1)}, bf16[160,256]{1,0:T(8,128)(2,1)S(1)}, u32[]{:S(2)}, u32[]{:S(2)}) collective-permute-start(bf16[160,256]{1,0:T(8,128)(2,1)S(1)} %get-tuple-element.26), channel_id=1, source_target_pairs={{0,28},{4,8},{8,4},{12,16},{16,12},{20,24},{24,20},{28,0},{1,29},{... | collective-permute-start | bytes 245768 | tf_op jit(solution)/shard_map/ppermute | solution.py:46
  7.5 0.7 %collective-permute-start.2 = (bf16[64,256]{1,0:T(8,128)(2,1)S(1)}, bf16[64,256]{1,0:T(8,128)(2,1)S(1)}, u32[]{:S(2)}, u32[]{:S(2)}) collective-permute-start(bf16[64,256]{1,0:T(8,128)(2,1)S(1)} %get-tuple-element.27), channel_id=1, source_target_pairs={{0,12},{4,24},{8,20},{12,0},{16,28},{20,8},{24,4},{28,16},{1,13},{... | collective-permute-start | bytes 98312 | tf_op jit(solution)/shard_map/ppermute | solution.py:46
  8.2 0.0 collective-permute-start.3
  8.2 4.1 %collective-permute-start.7 = (bf16[80,512]{1,0:T(8,128)(2,1)S(1)}, bf16[80,512]{1,0:T(8,128)(2,1)S(1)}, u32[]{:S(2)}, u32[]{:S(2)}) collective-permute-start(bf16[80,512]{1,0:T(8,128)(2,1)S(1)} %get-tuple-element.35), channel_id=1, source_target_pairs={{0,3},{1,2},{2,1},{3,0},{4,7},{5,6},{6,5},{7,4},{8,11},{9,10},{10,... | collective-permute-start | bytes 245768 | tf_op jit(solution)/shard_map/ppermute | solution.py:53
  12.3 0.0 collective-permute-start.6
  12.3 0.0 collective-permute-done.2.refs_6_
  12.3 0.0 collective-permute-done.3.refs_7_
  12.3 0.0 collective-permute-done.1.refs_5_
  12.3 1.0 %attend.1 = (bf16[128,128]{1,0:T(8,128)(2,1)S(1)}, bf16[128,128]{1,0:T(8,128)(2,1)S(1)}, f32[128,256]{1,0:T(8,128)S(1)}, f32[128,256]{1,0:T(8,128)S(1)}, f32[128...) custom-call(f32[8,640]{1,0:T(8,128)S(1)} %get-tuple-element.23.mult_ref.refs_0_, ...), custom_call_target="tpu_custom_call" | custom-call | flops 10000000000 | tf_op jit(solution)/shard_map/attend/pallas_call | solution.py:233
  13.3 0.6 %collective-permute-start.4 = (bf16[96,256]{1,0:T(8,128)(2,1)S(1)}, bf16[96,256]{1,0:T(8,128)(2,1)S(1)}, u32[]{:S(2)}, u32[]{:S(2)}) collective-permute-start(bf16[96,256]{1,0:T(8,128)(2,1)S(1)} %get-tuple-element.32), channel_id=1, source_target_pairs={{0,12},{4,24},{8,20},{12,0},{16,28},{20,8},{24,4},{28,16},{1,13},{... | collective-permute-start | bytes 147464 | tf_op jit(solution)/shard_map/ppermute | solution.py:46
  13.9 2.2 %collective-permute-start.5 = (bf16[64,256]{1,0:T(8,128)(2,1)S(1)}, bf16[64,256]{1,0:T(8,128)(2,1)S(1)}, u32[]{:S(2)}, u32[]{:S(2)}) collective-permute-start(bf16[64,256]{1,0:T(8,128)(2,1)S(1)} %get-tuple-element.33), channel_id=1, source_target_pairs={{0,20},{4,16},{8,28},{12,24},{16,4},{20,0},{24,12},{28,8},{1,21},{... | collective-permute-start | bytes 98312 | tf_op jit(solution)/shard_map/ppermute | solution.py:46
  16.1 3.4 %collective-permute-start.10 = (bf16[128,128]{1,0:T(8,128)(2,1)S(1)}, bf16[128,128]{1,0:T(8,128)(2,1)S(1)}, u32[]{:S(2)}, u32[]{:S(2)}) collective-permute-start(bf16[128,128]{1,0:T(8,128)(2,1)S(1)} %get-tuple-element.28.att_ref.refs_0_), channel_id=1, source_target_pairs={{0,3},{1,2},{2,1},{3,0},{4,7},{5,6},{6,5},{7,4},{8,11},{9,10},{10,... | collective-permute-start | bytes 98312 | tf_op jit(solution)/shard_map/ppermute | solution.py:53
  19.5 0.0 collective-permute-done.7.half_ref.refs_5_
  19.5 0.3 collective-permute-start.9
  19.7 0.0 collective-permute-done.5.minus_ref
  19.7 0.0 collective-permute-done.4.plus_ref
  19.7 0.0 collective-permute-done.6.whole_ref.refs_4_
  19.7 0.1 combine.1
  19.8 0.1 collective-permute-start.11
  19.9 2.5 %collective-permute-start.12 = (bf16[128,256]{1,0:T(8,128)(2,1)S(1)}, bf16[128,256]{1,0:T(8,128)(2,1)S(1)}, u32[]{:S(2)}, u32[]{:S(2)}) collective-permute-start(bf16[128,256]{1,0:T(8,128)(2,1)S(1)} %get-tuple-element.40), channel_id=1, source_target_pairs={{0,28},{4,8},{8,4},{12,16},{16,12},{20,24},{24,20},{28,0},{1,29},{... | collective-permute-start | bytes 196616 | tf_op jit(solution)/shard_map/ppermute | solution.py:46
  22.4 0.3 %collective-permute-start.8 = (bf16[128,128]{1,0:T(8,128)(2,1)S(1)}, bf16[128,128]{1,0:T(8,128)(2,1)S(1)}, u32[]{:S(2)}, u32[]{:S(2)}) collective-permute-start(bf16[128,128]{1,0:T(8,128)(2,1)S(1)} %get-tuple-element.36), channel_id=1, source_target_pairs={{0,1},{1,0},{2,3},{3,2},{4,5},{5,4},{6,7},{7,6},{8,9},{9,8},{10,11... | collective-permute-start | bytes 98312 | tf_op jit(solution)/shard_map/ppermute | solution.py:53
  22.7 0.0 collective-permute-done.10.refs_1_
  22.7 1.6 %collective-permute-done.9.refs_0_ = bf16[128,128]{1,0:T(8,128)(2,1)S(1)} collective-permute-done((bf16[128,128]{1,0:T(8,128)(2,1)S(1)}, bf16[128,128]{1,0:T(8,128)(2,1)S(1)}, u32[]{:S(2)}, u32[]{:S(2)}) %collective-permute-start.9) | collective-permute-done | bytes 32800 | tf_op jit(solution)/shard_map/ppermute | solution.py:53
  24.3 2.0 %collective-permute-done.8.refs_1_ = bf16[128,128]{1,0:T(8,128)(2,1)S(1)} collective-permute-done((bf16[128,128]{1,0:T(8,128)(2,1)S(1)}, bf16[128,128]{1,0:T(8,128)(2,1)S(1)}, u32[]{:S(2)}, u32[]{:S(2)}) %collective-permute-start.8) | collective-permute-done | bytes 32800 | tf_op jit(solution)/shard_map/ppermute | solution.py:53
  26.3 1.0 %finish.1 = (bf16[128,512]{1,0:T(8,128)(2,1)}, bf16[128,128]{1,0:T(8,128)(2,1)}, bf16[128,128]{1,0:T(8,128)(2,1)}, bf16[128,128]{1,0:T(8,128)(2,1)}) custom-call(bf16[128,128]{1,0:T(8,128)(2,1)S(1)} %get-tuple-element.28.att_ref.refs_0_, bf16[128,128]{1,0:T(8,128)(2,1)S(1)} %collective-permute-done.8.refs_1_, bf16[128,256]{1,0:T(8,128)(2,1)S(1)} %gather.1.refs_2_, ...), custom_call_target="tpu_custom_call" | custom-call | tf_op jit(solution)/shard_map/finish/pallas_call | solution.py:347
  (8 shorter events, 0.1 us)
Async XLA Ops:
  0.6 0.8 %copy-start.2 = (bf16[128,128]{1,0:T(8,128)(2,1)S(1)}, bf16[128,128]{1,0:T(8,128)(2,1)}, u32[]{:S(2)}) copy-start(bf16[128,128]{1,0:T(8,128)(2,1)} %param.8) | copy-start | bytes 98308
  1.4 0.7 %copy-start.1 = (s32[1,8]{1,0:T(1,128)S(1)}, s32[1,8]{1,0:T(1,128)}, u32[]{:S(2)}) copy-start(s32[1,8]{1,0:T(1,128)} %refs_0_.1) | copy-start | bytes 100
  1.4 2.4 %collective-permute-start = (bf16[128,256]{1,0:T(8,128)(2,1)S(1)}, bf16[128,256]{1,0:T(8,128)(2,1)S(1)}, u32[]{:S(2)}, u32[]{:S(2)}) collective-permute-start(bf16[128,256]{1,0:T(8,128)(2,1)S(1)} %constant_dynamic-update-slice_fusion.refs_3_.own_ref), channel_id=1, source_target_pairs={{0,4},{4,0},{8,12},{12,8},{16,20},{20,16},{24,28},{28,24},{1,5},{5... | collective-permute-start | bytes 196616 | tf_op jit(solution)/shard_map/ppermute | solution.py:46
  3.9 8.4 %copy-start = (bf16[128,128]{1,0:T(8,128)(2,1)S(1)}, bf16[128,128]{1,0:T(8,128)(2,1)}, u32[]{:S(2)}) copy-start(bf16[128,128]{1,0:T(8,128)(2,1)} %refs_1_.3) | copy-start | bytes 98308
  3.9 8.3 %collective-permute-start.1 = (bf16[160,256]{1,0:T(8,128)(2,1)S(1)}, bf16[160,256]{1,0:T(8,128)(2,1)S(1)}, u32[]{:S(2)}, u32[]{:S(2)}) collective-permute-start(bf16[160,256]{1,0:T(8,128)(2,1)S(1)} %get-tuple-element.26), channel_id=1, source_target_pairs={{0,28},{4,8},{8,4},{12,16},{16,12},{20,24},{24,20},{28,0},{1,29},{... | collective-permute-start | bytes 245768 | tf_op jit(solution)/shard_map/ppermute | solution.py:46
  7.5 4.8 %collective-permute-start.2 = (bf16[64,256]{1,0:T(8,128)(2,1)S(1)}, bf16[64,256]{1,0:T(8,128)(2,1)S(1)}, u32[]{:S(2)}, u32[]{:S(2)}) collective-permute-start(bf16[64,256]{1,0:T(8,128)(2,1)S(1)} %get-tuple-element.27), channel_id=1, source_target_pairs={{0,12},{4,24},{8,20},{12,0},{16,28},{20,8},{24,4},{28,16},{1,13},{... | collective-permute-start | bytes 98312 | tf_op jit(solution)/shard_map/ppermute | solution.py:46
  8.2 4.1 %collective-permute-start.3 = (bf16[64,256]{1,0:T(8,128)(2,1)S(1)}, bf16[64,256]{1,0:T(8,128)(2,1)S(1)}, u32[]{:S(2)}, u32[]{:S(2)}) collective-permute-start(bf16[64,256]{1,0:T(8,128)(2,1)S(1)} %get-tuple-element.27), channel_id=1, source_target_pairs={{0,16},{4,20},{8,24},{12,28},{16,0},{20,4},{24,8},{28,12},{1,17},{... | collective-permute-start | bytes 98312 | tf_op jit(solution)/shard_map/ppermute | solution.py:46
  8.2 11.3 %collective-permute-start.7 = (bf16[80,512]{1,0:T(8,128)(2,1)S(1)}, bf16[80,512]{1,0:T(8,128)(2,1)S(1)}, u32[]{:S(2)}, u32[]{:S(2)}) collective-permute-start(bf16[80,512]{1,0:T(8,128)(2,1)S(1)} %get-tuple-element.35), channel_id=1, source_target_pairs={{0,3},{1,2},{2,1},{3,0},{4,7},{5,6},{6,5},{7,4},{8,11},{9,10},{10,... | collective-permute-start | bytes 245768 | tf_op jit(solution)/shard_map/ppermute | solution.py:53
  12.3 7.5 %collective-permute-start.6 = (bf16[128,512]{1,0:T(8,128)(2,1)S(1)}, bf16[128,512]{1,0:T(8,128)(2,1)S(1)}, u32[]{:S(2)}, u32[]{:S(2)}) collective-permute-start(bf16[128,512]{1,0:T(8,128)(2,1)S(1)} %get-tuple-element.34), channel_id=1, source_target_pairs={{0,1},{1,0},{2,3},{3,2},{4,6},{5,7},{6,4},{7,5},{8,9},{9,8},{10,11... | collective-permute-start | bytes 393224 | tf_op jit(solution)/shard_map/ppermute | solution.py:401
  13.3 6.4 %collective-permute-start.4 = (bf16[96,256]{1,0:T(8,128)(2,1)S(1)}, bf16[96,256]{1,0:T(8,128)(2,1)S(1)}, u32[]{:S(2)}, u32[]{:S(2)}) collective-permute-start(bf16[96,256]{1,0:T(8,128)(2,1)S(1)} %get-tuple-element.32), channel_id=1, source_target_pairs={{0,12},{4,24},{8,20},{12,0},{16,28},{20,8},{24,4},{28,16},{1,13},{... | collective-permute-start | bytes 147464 | tf_op jit(solution)/shard_map/ppermute | solution.py:46
  13.9 5.9 %collective-permute-start.5 = (bf16[64,256]{1,0:T(8,128)(2,1)S(1)}, bf16[64,256]{1,0:T(8,128)(2,1)S(1)}, u32[]{:S(2)}, u32[]{:S(2)}) collective-permute-start(bf16[64,256]{1,0:T(8,128)(2,1)S(1)} %get-tuple-element.33), channel_id=1, source_target_pairs={{0,20},{4,16},{8,28},{12,24},{16,4},{20,0},{24,12},{28,8},{1,21},{... | collective-permute-start | bytes 98312 | tf_op jit(solution)/shard_map/ppermute | solution.py:46
  16.1 6.7 %collective-permute-start.10 = (bf16[128,128]{1,0:T(8,128)(2,1)S(1)}, bf16[128,128]{1,0:T(8,128)(2,1)S(1)}, u32[]{:S(2)}, u32[]{:S(2)}) collective-permute-start(bf16[128,128]{1,0:T(8,128)(2,1)S(1)} %get-tuple-element.28.att_ref.refs_0_), channel_id=1, source_target_pairs={{0,3},{1,2},{2,1},{3,0},{4,7},{5,6},{6,5},{7,4},{8,11},{9,10},{10,... | collective-permute-start | bytes 98312 | tf_op jit(solution)/shard_map/ppermute | solution.py:53
  19.5 4.8 %collective-permute-start.9 = (bf16[128,128]{1,0:T(8,128)(2,1)S(1)}, bf16[128,128]{1,0:T(8,128)(2,1)S(1)}, u32[]{:S(2)}, u32[]{:S(2)}) collective-permute-start(bf16[128,128]{1,0:T(8,128)(2,1)S(1)} %get-tuple-element.28.att_ref.refs_0_), channel_id=1, source_target_pairs={{0,2},{1,3},{2,0},{3,1},{4,6},{5,7},{6,4},{7,5},{8,10},{9,11},{10,... | collective-permute-start | bytes 98312 | tf_op jit(solution)/shard_map/ppermute | solution.py:53
  19.8 6.5 %collective-permute-start.11 = (bf16[512,256]{1,0:T(8,128)(2,1)S(1)}, bf16[512,256]{1,0:T(8,128)(2,1)S(1)}, u32[]{:S(2)}, u32[]{:S(2)}) collective-permute-start(bf16[512,256]{1,0:T(8,128)(2,1)S(1)} %get-tuple-element.38), channel_id=1, source_target_pairs={{0,4},{4,0},{8,12},{12,8},{16,20},{20,16},{24,28},{28,24},{1,5},{5... | collective-permute-start | bytes 786440 | tf_op jit(solution)/shard_map/ppermute | solution.py:46
  19.9 6.5 %collective-permute-start.12 = (bf16[128,256]{1,0:T(8,128)(2,1)S(1)}, bf16[128,256]{1,0:T(8,128)(2,1)S(1)}, u32[]{:S(2)}, u32[]{:S(2)}) collective-permute-start(bf16[128,256]{1,0:T(8,128)(2,1)S(1)} %get-tuple-element.40), channel_id=1, source_target_pairs={{0,28},{4,8},{8,4},{12,16},{16,12},{20,24},{24,20},{28,0},{1,29},{... | collective-permute-start | bytes 196616 | tf_op jit(solution)/shard_map/ppermute | solution.py:46
  22.4 3.9 %collective-permute-start.8 = (bf16[128,128]{1,0:T(8,128)(2,1)S(1)}, bf16[128,128]{1,0:T(8,128)(2,1)S(1)}, u32[]{:S(2)}, u32[]{:S(2)}) collective-permute-start(bf16[128,128]{1,0:T(8,128)(2,1)S(1)} %get-tuple-element.36), channel_id=1, source_target_pairs={{0,1},{1,0},{2,3},{3,2},{4,5},{5,4},{6,7},{7,6},{8,9},{9,8},{10,11... | collective-permute-start | bytes 98312 | tf_op jit(solution)/shard_map/ppermute | solution.py:53

commit v12 on v11

--- a/solution.py
+++ b/solution.py
@@ -22,6 +22,7 @@
 ATTEND_COST = 10**10
 COMBINE_COST = 10**10
 GATHER_COST = 10**10
+PACK_COST = 10**10
 F32 = jnp.float32
 
 
@@ -248,7 +249,7 @@
 
 
 def combine_kernel(own_ref, first_ref, second_ref, plus_ref, minus_ref, whole_ref, half_ref,
-                   att_ref, own_out, first_out, second_out, att_out):
+                   att_ref, own_out, first_out, second_out, slices_out, att_out):
     plus = plus_ref[...].astype(F32)
     minus = minus_ref[...].astype(F32)
     n = STRIDE_ROWS
@@ -256,14 +257,14 @@
     own_out[:n] = own_ref[:n] + plus[:n] + minus[:n]
     second_out[n:] = second_ref[n:].astype(BF16)
     second_out[:n] = (second_ref[:n] + plus[2 * n:] + minus[n:]).astype(BF16)
-    first_out[n:BLK] = first_ref[n:].astype(BF16)
+    first_out[n:] = first_ref[n:].astype(BF16)
     first_out[:n] = (first_ref[:n] + plus[n:2 * n]).astype(BF16)
     att_out[...] = att_ref[...]
-    row = BLK
+    row = 0
     for ref, rows in ((whole_ref, slice(0, HD)), (half_ref, half_rows())):
         for c in range(0, ref.shape[1], PAIR):
             piece = ref[rows, c:c + PAIR]
-            first_out[row:row + piece.shape[0]] = piece
+            slices_out[row:row + piece.shape[0]] = piece
             row += piece.shape[0]
 
 
@@ -271,31 +272,49 @@
     extra = (HD + HD // 2) * whole.shape[1] // PAIR
     return pl.pallas_call(
         combine_kernel,
-        out_shape=(shape(BLK, PAIR, kind=F32), shape(BLK + extra, PAIR), shape(BLK, PAIR),
-                   shape(BLK, HD)),
+        out_shape=(shape(BLK, PAIR, kind=F32), shape(BLK, PAIR), shape(BLK, PAIR),
+                   shape(extra, PAIR), shape(BLK, HD)),
         in_specs=[VMEM] * 8,
-        out_specs=(VMEM,) * 4,
+        out_specs=(VMEM,) * 5,
         compiler_params=PARAMS,
         cost_estimate=cost(COMBINE_COST),
         name="combine",
     )(own, first, second, plus, minus, whole, half, att)
 
 
+def pack_kernel(first_ref, slices_ref, after_ref, out_ref):
+    del after_ref
+    out_ref[:BLK] = first_ref[...]
+    out_ref[BLK:] = slices_ref[...]
+
+
+def pack(first, slices, after):
+    return pl.pallas_call(
+        pack_kernel,
+        out_shape=shape(BLK + slices.shape[0], PAIR),
+        in_specs=[VMEM] * 3,
+        out_specs=VMEM,
+        compiler_params=PARAMS,
+        cost_estimate=cost(PACK_COST),
+        name="pack",
+    )(first, slices, after)
+
+
 def gather_kernel(*refs):
-    for r, ref in enumerate(refs[:-1]):
+    for r, ref in enumerate(refs[:-2]):
         refs[-1][:, r * HD:(r + 1) * HD] = ref[...]
 
 
-def gather(attentions):
+def gather(attentions, after):
     return pl.pallas_call(
         gather_kernel,
         out_shape=shape(BLK, len(attentions) * HD),
-        in_specs=[VMEM] * len(attentions),
+        in_specs=[VMEM] * (len(attentions) + 1),
         out_specs=VMEM,
         compiler_params=PARAMS,
         cost_estimate=cost(GATHER_COST),
         name="gather",
-    )(*attentions)
+    )(*attentions, after)
 
 
 def settle(total, lead, dk_ref, dv_ref):
@@ -305,9 +324,9 @@
 
 
 def finish_ring_kernel(*refs):
-    att_ref, near_ref, far_ref, mine_ref, whole_ref, half_ref = refs[:6]
-    first_ref, own_ref, second_ref, dq_ref = refs[6:10]
-    mixed_hbm, dq_hbm, dk_hbm, dv_hbm, mixed_ref, dk_ref, dv_ref, sems = refs[10:]
+    att_ref, others_ref, mine_ref, whole_ref, half_ref = refs[:5]
+    first_ref, own_ref, second_ref, dq_ref = refs[5:9]
+    mixed_hbm, dq_hbm, dk_hbm, dv_hbm, mixed_ref, dk_ref, dv_ref, sems = refs[9:]
     copies = []
 
     def send(src, dst):
@@ -320,7 +339,7 @@
     settle(total, total[:STRIDE_ROWS], dk_ref, dv_ref)
     send(dk_ref, dk_hbm)
     send(dv_ref, dv_hbm)
-    att = [att_ref[...], near_ref[...], far_ref[:, :HD], far_ref[:, HD:]]
+    att = [att_ref[...]] + [others_ref[:, r * HD:(r + 1) * HD] for r in range(3)]
     core = lax.axis_index("seq") & 1
     half = HD // 2
     here = jnp.where(core == 0, att[1], att[2])
@@ -347,7 +366,7 @@
     return pl.pallas_call(
         finish_ring_kernel,
         out_shape=(shape(BLK, width),) + (shape(BLK, HD),) * 3,
-        in_specs=[VMEM] * 10,
+        in_specs=[VMEM] * 9,
         out_specs=(HBM,) * 4,
         scratch_shapes=[
             pltpu.VMEM((BLK, width), BF16),
@@ -427,14 +446,16 @@
         att, dq, own_sum, first_sum, second_sum, to_plus, to_minus = attend(
             mult, queries, grad, blocks, pieces, 3
         )
-        far = gather([swap(att, 2), swap(att, 3)])
-        own_sum, to_first, to_second, last = combine(
+        far = [swap(att, 2), swap(att, 3)]
+        own_sum, to_first, to_second, out_slices, last = combine(
             own_sum, first_sum, second_sum, trade(to_plus, 3), trade(to_minus, -3), whole, half,
             att,
         )
+        from_second = trade(to_second, -1)
+        packed = trade(pack(to_first, out_slices, far[1]), 1)
+        others = gather([swap(last, 1)] + far, from_second)
         mixed, dq, dk, dv = finish_ring(
-            [att, swap(last, 1), far], mine, whole, half, trade(to_first, 1), own_sum,
-            trade(to_second, -1), dq,
+            [att, others], mine, whole, half, packed, own_sum, from_second, dq
         )
     else:
         second = trade(own, -1)

time: 27.6 us -> 26.3 us (0.953)
  waiting for transfers between devices: 3.61 us -> 2.58 us
  starting transfers between devices: 18.2 us -> 17.9 us
    ppermute x8, starting transfers between devices: 10.1 us -> 8.12 us  [trade(): lax.ppermute(array, 'seq', [(i, (i + (step if i % 2 == 0 else -step)) % c...]
    ppermute x4, starting transfers between devices: 8.08 us -> 9.79 us  [swap(): return lax.ppermute(array, 'head', [(i, i ^ mask) for i in range(count)])]
    ppermute x4, waiting for transfers between devices: 3.59 us -> 2.4 us  [swap(): return lax.ppermute(array, 'head', [(i, i ^ mask) for i in range(count)])]
  transfers between devices with their start and end apart: 13 -> 13, of which waited for: 2 -> 3; matrix products, arithmetic and copies ran while one was open for 0% -> 0% of each run, Pallas kernels for 11% -> 11%
where the time goes in v12:
time: 26.3 us; the launch traced here: 26.1 us
  starting transfers between devices  17.9 us (68%)
  Pallas kernels  3.96 us (15%)
  waiting for transfers between devices  2.58 us (10%)
  local copies, waits for them, and re-layouts  0.91 us (3%)
  between operations  0.76 us (3%)
    ppermute x4, starting transfers between devices, swap(): return lax.ppermute(array, 'head', [(i, i ^ mask) for i in range(count)])  9.79 us
    ppermute x8, starting transfers between devices, trade(): lax.ppermute(array, 'seq', [(i, (i + (step if i % 2 == 0 else -step)) % c...  8.12 us
    ppermute x4, waiting for transfers between devices, swap(): return lax.ppermute(array, 'head', [(i, i ^ mask) for i in range(count)])  2.4 us
    pallas_call x1, Pallas kernels, prepare(): pl.pallas_call(body, out_shape=(shape(BLK, HD), shape(8, columns, kind=F3...  1.8 us
    pallas_call x1, Pallas kernels, finish_ring(): pl.pallas_call(finish_ring_kernel, out_shape=(shape(BLK, width),) + (shap...  1.03 us
    pallas_call x1, Pallas kernels, attend(): pl.pallas_call(body, out_shape=(shape(BLK, HD), shape(BLK, HD), *sums), i...  1.02 us
    unnamed x7, local copies, waits for them, and re-layouts  0.89 us
  transfers between devices with their start and end apart: 13, of which 3 were waited for; matrix products, arithmetic and copies ran while one was open for 0% of the time, Pallas kernels for 11%

profile of v12, /device:TPU:0, one launch (start us, length us, event | category | flops | bytes accessed | tf_op | source)
XLA Modules:
  0.0 26.1 jit_solution(8791587695804592828)
XLA Ops:
  0.6 0.8 %constant_dynamic-update-slice_fusion.1 = bf16[128,256]{1,0:T(8,128)(2,1)S(1)} fusion(bf16[128,128]{1,0:T(8,128)(2,1)} %param.7), kind=kLoop, calls=%fused_computation.1 | loop fusion | bytes 65536
  1.4 0.0 copy-start.1
  1.4 0.5 %collective-permute-start = (bf16[128,256]{1,0:T(8,128)(2,1)S(1)}, bf16[128,256]{1,0:T(8,128)(2,1)S(1)}, u32[]{:S(2)}, u32[]{:S(2)}) collective-permute-start(bf16[128,256]{1,0:T(8,128)(2,1)S(1)} %constant_dynamic-update-slice_fusion.refs_3_.own_ref), channel_id=1, source_target_pairs={{0,4},{4,0},{8,12},{12,8},{16,20},{20,16},{24,28},{28,24},{1,5},{5... | collective-permute-start | bytes 196616 | tf_op jit(solution)/shard_map/ppermute | solution.py:47
  2.0 0.1 copy-done.1
  2.1 1.8 %prepare.1 = (bf16[128,128]{1,0:T(8,128)(2,1)S(1)}, f32[8,640]{1,0:T(8,128)S(1)}, bf16[128,512]{1,0:T(8,128)(2,1)S(1)}, bf16[128,512]{1,0:T(8,128)(2,1)S(1)}, bf16[80,512]{1,0:T(8,128)(2,1)S(1)}) custom-call(s32[1,8]{1,0:T(1,128)S(1)} %copy-done.1, bf16[128,2048]{1,0:T(8,128)(2,1)} %refs_1_.2, bf16[128,2048]{1,0:T(8,128)(2,1)} %refs_2_.1, ...), custom_call_target="tpu_custom_call" | custom-call | flops 10000000000 | tf_op jit(solution)/shard_map/prepare/pallas_call | solution.py:146
  3.9 0.0 collective-permute-done.first_ref.refs_4_
  3.9 0.0 copy-start
  3.9 3.5 %collective-permute-start.1 = (bf16[160,256]{1,0:T(8,128)(2,1)S(1)}, bf16[160,256]{1,0:T(8,128)(2,1)S(1)}, u32[]{:S(2)}, u32[]{:S(2)}) collective-permute-start(bf16[160,256]{1,0:T(8,128)(2,1)S(1)} %get-tuple-element.27), channel_id=1, source_target_pairs={{0,28},{4,8},{8,4},{12,16},{16,12},{20,24},{24,20},{28,0},{1,29},{... | collective-permute-start | bytes 245768 | tf_op jit(solution)/shard_map/ppermute | solution.py:47
  7.5 0.7 %collective-permute-start.2 = (bf16[64,256]{1,0:T(8,128)(2,1)S(1)}, bf16[64,256]{1,0:T(8,128)(2,1)S(1)}, u32[]{:S(2)}, u32[]{:S(2)}) collective-permute-start(bf16[64,256]{1,0:T(8,128)(2,1)S(1)} %get-tuple-element.28), channel_id=1, source_target_pairs={{0,12},{4,24},{8,20},{12,0},{16,28},{20,8},{24,4},{28,16},{1,13},{... | collective-permute-start | bytes 98312 | tf_op jit(solution)/shard_map/ppermute | solution.py:47
  8.2 0.0 collective-permute-start.3
  8.2 4.1 %collective-permute-start.7 = (bf16[80,512]{1,0:T(8,128)(2,1)S(1)}, bf16[80,512]{1,0:T(8,128)(2,1)S(1)}, u32[]{:S(2)}, u32[]{:S(2)}) collective-permute-start(bf16[80,512]{1,0:T(8,128)(2,1)S(1)} %get-tuple-element.36), channel_id=1, source_target_pairs={{0,3},{1,2},{2,1},{3,0},{4,7},{5,6},{6,5},{7,4},{8,11},{9,10},{10,... | collective-permute-start | bytes 245768 | tf_op jit(solution)/shard_map/ppermute | solution.py:54
  12.3 0.0 collective-permute-start.6
  12.3 0.0 collective-permute-done.3.refs_7_
  12.3 0.0 collective-permute-done.1.refs_5_
  12.3 1.0 %attend.1 = (bf16[128,128]{1,0:T(8,128)(2,1)S(1)}, bf16[128,128]{1,0:T(8,128)(2,1)S(1)}, f32[128,256]{1,0:T(8,128)S(1)}, f32[128,256]{1,0:T(8,128)S(1)}, f32[128...) custom-call(f32[8,640]{1,0:T(8,128)S(1)} %get-tuple-element.24.mult_ref.refs_0_, ...), custom_call_target="tpu_custom_call" | custom-call | flops 10000000000 | tf_op jit(solution)/shard_map/attend/pallas_call | solution.py:234
  13.3 0.6 %collective-permute-start.4 = (bf16[96,256]{1,0:T(8,128)(2,1)S(1)}, bf16[96,256]{1,0:T(8,128)(2,1)S(1)}, u32[]{:S(2)}, u32[]{:S(2)}) collective-permute-start(bf16[96,256]{1,0:T(8,128)(2,1)S(1)} %get-tuple-element.33), channel_id=1, source_target_pairs={{0,12},{4,24},{8,20},{12,0},{16,28},{20,8},{24,4},{28,16},{1,13},{... | collective-permute-start | bytes 147464 | tf_op jit(solution)/shard_map/ppermute | solution.py:47
  13.9 2.2 %collective-permute-start.5 = (bf16[64,256]{1,0:T(8,128)(2,1)S(1)}, bf16[64,256]{1,0:T(8,128)(2,1)S(1)}, u32[]{:S(2)}, u32[]{:S(2)}) collective-permute-start(bf16[64,256]{1,0:T(8,128)(2,1)S(1)} %get-tuple-element.34), channel_id=1, source_target_pairs={{0,20},{4,16},{8,28},{12,24},{16,4},{20,0},{24,12},{28,8},{1,21},{... | collective-permute-start | bytes 98312 | tf_op jit(solution)/shard_map/ppermute | solution.py:47
  16.1 3.4 %collective-permute-start.10 = (bf16[128,128]{1,0:T(8,128)(2,1)S(1)}, bf16[128,128]{1,0:T(8,128)(2,1)S(1)}, u32[]{:S(2)}, u32[]{:S(2)}) collective-permute-start(bf16[128,128]{1,0:T(8,128)(2,1)S(1)} %get-tuple-element.29.att_ref.refs_0_), channel_id=1, source_target_pairs={{0,3},{1,2},{2,1},{3,0},{4,7},{5,6},{6,5},{7,4},{8,11},{9,10},{10,... | collective-permute-start | bytes 98312 | tf_op jit(solution)/shard_map/ppermute | solution.py:54
  19.5 0.0 collective-permute-done.7.half_ref.refs_4_
  19.5 0.3 collective-permute-start.9
  19.7 0.0 collective-permute-done.5.minus_ref
  19.7 0.0 collective-permute-done.4.plus_ref
  19.7 0.0 collective-permute-done.6.whole_ref.refs_3_
  19.8 0.6 %collective-permute-start.11 = (bf16[128,256]{1,0:T(8,128)(2,1)S(1)}, bf16[128,256]{1,0:T(8,128)(2,1)S(1)}, u32[]{:S(2)}, u32[]{:S(2)}) collective-permute-start(bf16[128,256]{1,0:T(8,128)(2,1)S(1)} %get-tuple-element.38), channel_id=1, source_target_pairs={{0,28},{4,8},{8,4},{12,16},{16,12},{20,24},{24,20},{28,0},{1,29},{... | collective-permute-start | bytes 196616 | tf_op jit(solution)/shard_map/ppermute | solution.py:47
  20.4 2.0 %collective-permute-start.8 = (bf16[128,128]{1,0:T(8,128)(2,1)S(1)}, bf16[128,128]{1,0:T(8,128)(2,1)S(1)}, u32[]{:S(2)}, u32[]{:S(2)}) collective-permute-start(bf16[128,128]{1,0:T(8,128)(2,1)S(1)} %get-tuple-element.37), channel_id=1, source_target_pairs={{0,1},{1,0},{2,3},{3,2},{4,5},{5,4},{6,7},{7,6},{8,9},{9,8},{10,11... | collective-permute-start | bytes 98312 | tf_op jit(solution)/shard_map/ppermute | solution.py:54
  22.4 0.0 collective-permute-done.10.refs_2_.after_ref
  22.4 0.1 collective-permute-start.12
  22.5 1.9 %collective-permute-done.9.refs_1_ = bf16[128,128]{1,0:T(8,128)(2,1)S(1)} collective-permute-done((bf16[128,128]{1,0:T(8,128)(2,1)S(1)}, bf16[128,128]{1,0:T(8,128)(2,1)S(1)}, u32[]{:S(2)}, u32[]{:S(2)}) %collective-permute-start.9) | collective-permute-done | bytes 32800 | tf_op jit(solution)/shard_map/ppermute | solution.py:54
  24.4 0.5 %collective-permute-done.8.refs_0_ = bf16[128,128]{1,0:T(8,128)(2,1)S(1)} collective-permute-done((bf16[128,128]{1,0:T(8,128)(2,1)S(1)}, bf16[128,128]{1,0:T(8,128)(2,1)S(1)}, u32[]{:S(2)}, u32[]{:S(2)}) %collective-permute-start.8) | collective-permute-done | bytes 32800 | tf_op jit(solution)/shard_map/ppermute | solution.py:54
  24.9 0.2 collective-permute-done.11.refs_3_.refs_7_
  25.1 0.0 collective-permute-done.12.refs_5_
  25.1 1.0 %finish.1 = (bf16[128,512]{1,0:T(8,128)(2,1)}, bf16[128,128]{1,0:T(8,128)(2,1)}, bf16[128,128]{1,0:T(8,128)(2,1)}, bf16[128,128]{1,0:T(8,128)(2,1)}) custom-call(bf16[128,128]{1,0:T(8,128)(2,1)S(1)} %get-tuple-element.29.att_ref.refs_0_, bf16[128,384]{1,0:T(8,128)(2,1)S(1)} %gather.1.refs_1_, bf16[128,512]{1,0:T(8,128)(2,1)S(1)} %get-tuple-element.39.refs_2_, ...), custom_call_target="tpu_custom_call" | custom-call | tf_op jit(solution)/shard_map/finish/pallas_call | solution.py:366
  (9 shorter events, 0.1 us)
Async XLA Ops:
  0.6 0.8 %copy-start.2 = (bf16[128,128]{1,0:T(8,128)(2,1)S(1)}, bf16[128,128]{1,0:T(8,128)(2,1)}, u32[]{:S(2)}) copy-start(bf16[128,128]{1,0:T(8,128)(2,1)} %param.8) | copy-start | bytes 98308
  1.4 0.7 %copy-start.1 = (s32[1,8]{1,0:T(1,128)S(1)}, s32[1,8]{1,0:T(1,128)}, u32[]{:S(2)}) copy-start(s32[1,8]{1,0:T(1,128)} %refs_0_.1) | copy-start | bytes 100
  1.4 2.4 %collective-permute-start = (bf16[128,256]{1,0:T(8,128)(2,1)S(1)}, bf16[128,256]{1,0:T(8,128)(2,1)S(1)}, u32[]{:S(2)}, u32[]{:S(2)}) collective-permute-start(bf16[128,256]{1,0:T(8,128)(2,1)S(1)} %constant_dynamic-update-slice_fusion.refs_3_.own_ref), channel_id=1, source_target_pairs={{0,4},{4,0},{8,12},{12,8},{16,20},{20,16},{24,28},{28,24},{1,5},{5... | collective-permute-start | bytes 196616 | tf_op jit(solution)/shard_map/ppermute | solution.py:47
  3.9 8.4 %copy-start = (bf16[128,128]{1,0:T(8,128)(2,1)S(1)}, bf16[128,128]{1,0:T(8,128)(2,1)}, u32[]{:S(2)}) copy-start(bf16[128,128]{1,0:T(8,128)(2,1)} %refs_1_.3) | copy-start | bytes 98308
  3.9 8.3 %collective-permute-start.1 = (bf16[160,256]{1,0:T(8,128)(2,1)S(1)}, bf16[160,256]{1,0:T(8,128)(2,1)S(1)}, u32[]{:S(2)}, u32[]{:S(2)}) collective-permute-start(bf16[160,256]{1,0:T(8,128)(2,1)S(1)} %get-tuple-element.27), channel_id=1, source_target_pairs={{0,28},{4,8},{8,4},{12,16},{16,12},{20,24},{24,20},{28,0},{1,29},{... | collective-permute-start | bytes 245768 | tf_op jit(solution)/shard_map/ppermute | solution.py:47
  7.5 4.8 %collective-permute-start.2 = (bf16[64,256]{1,0:T(8,128)(2,1)S(1)}, bf16[64,256]{1,0:T(8,128)(2,1)S(1)}, u32[]{:S(2)}, u32[]{:S(2)}) collective-permute-start(bf16[64,256]{1,0:T(8,128)(2,1)S(1)} %get-tuple-element.28), channel_id=1, source_target_pairs={{0,12},{4,24},{8,20},{12,0},{16,28},{20,8},{24,4},{28,16},{1,13},{... | collective-permute-start | bytes 98312 | tf_op jit(solution)/shard_map/ppermute | solution.py:47
  8.2 4.1 %collective-permute-start.3 = (bf16[64,256]{1,0:T(8,128)(2,1)S(1)}, bf16[64,256]{1,0:T(8,128)(2,1)S(1)}, u32[]{:S(2)}, u32[]{:S(2)}) collective-permute-start(bf16[64,256]{1,0:T(8,128)(2,1)S(1)} %get-tuple-element.28), channel_id=1, source_target_pairs={{0,16},{4,20},{8,24},{12,28},{16,0},{20,4},{24,8},{28,12},{1,17},{... | collective-permute-start | bytes 98312 | tf_op jit(solution)/shard_map/ppermute | solution.py:47
  8.2 11.3 %collective-permute-start.7 = (bf16[80,512]{1,0:T(8,128)(2,1)S(1)}, bf16[80,512]{1,0:T(8,128)(2,1)S(1)}, u32[]{:S(2)}, u32[]{:S(2)}) collective-permute-start(bf16[80,512]{1,0:T(8,128)(2,1)S(1)} %get-tuple-element.36), channel_id=1, source_target_pairs={{0,3},{1,2},{2,1},{3,0},{4,7},{5,6},{6,5},{7,4},{8,11},{9,10},{10,... | collective-permute-start | bytes 245768 | tf_op jit(solution)/shard_map/ppermute | solution.py:54
  12.3 7.5 %collective-permute-start.6 = (bf16[128,512]{1,0:T(8,128)(2,1)S(1)}, bf16[128,512]{1,0:T(8,128)(2,1)S(1)}, u32[]{:S(2)}, u32[]{:S(2)}) collective-permute-start(bf16[128,512]{1,0:T(8,128)(2,1)S(1)} %get-tuple-element.35), channel_id=1, source_target_pairs={{0,1},{1,0},{2,3},{3,2},{4,6},{5,7},{6,4},{7,5},{8,9},{9,8},{10,11... | collective-permute-start | bytes 393224 | tf_op jit(solution)/shard_map/ppermute | solution.py:420
  13.3 6.4 %collective-permute-start.4 = (bf16[96,256]{1,0:T(8,128)(2,1)S(1)}, bf16[96,256]{1,0:T(8,128)(2,1)S(1)}, u32[]{:S(2)}, u32[]{:S(2)}) collective-permute-start(bf16[96,256]{1,0:T(8,128)(2,1)S(1)} %get-tuple-element.33), channel_id=1, source_target_pairs={{0,12},{4,24},{8,20},{12,0},{16,28},{20,8},{24,4},{28,16},{1,13},{... | collective-permute-start | bytes 147464 | tf_op jit(solution)/shard_map/ppermute | solution.py:47
  13.9 5.9 %collective-permute-start.5 = (bf16[64,256]{1,0:T(8,128)(2,1)S(1)}, bf16[64,256]{1,0:T(8,128)(2,1)S(1)}, u32[]{:S(2)}, u32[]{:S(2)}) collective-permute-start(bf16[64,256]{1,0:T(8,128)(2,1)S(1)} %get-tuple-element.34), channel_id=1, source_target_pairs={{0,20},{4,16},{8,28},{12,24},{16,4},{20,0},{24,12},{28,8},{1,21},{... | collective-permute-start | bytes 98312 | tf_op jit(solution)/shard_map/ppermute | solution.py:47
  16.1 6.3 %collective-permute-start.10 = (bf16[128,128]{1,0:T(8,128)(2,1)S(1)}, bf16[128,128]{1,0:T(8,128)(2,1)S(1)}, u32[]{:S(2)}, u32[]{:S(2)}) collective-permute-start(bf16[128,128]{1,0:T(8,128)(2,1)S(1)} %get-tuple-element.29.att_ref.refs_0_), channel_id=1, source_target_pairs={{0,3},{1,2},{2,1},{3,0},{4,7},{5,6},{6,5},{7,4},{8,11},{9,10},{10,... | collective-permute-start | bytes 98312 | tf_op jit(solution)/shard_map/ppermute | solution.py:54
  19.5 4.9 %collective-permute-start.9 = (bf16[128,128]{1,0:T(8,128)(2,1)S(1)}, bf16[128,128]{1,0:T(8,128)(2,1)S(1)}, u32[]{:S(2)}, u32[]{:S(2)}) collective-permute-start(bf16[128,128]{1,0:T(8,128)(2,1)S(1)} %get-tuple-element.29.att_ref.refs_0_), channel_id=1, source_target_pairs={{0,2},{1,3},{2,0},{3,1},{4,6},{5,7},{6,4},{7,5},{8,10},{9,11},{10,... | collective-permute-start | bytes 98312 | tf_op jit(solution)/shard_map/ppermute | solution.py:54
  19.8 5.3 %collective-permute-start.11 = (bf16[128,256]{1,0:T(8,128)(2,1)S(1)}, bf16[128,256]{1,0:T(8,128)(2,1)S(1)}, u32[]{:S(2)}, u32[]{:S(2)}) collective-permute-start(bf16[128,256]{1,0:T(8,128)(2,1)S(1)} %get-tuple-element.38), channel_id=1, source_target_pairs={{0,28},{4,8},{8,4},{12,16},{16,12},{20,24},{24,20},{28,0},{1,29},{... | collective-permute-start | bytes 196616 | tf_op jit(solution)/shard_map/ppermute | solution.py:47
  20.4 4.5 %collective-permute-start.8 = (bf16[128,128]{1,0:T(8,128)(2,1)S(1)}, bf16[128,128]{1,0:T(8,128)(2,1)S(1)}, u32[]{:S(2)}, u32[]{:S(2)}) collective-permute-start(bf16[128,128]{1,0:T(8,128)(2,1)S(1)} %get-tuple-element.37), channel_id=1, source_target_pairs={{0,1},{1,0},{2,3},{3,2},{4,5},{5,4},{6,7},{7,6},{8,9},{9,8},{10,11... | collective-permute-start | bytes 98312 | tf_op jit(solution)/shard_map/ppermute | solution.py:54
  22.4 2.7 %collective-permute-start.12 = (bf16[512,256]{1,0:T(8,128)(2,1)S(1)}, bf16[512,256]{1,0:T(8,128)(2,1)S(1)}, u32[]{:S(2)}, u32[]{:S(2)}) collective-permute-start(bf16[512,256]{1,0:T(8,128)(2,1)S(1)} %pack.1), channel_id=1, source_target_pairs={{0,4},{4,0},{8,12},{12,8},{16,20},{20,16},{24,28},{28,24},{1,5},{5... | collective-permute-start | bytes 786440 | tf_op jit(solution)/shard_map/ppermute | solution.py:47

commit v13 on v12

--- a/solution.py
+++ b/solution.py
@@ -98,25 +98,18 @@
     index_ref, cot_ref, w_ref, sems = refs[-4:]
     slice_refs = refs[:-4]
     copies = [(index_hbm, index_ref)]
-    depth = cot_ref.shape[1] // CHUNKS
-    for i in range(CHUNKS):
-        span = pl.ds(i * depth, depth)
-        copies.append((w_hbm.at[:, span], w_ref.at[:, span]))
-        copies.append((cot_hbm.at[:, span], cot_ref.at[:, span]))
+    for src, dst in ((w_hbm, w_ref), (cot_hbm, cot_ref)):
+        rows = dst.shape[0] // CHUNKS
+        for i in range(CHUNKS):
+            span = pl.ds(i * rows, rows)
+            copies.append((src.at[span], dst.at[span]))
     copies = [pltpu.make_async_copy(src, dst, sems.at[i]) for i, (src, dst) in enumerate(copies)]
     for copy in copies:
         copy.start()
     copies[0].wait()
     fill_multiplicity(ring, index_ref, mult_ref)
-    total = None
-    for i in range(CHUNKS):
-        copies[1 + 2 * i].wait()
-        copies[2 + 2 * i].wait()
-        span = slice(i * depth, (i + 1) * depth)
-        term = dot_nt(cot_ref[:, span], w_ref[:, span])
-        total = term if total is None else total + term
-    grad_ref[...] = total.astype(grad_ref.dtype)
-
+    for copy in copies[1:1 + CHUNKS]:
+        copy.wait()
     width = slice_refs[0].shape[1]
     head = lax.axis_index("head")
 
@@ -134,6 +127,9 @@
     else:
         for r, ref in enumerate(slice_refs):
             ref[...] = w_ref[:, columns(head ^ r)]
+    for copy in copies[1 + CHUNKS:]:
+        copy.wait()
+    grad_ref[...] = dot_nt(cot_ref[...], w_ref[...]).astype(grad_ref.dtype)
 
 
 def prepare(ring, index, cotangent, out_weight, heads, columns, after):
@@ -300,21 +296,41 @@
     )(first, slices, after)
 
 
-def gather_kernel(*refs):
-    for r, ref in enumerate(refs[:-2]):
-        refs[-1][:, r * HD:(r + 1) * HD] = ref[...]
-
-
-def gather(attentions, after):
+def project_kernel(att_ref, two_ref, three_ref, mine_ref, whole_ref, half_ref, out_ref):
+    core = lax.axis_index("seq") & 1
+    half = HD // 2
+    two = jnp.where(core == 0, jnp.zeros((BLK, HD), BF16), two_ref[...])
+    three = jnp.where(core == 0, three_ref[:, :half], three_ref[:, half:])
+    total = dot_nn(att_ref[...], mine_ref[...]) + dot_nn(two, whole_ref[...])
+    out_ref[...] = total + dot_nn(three, half_ref[half_rows(), :])
+
+
+def project(att, two, three, mine, whole, half):
+    return pl.pallas_call(
+        project_kernel,
+        out_shape=shape(BLK, mine.shape[1], kind=F32),
+        in_specs=[VMEM] * 6,
+        out_specs=VMEM,
+        compiler_params=PARAMS,
+        name="project",
+    )(att, two, three, mine, whole, half)
+
+
+def gather_kernel(one_ref, second_ref, partial_ref, out_ref):
+    del second_ref, partial_ref
+    out_ref[...] = one_ref[...]
+
+
+def gather(one, second, partial):
     return pl.pallas_call(
         gather_kernel,
-        out_shape=shape(BLK, len(attentions) * HD),
-        in_specs=[VMEM] * (len(attentions) + 1),
+        out_shape=shape(BLK, HD),
+        in_specs=[VMEM] * 3,
         out_specs=VMEM,
         compiler_params=PARAMS,
         cost_estimate=cost(GATHER_COST),
         name="gather",
-    )(*attentions, after)
+    )(one, second, partial)
 
 
 def settle(total, lead, dk_ref, dv_ref):
@@ -323,10 +339,9 @@
         ref[STRIDE_ROWS:] = total[STRIDE_ROWS:, c:c + HD].astype(ref.dtype)
 
 
-def finish_ring_kernel(*refs):
-    att_ref, others_ref, mine_ref, whole_ref, half_ref = refs[:5]
-    first_ref, own_ref, second_ref, dq_ref = refs[5:9]
-    mixed_hbm, dq_hbm, dk_hbm, dv_hbm, mixed_ref, dk_ref, dv_ref, sems = refs[9:]
+def finish_ring_kernel(partial_ref, one_ref, two_ref, three_ref, whole_ref, first_ref, own_ref,
+                       second_ref, dq_ref, mixed_hbm, dq_hbm, dk_hbm, dv_hbm,
+                       mixed_ref, dk_ref, dv_ref, sems):
     copies = []
 
     def send(src, dst):
@@ -335,38 +350,36 @@
         copies.append(copy)
 
     send(dq_ref, dq_hbm)
+    core = lax.axis_index("seq") & 1
+    half = HD // 2
+    one, two, three = one_ref[...], two_ref[...], three_ref[...]
+    here = jnp.where(core == 0, one, jnp.zeros_like(one))
+    there = jnp.where(core == 0, two, one)
+    there_half = jnp.where(core == 0, three[:, half:], three[:, :half])
+    width = whole_ref.shape[1]
+    half_row = BLK + (width // PAIR) * HD
+    for i, c in enumerate(range(0, width, PAIR)):
+        span = slice(c, c + PAIR)
+        other_whole = first_ref[BLK + i * HD:BLK + (i + 1) * HD]
+        other_half = first_ref[half_row + i * half:half_row + (i + 1) * half]
+        mixed = partial_ref[:, span] + dot_nn(here, whole_ref[:, span])
+        mixed = mixed + dot_nn(there, other_whole) + dot_nn(there_half, other_half)
+        mixed_ref[:, span] = mixed.astype(mixed_ref.dtype)
+        send(mixed_ref.at[:, pl.ds(c, PAIR)], mixed_hbm.at[:, pl.ds(c, PAIR)])
     total = own_ref[...] + first_ref[:BLK].astype(F32) + second_ref[...].astype(F32)
     settle(total, total[:STRIDE_ROWS], dk_ref, dv_ref)
     send(dk_ref, dk_hbm)
     send(dv_ref, dv_hbm)
-    att = [att_ref[...]] + [others_ref[:, r * HD:(r + 1) * HD] for r in range(3)]
-    core = lax.axis_index("seq") & 1
-    half = HD // 2
-    here = jnp.where(core == 0, att[1], att[2])
-    there = jnp.where(core == 0, att[2], att[1])
-    here_half = jnp.where(core == 0, att[3][:, :half], att[3][:, half:])
-    there_half = jnp.where(core == 0, att[3][:, half:], att[3][:, :half])
-    whole_row = BLK
-    half_row = BLK + (mine_ref.shape[1] // PAIR) * HD
-    for i, c in enumerate(range(0, mine_ref.shape[1], PAIR)):
-        span = slice(c, c + PAIR)
-        other_whole = first_ref[whole_row + i * HD:whole_row + (i + 1) * HD]
-        other_half = first_ref[half_row + i * half:half_row + (i + 1) * half]
-        mixed = dot_nn(att[0], mine_ref[:, span]) + dot_nn(here, whole_ref[:, span])
-        mixed = mixed + dot_nn(there, other_whole) + dot_nn(here_half, half_ref[half_rows(), span])
-        mixed = mixed + dot_nn(there_half, other_half)
-        mixed_ref[:, span] = mixed.astype(mixed_ref.dtype)
-        send(mixed_ref.at[:, pl.ds(c, PAIR)], mixed_hbm.at[:, pl.ds(c, PAIR)])
     for copy in copies:
         copy.wait()
 
 
-def finish_ring(attentions, mine, whole, half, first, own, second, dq):
-    width = mine.shape[1]
+def finish_ring(*args):
+    width = args[0].shape[1]
     return pl.pallas_call(
         finish_ring_kernel,
         out_shape=(shape(BLK, width),) + (shape(BLK, HD),) * 3,
-        in_specs=[VMEM] * 9,
+        in_specs=[VMEM] * len(args),
         out_specs=(HBM,) * 4,
         scratch_shapes=[
             pltpu.VMEM((BLK, width), BF16),
@@ -376,7 +389,7 @@
         ],
         compiler_params=PARAMS,
         name="finish",
-    )(*attentions, mine, whole, half, first, own, second, dq)
+    )(*args)
 
 
 def finish_kernel(count, *refs):
@@ -453,9 +466,10 @@
         )
         from_second = trade(to_second, -1)
         packed = trade(pack(to_first, out_slices, far[1]), 1)
-        others = gather([swap(last, 1)] + far, from_second)
+        partial = project(att, *far, mine, whole, half)
+        one = gather(swap(last, 1), from_second, partial)
         mixed, dq, dk, dv = finish_ring(
-            [att, others], mine, whole, half, packed, own_sum, from_second, dq
+            partial, one, *far, whole, packed, own_sum, from_second, dq
         )
     else:
         second = trade(own, -1)

time: 26.3 us -> 26.2 us (level)
  transfers between devices with their start and end apart: 13 -> 13, of which waited for: 3 -> 3; matrix products, arithmetic and copies ran while one was open for 0% -> 0% of each run, Pallas kernels for 11% -> 12%
where the time goes in v13:
time: 26.2 us; the launch traced here: 25.9 us
  starting transfers between devices  17.9 us (68%)
  Pallas kernels  4.05 us (15%)
  waiting for transfers between devices  2.33 us (9%)
  local copies, waits for them, and re-layouts  0.91 us (3%)
  between operations  0.75 us (3%)
    ppermute x4, starting transfers between devices, swap(): return lax.ppermute(array, 'head', [(i, i ^ mask) for i in range(count)])  9.78 us
    ppermute x8, starting transfers between devices, trade(): lax.ppermute(array, 'seq', [(i, (i + (step if i % 2 == 0 else -step)) % c...  8.12 us
    ppermute x4, waiting for transfers between devices, swap(): return lax.ppermute(array, 'head', [(i, i ^ mask) for i in range(count)])  2.24 us
    pallas_call x1, Pallas kernels, prepare(): pl.pallas_call(body, out_shape=(shape(BLK, HD), shape(8, columns, kind=F3...  1.66 us
    pallas_call x1, Pallas kernels, finish_ring(): pl.pallas_call(finish_ring_kernel, out_shape=(shape(BLK, width),) + (shap...  1.03 us
    pallas_call x1, Pallas kernels, attend(): pl.pallas_call(body, out_shape=(shape(BLK, HD), shape(BLK, HD), *sums), i...  1.02 us
    unnamed x7, local copies, waits for them, and re-layouts  0.89 us
  transfers between devices with their start and end apart: 13, of which 3 were waited for; matrix products, arithmetic and copies ran while one was open for 0% of the time, Pallas kernels for 12%

profile of v13, /device:TPU:0, one launch (start us, length us, event | category | flops | bytes accessed | tf_op | source)
XLA Modules:
  0.0 25.9 jit_solution(4550026172719634996)
XLA Ops:
  0.6 0.8 %constant_dynamic-update-slice_fusion.1 = bf16[128,256]{1,0:T(8,128)(2,1)S(1)} fusion(bf16[128,128]{1,0:T(8,128)(2,1)} %param.7), kind=kLoop, calls=%fused_computation.1 | loop fusion | bytes 65536
  1.4 0.0 copy-start.1
  1.4 0.5 %collective-permute-start = (bf16[128,256]{1,0:T(8,128)(2,1)S(1)}, bf16[128,256]{1,0:T(8,128)(2,1)S(1)}, u32[]{:S(2)}, u32[]{:S(2)}) collective-permute-start(bf16[128,256]{1,0:T(8,128)(2,1)S(1)} %constant_dynamic-update-slice_fusion.refs_3_.own_ref), channel_id=1, source_target_pairs={{0,4},{4,0},{8,12},{12,8},{16,20},{20,16},{24,28},{28,24},{1,5},{5... | collective-permute-start | bytes 196616 | tf_op jit(solution)/shard_map/ppermute | solution.py:47
  2.0 0.1 copy-done.1
  2.1 1.7 %prepare.1 = (bf16[128,128]{1,0:T(8,128)(2,1)S(1)}, f32[8,640]{1,0:T(8,128)S(1)}, bf16[128,512]{1,0:T(8,128)(2,1)S(1)}, bf16[128,512]{1,0:T(8,128)(2,1)S(1)}, bf16[80,512]{1,0:T(8,128)(2,1)S(1)}) custom-call(s32[1,8]{1,0:T(1,128)S(1)} %copy-done.1, bf16[128,2048]{1,0:T(8,128)(2,1)} %refs_1_.2, bf16[128,2048]{1,0:T(8,128)(2,1)} %refs_2_.1, ...), custom_call_target="tpu_custom_call" | custom-call | flops 10000000000 | tf_op jit(solution)/shard_map/prepare/pallas_call | solution.py:142
  3.7 0.0 collective-permute-done.first_ref.refs_4_
  3.8 0.0 copy-start
  3.8 3.5 %collective-permute-start.1 = (bf16[160,256]{1,0:T(8,128)(2,1)S(1)}, bf16[160,256]{1,0:T(8,128)(2,1)S(1)}, u32[]{:S(2)}, u32[]{:S(2)}) collective-permute-start(bf16[160,256]{1,0:T(8,128)(2,1)S(1)} %get-tuple-element.27), channel_id=1, source_target_pairs={{0,28},{4,8},{8,4},{12,16},{16,12},{20,24},{24,20},{28,0},{1,29},{... | collective-permute-start | bytes 245768 | tf_op jit(solution)/shard_map/ppermute | solution.py:47
  7.3 0.7 %collective-permute-start.2 = (bf16[64,256]{1,0:T(8,128)(2,1)S(1)}, bf16[64,256]{1,0:T(8,128)(2,1)S(1)}, u32[]{:S(2)}, u32[]{:S(2)}) collective-permute-start(bf16[64,256]{1,0:T(8,128)(2,1)S(1)} %get-tuple-element.28), channel_id=1, source_target_pairs={{0,12},{4,24},{8,20},{12,0},{16,28},{20,8},{24,4},{28,16},{1,13},{... | collective-permute-start | bytes 98312 | tf_op jit(solution)/shard_map/ppermute | solution.py:47
  8.0 0.0 collective-permute-start.3
  8.0 4.1 %collective-permute-start.7 = (bf16[80,512]{1,0:T(8,128)(2,1)S(1)}, bf16[80,512]{1,0:T(8,128)(2,1)S(1)}, u32[]{:S(2)}, u32[]{:S(2)}) collective-permute-start(bf16[80,512]{1,0:T(8,128)(2,1)S(1)} %get-tuple-element.32), channel_id=1, source_target_pairs={{0,3},{1,2},{2,1},{3,0},{4,7},{5,6},{6,5},{7,4},{8,11},{9,10},{10,... | collective-permute-start | bytes 245768 | tf_op jit(solution)/shard_map/ppermute | solution.py:54
  12.1 0.0 collective-permute-start.6
  12.1 0.0 collective-permute-done.2.refs_6_
  12.1 0.0 collective-permute-done.3.refs_7_
  12.1 0.0 collective-permute-done.1.refs_5_
  12.2 1.0 %attend.1 = (bf16[128,128]{1,0:T(8,128)(2,1)S(1)}, bf16[128,128]{1,0:T(8,128)(2,1)S(1)}, f32[128,256]{1,0:T(8,128)S(1)}, f32[128,256]{1,0:T(8,128)S(1)}, f32[128...) custom-call(f32[8,640]{1,0:T(8,128)S(1)} %get-tuple-element.24.mult_ref.refs_0_, ...), custom_call_target="tpu_custom_call" | custom-call | flops 10000000000 | tf_op jit(solution)/shard_map/attend/pallas_call | solution.py:230
  13.2 0.5 %collective-permute-start.8 = (bf16[96,256]{1,0:T(8,128)(2,1)S(1)}, bf16[96,256]{1,0:T(8,128)(2,1)S(1)}, u32[]{:S(2)}, u32[]{:S(2)}) collective-permute-start(bf16[96,256]{1,0:T(8,128)(2,1)S(1)} %get-tuple-element.36), channel_id=1, source_target_pairs={{0,12},{4,24},{8,20},{12,0},{16,28},{20,8},{24,4},{28,16},{1,13},{... | collective-permute-start | bytes 147464 | tf_op jit(solution)/shard_map/ppermute | solution.py:47
  13.7 2.2 %collective-permute-start.9 = (bf16[64,256]{1,0:T(8,128)(2,1)S(1)}, bf16[64,256]{1,0:T(8,128)(2,1)S(1)}, u32[]{:S(2)}, u32[]{:S(2)}) collective-permute-start(bf16[64,256]{1,0:T(8,128)(2,1)S(1)} %get-tuple-element.37), channel_id=1, source_target_pairs={{0,20},{4,16},{8,28},{12,24},{16,4},{20,0},{24,12},{28,8},{1,21},{... | collective-permute-start | bytes 98312 | tf_op jit(solution)/shard_map/ppermute | solution.py:47
  15.9 3.4 %collective-permute-start.5 = (bf16[128,128]{1,0:T(8,128)(2,1)S(1)}, bf16[128,128]{1,0:T(8,128)(2,1)S(1)}, u32[]{:S(2)}, u32[]{:S(2)}) collective-permute-start(bf16[128,128]{1,0:T(8,128)(2,1)S(1)} %get-tuple-element.29.att_ref), channel_id=1, source_target_pairs={{0,3},{1,2},{2,1},{3,0},{4,7},{5,6},{6,5},{7,4},{8,11},{9,10},{10,... | collective-permute-start | bytes 98312 | tf_op jit(solution)/shard_map/ppermute | solution.py:54
  19.3 0.0 collective-permute-done.7.half_ref
  19.3 0.3 collective-permute-start.4
  19.6 0.0 collective-permute-done.9.minus_ref
  19.6 0.1 combine.1
  19.7 0.6 %collective-permute-start.11 = (bf16[128,256]{1,0:T(8,128)(2,1)S(1)}, bf16[128,256]{1,0:T(8,128)(2,1)S(1)}, u32[]{:S(2)}, u32[]{:S(2)}) collective-permute-start(bf16[128,256]{1,0:T(8,128)(2,1)S(1)} %get-tuple-element.39), channel_id=1, source_target_pairs={{0,28},{4,8},{8,4},{12,16},{16,12},{20,24},{24,20},{28,0},{1,29},{... | collective-permute-start | bytes 196616 | tf_op jit(solution)/shard_map/ppermute | solution.py:47
  20.2 2.0 %collective-permute-start.10 = (bf16[128,128]{1,0:T(8,128)(2,1)S(1)}, bf16[128,128]{1,0:T(8,128)(2,1)S(1)}, u32[]{:S(2)}, u32[]{:S(2)}) collective-permute-start(bf16[128,128]{1,0:T(8,128)(2,1)S(1)} %get-tuple-element.38), channel_id=1, source_target_pairs={{0,1},{1,0},{2,3},{3,2},{4,5},{5,4},{6,7},{7,6},{8,9},{9,8},{10,11... | collective-permute-start | bytes 98312 | tf_op jit(solution)/shard_map/ppermute | solution.py:54
  22.3 0.1 collective-permute-start.12
  22.4 1.8 %collective-permute-done.4.two_ref = bf16[128,128]{1,0:T(8,128)(2,1)S(1)} collective-permute-done((bf16[128,128]{1,0:T(8,128)(2,1)S(1)}, bf16[128,128]{1,0:T(8,128)(2,1)S(1)}, u32[]{:S(2)}, u32[]{:S(2)}) %collective-permute-start.4) | collective-permute-done | bytes 32800 | tf_op jit(solution)/shard_map/ppermute | solution.py:54
  24.2 0.2 project.1.partial_ref
  24.4 0.4 %collective-permute-done.10.one_ref = bf16[128,128]{1,0:T(8,128)(2,1)S(1)} collective-permute-done((bf16[128,128]{1,0:T(8,128)(2,1)S(1)}, bf16[128,128]{1,0:T(8,128)(2,1)S(1)}, u32[]{:S(2)}, u32[]{:S(2)}) %collective-permute-start.10) | collective-permute-done | bytes 32800 | tf_op jit(solution)/shard_map/ppermute | solution.py:54
  24.8 0.1 collective-permute-done.11.second_ref
  24.9 0.0 collective-permute-done.12.first_ref
  24.9 1.0 %finish.1 = (bf16[128,512]{1,0:T(8,128)(2,1)}, bf16[128,128]{1,0:T(8,128)(2,1)}, bf16[128,128]{1,0:T(8,128)(2,1)}, bf16[128,128]{1,0:T(8,128)(2,1)}) custom-call(f32[128,512]{1,0:T(8,128)S(1)} %project.1.partial_ref, bf16[128,128]{1,0:T(8,128)(2,1)S(1)} %gather.1.one_ref, bf16[128,128]{1,0:T(8,128)(2,1)S(1)} %collective-permute-done.4.two_ref, ...), custom_call_target="tpu_custom_call" | custom-call | tf_op jit(solution)/shard_map/finish/pallas_call | solution.py:379
  (10 shorter events, 0.1 us)
Async XLA Ops:
  0.6 0.8 %copy-start.2 = (bf16[128,128]{1,0:T(8,128)(2,1)S(1)}, bf16[128,128]{1,0:T(8,128)(2,1)}, u32[]{:S(2)}) copy-start(bf16[128,128]{1,0:T(8,128)(2,1)} %param.8) | copy-start | bytes 98308
  1.4 0.7 %copy-start.1 = (s32[1,8]{1,0:T(1,128)S(1)}, s32[1,8]{1,0:T(1,128)}, u32[]{:S(2)}) copy-start(s32[1,8]{1,0:T(1,128)} %refs_0_.1) | copy-start | bytes 100
  1.4 2.3 %collective-permute-start = (bf16[128,256]{1,0:T(8,128)(2,1)S(1)}, bf16[128,256]{1,0:T(8,128)(2,1)S(1)}, u32[]{:S(2)}, u32[]{:S(2)}) collective-permute-start(bf16[128,256]{1,0:T(8,128)(2,1)S(1)} %constant_dynamic-update-slice_fusion.refs_3_.own_ref), channel_id=1, source_target_pairs={{0,4},{4,0},{8,12},{12,8},{16,20},{20,16},{24,28},{28,24},{1,5},{5... | collective-permute-start | bytes 196616 | tf_op jit(solution)/shard_map/ppermute | solution.py:47
  3.8 8.4 %copy-start = (bf16[128,128]{1,0:T(8,128)(2,1)S(1)}, bf16[128,128]{1,0:T(8,128)(2,1)}, u32[]{:S(2)}) copy-start(bf16[128,128]{1,0:T(8,128)(2,1)} %refs_1_.3) | copy-start | bytes 98308
  3.8 8.3 %collective-permute-start.1 = (bf16[160,256]{1,0:T(8,128)(2,1)S(1)}, bf16[160,256]{1,0:T(8,128)(2,1)S(1)}, u32[]{:S(2)}, u32[]{:S(2)}) collective-permute-start(bf16[160,256]{1,0:T(8,128)(2,1)S(1)} %get-tuple-element.27), channel_id=1, source_target_pairs={{0,28},{4,8},{8,4},{12,16},{16,12},{20,24},{24,20},{28,0},{1,29},{... | collective-permute-start | bytes 245768 | tf_op jit(solution)/shard_map/ppermute | solution.py:47
  7.3 4.8 %collective-permute-start.2 = (bf16[64,256]{1,0:T(8,128)(2,1)S(1)}, bf16[64,256]{1,0:T(8,128)(2,1)S(1)}, u32[]{:S(2)}, u32[]{:S(2)}) collective-permute-start(bf16[64,256]{1,0:T(8,128)(2,1)S(1)} %get-tuple-element.28), channel_id=1, source_target_pairs={{0,12},{4,24},{8,20},{12,0},{16,28},{20,8},{24,4},{28,16},{1,13},{... | collective-permute-start | bytes 98312 | tf_op jit(solution)/shard_map/ppermute | solution.py:47
  8.0 4.1 %collective-permute-start.3 = (bf16[64,256]{1,0:T(8,128)(2,1)S(1)}, bf16[64,256]{1,0:T(8,128)(2,1)S(1)}, u32[]{:S(2)}, u32[]{:S(2)}) collective-permute-start(bf16[64,256]{1,0:T(8,128)(2,1)S(1)} %get-tuple-element.28), channel_id=1, source_target_pairs={{0,16},{4,20},{8,24},{12,28},{16,0},{20,4},{24,8},{28,12},{1,17},{... | collective-permute-start | bytes 98312 | tf_op jit(solution)/shard_map/ppermute | solution.py:47
  8.0 11.3 %collective-permute-start.7 = (bf16[80,512]{1,0:T(8,128)(2,1)S(1)}, bf16[80,512]{1,0:T(8,128)(2,1)S(1)}, u32[]{:S(2)}, u32[]{:S(2)}) collective-permute-start(bf16[80,512]{1,0:T(8,128)(2,1)S(1)} %get-tuple-element.32), channel_id=1, source_target_pairs={{0,3},{1,2},{2,1},{3,0},{4,7},{5,6},{6,5},{7,4},{8,11},{9,10},{10,... | collective-permute-start | bytes 245768 | tf_op jit(solution)/shard_map/ppermute | solution.py:54
  12.1 7.5 %collective-permute-start.6 = (bf16[128,512]{1,0:T(8,128)(2,1)S(1)}, bf16[128,512]{1,0:T(8,128)(2,1)S(1)}, u32[]{:S(2)}, u32[]{:S(2)}) collective-permute-start(bf16[128,512]{1,0:T(8,128)(2,1)S(1)} %get-tuple-element.31), channel_id=1, source_target_pairs={{0,1},{1,0},{2,3},{3,2},{4,6},{5,7},{6,4},{7,5},{8,9},{9,8},{10,11... | collective-permute-start | bytes 393224 | tf_op jit(solution)/shard_map/ppermute | solution.py:433
  13.2 6.4 %collective-permute-start.8 = (bf16[96,256]{1,0:T(8,128)(2,1)S(1)}, bf16[96,256]{1,0:T(8,128)(2,1)S(1)}, u32[]{:S(2)}, u32[]{:S(2)}) collective-permute-start(bf16[96,256]{1,0:T(8,128)(2,1)S(1)} %get-tuple-element.36), channel_id=1, source_target_pairs={{0,12},{4,24},{8,20},{12,0},{16,28},{20,8},{24,4},{28,16},{1,13},{... | collective-permute-start | bytes 147464 | tf_op jit(solution)/shard_map/ppermute | solution.py:47
  13.7 5.9 %collective-permute-start.9 = (bf16[64,256]{1,0:T(8,128)(2,1)S(1)}, bf16[64,256]{1,0:T(8,128)(2,1)S(1)}, u32[]{:S(2)}, u32[]{:S(2)}) collective-permute-start(bf16[64,256]{1,0:T(8,128)(2,1)S(1)} %get-tuple-element.37), channel_id=1, source_target_pairs={{0,20},{4,16},{8,28},{12,24},{16,4},{20,0},{24,12},{28,8},{1,21},{... | collective-permute-start | bytes 98312 | tf_op jit(solution)/shard_map/ppermute | solution.py:47
  15.9 6.3 %collective-permute-start.5 = (bf16[128,128]{1,0:T(8,128)(2,1)S(1)}, bf16[128,128]{1,0:T(8,128)(2,1)S(1)}, u32[]{:S(2)}, u32[]{:S(2)}) collective-permute-start(bf16[128,128]{1,0:T(8,128)(2,1)S(1)} %get-tuple-element.29.att_ref), channel_id=1, source_target_pairs={{0,3},{1,2},{2,1},{3,0},{4,7},{5,6},{6,5},{7,4},{8,11},{9,10},{10,... | collective-permute-start | bytes 98312 | tf_op jit(solution)/shard_map/ppermute | solution.py:54
  19.3 4.8 %collective-permute-start.4 = (bf16[128,128]{1,0:T(8,128)(2,1)S(1)}, bf16[128,128]{1,0:T(8,128)(2,1)S(1)}, u32[]{:S(2)}, u32[]{:S(2)}) collective-permute-start(bf16[128,128]{1,0:T(8,128)(2,1)S(1)} %get-tuple-element.29.att_ref), channel_id=1, source_target_pairs={{0,2},{1,3},{2,0},{3,1},{4,6},{5,7},{6,4},{7,5},{8,10},{9,11},{10,... | collective-permute-start | bytes 98312 | tf_op jit(solution)/shard_map/ppermute | solution.py:54
  19.7 5.3 %collective-permute-start.11 = (bf16[128,256]{1,0:T(8,128)(2,1)S(1)}, bf16[128,256]{1,0:T(8,128)(2,1)S(1)}, u32[]{:S(2)}, u32[]{:S(2)}) collective-permute-start(bf16[128,256]{1,0:T(8,128)(2,1)S(1)} %get-tuple-element.39), channel_id=1, source_target_pairs={{0,28},{4,8},{8,4},{12,16},{16,12},{20,24},{24,20},{28,0},{1,29},{... | collective-permute-start | bytes 196616 | tf_op jit(solution)/shard_map/ppermute | solution.py:47
  20.2 4.6 %collective-permute-start.10 = (bf16[128,128]{1,0:T(8,128)(2,1)S(1)}, bf16[128,128]{1,0:T(8,128)(2,1)S(1)}, u32[]{:S(2)}, u32[]{:S(2)}) collective-permute-start(bf16[128,128]{1,0:T(8,128)(2,1)S(1)} %get-tuple-element.38), channel_id=1, source_target_pairs={{0,1},{1,0},{2,3},{3,2},{4,5},{5,4},{6,7},{7,6},{8,9},{9,8},{10,11... | collective-permute-start | bytes 98312 | tf_op jit(solution)/shard_map/ppermute | solution.py:54
  22.3 2.6 %collective-permute-start.12 = (bf16[512,256]{1,0:T(8,128)(2,1)S(1)}, bf16[512,256]{1,0:T(8,128)(2,1)S(1)}, u32[]{:S(2)}, u32[]{:S(2)}) collective-permute-start(bf16[512,256]{1,0:T(8,128)(2,1)S(1)} %pack.1), channel_id=1, source_target_pairs={{0,4},{4,0},{8,12},{12,8},{16,20},{20,16},{24,28},{28,24},{1,5},{5... | collective-permute-start | bytes 786440 | tf_op jit(solution)/shard_map/ppermute | solution.py:47

commit v14 on v13

--- a/solution.py
+++ b/solution.py
@@ -16,7 +16,7 @@
 VMEM = pl.BlockSpec(memory_space=pltpu.VMEM)
 HBM = pl.BlockSpec(memory_space=pltpu.HBM)
 PARAMS = pltpu.CompilerParams(vmem_limit_bytes=40 * 1024 * 1024)
-FULL = pltpu.CompilerParams(vmem_limit_bytes=int(53.3 * 1024 * 1024))
+FULL = pltpu.CompilerParams(vmem_limit_bytes=int(52.8 * 1024 * 1024))
 BF16 = jnp.bfloat16
 PREPARE_COST = 10**10
 ATTEND_COST = 10**10
@@ -93,22 +93,24 @@
 CHUNKS = 4
 
 
-def prepare_kernel(ring, index_hbm, cot_hbm, w_hbm, after_ref, grad_ref, mult_ref, *refs):
+def row_copies(src, dst, sems, first):
+    rows = dst.shape[0] // CHUNKS
+    spans = [pl.ds(i * rows, rows) for i in range(CHUNKS)]
+    return [pltpu.make_async_copy(src.at[span], dst.at[span], sems.at[first + i])
+            for i, span in enumerate(spans)]
+
+
+def slices_kernel(ring, index_hbm, w_hbm, after_ref, mult_ref, w_ref, *refs):
     del after_ref
-    index_ref, cot_ref, w_ref, sems = refs[-4:]
-    slice_refs = refs[:-4]
-    copies = [(index_hbm, index_ref)]
-    for src, dst in ((w_hbm, w_ref), (cot_hbm, cot_ref)):
-        rows = dst.shape[0] // CHUNKS
-        for i in range(CHUNKS):
-            span = pl.ds(i * rows, rows)
-            copies.append((src.at[span], dst.at[span]))
-    copies = [pltpu.make_async_copy(src, dst, sems.at[i]) for i, (src, dst) in enumerate(copies)]
+    index_ref, sems = refs[-2:]
+    slice_refs = refs[:-2]
+    copies = [pltpu.make_async_copy(index_hbm, index_ref, sems.at[CHUNKS])]
+    copies += row_copies(w_hbm, w_ref, sems, 0)
     for copy in copies:
         copy.start()
     copies[0].wait()
     fill_multiplicity(ring, index_ref, mult_ref)
-    for copy in copies[1:1 + CHUNKS]:
+    for copy in copies[1:]:
         copy.wait()
     width = slice_refs[0].shape[1]
     head = lax.axis_index("head")
@@ -121,40 +123,52 @@
         half = HD // 2
         mine_ref, whole_ref, half_ref = slice_refs
         mine_ref[...] = w_ref[:, columns(head)]
-        whole_ref[...] = w_ref[:, columns(head ^ (1 + core))]
+        whole_ref[...] = w_ref[:, columns(head ^ (3 - core))]
         rows = pl.ds(pl.multiple_of(core * (half - MARGIN), MARGIN), half + MARGIN)
-        half_ref[...] = w_ref[rows, columns(head ^ 3)]
+        half_ref[...] = w_ref[rows, columns(head ^ 1)]
     else:
         for r, ref in enumerate(slice_refs):
             ref[...] = w_ref[:, columns(head ^ r)]
-    for copy in copies[1 + CHUNKS:]:
-        copy.wait()
-    grad_ref[...] = dot_nt(cot_ref[...], w_ref[...]).astype(grad_ref.dtype)
-
-
-def prepare(ring, index, cotangent, out_weight, heads, columns, after):
+
+
+def weight_slices(ring, index, out_weight, heads, columns, after):
     width = out_weight.shape[1] // heads
     rows = (HD, HD, HD // 2 + MARGIN) if ring else (HD,) * heads
 
     def body(*refs):
-        prepare_kernel(ring, *refs)
+        slices_kernel(ring, *refs)
 
     return pl.pallas_call(
         body,
-        out_shape=(shape(BLK, HD), shape(8, columns, kind=F32))
+        out_shape=(shape(8, columns, kind=F32), shape(*out_weight.shape))
         + tuple(shape(r, width) for r in rows),
-        in_specs=[HBM] * 3 + [VMEM],
+        in_specs=[HBM] * 2 + [VMEM],
         out_specs=(VMEM,) * (2 + len(rows)),
         scratch_shapes=[
             pltpu.SMEM(index.shape, jnp.int32),
-            pltpu.VMEM(cotangent.shape, BF16),
-            pltpu.VMEM(out_weight.shape, BF16),
-            pltpu.SemaphoreType.DMA((1 + 2 * CHUNKS,)),
+            pltpu.SemaphoreType.DMA((1 + CHUNKS,)),
         ],
         compiler_params=FULL,
         cost_estimate=cost(PREPARE_COST),
+        name="slices",
+    )(index, out_weight, after)
+
+
+def prepare_kernel(cot_ref, w_ref, after_ref, grad_ref):
+    del after_ref
+    grad_ref[...] = dot_nt(cot_ref[...], w_ref[...]).astype(grad_ref.dtype)
+
+
+def prepare(cotangent, out_weight, after):
+    return pl.pallas_call(
+        prepare_kernel,
+        out_shape=shape(BLK, HD),
+        in_specs=[VMEM] * 3,
+        out_specs=VMEM,
+        compiler_params=PARAMS,
+        cost_estimate=cost(PREPARE_COST),
         name="prepare",
-    )(index, cotangent, out_weight, after)
+    )(cotangent, out_weight, after)
 
 
 def lead_kernel(own_ref, first_ref, mult_ref, whole_ref, near_ref, pair_ref, whole_out):
@@ -296,24 +310,21 @@
     )(first, slices, after)
 
 
-def project_kernel(att_ref, two_ref, three_ref, mine_ref, whole_ref, half_ref, out_ref):
+def project_kernel(att_ref, two_ref, three_ref, mine_ref, whole_ref, out_ref):
     core = lax.axis_index("seq") & 1
-    half = HD // 2
-    two = jnp.where(core == 0, jnp.zeros((BLK, HD), BF16), two_ref[...])
-    three = jnp.where(core == 0, three_ref[:, :half], three_ref[:, half:])
-    total = dot_nn(att_ref[...], mine_ref[...]) + dot_nn(two, whole_ref[...])
-    out_ref[...] = total + dot_nn(three, half_ref[half_rows(), :])
-
-
-def project(att, two, three, mine, whole, half):
+    here = jnp.where(core == 0, three_ref[...], two_ref[...])
+    out_ref[...] = dot_nn(att_ref[...], mine_ref[...]) + dot_nn(here, whole_ref[...])
+
+
+def project(att, two, three, mine, whole):
     return pl.pallas_call(
         project_kernel,
         out_shape=shape(BLK, mine.shape[1], kind=F32),
-        in_specs=[VMEM] * 6,
+        in_specs=[VMEM] * 5,
         out_specs=VMEM,
         compiler_params=PARAMS,
         name="project",
-    )(att, two, three, mine, whole, half)
+    )(att, two, three, mine, whole)
 
 
 def gather_kernel(one_ref, second_ref, partial_ref, out_ref):
@@ -339,7 +350,7 @@
         ref[STRIDE_ROWS:] = total[STRIDE_ROWS:, c:c + HD].astype(ref.dtype)
 
 
-def finish_ring_kernel(partial_ref, one_ref, two_ref, three_ref, whole_ref, first_ref, own_ref,
+def finish_ring_kernel(partial_ref, one_ref, two_ref, three_ref, half_ref, first_ref, own_ref,
                        second_ref, dq_ref, mixed_hbm, dq_hbm, dk_hbm, dv_hbm,
                        mixed_ref, dk_ref, dv_ref, sems):
     copies = []
@@ -352,20 +363,23 @@
     send(dq_ref, dq_hbm)
     core = lax.axis_index("seq") & 1
     half = HD // 2
-    one, two, three = one_ref[...], two_ref[...], three_ref[...]
-    here = jnp.where(core == 0, one, jnp.zeros_like(one))
-    there = jnp.where(core == 0, two, one)
-    there_half = jnp.where(core == 0, three[:, half:], three[:, :half])
-    width = whole_ref.shape[1]
+    one = one_ref[...]
+    there = jnp.where(core == 0, two_ref[...], three_ref[...])
+    here_half = jnp.where(core == 0, one[:, :half], one[:, half:])
+    there_half = jnp.where(core == 0, one[:, half:], one[:, :half])
+    width = half_ref.shape[1]
     half_row = BLK + (width // PAIR) * HD
-    for i, c in enumerate(range(0, width, PAIR)):
-        span = slice(c, c + PAIR)
-        other_whole = first_ref[BLK + i * HD:BLK + (i + 1) * HD]
-        other_half = first_ref[half_row + i * half:half_row + (i + 1) * half]
-        mixed = partial_ref[:, span] + dot_nn(here, whole_ref[:, span])
-        mixed = mixed + dot_nn(there, other_whole) + dot_nn(there_half, other_half)
-        mixed_ref[:, span] = mixed.astype(mixed_ref.dtype)
-        send(mixed_ref.at[:, pl.ds(c, PAIR)], mixed_hbm.at[:, pl.ds(c, PAIR)])
+    for r in range(0, BLK, half):
+        rows = slice(r, r + half)
+        for i, c in enumerate(range(0, width, PAIR)):
+            span = slice(c, c + PAIR)
+            other_whole = first_ref[BLK + i * HD:BLK + (i + 1) * HD]
+            other_half = first_ref[half_row + i * half:half_row + (i + 1) * half]
+            mixed = partial_ref[rows, span] + dot_nn(there[rows], other_whole)
+            mixed = mixed + dot_nn(here_half[rows], half_ref[half_rows(), span])
+            mixed = mixed + dot_nn(there_half[rows], other_half)
+            mixed_ref[rows, span] = mixed.astype(mixed_ref.dtype)
+        send(mixed_ref.at[pl.ds(r, half)], mixed_hbm.at[pl.ds(r, half)])
     total = own_ref[...] + first_ref[:BLK].astype(F32) + second_ref[...].astype(F32)
     settle(total, total[:STRIDE_ROWS], dk_ref, dv_ref)
     send(dk_ref, dk_hbm)
@@ -385,7 +399,7 @@
             pltpu.VMEM((BLK, width), BF16),
             pltpu.VMEM((BLK, HD), BF16),
             pltpu.VMEM((BLK, HD), BF16),
-            pltpu.SemaphoreType.DMA((3 + width // PAIR,)),
+            pltpu.SemaphoreType.DMA((5,)),
         ],
         compiler_params=PARAMS,
         name="finish",
@@ -428,7 +442,7 @@
 def spread_slice(array):
     seq = lax.axis_size("seq")
     heads = lax.axis_size("head")
-    pairs = [(b * heads + h, b * heads + (h ^ (1 + b % 2))) for b in range(seq)
+    pairs = [(b * heads + h, b * heads + (h ^ (3 - b % 2))) for b in range(seq)
              for h in range(heads)]
     return lax.ppermute(array, ("seq", "head"), pairs)
 
@@ -442,13 +456,14 @@
     columns = 3 * BLK + side_rows
     own = jnp.concatenate([key_rows, value_rows], axis=1)
     first = trade(own, 1)
-    grad, mult, *slices = prepare(
-        ring, strided_index, cotangent, out_weight, heads, columns, own
+    mult, weight, *slices = weight_slices(
+        ring, strided_index, out_weight, heads, columns, own
     )
     if ring:
         mine, whole, half = slices
-        half = swap(half, 3)
+        half = swap(half, 1)
         near, pair, whole = leads(own, first, mult, whole)
+        grad = prepare(cotangent, weight, pair)
         whole = spread_slice(whole)
         near = trade(near, -1)
         blocks = (own, first, near, trade(pair, 3), trade(pair, 4))
@@ -466,13 +481,14 @@
         )
         from_second = trade(to_second, -1)
         packed = trade(pack(to_first, out_slices, far[1]), 1)
-        partial = project(att, *far, mine, whole, half)
+        partial = project(att, *far, mine, whole)
         one = gather(swap(last, 1), from_second, partial)
         mixed, dq, dk, dv = finish_ring(
-            partial, one, *far, whole, packed, own_sum, from_second, dq
+            partial, one, *far, half, packed, own_sum, from_second, dq
         )
     else:
         second = trade(own, -1)
+        grad = prepare(cotangent, weight, own)
         slices = [slices[0]] + [swap(slices[r], r) for r in range(1, heads)]
         spread = jnp.broadcast_to(own[None, :n], (seq, n, PAIR))
         side = lax.all_to_all(spread, "seq", 0, 0).reshape(side_rows, PAIR)

time: 26.2 us -> 26.2 us (level)
  waiting for transfers between devices: 2.33 us -> 4.11 us
  starting transfers between devices: 17.9 us -> 16.4 us
    ppermute x4, starting transfers between devices: 9.78 us -> 6.55 us  [swap(): return lax.ppermute(array, 'head', [(i, i ^ mask) for i in range(count)])]
    ppermute x1, starting transfers between devices: 0.01 us -> 2.47 us  [spread_slice(): return lax.ppermute(array, ('seq', 'head'), pairs)]
    ppermute x8, waiting for transfers between devices: 0.08 us -> 1.54 us  [trade(): lax.ppermute(array, 'seq', [(i, (i + (step if i % 2 == 0 else -step)) % c...]
    ppermute x8, starting transfers between devices: 8.12 us -> 7.41 us  [trade(): lax.ppermute(array, 'seq', [(i, (i + (step if i % 2 == 0 else -step)) % c...]
    ppermute x4, waiting for transfers between devices: 2.24 us -> 2.57 us  [swap(): return lax.ppermute(array, 'head', [(i, i ^ mask) for i in range(count)])]
    pallas_call x1 -> x2, Pallas kernels: 1.66 us -> 1.46 us  [the longest x1 1.16 us: weight_slices(): pl.pallas_call(body, out_shape=(shape(8, columns, kind=F32), shape(*out_w...]
    unnamed x7 -> x9, local copies, waits for them, and re-layouts: 0.89 us -> 0.89 us
  transfers between devices with their start and end apart: 13 -> 13, of which waited for: 3 -> 3; matrix products, arithmetic and copies ran while one was open for 0% -> 0% of each run, Pallas kernels for 12% -> 11%
where the time goes in v14:
time: 26.2 us; the launch traced here: 26 us
  starting transfers between devices  16.4 us (63%)
  waiting for transfers between devices  4.11 us (16%)
  Pallas kernels  3.82 us (15%)
  local copies, waits for them, and re-layouts  0.9 us (3%)
  between operations  0.75 us (3%)
    ppermute x8, starting transfers between devices, trade(): lax.ppermute(array, 'seq', [(i, (i + (step if i % 2 == 0 else -step)) % c...  7.41 us
    ppermute x4, starting transfers between devices, swap(): return lax.ppermute(array, 'head', [(i, i ^ mask) for i in range(count)])  6.55 us
    ppermute x4, waiting for transfers between devices, swap(): return lax.ppermute(array, 'head', [(i, i ^ mask) for i in range(count)])  2.57 us
    ppermute x1, starting transfers between devices, spread_slice(): return lax.ppermute(array, ('seq', 'head'), pairs)  2.47 us
    ppermute x8, waiting for transfers between devices, trade(): lax.ppermute(array, 'seq', [(i, (i + (step if i % 2 == 0 else -step)) % c...  1.54 us
    pallas_call x1, Pallas kernels, weight_slices(): pl.pallas_call(body, out_shape=(shape(8, columns, kind=F32), shape(*out_w...  1.16 us
    pallas_call x1, Pallas kernels, finish_ring(): pl.pallas_call(finish_ring_kernel, out_shape=(shape(BLK, width),) + (shap...  1.05 us
    pallas_call x1, Pallas kernels, attend(): pl.pallas_call(body, out_shape=(shape(BLK, HD), shape(BLK, HD), *sums), i...  1.01 us
  transfers between devices with their start and end apart: 13, of which 3 were waited for; matrix products, arithmetic and copies ran while one was open for 0% of the time, Pallas kernels for 11%

profile of v14, /device:TPU:0, one launch (start us, length us, event | category | flops | bytes accessed | tf_op | source)
XLA Modules:
  0.0 26.0 jit_solution(6859515386151991192)
XLA Ops:
  0.6 0.8 %constant_dynamic-update-slice_fusion.1 = bf16[128,256]{1,0:T(8,128)(2,1)S(1)} fusion(bf16[128,128]{1,0:T(8,128)(2,1)} %param.7), kind=kLoop, calls=%fused_computation.1 | loop fusion | bytes 65536
  1.4 0.0 copy-start.2
  1.4 0.0 copy-start
  1.5 0.5 %collective-permute-start = (bf16[128,256]{1,0:T(8,128)(2,1)S(1)}, bf16[128,256]{1,0:T(8,128)(2,1)S(1)}, u32[]{:S(2)}, u32[]{:S(2)}) collective-permute-start(bf16[128,256]{1,0:T(8,128)(2,1)S(1)} %constant_dynamic-update-slice_fusion.refs_2_.own_ref.refs_3_), channel_id=1, source_target_pairs={{0,4},{4,0},{8,12},{12,8},{16,20},{20,16},{24,28},{28,24},{1,5},{5... | collective-permute-start | bytes 196616 | tf_op jit(solution)/shard_map/ppermute | solution.py:47
  2.0 0.1 copy-done.2
  2.1 1.2 %slices.1 = (f32[8,640]{1,0:T(8,128)S(1)}, bf16[128,2048]{1,0:T(8,128)(2,1)S(1)}, bf16[128,512]{1,0:T(8,128)(2,1)S(1)}, bf16[128,512]{1,0:T(8,128)(2,1)S(1)}, bf16[80,512]{1,0:T(8,128)(2,1)S(1)}) custom-call(s32[1,8]{1,0:T(1,128)S(1)} %copy-done.2, bf16[128,2048]{1,0:T(8,128)(2,1)} %refs_1_.2, ...), custom_call_target="tpu_custom_call" | custom-call | flops 10000000000 | tf_op jit(solution)/shard_map/slices/pallas_call | solution.py:141
  3.2 3.1 %collective-permute-start.9 = (bf16[80,512]{1,0:T(8,128)(2,1)S(1)}, bf16[80,512]{1,0:T(8,128)(2,1)S(1)}, u32[]{:S(2)}, u32[]{:S(2)}) collective-permute-start(bf16[80,512]{1,0:T(8,128)(2,1)S(1)} %get-tuple-element.37), channel_id=1, source_target_pairs={{0,1},{1,0},{2,3},{3,2},{4,5},{5,4},{6,7},{7,6},{8,9},{9,8},{10,11... | collective-permute-start | bytes 245768 | tf_op jit(solution)/shard_map/ppermute | solution.py:54
  6.3 0.0 collective-permute-done.first_ref.refs_4_
  6.4 0.8 %collective-permute-start.2 = (bf16[64,256]{1,0:T(8,128)(2,1)S(1)}, bf16[64,256]{1,0:T(8,128)(2,1)S(1)}, u32[]{:S(2)}, u32[]{:S(2)}) collective-permute-start(bf16[64,256]{1,0:T(8,128)(2,1)S(1)} %get-tuple-element.27.after_ref), channel_id=1, source_target_pairs={{0,12},{4,24},{8,20},{12,0},{16,28},{20,8},{24,4},{28,16},{1,13},{... | collective-permute-start | bytes 98312 | tf_op jit(solution)/shard_map/ppermute | solution.py:47
  7.2 1.5 %collective-permute-start.3 = (bf16[64,256]{1,0:T(8,128)(2,1)S(1)}, bf16[64,256]{1,0:T(8,128)(2,1)S(1)}, u32[]{:S(2)}, u32[]{:S(2)}) collective-permute-start(bf16[64,256]{1,0:T(8,128)(2,1)S(1)} %get-tuple-element.27.after_ref), channel_id=1, source_target_pairs={{0,16},{4,20},{8,24},{12,28},{16,0},{20,4},{24,8},{28,12},{1,17},{... | collective-permute-start | bytes 98312 | tf_op jit(solution)/shard_map/ppermute | solution.py:47
  8.7 0.6 %collective-permute-start.1 = (bf16[160,256]{1,0:T(8,128)(2,1)S(1)}, bf16[160,256]{1,0:T(8,128)(2,1)S(1)}, u32[]{:S(2)}, u32[]{:S(2)}) collective-permute-start(bf16[160,256]{1,0:T(8,128)(2,1)S(1)} %get-tuple-element.28), channel_id=1, source_target_pairs={{0,28},{4,8},{8,4},{12,16},{16,12},{20,24},{24,20},{28,0},{1,29},{... | collective-permute-start | bytes 245768 | tf_op jit(solution)/shard_map/ppermute | solution.py:47
  9.4 2.5 %collective-permute-start.6 = (bf16[128,512]{1,0:T(8,128)(2,1)S(1)}, bf16[128,512]{1,0:T(8,128)(2,1)S(1)}, u32[]{:S(2)}, u32[]{:S(2)}) collective-permute-start(bf16[128,512]{1,0:T(8,128)(2,1)S(1)} %get-tuple-element.31), channel_id=1, source_target_pairs={{0,3},{1,2},{2,1},{3,0},{4,6},{5,7},{6,4},{7,5},{8,11},{9,10},{10,... | collective-permute-start | bytes 393224 | tf_op jit(solution)/shard_map/ppermute | solution.py:447
  11.8 0.3 %prepare.1.refs_2_ = bf16[128,128]{1,0:T(8,128)(2,1)S(1)} custom-call(bf16[128,2048]{1,0:T(8,128)(2,1)S(1)} %copy-done, bf16[128,2048]{1,0:T(8,128)(2,1)S(1)} %get-tuple-element.25.w_ref, bf16[64,256]{1,0:T(8,128)(2,1)S(1)} %get-tuple-element.27.after_ref), custom_call_target="tpu_custom_call" | custom-call | flops 10000000000 | tf_op jit(solution)/shard_map/prepare/pallas_call | solution.py:163
  12.1 0.0 collective-permute-done.3.refs_7_
  12.2 1.5 %collective-permute-done.1.refs_5_ = bf16[160,256]{1,0:T(8,128)(2,1)S(1)} collective-permute-done((bf16[160,256]{1,0:T(8,128)(2,1)S(1)}, bf16[160,256]{1,0:T(8,128)(2,1)S(1)}, u32[]{:S(2)}, u32[]{:S(2)}) %collective-permute-start.1) | collective-permute-done | bytes 81952 | tf_op jit(solution)/shard_map/ppermute | solution.py:47
  13.7 1.0 %attend.1 = (bf16[128,128]{1,0:T(8,128)(2,1)S(1)}, bf16[128,128]{1,0:T(8,128)(2,1)S(1)}, f32[128,256]{1,0:T(8,128)S(1)}, f32[128,256]{1,0:T(8,128)S(1)}, f32[128...) custom-call(f32[8,640]{1,0:T(8,128)S(1)} %get-tuple-element.24.mult_ref.refs_0_, ...), custom_call_target="tpu_custom_call" | custom-call | flops 10000000000 | tf_op jit(solution)/shard_map/attend/pallas_call | solution.py:244
  14.7 0.7 %collective-permute-start.7 = (bf16[96,256]{1,0:T(8,128)(2,1)S(1)}, bf16[96,256]{1,0:T(8,128)(2,1)S(1)}, u32[]{:S(2)}, u32[]{:S(2)}) collective-permute-start(bf16[96,256]{1,0:T(8,128)(2,1)S(1)} %get-tuple-element.35), channel_id=1, source_target_pairs={{0,12},{4,24},{8,20},{12,0},{16,28},{20,8},{24,4},{28,16},{1,13},{... | collective-permute-start | bytes 147464 | tf_op jit(solution)/shard_map/ppermute | solution.py:47
  15.4 0.9 %collective-permute-start.8 = (bf16[64,256]{1,0:T(8,128)(2,1)S(1)}, bf16[64,256]{1,0:T(8,128)(2,1)S(1)}, u32[]{:S(2)}, u32[]{:S(2)}) collective-permute-start(bf16[64,256]{1,0:T(8,128)(2,1)S(1)} %get-tuple-element.36), channel_id=1, source_target_pairs={{0,20},{4,16},{8,28},{12,24},{16,4},{20,0},{24,12},{28,8},{1,21},{... | collective-permute-start | bytes 98312 | tf_op jit(solution)/shard_map/ppermute | solution.py:47
  16.4 2.3 %collective-permute-start.5 = (bf16[128,128]{1,0:T(8,128)(2,1)S(1)}, bf16[128,128]{1,0:T(8,128)(2,1)S(1)}, u32[]{:S(2)}, u32[]{:S(2)}) collective-permute-start(bf16[128,128]{1,0:T(8,128)(2,1)S(1)} %get-tuple-element.29.att_ref), channel_id=1, source_target_pairs={{0,3},{1,2},{2,1},{3,0},{4,7},{5,6},{6,5},{7,4},{8,11},{9,10},{10,... | collective-permute-start | bytes 98312 | tf_op jit(solution)/shard_map/ppermute | solution.py:54
  18.7 0.0 collective-permute-done.9.half_ref
  18.7 0.1 collective-permute-start.4
  18.8 0.0 collective-permute-done.6.whole_ref
  18.8 0.1 combine.1
  18.9 2.2 %collective-permute-start.11 = (bf16[128,256]{1,0:T(8,128)(2,1)S(1)}, bf16[128,256]{1,0:T(8,128)(2,1)S(1)}, u32[]{:S(2)}, u32[]{:S(2)}) collective-permute-start(bf16[128,256]{1,0:T(8,128)(2,1)S(1)} %get-tuple-element.39), channel_id=1, source_target_pairs={{0,28},{4,8},{8,4},{12,16},{16,12},{20,24},{24,20},{28,0},{1,29},{... | collective-permute-start | bytes 196616 | tf_op jit(solution)/shard_map/ppermute | solution.py:47
  21.0 1.0 %collective-permute-start.10 = (bf16[128,128]{1,0:T(8,128)(2,1)S(1)}, bf16[128,128]{1,0:T(8,128)(2,1)S(1)}, u32[]{:S(2)}, u32[]{:S(2)}) collective-permute-start(bf16[128,128]{1,0:T(8,128)(2,1)S(1)} %get-tuple-element.38), channel_id=1, source_target_pairs={{0,1},{1,0},{2,3},{3,2},{4,5},{5,4},{6,7},{7,6},{8,9},{9,8},{10,11... | collective-permute-start | bytes 98312 | tf_op jit(solution)/shard_map/ppermute | solution.py:54
  22.1 0.0 collective-permute-done.5.three_ref.after_ref
  22.1 0.1 collective-permute-start.12
  22.2 1.7 %collective-permute-done.4.two_ref = bf16[128,128]{1,0:T(8,128)(2,1)S(1)} collective-permute-done((bf16[128,128]{1,0:T(8,128)(2,1)S(1)}, bf16[128,128]{1,0:T(8,128)(2,1)S(1)}, u32[]{:S(2)}, u32[]{:S(2)}) %collective-permute-start.4) | collective-permute-done | bytes 32800 | tf_op jit(solution)/shard_map/ppermute | solution.py:54
  23.9 0.2 project.1.partial_ref
  24.1 0.9 %collective-permute-done.10.one_ref = bf16[128,128]{1,0:T(8,128)(2,1)S(1)} collective-permute-done((bf16[128,128]{1,0:T(8,128)(2,1)S(1)}, bf16[128,128]{1,0:T(8,128)(2,1)S(1)}, u32[]{:S(2)}, u32[]{:S(2)}) %collective-permute-start.10) | collective-permute-done | bytes 32800 | tf_op jit(solution)/shard_map/ppermute | solution.py:54
  24.9 0.0 collective-permute-done.11.second_ref
  25.0 1.1 %finish.1 = (bf16[128,512]{1,0:T(8,128)(2,1)}, bf16[128,128]{1,0:T(8,128)(2,1)}, bf16[128,128]{1,0:T(8,128)(2,1)}, bf16[128,128]{1,0:T(8,128)(2,1)}) custom-call(f32[128,512]{1,0:T(8,128)S(1)} %project.1.partial_ref, bf16[128,128]{1,0:T(8,128)(2,1)S(1)} %gather.1.one_ref, bf16[128,128]{1,0:T(8,128)(2,1)S(1)} %collective-permute-done.4.two_ref, ...), custom_call_target="tpu_custom_call" | custom-call | tf_op jit(solution)/shard_map/finish/pallas_call | solution.py:393
  (13 shorter events, 0.1 us)
Async XLA Ops:
  0.6 0.8 %copy-start.3 = (bf16[128,128]{1,0:T(8,128)(2,1)S(1)}, bf16[128,128]{1,0:T(8,128)(2,1)}, u32[]{:S(2)}) copy-start(bf16[128,128]{1,0:T(8,128)(2,1)} %param.8) | copy-start | bytes 98308
  1.4 0.7 %copy-start.2 = (s32[1,8]{1,0:T(1,128)S(1)}, s32[1,8]{1,0:T(1,128)}, u32[]{:S(2)}) copy-start(s32[1,8]{1,0:T(1,128)} %refs_0_.1) | copy-start | bytes 100
  1.4 10.4 %copy-start = (bf16[128,2048]{1,0:T(8,128)(2,1)S(1)}, bf16[128,2048]{1,0:T(8,128)(2,1)}, u32[]{:S(2)}) copy-start(bf16[128,2048]{1,0:T(8,128)(2,1)} %cot_ref.1) | copy-start | bytes 1572868
  1.5 4.9 %collective-permute-start = (bf16[128,256]{1,0:T(8,128)(2,1)S(1)}, bf16[128,256]{1,0:T(8,128)(2,1)S(1)}, u32[]{:S(2)}, u32[]{:S(2)}) collective-permute-start(bf16[128,256]{1,0:T(8,128)(2,1)S(1)} %constant_dynamic-update-slice_fusion.refs_2_.own_ref.refs_3_), channel_id=1, source_target_pairs={{0,4},{4,0},{8,12},{12,8},{16,20},{20,16},{24,28},{28,24},{1,5},{5... | collective-permute-start | bytes 196616 | tf_op jit(solution)/shard_map/ppermute | solution.py:47
  3.2 15.4 %collective-permute-start.9 = (bf16[80,512]{1,0:T(8,128)(2,1)S(1)}, bf16[80,512]{1,0:T(8,128)(2,1)S(1)}, u32[]{:S(2)}, u32[]{:S(2)}) collective-permute-start(bf16[80,512]{1,0:T(8,128)(2,1)S(1)} %get-tuple-element.37), channel_id=1, source_target_pairs={{0,1},{1,0},{2,3},{3,2},{4,5},{5,4},{6,7},{7,6},{8,9},{9,8},{10,11... | collective-permute-start | bytes 245768 | tf_op jit(solution)/shard_map/ppermute | solution.py:54
  6.4 5.8 %collective-permute-start.2 = (bf16[64,256]{1,0:T(8,128)(2,1)S(1)}, bf16[64,256]{1,0:T(8,128)(2,1)S(1)}, u32[]{:S(2)}, u32[]{:S(2)}) collective-permute-start(bf16[64,256]{1,0:T(8,128)(2,1)S(1)} %get-tuple-element.27.after_ref), channel_id=1, source_target_pairs={{0,12},{4,24},{8,20},{12,0},{16,28},{20,8},{24,4},{28,16},{1,13},{... | collective-permute-start | bytes 98312 | tf_op jit(solution)/shard_map/ppermute | solution.py:47
  7.2 4.9 %collective-permute-start.3 = (bf16[64,256]{1,0:T(8,128)(2,1)S(1)}, bf16[64,256]{1,0:T(8,128)(2,1)S(1)}, u32[]{:S(2)}, u32[]{:S(2)}) collective-permute-start(bf16[64,256]{1,0:T(8,128)(2,1)S(1)} %get-tuple-element.27.after_ref), channel_id=1, source_target_pairs={{0,16},{4,20},{8,24},{12,28},{16,0},{20,4},{24,8},{28,12},{1,17},{... | collective-permute-start | bytes 98312 | tf_op jit(solution)/shard_map/ppermute | solution.py:47
  8.7 5.0 %collective-permute-start.1 = (bf16[160,256]{1,0:T(8,128)(2,1)S(1)}, bf16[160,256]{1,0:T(8,128)(2,1)S(1)}, u32[]{:S(2)}, u32[]{:S(2)}) collective-permute-start(bf16[160,256]{1,0:T(8,128)(2,1)S(1)} %get-tuple-element.28), channel_id=1, source_target_pairs={{0,28},{4,8},{8,4},{12,16},{16,12},{20,24},{24,20},{28,0},{1,29},{... | collective-permute-start | bytes 245768 | tf_op jit(solution)/shard_map/ppermute | solution.py:47
  9.4 9.4 %collective-permute-start.6 = (bf16[128,512]{1,0:T(8,128)(2,1)S(1)}, bf16[128,512]{1,0:T(8,128)(2,1)S(1)}, u32[]{:S(2)}, u32[]{:S(2)}) collective-permute-start(bf16[128,512]{1,0:T(8,128)(2,1)S(1)} %get-tuple-element.31), channel_id=1, source_target_pairs={{0,3},{1,2},{2,1},{3,0},{4,6},{5,7},{6,4},{7,5},{8,11},{9,10},{10,... | collective-permute-start | bytes 393224 | tf_op jit(solution)/shard_map/ppermute | solution.py:447
  11.8 1.8 %copy-start.1 = (bf16[128,128]{1,0:T(8,128)(2,1)S(1)}, bf16[128,128]{1,0:T(8,128)(2,1)}, u32[]{:S(2)}) copy-start(bf16[128,128]{1,0:T(8,128)(2,1)} %refs_1_.3) | copy-start | bytes 98308
  14.7 4.1 %collective-permute-start.7 = (bf16[96,256]{1,0:T(8,128)(2,1)S(1)}, bf16[96,256]{1,0:T(8,128)(2,1)S(1)}, u32[]{:S(2)}, u32[]{:S(2)}) collective-permute-start(bf16[96,256]{1,0:T(8,128)(2,1)S(1)} %get-tuple-element.35), channel_id=1, source_target_pairs={{0,12},{4,24},{8,20},{12,0},{16,28},{20,8},{24,4},{28,16},{1,13},{... | collective-permute-start | bytes 147464 | tf_op jit(solution)/shard_map/ppermute | solution.py:47
  15.4 3.4 %collective-permute-start.8 = (bf16[64,256]{1,0:T(8,128)(2,1)S(1)}, bf16[64,256]{1,0:T(8,128)(2,1)S(1)}, u32[]{:S(2)}, u32[]{:S(2)}) collective-permute-start(bf16[64,256]{1,0:T(8,128)(2,1)S(1)} %get-tuple-element.36), channel_id=1, source_target_pairs={{0,20},{4,16},{8,28},{12,24},{16,4},{20,0},{24,12},{28,8},{1,21},{... | collective-permute-start | bytes 98312 | tf_op jit(solution)/shard_map/ppermute | solution.py:47
  16.4 5.7 %collective-permute-start.5 = (bf16[128,128]{1,0:T(8,128)(2,1)S(1)}, bf16[128,128]{1,0:T(8,128)(2,1)S(1)}, u32[]{:S(2)}, u32[]{:S(2)}) collective-permute-start(bf16[128,128]{1,0:T(8,128)(2,1)S(1)} %get-tuple-element.29.att_ref), channel_id=1, source_target_pairs={{0,3},{1,2},{2,1},{3,0},{4,7},{5,6},{6,5},{7,4},{8,11},{9,10},{10,... | collective-permute-start | bytes 98312 | tf_op jit(solution)/shard_map/ppermute | solution.py:54
  18.7 5.2 %collective-permute-start.4 = (bf16[128,128]{1,0:T(8,128)(2,1)S(1)}, bf16[128,128]{1,0:T(8,128)(2,1)S(1)}, u32[]{:S(2)}, u32[]{:S(2)}) collective-permute-start(bf16[128,128]{1,0:T(8,128)(2,1)S(1)} %get-tuple-element.29.att_ref), channel_id=1, source_target_pairs={{0,2},{1,3},{2,0},{3,1},{4,6},{5,7},{6,4},{7,5},{8,10},{9,11},{10,... | collective-permute-start | bytes 98312 | tf_op jit(solution)/shard_map/ppermute | solution.py:54
  18.9 6.1 %collective-permute-start.11 = (bf16[128,256]{1,0:T(8,128)(2,1)S(1)}, bf16[128,256]{1,0:T(8,128)(2,1)S(1)}, u32[]{:S(2)}, u32[]{:S(2)}) collective-permute-start(bf16[128,256]{1,0:T(8,128)(2,1)S(1)} %get-tuple-element.39), channel_id=1, source_target_pairs={{0,28},{4,8},{8,4},{12,16},{16,12},{20,24},{24,20},{28,0},{1,29},{... | collective-permute-start | bytes 196616 | tf_op jit(solution)/shard_map/ppermute | solution.py:47
  21.0 3.9 %collective-permute-start.10 = (bf16[128,128]{1,0:T(8,128)(2,1)S(1)}, bf16[128,128]{1,0:T(8,128)(2,1)S(1)}, u32[]{:S(2)}, u32[]{:S(2)}) collective-permute-start(bf16[128,128]{1,0:T(8,128)(2,1)S(1)} %get-tuple-element.38), channel_id=1, source_target_pairs={{0,1},{1,0},{2,3},{3,2},{4,5},{5,4},{6,7},{7,6},{8,9},{9,8},{10,11... | collective-permute-start | bytes 98312 | tf_op jit(solution)/shard_map/ppermute | solution.py:54
  22.1 2.9 %collective-permute-start.12 = (bf16[512,256]{1,0:T(8,128)(2,1)S(1)}, bf16[512,256]{1,0:T(8,128)(2,1)S(1)}, u32[]{:S(2)}, u32[]{:S(2)}) collective-permute-start(bf16[512,256]{1,0:T(8,128)(2,1)S(1)} %pack.1), channel_id=1, source_target_pairs={{0,4},{4,0},{8,12},{12,8},{16,20},{20,16},{24,28},{28,24},{1,5},{5... | collective-permute-start | bytes 786440 | tf_op jit(solution)/shard_map/ppermute | solution.py:47

commit v15 on v14

--- a/solution.py
+++ b/solution.py
@@ -20,6 +20,7 @@
 BF16 = jnp.bfloat16
 PREPARE_COST = 10**10
 ATTEND_COST = 10**10
+GRAD_COST = 0
 COMBINE_COST = 10**10
 GATHER_COST = 10**10
 PACK_COST = 10**10
@@ -166,7 +167,7 @@
         in_specs=[VMEM] * 3,
         out_specs=VMEM,
         compiler_params=PARAMS,
-        cost_estimate=cost(PREPARE_COST),
+        cost_estimate=cost(GRAD_COST),
         name="prepare",
     )(cotangent, out_weight, after)
 

time: 26.2 us -> 25.9 us (0.989)
  waiting for transfers between devices: 4.11 us -> 2.66 us
  starting transfers between devices: 16.4 us -> 17 us
  local copies, waits for them, and re-layouts: 0.9 us -> 1.33 us
    ppermute x8, starting transfers between devices: 7.41 us -> 9.24 us  [trade(): lax.ppermute(array, 'seq', [(i, (i + (step if i % 2 == 0 else -step)) % c...]
    ppermute x8, waiting for transfers between devices: 1.54 us -> 0.02 us  [trade(): lax.ppermute(array, 'seq', [(i, (i + (step if i % 2 == 0 else -step)) % c...]
    ppermute x4, starting transfers between devices: 6.55 us -> 5.28 us  [swap(): return lax.ppermute(array, 'head', [(i, i ^ mask) for i in range(count)])]
    unnamed x9, local copies, waits for them, and re-layouts: 0.89 us -> 1.31 us
where the time goes in v15:
time: 25.9 us; the launch traced here: 25.6 us
  starting transfers between devices  17 us (66%)
  Pallas kernels  3.88 us (15%)
  waiting for transfers between devices  2.66 us (10%)
  local copies, waits for them, and re-layouts  1.33 us (5%)
  between operations  0.78 us (3%)
    ppermute x8, starting transfers between devices, trade(): lax.ppermute(array, 'seq', [(i, (i + (step if i % 2 == 0 else -step)) % c...  9.24 us
    ppermute x4, starting transfers between devices, swap(): return lax.ppermute(array, 'head', [(i, i ^ mask) for i in range(count)])  5.28 us
    ppermute x4, waiting for transfers between devices, swap(): return lax.ppermute(array, 'head', [(i, i ^ mask) for i in range(count)])  2.64 us
    ppermute x1, starting transfers between devices, spread_slice(): return lax.ppermute(array, ('seq', 'head'), pairs)  2.47 us
    unnamed x9, local copies, waits for them, and re-layouts  1.31 us
    pallas_call x1, Pallas kernels, weight_slices(): pl.pallas_call(body, out_shape=(shape(8, columns, kind=F32), shape(*out_w...  1.22 us
    pallas_call x1, Pallas kernels, finish_ring(): pl.pallas_call(finish_ring_kernel, out_shape=(shape(BLK, width),) + (shap...  1.05 us
    pallas_call x1, Pallas kernels, attend(): pl.pallas_call(body, out_shape=(shape(BLK, HD), shape(BLK, HD), *sums), i...  1.02 us
  transfers between devices with their start and end apart: 13, of which 3 were waited for; matrix products, arithmetic and copies ran while one was open for 0% of the time, Pallas kernels for 11%

profile of v15, /device:TPU:0, one launch (start us, length us, event | category | flops | bytes accessed | tf_op | source)
XLA Modules:
  0.0 25.6 jit_solution(318401127719979312)
XLA Ops:
  0.6 0.8 %constant_dynamic-update-slice_fusion.1 = bf16[128,256]{1,0:T(8,128)(2,1)S(1)} fusion(bf16[128,128]{1,0:T(8,128)(2,1)} %param.7), kind=kLoop, calls=%fused_computation.1 | loop fusion | bytes 65536
  1.4 0.0 copy-start.2
  1.4 0.5 %collective-permute-start = (bf16[128,256]{1,0:T(8,128)(2,1)S(1)}, bf16[128,256]{1,0:T(8,128)(2,1)S(1)}, u32[]{:S(2)}, u32[]{:S(2)}) collective-permute-start(bf16[128,256]{1,0:T(8,128)(2,1)S(1)} %constant_dynamic-update-slice_fusion.refs_2_.own_ref.refs_3_), channel_id=1, source_target_pairs={{0,4},{4,0},{8,12},{12,8},{16,20},{20,16},{24,28},{28,24},{1,5},{5... | collective-permute-start | bytes 196616 | tf_op jit(solution)/shard_map/ppermute | solution.py:48
  2.0 0.1 copy-done.2
  2.1 1.2 %slices.1 = (f32[8,640]{1,0:T(8,128)S(1)}, bf16[128,2048]{1,0:T(8,128)(2,1)S(1)}, bf16[128,512]{1,0:T(8,128)(2,1)S(1)}, bf16[128,512]{1,0:T(8,128)(2,1)S(1)}, bf16[80,512]{1,0:T(8,128)(2,1)S(1)}) custom-call(s32[1,8]{1,0:T(1,128)S(1)} %copy-done.2, bf16[128,2048]{1,0:T(8,128)(2,1)} %refs_1_.2, ...), custom_call_target="tpu_custom_call" | custom-call | flops 10000000000 | tf_op jit(solution)/shard_map/slices/pallas_call | solution.py:142
  3.3 3.5 %collective-permute-start.1 = (bf16[160,256]{1,0:T(8,128)(2,1)S(1)}, bf16[160,256]{1,0:T(8,128)(2,1)S(1)}, u32[]{:S(2)}, u32[]{:S(2)}) collective-permute-start(bf16[160,256]{1,0:T(8,128)(2,1)S(1)} %get-tuple-element.28), channel_id=1, source_target_pairs={{0,28},{4,8},{8,4},{12,16},{16,12},{20,24},{24,20},{28,0},{1,29},{... | collective-permute-start | bytes 245768 | tf_op jit(solution)/shard_map/ppermute | solution.py:48
  6.9 0.7 %collective-permute-start.2 = (bf16[64,256]{1,0:T(8,128)(2,1)S(1)}, bf16[64,256]{1,0:T(8,128)(2,1)S(1)}, u32[]{:S(2)}, u32[]{:S(2)}) collective-permute-start(bf16[64,256]{1,0:T(8,128)(2,1)S(1)} %get-tuple-element.27.after_ref), channel_id=1, source_target_pairs={{0,12},{4,24},{8,20},{12,0},{16,28},{20,8},{24,4},{28,16},{1,13},{... | collective-permute-start | bytes 98312 | tf_op jit(solution)/shard_map/ppermute | solution.py:48
  7.6 0.0 collective-permute-start.3
  7.6 2.1 %collective-permute-start.9 = (bf16[80,512]{1,0:T(8,128)(2,1)S(1)}, bf16[80,512]{1,0:T(8,128)(2,1)S(1)}, u32[]{:S(2)}, u32[]{:S(2)}) collective-permute-start(bf16[80,512]{1,0:T(8,128)(2,1)S(1)} %get-tuple-element.37), channel_id=1, source_target_pairs={{0,1},{1,0},{2,3},{3,2},{4,5},{5,4},{6,7},{7,6},{8,9},{9,8},{10,11... | collective-permute-start | bytes 245768 | tf_op jit(solution)/shard_map/ppermute | solution.py:55
  9.6 2.5 %collective-permute-start.6 = (bf16[128,512]{1,0:T(8,128)(2,1)S(1)}, bf16[128,512]{1,0:T(8,128)(2,1)S(1)}, u32[]{:S(2)}, u32[]{:S(2)}) collective-permute-start(bf16[128,512]{1,0:T(8,128)(2,1)S(1)} %get-tuple-element.31), channel_id=1, source_target_pairs={{0,3},{1,2},{2,1},{3,0},{4,6},{5,7},{6,4},{7,5},{8,11},{9,10},{10,... | collective-permute-start | bytes 393224 | tf_op jit(solution)/shard_map/ppermute | solution.py:448
  12.1 0.3 %prepare.1.refs_2_ = bf16[128,128]{1,0:T(8,128)(2,1)S(1)} custom-call(bf16[128,2048]{1,0:T(8,128)(2,1)S(1)} %copy-done, bf16[128,2048]{1,0:T(8,128)(2,1)S(1)} %get-tuple-element.25.w_ref, bf16[64,256]{1,0:T(8,128)(2,1)S(1)} %get-tuple-element.27.after_ref), custom_call_target="tpu_custom_call" | custom-call | tf_op jit(solution)/shard_map/prepare/pallas_call | solution.py:164
  12.4 0.0 collective-permute-done.2.refs_6_
  12.4 0.0 collective-permute-done.3.refs_7_
  12.5 0.4 %copy-done.1 = bf16[128,128]{1,0:T(8,128)(2,1)S(1)} copy-done((bf16[128,128]{1,0:T(8,128)(2,1)S(1)}, bf16[128,128]{1,0:T(8,128)(2,1)}, u32[]{:S(2)}) %copy-start.1) | copy-done | bytes 32792
  12.9 1.0 %attend.1 = (bf16[128,128]{1,0:T(8,128)(2,1)S(1)}, bf16[128,128]{1,0:T(8,128)(2,1)S(1)}, f32[128,256]{1,0:T(8,128)S(1)}, f32[128,256]{1,0:T(8,128)S(1)}, f32[128...) custom-call(f32[8,640]{1,0:T(8,128)S(1)} %get-tuple-element.24.mult_ref.refs_0_, ...), custom_call_target="tpu_custom_call" | custom-call | flops 10000000000 | tf_op jit(solution)/shard_map/attend/pallas_call | solution.py:245
  13.9 0.4 %collective-permute-start.7 = (bf16[96,256]{1,0:T(8,128)(2,1)S(1)}, bf16[96,256]{1,0:T(8,128)(2,1)S(1)}, u32[]{:S(2)}, u32[]{:S(2)}) collective-permute-start(bf16[96,256]{1,0:T(8,128)(2,1)S(1)} %get-tuple-element.35), channel_id=1, source_target_pairs={{0,12},{4,24},{8,20},{12,0},{16,28},{20,8},{24,4},{28,16},{1,13},{... | collective-permute-start | bytes 147464 | tf_op jit(solution)/shard_map/ppermute | solution.py:48
  14.3 2.4 %collective-permute-start.8 = (bf16[64,256]{1,0:T(8,128)(2,1)S(1)}, bf16[64,256]{1,0:T(8,128)(2,1)S(1)}, u32[]{:S(2)}, u32[]{:S(2)}) collective-permute-start(bf16[64,256]{1,0:T(8,128)(2,1)S(1)} %get-tuple-element.36), channel_id=1, source_target_pairs={{0,20},{4,16},{8,28},{12,24},{16,4},{20,0},{24,12},{28,8},{1,21},{... | collective-permute-start | bytes 98312 | tf_op jit(solution)/shard_map/ppermute | solution.py:48
  16.6 2.2 %collective-permute-start.5 = (bf16[128,128]{1,0:T(8,128)(2,1)S(1)}, bf16[128,128]{1,0:T(8,128)(2,1)S(1)}, u32[]{:S(2)}, u32[]{:S(2)}) collective-permute-start(bf16[128,128]{1,0:T(8,128)(2,1)S(1)} %get-tuple-element.29.att_ref), channel_id=1, source_target_pairs={{0,3},{1,2},{2,1},{3,0},{4,7},{5,6},{6,5},{7,4},{8,11},{9,10},{10,... | collective-permute-start | bytes 98312 | tf_op jit(solution)/shard_map/ppermute | solution.py:55
  18.9 0.0 collective-permute-done.9.half_ref
  18.9 0.0 collective-permute-start.4
  18.9 0.0 collective-permute-done.8.minus_ref
  18.9 0.0 collective-permute-done.7.plus_ref
  19.0 1.7 %collective-permute-start.11 = (bf16[128,256]{1,0:T(8,128)(2,1)S(1)}, bf16[128,256]{1,0:T(8,128)(2,1)S(1)}, u32[]{:S(2)}, u32[]{:S(2)}) collective-permute-start(bf16[128,256]{1,0:T(8,128)(2,1)S(1)} %get-tuple-element.39), channel_id=1, source_target_pairs={{0,28},{4,8},{8,4},{12,16},{16,12},{20,24},{24,20},{28,0},{1,29},{... | collective-permute-start | bytes 196616 | tf_op jit(solution)/shard_map/ppermute | solution.py:48
  20.7 1.0 %collective-permute-start.10 = (bf16[128,128]{1,0:T(8,128)(2,1)S(1)}, bf16[128,128]{1,0:T(8,128)(2,1)S(1)}, u32[]{:S(2)}, u32[]{:S(2)}) collective-permute-start(bf16[128,128]{1,0:T(8,128)(2,1)S(1)} %get-tuple-element.38), channel_id=1, source_target_pairs={{0,1},{1,0},{2,3},{3,2},{4,5},{5,4},{6,7},{7,6},{8,9},{9,8},{10,11... | collective-permute-start | bytes 98312 | tf_op jit(solution)/shard_map/ppermute | solution.py:55
  21.6 0.7 %collective-permute-done.5.three_ref.after_ref = bf16[128,128]{1,0:T(8,128)(2,1)S(1)} collective-permute-done((bf16[128,128]{1,0:T(8,128)(2,1)S(1)}, bf16[128,128]{1,0:T(8,128)(2,1)S(1)}, u32[]{:S(2)}, u32[]{:S(2)}) %collective-permute-start.5) | collective-permute-done | bytes 32800 | tf_op jit(solution)/shard_map/ppermute | solution.py:55
  22.4 0.1 collective-permute-start.12
  22.4 1.2 %collective-permute-done.4.two_ref = bf16[128,128]{1,0:T(8,128)(2,1)S(1)} collective-permute-done((bf16[128,128]{1,0:T(8,128)(2,1)S(1)}, bf16[128,128]{1,0:T(8,128)(2,1)S(1)}, u32[]{:S(2)}, u32[]{:S(2)}) %collective-permute-start.4) | collective-permute-done | bytes 32800 | tf_op jit(solution)/shard_map/ppermute | solution.py:55
  23.7 0.2 project.1.partial_ref
  23.9 0.7 %collective-permute-done.10.one_ref = bf16[128,128]{1,0:T(8,128)(2,1)S(1)} collective-permute-done((bf16[128,128]{1,0:T(8,128)(2,1)S(1)}, bf16[128,128]{1,0:T(8,128)(2,1)S(1)}, u32[]{:S(2)}, u32[]{:S(2)}) %collective-permute-start.10) | collective-permute-done | bytes 32800 | tf_op jit(solution)/shard_map/ppermute | solution.py:55
  24.6 0.0 collective-permute-done.11.second_ref
  24.6 0.0 collective-permute-done.12.first_ref
  24.6 1.1 %finish.1 = (bf16[128,512]{1,0:T(8,128)(2,1)}, bf16[128,128]{1,0:T(8,128)(2,1)}, bf16[128,128]{1,0:T(8,128)(2,1)}, bf16[128,128]{1,0:T(8,128)(2,1)}) custom-call(f32[128,512]{1,0:T(8,128)S(1)} %project.1.partial_ref, bf16[128,128]{1,0:T(8,128)(2,1)S(1)} %gather.1.one_ref, bf16[128,128]{1,0:T(8,128)(2,1)S(1)} %collective-permute-done.4.two_ref, ...), custom_call_target="tpu_custom_call" | custom-call | tf_op jit(solution)/shard_map/finish/pallas_call | solution.py:394
  (13 shorter events, 0.1 us)
Async XLA Ops:
  0.6 0.8 %copy-start.3 = (bf16[128,128]{1,0:T(8,128)(2,1)S(1)}, bf16[128,128]{1,0:T(8,128)(2,1)}, u32[]{:S(2)}) copy-start(bf16[128,128]{1,0:T(8,128)(2,1)} %param.8) | copy-start | bytes 98308
  1.4 0.7 %copy-start.2 = (s32[1,8]{1,0:T(1,128)S(1)}, s32[1,8]{1,0:T(1,128)}, u32[]{:S(2)}) copy-start(s32[1,8]{1,0:T(1,128)} %refs_0_.1) | copy-start | bytes 100
  1.4 1.9 %collective-permute-start = (bf16[128,256]{1,0:T(8,128)(2,1)S(1)}, bf16[128,256]{1,0:T(8,128)(2,1)S(1)}, u32[]{:S(2)}, u32[]{:S(2)}) collective-permute-start(bf16[128,256]{1,0:T(8,128)(2,1)S(1)} %constant_dynamic-update-slice_fusion.refs_2_.own_ref.refs_3_), channel_id=1, source_target_pairs={{0,4},{4,0},{8,12},{12,8},{16,20},{20,16},{24,28},{28,24},{1,5},{5... | collective-permute-start | bytes 196616 | tf_op jit(solution)/shard_map/ppermute | solution.py:48
  2.1 10.0 %copy-start = (bf16[128,2048]{1,0:T(8,128)(2,1)S(1)}, bf16[128,2048]{1,0:T(8,128)(2,1)}, u32[]{:S(2)}) copy-start(bf16[128,2048]{1,0:T(8,128)(2,1)} %cot_ref.1) | copy-start | bytes 1572868
  3.3 9.1 %collective-permute-start.1 = (bf16[160,256]{1,0:T(8,128)(2,1)S(1)}, bf16[160,256]{1,0:T(8,128)(2,1)S(1)}, u32[]{:S(2)}, u32[]{:S(2)}) collective-permute-start(bf16[160,256]{1,0:T(8,128)(2,1)S(1)} %get-tuple-element.28), channel_id=1, source_target_pairs={{0,28},{4,8},{8,4},{12,16},{16,12},{20,24},{24,20},{28,0},{1,29},{... | collective-permute-start | bytes 245768 | tf_op jit(solution)/shard_map/ppermute | solution.py:48
  6.9 5.6 %collective-permute-start.2 = (bf16[64,256]{1,0:T(8,128)(2,1)S(1)}, bf16[64,256]{1,0:T(8,128)(2,1)S(1)}, u32[]{:S(2)}, u32[]{:S(2)}) collective-permute-start(bf16[64,256]{1,0:T(8,128)(2,1)S(1)} %get-tuple-element.27.after_ref), channel_id=1, source_target_pairs={{0,12},{4,24},{8,20},{12,0},{16,28},{20,8},{24,4},{28,16},{1,13},{... | collective-permute-start | bytes 98312 | tf_op jit(solution)/shard_map/ppermute | solution.py:48
  7.6 4.9 %collective-permute-start.3 = (bf16[64,256]{1,0:T(8,128)(2,1)S(1)}, bf16[64,256]{1,0:T(8,128)(2,1)S(1)}, u32[]{:S(2)}, u32[]{:S(2)}) collective-permute-start(bf16[64,256]{1,0:T(8,128)(2,1)S(1)} %get-tuple-element.27.after_ref), channel_id=1, source_target_pairs={{0,16},{4,20},{8,24},{12,28},{16,0},{20,4},{24,8},{28,12},{1,17},{... | collective-permute-start | bytes 98312 | tf_op jit(solution)/shard_map/ppermute | solution.py:48
  7.6 11.3 %collective-permute-start.9 = (bf16[80,512]{1,0:T(8,128)(2,1)S(1)}, bf16[80,512]{1,0:T(8,128)(2,1)S(1)}, u32[]{:S(2)}, u32[]{:S(2)}) collective-permute-start(bf16[80,512]{1,0:T(8,128)(2,1)S(1)} %get-tuple-element.37), channel_id=1, source_target_pairs={{0,1},{1,0},{2,3},{3,2},{4,5},{5,4},{6,7},{7,6},{8,9},{9,8},{10,11... | collective-permute-start | bytes 245768 | tf_op jit(solution)/shard_map/ppermute | solution.py:55
  9.6 9.3 %collective-permute-start.6 = (bf16[128,512]{1,0:T(8,128)(2,1)S(1)}, bf16[128,512]{1,0:T(8,128)(2,1)S(1)}, u32[]{:S(2)}, u32[]{:S(2)}) collective-permute-start(bf16[128,512]{1,0:T(8,128)(2,1)S(1)} %get-tuple-element.31), channel_id=1, source_target_pairs={{0,3},{1,2},{2,1},{3,0},{4,6},{5,7},{6,4},{7,5},{8,11},{9,10},{10,... | collective-permute-start | bytes 393224 | tf_op jit(solution)/shard_map/ppermute | solution.py:448
  12.1 0.8 %copy-start.1 = (bf16[128,128]{1,0:T(8,128)(2,1)S(1)}, bf16[128,128]{1,0:T(8,128)(2,1)}, u32[]{:S(2)}) copy-start(bf16[128,128]{1,0:T(8,128)(2,1)} %refs_1_.3) | copy-start | bytes 98308
  13.9 5.0 %collective-permute-start.7 = (bf16[96,256]{1,0:T(8,128)(2,1)S(1)}, bf16[96,256]{1,0:T(8,128)(2,1)S(1)}, u32[]{:S(2)}, u32[]{:S(2)}) collective-permute-start(bf16[96,256]{1,0:T(8,128)(2,1)S(1)} %get-tuple-element.35), channel_id=1, source_target_pairs={{0,12},{4,24},{8,20},{12,0},{16,28},{20,8},{24,4},{28,16},{1,13},{... | collective-permute-start | bytes 147464 | tf_op jit(solution)/shard_map/ppermute | solution.py:48
  14.3 4.6 %collective-permute-start.8 = (bf16[64,256]{1,0:T(8,128)(2,1)S(1)}, bf16[64,256]{1,0:T(8,128)(2,1)S(1)}, u32[]{:S(2)}, u32[]{:S(2)}) collective-permute-start(bf16[64,256]{1,0:T(8,128)(2,1)S(1)} %get-tuple-element.36), channel_id=1, source_target_pairs={{0,20},{4,16},{8,28},{12,24},{16,4},{20,0},{24,12},{28,8},{1,21},{... | collective-permute-start | bytes 98312 | tf_op jit(solution)/shard_map/ppermute | solution.py:48
  16.6 5.7 %collective-permute-start.5 = (bf16[128,128]{1,0:T(8,128)(2,1)S(1)}, bf16[128,128]{1,0:T(8,128)(2,1)S(1)}, u32[]{:S(2)}, u32[]{:S(2)}) collective-permute-start(bf16[128,128]{1,0:T(8,128)(2,1)S(1)} %get-tuple-element.29.att_ref), channel_id=1, source_target_pairs={{0,3},{1,2},{2,1},{3,0},{4,7},{5,6},{6,5},{7,4},{8,11},{9,10},{10,... | collective-permute-start | bytes 98312 | tf_op jit(solution)/shard_map/ppermute | solution.py:55
  18.9 4.8 %collective-permute-start.4 = (bf16[128,128]{1,0:T(8,128)(2,1)S(1)}, bf16[128,128]{1,0:T(8,128)(2,1)S(1)}, u32[]{:S(2)}, u32[]{:S(2)}) collective-permute-start(bf16[128,128]{1,0:T(8,128)(2,1)S(1)} %get-tuple-element.29.att_ref), channel_id=1, source_target_pairs={{0,2},{1,3},{2,0},{3,1},{4,6},{5,7},{6,4},{7,5},{8,10},{9,11},{10,... | collective-permute-start | bytes 98312 | tf_op jit(solution)/shard_map/ppermute | solution.py:55
  19.0 5.6 %collective-permute-start.11 = (bf16[128,256]{1,0:T(8,128)(2,1)S(1)}, bf16[128,256]{1,0:T(8,128)(2,1)S(1)}, u32[]{:S(2)}, u32[]{:S(2)}) collective-permute-start(bf16[128,256]{1,0:T(8,128)(2,1)S(1)} %get-tuple-element.39), channel_id=1, source_target_pairs={{0,28},{4,8},{8,4},{12,16},{16,12},{20,24},{24,20},{28,0},{1,29},{... | collective-permute-start | bytes 196616 | tf_op jit(solution)/shard_map/ppermute | solution.py:48
  20.7 3.9 %collective-permute-start.10 = (bf16[128,128]{1,0:T(8,128)(2,1)S(1)}, bf16[128,128]{1,0:T(8,128)(2,1)S(1)}, u32[]{:S(2)}, u32[]{:S(2)}) collective-permute-start(bf16[128,128]{1,0:T(8,128)(2,1)S(1)} %get-tuple-element.38), channel_id=1, source_target_pairs={{0,1},{1,0},{2,3},{3,2},{4,5},{5,4},{6,7},{7,6},{8,9},{9,8},{10,11... | collective-permute-start | bytes 98312 | tf_op jit(solution)/shard_map/ppermute | solution.py:55
  22.4 2.2 %collective-permute-start.12 = (bf16[512,256]{1,0:T(8,128)(2,1)S(1)}, bf16[512,256]{1,0:T(8,128)(2,1)S(1)}, u32[]{:S(2)}, u32[]{:S(2)}) collective-permute-start(bf16[512,256]{1,0:T(8,128)(2,1)S(1)} %pack.1), channel_id=1, source_target_pairs={{0,4},{4,0},{8,12},{12,8},{16,20},{20,16},{24,28},{28,24},{1,5},{5... | collective-permute-start | bytes 786440 | tf_op jit(solution)/shard_map/ppermute | solution.py:48

commit v16 on v15

--- a/solution.py
+++ b/solution.py
@@ -101,12 +101,13 @@
             for i, span in enumerate(spans)]
 
 
-def slices_kernel(ring, index_hbm, w_hbm, after_ref, mult_ref, w_ref, *refs):
+def slices_kernel(ring, index_hbm, q_hbm, w_hbm, after_ref, mult_ref, q_ref, w_ref, *refs):
     del after_ref
     index_ref, sems = refs[-2:]
     slice_refs = refs[:-2]
     copies = [pltpu.make_async_copy(index_hbm, index_ref, sems.at[CHUNKS])]
     copies += row_copies(w_hbm, w_ref, sems, 0)
+    copies.append(pltpu.make_async_copy(q_hbm, q_ref, sems.at[CHUNKS + 1]))
     for copy in copies:
         copy.start()
     copies[0].wait()
@@ -132,7 +133,7 @@
             ref[...] = w_ref[:, columns(head ^ r)]
 
 
-def weight_slices(ring, index, out_weight, heads, columns, after):
+def weight_slices(ring, index, queries, out_weight, heads, columns, after):
     width = out_weight.shape[1] // heads
     rows = (HD, HD, HD // 2 + MARGIN) if ring else (HD,) * heads
 
@@ -141,18 +142,18 @@
 
     return pl.pallas_call(
         body,
-        out_shape=(shape(8, columns, kind=F32), shape(*out_weight.shape))
+        out_shape=(shape(8, columns, kind=F32), shape(BLK, HD), shape(*out_weight.shape))
         + tuple(shape(r, width) for r in rows),
-        in_specs=[HBM] * 2 + [VMEM],
-        out_specs=(VMEM,) * (2 + len(rows)),
+        in_specs=[HBM] * 3 + [VMEM],
+        out_specs=(VMEM,) * (3 + len(rows)),
         scratch_shapes=[
             pltpu.SMEM(index.shape, jnp.int32),
-            pltpu.SemaphoreType.DMA((1 + CHUNKS,)),
+            pltpu.SemaphoreType.DMA((2 + CHUNKS,)),
         ],
         compiler_params=FULL,
         cost_estimate=cost(PREPARE_COST),
         name="slices",
-    )(index, out_weight, after)
+    )(index, queries, out_weight, after)
 
 
 def prepare_kernel(cot_ref, w_ref, after_ref, grad_ref):
@@ -457,8 +458,8 @@
     columns = 3 * BLK + side_rows
     own = jnp.concatenate([key_rows, value_rows], axis=1)
     first = trade(own, 1)
-    mult, weight, *slices = weight_slices(
-        ring, strided_index, out_weight, heads, columns, own
+    mult, queries, weight, *slices = weight_slices(
+        ring, strided_index, queries, out_weight, heads, columns, own
     )
     if ring:
         mine, whole, half = slices

time: 25.9 us -> 25.6 us (0.988)
  local copies, waits for them, and re-layouts: 1.33 us -> 1 us
    ppermute x4, starting transfers between devices: 5.28 us -> 5.74 us  [swap(): return lax.ppermute(array, 'head', [(i, i ^ mask) for i in range(count)])]
    ppermute x8, starting transfers between devices: 9.24 us -> 8.79 us  [trade(): lax.ppermute(array, 'seq', [(i, (i + (step if i % 2 == 0 else -step)) % c...]
    unnamed x9, local copies, waits for them, and re-layouts: 1.31 us -> 0.99 us
where the time goes in v16:
time: 25.6 us; the launch traced here: 25.3 us
  starting transfers between devices  17 us (66%)
  Pallas kernels  3.89 us (15%)
  waiting for transfers between devices  2.66 us (10%)
  local copies, waits for them, and re-layouts  1 us (4%)
  between operations  0.78 us (3%)
    ppermute x8, starting transfers between devices, trade(): lax.ppermute(array, 'seq', [(i, (i + (step if i % 2 == 0 else -step)) % c...  8.79 us
    ppermute x4, starting transfers between devices, swap(): return lax.ppermute(array, 'head', [(i, i ^ mask) for i in range(count)])  5.74 us
    ppermute x4, waiting for transfers between devices, swap(): return lax.ppermute(array, 'head', [(i, i ^ mask) for i in range(count)])  2.64 us
    ppermute x1, starting transfers between devices, spread_slice(): return lax.ppermute(array, ('seq', 'head'), pairs)  2.47 us
    pallas_call x1, Pallas kernels, weight_slices(): pl.pallas_call(body, out_shape=(shape(8, columns, kind=F32), shape(BLK, H...  1.23 us
    pallas_call x1, Pallas kernels, finish_ring(): pl.pallas_call(finish_ring_kernel, out_shape=(shape(BLK, width),) + (shap...  1.05 us
    pallas_call x1, Pallas kernels, attend(): pl.pallas_call(body, out_shape=(shape(BLK, HD), shape(BLK, HD), *sums), i...  1.02 us
    unnamed x9, local copies, waits for them, and re-layouts  0.99 us
  transfers between devices with their start and end apart: 13, of which 3 were waited for; matrix products, arithmetic and copies ran while one was open for 0% of the time, Pallas kernels for 11%

profile of v16, /device:TPU:0, one launch (start us, length us, event | category | flops | bytes accessed | tf_op | source)
XLA Modules:
  0.0 25.3 jit_solution(14675529641616108066)
XLA Ops:
  0.6 0.8 %constant_dynamic-update-slice_fusion.1 = bf16[128,256]{1,0:T(8,128)(2,1)S(1)} fusion(bf16[128,128]{1,0:T(8,128)(2,1)} %param.7), kind=kLoop, calls=%fused_computation.1 | loop fusion | bytes 65536
  1.4 0.0 copy-start.1
  1.4 0.0 copy-start.2
  1.5 0.5 %collective-permute-start = (bf16[128,256]{1,0:T(8,128)(2,1)S(1)}, bf16[128,256]{1,0:T(8,128)(2,1)S(1)}, u32[]{:S(2)}, u32[]{:S(2)}) collective-permute-start(bf16[128,256]{1,0:T(8,128)(2,1)S(1)} %constant_dynamic-update-slice_fusion.refs_3_.own_ref), channel_id=1, source_target_pairs={{0,4},{4,0},{8,12},{12,8},{16,20},{20,16},{24,28},{28,24},{1,5},{5... | collective-permute-start | bytes 196616 | tf_op jit(solution)/shard_map/ppermute | solution.py:48
  2.0 0.2 copy-done.1
  2.2 1.2 %slices.1 = (f32[8,640]{1,0:T(8,128)S(1)}, bf16[128,128]{1,0:T(8,128)(2,1)S(1)}, bf16[128,2048]{1,0:T(8,128)(2,1)S(1)}, bf16[128,512]{1,0:T(8,128)(2,1)S(1)}, bf...) custom-call(s32[1,8]{1,0:T(1,128)S(1)} %copy-done.2, bf16[128,128]{1,0:T(8,128)(2,1)S(1)} %copy-done.1, ...), custom_call_target="tpu_custom_call" | custom-call | flops 10000000000 | tf_op jit(solution)/shard_map/slices/pallas_call | solution.py:143
  3.4 0.0 collective-permute-done.first_ref.refs_4_
  3.5 3.4 %collective-permute-start.1 = (bf16[160,256]{1,0:T(8,128)(2,1)S(1)}, bf16[160,256]{1,0:T(8,128)(2,1)S(1)}, u32[]{:S(2)}, u32[]{:S(2)}) collective-permute-start(bf16[160,256]{1,0:T(8,128)(2,1)S(1)} %get-tuple-element.30), channel_id=1, source_target_pairs={{0,28},{4,8},{8,4},{12,16},{16,12},{20,24},{24,20},{28,0},{1,29},{... | collective-permute-start | bytes 245768 | tf_op jit(solution)/shard_map/ppermute | solution.py:48
  6.9 0.8 %collective-permute-start.2 = (bf16[64,256]{1,0:T(8,128)(2,1)S(1)}, bf16[64,256]{1,0:T(8,128)(2,1)S(1)}, u32[]{:S(2)}, u32[]{:S(2)}) collective-permute-start(bf16[64,256]{1,0:T(8,128)(2,1)S(1)} %get-tuple-element.29.after_ref), channel_id=1, source_target_pairs={{0,12},{4,24},{8,20},{12,0},{16,28},{20,8},{24,4},{28,16},{1,13},{... | collective-permute-start | bytes 98312 | tf_op jit(solution)/shard_map/ppermute | solution.py:48
  7.7 0.0 collective-permute-start.3
  7.7 2.1 %collective-permute-start.9 = (bf16[80,512]{1,0:T(8,128)(2,1)S(1)}, bf16[80,512]{1,0:T(8,128)(2,1)S(1)}, u32[]{:S(2)}, u32[]{:S(2)}) collective-permute-start(bf16[80,512]{1,0:T(8,128)(2,1)S(1)} %get-tuple-element.39), channel_id=1, source_target_pairs={{0,1},{1,0},{2,3},{3,2},{4,5},{5,4},{6,7},{7,6},{8,9},{9,8},{10,11... | collective-permute-start | bytes 245768 | tf_op jit(solution)/shard_map/ppermute | solution.py:55
  9.8 2.5 %collective-permute-start.6 = (bf16[128,512]{1,0:T(8,128)(2,1)S(1)}, bf16[128,512]{1,0:T(8,128)(2,1)S(1)}, u32[]{:S(2)}, u32[]{:S(2)}) collective-permute-start(bf16[128,512]{1,0:T(8,128)(2,1)S(1)} %get-tuple-element.33), channel_id=1, source_target_pairs={{0,3},{1,2},{2,1},{3,0},{4,6},{5,7},{6,4},{7,5},{8,11},{9,10},{10,... | collective-permute-start | bytes 393224 | tf_op jit(solution)/shard_map/ppermute | solution.py:449
  12.2 0.3 %prepare.1.refs_2_ = bf16[128,128]{1,0:T(8,128)(2,1)S(1)} custom-call(bf16[128,2048]{1,0:T(8,128)(2,1)S(1)} %copy-done, bf16[128,2048]{1,0:T(8,128)(2,1)S(1)} %get-tuple-element.27.w_ref, bf16[64,256]{1,0:T(8,128)(2,1)S(1)} %get-tuple-element.29.after_ref), custom_call_target="tpu_custom_call" | custom-call | tf_op jit(solution)/shard_map/prepare/pallas_call | solution.py:165
  12.5 0.0 collective-permute-done.2.refs_6_
  12.6 0.0 collective-permute-done.3.refs_7_
  12.6 0.0 collective-permute-done.1.refs_5_
  12.6 1.0 %attend.1 = (bf16[128,128]{1,0:T(8,128)(2,1)S(1)}, bf16[128,128]{1,0:T(8,128)(2,1)S(1)}, f32[128,256]{1,0:T(8,128)S(1)}, f32[128,256]{1,0:T(8,128)S(1)}, f32[128...) custom-call(f32[8,640]{1,0:T(8,128)S(1)} %get-tuple-element.25.mult_ref.refs_0_, ...), custom_call_target="tpu_custom_call" | custom-call | flops 10000000000 | tf_op jit(solution)/shard_map/attend/pallas_call | solution.py:246
  13.6 0.3 %collective-permute-start.7 = (bf16[96,256]{1,0:T(8,128)(2,1)S(1)}, bf16[96,256]{1,0:T(8,128)(2,1)S(1)}, u32[]{:S(2)}, u32[]{:S(2)}) collective-permute-start(bf16[96,256]{1,0:T(8,128)(2,1)S(1)} %get-tuple-element.37), channel_id=1, source_target_pairs={{0,12},{4,24},{8,20},{12,0},{16,28},{20,8},{24,4},{28,16},{1,13},{... | collective-permute-start | bytes 147464 | tf_op jit(solution)/shard_map/ppermute | solution.py:48
  13.9 2.4 %collective-permute-start.8 = (bf16[64,256]{1,0:T(8,128)(2,1)S(1)}, bf16[64,256]{1,0:T(8,128)(2,1)S(1)}, u32[]{:S(2)}, u32[]{:S(2)}) collective-permute-start(bf16[64,256]{1,0:T(8,128)(2,1)S(1)} %get-tuple-element.38), channel_id=1, source_target_pairs={{0,20},{4,16},{8,28},{12,24},{16,4},{20,0},{24,12},{28,8},{1,21},{... | collective-permute-start | bytes 98312 | tf_op jit(solution)/shard_map/ppermute | solution.py:48
  16.3 2.7 %collective-permute-start.5 = (bf16[128,128]{1,0:T(8,128)(2,1)S(1)}, bf16[128,128]{1,0:T(8,128)(2,1)S(1)}, u32[]{:S(2)}, u32[]{:S(2)}) collective-permute-start(bf16[128,128]{1,0:T(8,128)(2,1)S(1)} %get-tuple-element.31.att_ref), channel_id=1, source_target_pairs={{0,3},{1,2},{2,1},{3,0},{4,7},{5,6},{6,5},{7,4},{8,11},{9,10},{10,... | collective-permute-start | bytes 98312 | tf_op jit(solution)/shard_map/ppermute | solution.py:55
  19.0 0.0 collective-permute-done.9.half_ref
  19.0 0.0 collective-permute-start.4
  19.0 0.0 collective-permute-done.8.minus_ref
  19.1 0.0 collective-permute-done.6.whole_ref
  19.1 1.3 %collective-permute-start.11 = (bf16[128,256]{1,0:T(8,128)(2,1)S(1)}, bf16[128,256]{1,0:T(8,128)(2,1)S(1)}, u32[]{:S(2)}, u32[]{:S(2)}) collective-permute-start(bf16[128,256]{1,0:T(8,128)(2,1)S(1)} %get-tuple-element.41), channel_id=1, source_target_pairs={{0,28},{4,8},{8,4},{12,16},{16,12},{20,24},{24,20},{28,0},{1,29},{... | collective-permute-start | bytes 196616 | tf_op jit(solution)/shard_map/ppermute | solution.py:48
  20.4 1.0 %collective-permute-start.10 = (bf16[128,128]{1,0:T(8,128)(2,1)S(1)}, bf16[128,128]{1,0:T(8,128)(2,1)S(1)}, u32[]{:S(2)}, u32[]{:S(2)}) collective-permute-start(bf16[128,128]{1,0:T(8,128)(2,1)S(1)} %get-tuple-element.40), channel_id=1, source_target_pairs={{0,1},{1,0},{2,3},{3,2},{4,5},{5,4},{6,7},{7,6},{8,9},{9,8},{10,11... | collective-permute-start | bytes 98312 | tf_op jit(solution)/shard_map/ppermute | solution.py:55
  21.3 0.8 %collective-permute-done.5.three_ref.after_ref = bf16[128,128]{1,0:T(8,128)(2,1)S(1)} collective-permute-done((bf16[128,128]{1,0:T(8,128)(2,1)S(1)}, bf16[128,128]{1,0:T(8,128)(2,1)S(1)}, u32[]{:S(2)}, u32[]{:S(2)}) %collective-permute-start.5) | collective-permute-done | bytes 32800 | tf_op jit(solution)/shard_map/ppermute | solution.py:55
  22.2 0.1 collective-permute-start.12
  22.3 1.6 %collective-permute-done.4.two_ref = bf16[128,128]{1,0:T(8,128)(2,1)S(1)} collective-permute-done((bf16[128,128]{1,0:T(8,128)(2,1)S(1)}, bf16[128,128]{1,0:T(8,128)(2,1)S(1)}, u32[]{:S(2)}, u32[]{:S(2)}) %collective-permute-start.4) | collective-permute-done | bytes 32800 | tf_op jit(solution)/shard_map/ppermute | solution.py:55
  23.8 0.2 project.1.partial_ref
  24.1 0.2 collective-permute-done.10.one_ref
  24.3 1.1 %finish.1 = (bf16[128,512]{1,0:T(8,128)(2,1)}, bf16[128,128]{1,0:T(8,128)(2,1)}, bf16[128,128]{1,0:T(8,128)(2,1)}, bf16[128,128]{1,0:T(8,128)(2,1)}) custom-call(f32[128,512]{1,0:T(8,128)S(1)} %project.1.partial_ref, bf16[128,128]{1,0:T(8,128)(2,1)S(1)} %gather.1.one_ref, bf16[128,128]{1,0:T(8,128)(2,1)S(1)} %collective-permute-done.4.two_ref, ...), custom_call_target="tpu_custom_call" | custom-call | tf_op jit(solution)/shard_map/finish/pallas_call | solution.py:395
  (13 shorter events, 0.1 us)
Async XLA Ops:
  0.6 0.8 %copy-start.3 = (bf16[128,128]{1,0:T(8,128)(2,1)S(1)}, bf16[128,128]{1,0:T(8,128)(2,1)}, u32[]{:S(2)}) copy-start(bf16[128,128]{1,0:T(8,128)(2,1)} %param.8) | copy-start | bytes 98308
  1.4 0.8 %copy-start.1 = (bf16[128,128]{1,0:T(8,128)(2,1)S(1)}, bf16[128,128]{1,0:T(8,128)(2,1)}, u32[]{:S(2)}) copy-start(bf16[128,128]{1,0:T(8,128)(2,1)} %refs_1_.1) | copy-start | bytes 98308
  1.4 0.8 %copy-start.2 = (s32[1,8]{1,0:T(1,128)S(1)}, s32[1,8]{1,0:T(1,128)}, u32[]{:S(2)}) copy-start(s32[1,8]{1,0:T(1,128)} %refs_0_.1) | copy-start | bytes 100
  1.5 2.0 %collective-permute-start = (bf16[128,256]{1,0:T(8,128)(2,1)S(1)}, bf16[128,256]{1,0:T(8,128)(2,1)S(1)}, u32[]{:S(2)}, u32[]{:S(2)}) collective-permute-start(bf16[128,256]{1,0:T(8,128)(2,1)S(1)} %constant_dynamic-update-slice_fusion.refs_3_.own_ref), channel_id=1, source_target_pairs={{0,4},{4,0},{8,12},{12,8},{16,20},{20,16},{24,28},{28,24},{1,5},{5... | collective-permute-start | bytes 196616 | tf_op jit(solution)/shard_map/ppermute | solution.py:48
  2.2 10.1 %copy-start = (bf16[128,2048]{1,0:T(8,128)(2,1)S(1)}, bf16[128,2048]{1,0:T(8,128)(2,1)}, u32[]{:S(2)}) copy-start(bf16[128,2048]{1,0:T(8,128)(2,1)} %cot_ref.1) | copy-start | bytes 1572868
  3.5 9.1 %collective-permute-start.1 = (bf16[160,256]{1,0:T(8,128)(2,1)S(1)}, bf16[160,256]{1,0:T(8,128)(2,1)S(1)}, u32[]{:S(2)}, u32[]{:S(2)}) collective-permute-start(bf16[160,256]{1,0:T(8,128)(2,1)S(1)} %get-tuple-element.30), channel_id=1, source_target_pairs={{0,28},{4,8},{8,4},{12,16},{16,12},{20,24},{24,20},{28,0},{1,29},{... | collective-permute-start | bytes 245768 | tf_op jit(solution)/shard_map/ppermute | solution.py:48
  6.9 5.7 %collective-permute-start.2 = (bf16[64,256]{1,0:T(8,128)(2,1)S(1)}, bf16[64,256]{1,0:T(8,128)(2,1)S(1)}, u32[]{:S(2)}, u32[]{:S(2)}) collective-permute-start(bf16[64,256]{1,0:T(8,128)(2,1)S(1)} %get-tuple-element.29.after_ref), channel_id=1, source_target_pairs={{0,12},{4,24},{8,20},{12,0},{16,28},{20,8},{24,4},{28,16},{1,13},{... | collective-permute-start | bytes 98312 | tf_op jit(solution)/shard_map/ppermute | solution.py:48
  7.7 4.9 %collective-permute-start.3 = (bf16[64,256]{1,0:T(8,128)(2,1)S(1)}, bf16[64,256]{1,0:T(8,128)(2,1)S(1)}, u32[]{:S(2)}, u32[]{:S(2)}) collective-permute-start(bf16[64,256]{1,0:T(8,128)(2,1)S(1)} %get-tuple-element.29.after_ref), channel_id=1, source_target_pairs={{0,16},{4,20},{8,24},{12,28},{16,0},{20,4},{24,8},{28,12},{1,17},{... | collective-permute-start | bytes 98312 | tf_op jit(solution)/shard_map/ppermute | solution.py:48
  7.7 11.4 %collective-permute-start.9 = (bf16[80,512]{1,0:T(8,128)(2,1)S(1)}, bf16[80,512]{1,0:T(8,128)(2,1)S(1)}, u32[]{:S(2)}, u32[]{:S(2)}) collective-permute-start(bf16[80,512]{1,0:T(8,128)(2,1)S(1)} %get-tuple-element.39), channel_id=1, source_target_pairs={{0,1},{1,0},{2,3},{3,2},{4,5},{5,4},{6,7},{7,6},{8,9},{9,8},{10,11... | collective-permute-start | bytes 245768 | tf_op jit(solution)/shard_map/ppermute | solution.py:55
  9.8 9.3 %collective-permute-start.6 = (bf16[128,512]{1,0:T(8,128)(2,1)S(1)}, bf16[128,512]{1,0:T(8,128)(2,1)S(1)}, u32[]{:S(2)}, u32[]{:S(2)}) collective-permute-start(bf16[128,512]{1,0:T(8,128)(2,1)S(1)} %get-tuple-element.33), channel_id=1, source_target_pairs={{0,3},{1,2},{2,1},{3,0},{4,6},{5,7},{6,4},{7,5},{8,11},{9,10},{10,... | collective-permute-start | bytes 393224 | tf_op jit(solution)/shard_map/ppermute | solution.py:449
  13.6 5.4 %collective-permute-start.7 = (bf16[96,256]{1,0:T(8,128)(2,1)S(1)}, bf16[96,256]{1,0:T(8,128)(2,1)S(1)}, u32[]{:S(2)}, u32[]{:S(2)}) collective-permute-start(bf16[96,256]{1,0:T(8,128)(2,1)S(1)} %get-tuple-element.37), channel_id=1, source_target_pairs={{0,12},{4,24},{8,20},{12,0},{16,28},{20,8},{24,4},{28,16},{1,13},{... | collective-permute-start | bytes 147464 | tf_op jit(solution)/shard_map/ppermute | solution.py:48
  13.9 5.1 %collective-permute-start.8 = (bf16[64,256]{1,0:T(8,128)(2,1)S(1)}, bf16[64,256]{1,0:T(8,128)(2,1)S(1)}, u32[]{:S(2)}, u32[]{:S(2)}) collective-permute-start(bf16[64,256]{1,0:T(8,128)(2,1)S(1)} %get-tuple-element.38), channel_id=1, source_target_pairs={{0,20},{4,16},{8,28},{12,24},{16,4},{20,0},{24,12},{28,8},{1,21},{... | collective-permute-start | bytes 98312 | tf_op jit(solution)/shard_map/ppermute | solution.py:48
  16.3 5.8 %collective-permute-start.5 = (bf16[128,128]{1,0:T(8,128)(2,1)S(1)}, bf16[128,128]{1,0:T(8,128)(2,1)S(1)}, u32[]{:S(2)}, u32[]{:S(2)}) collective-permute-start(bf16[128,128]{1,0:T(8,128)(2,1)S(1)} %get-tuple-element.31.att_ref), channel_id=1, source_target_pairs={{0,3},{1,2},{2,1},{3,0},{4,7},{5,6},{6,5},{7,4},{8,11},{9,10},{10,... | collective-permute-start | bytes 98312 | tf_op jit(solution)/shard_map/ppermute | solution.py:55
  19.0 4.8 %collective-permute-start.4 = (bf16[128,128]{1,0:T(8,128)(2,1)S(1)}, bf16[128,128]{1,0:T(8,128)(2,1)S(1)}, u32[]{:S(2)}, u32[]{:S(2)}) collective-permute-start(bf16[128,128]{1,0:T(8,128)(2,1)S(1)} %get-tuple-element.31.att_ref), channel_id=1, source_target_pairs={{0,2},{1,3},{2,0},{3,1},{4,6},{5,7},{6,4},{7,5},{8,10},{9,11},{10,... | collective-permute-start | bytes 98312 | tf_op jit(solution)/shard_map/ppermute | solution.py:55
  19.1 5.2 %collective-permute-start.11 = (bf16[128,256]{1,0:T(8,128)(2,1)S(1)}, bf16[128,256]{1,0:T(8,128)(2,1)S(1)}, u32[]{:S(2)}, u32[]{:S(2)}) collective-permute-start(bf16[128,256]{1,0:T(8,128)(2,1)S(1)} %get-tuple-element.41), channel_id=1, source_target_pairs={{0,28},{4,8},{8,4},{12,16},{16,12},{20,24},{24,20},{28,0},{1,29},{... | collective-permute-start | bytes 196616 | tf_op jit(solution)/shard_map/ppermute | solution.py:48
  20.4 3.9 %collective-permute-start.10 = (bf16[128,128]{1,0:T(8,128)(2,1)S(1)}, bf16[128,128]{1,0:T(8,128)(2,1)S(1)}, u32[]{:S(2)}, u32[]{:S(2)}) collective-permute-start(bf16[128,128]{1,0:T(8,128)(2,1)S(1)} %get-tuple-element.40), channel_id=1, source_target_pairs={{0,1},{1,0},{2,3},{3,2},{4,5},{5,4},{6,7},{7,6},{8,9},{9,8},{10,11... | collective-permute-start | bytes 98312 | tf_op jit(solution)/shard_map/ppermute | solution.py:55
  22.2 2.1 %collective-permute-start.12 = (bf16[512,256]{1,0:T(8,128)(2,1)S(1)}, bf16[512,256]{1,0:T(8,128)(2,1)S(1)}, u32[]{:S(2)}, u32[]{:S(2)}) collective-permute-start(bf16[512,256]{1,0:T(8,128)(2,1)S(1)} %pack.1), channel_id=1, source_target_pairs={{0,4},{4,0},{8,12},{12,8},{16,20},{20,16},{24,28},{28,24},{1,5},{5... | collective-permute-start | bytes 786440 | tf_op jit(solution)/shard_map/ppermute | solution.py:48

commit v17 on v16

--- a/solution.py
+++ b/solution.py
@@ -23,7 +23,7 @@
 GRAD_COST = 0
 COMBINE_COST = 10**10
 GATHER_COST = 10**10
-PACK_COST = 10**10
+PACK_COST = 6*10**8
 F32 = jnp.float32
 
 
@@ -156,21 +156,24 @@
     )(index, queries, out_weight, after)
 
 
-def prepare_kernel(cot_ref, w_ref, after_ref, grad_ref):
+def prepare_kernel(cot_ref, w_ref, after_ref, mult_ref, q_ref, own_ref, first_ref,
+                   grad_ref, *near_refs):
     del after_ref
     grad_ref[...] = dot_nt(cot_ref[...], w_ref[...]).astype(grad_ref.dtype)
-
-
-def prepare(cotangent, out_weight, after):
+    near_kernel(mult_ref, q_ref, grad_ref, own_ref, first_ref, *near_refs)
+
+
+def prepare(cotangent, out_weight, after, mult, q, own, first):
     return pl.pallas_call(
         prepare_kernel,
-        out_shape=shape(BLK, HD),
-        in_specs=[VMEM] * 3,
-        out_specs=VMEM,
+        out_shape=(shape(BLK, HD), shape(BLK, 2 * BLK, kind=F32), shape(BLK, 2 * BLK, kind=F32),
+                   shape(BLK, HD, kind=F32), shape(3, BLK, HD, kind=F32)),
+        in_specs=[VMEM] * 7,
+        out_specs=(VMEM,) * 5,
         compiler_params=PARAMS,
         cost_estimate=cost(GRAD_COST),
         name="prepare",
-    )(cotangent, out_weight, after)
+    )(cotangent, out_weight, after, mult, q, own, first)
 
 
 def lead_kernel(own_ref, first_ref, mult_ref, whole_ref, near_ref, pair_ref, whole_out):
@@ -195,14 +198,34 @@
     )(own, first, mult, whole)
 
 
-def attend_kernel(blocks, pieces, mult_ref, q_ref, grad_ref, *refs):
+def near_kernel(mult_ref, q_ref, grad_ref, own_ref, first_ref,
+                terms_ref, products_ref, sum_ref, stats_ref):
+    q = q_ref[...]
+    grad = grad_ref[...]
+    keys = jnp.concatenate([own_ref[:, :HD], first_ref[:, :HD]], axis=0)
+    values = jnp.concatenate([own_ref[:, HD:], first_ref[:, HD:]], axis=0)
+    scores = dot_nt(q, keys)
+    top = jnp.max(scores, axis=1, keepdims=True)
+    terms = jnp.exp2((scores - top) * (SCALE * LOG2E)) * mult_ref[0:1, :2 * BLK]
+    products = dot_nt(grad, values)
+    terms_ref[...] = terms
+    products_ref[...] = products
+    sum_ref[...] = dot_nn(terms.astype(BF16), values)
+    stats_ref[0] = jnp.broadcast_to(top, (BLK, HD))
+    stats_ref[1] = jnp.broadcast_to(jnp.sum(terms, axis=1, keepdims=True), (BLK, HD))
+    delta = jnp.sum(terms * products, axis=1, keepdims=True)
+    stats_ref[2] = jnp.broadcast_to(delta, (BLK, HD))
+
+
+def attend_kernel(blocks, pieces, mult_ref, q_ref, grad_ref, terms_ref, products_ref, sum_ref,
+                  stats_ref, *refs):
     block_refs = refs[:blocks]
     att_ref, dq_ref = refs[blocks:blocks + 2]
-    sum_refs = refs[blocks + 2:-1]
+    out_refs = refs[blocks + 2:-1]
     keys_ref = refs[-1]
     total_rows = keys_ref.shape[0]
     row = 0
-    for ref in block_refs:
+    for ref in block_refs[2:]:
         keys_ref[row:row + ref.shape[0], :] = ref[...]
         row += ref.shape[0]
     if row < total_rows:
@@ -211,31 +234,45 @@
     values = keys_ref[:, HD:]
     q = q_ref[...]
     grad = grad_ref[...]
-    mult = mult_ref[0:1, :]
+    mult = mult_ref[0:1, 2 * BLK:]
 
     scores = dot_nt(q, keys) + jnp.where(mult > 0.0, 0.0, ABSENT)
-    top = jnp.max(scores, axis=1, keepdims=True)
+    grad_weights = dot_nt(grad, values)
+    near_top = stats_ref[0, :, 0:1]
+    top = jnp.maximum(near_top, jnp.max(scores, axis=1, keepdims=True))
     terms = jnp.exp2((scores - top) * (SCALE * LOG2E)) * mult
-    probability = terms * (1.0 / jnp.sum(terms, axis=1, keepdims=True))
+    near_factor = jnp.exp2((near_top - top) * (SCALE * LOG2E))
+    total = near_factor * stats_ref[1, :, 0:1] + jnp.sum(terms, axis=1, keepdims=True)
+    inverse = 1.0 / total
+    near_scale = near_factor * inverse
+    probability = terms * inverse
     weights = probability.astype(BF16)
-    att_ref[...] = dot_nn(weights, values).astype(BF16)
-
-    grad_weights = dot_nt(grad, values)
+    att_ref[...] = (dot_nn(weights, values) + sum_ref[...] * near_scale).astype(BF16)
+
     delta = jnp.sum(probability * grad_weights, axis=1, keepdims=True)
+    delta = delta + near_scale * stats_ref[2, :, 0:1]
+    near_probability = terms_ref[...] * near_scale
+    near_weights = near_probability.astype(BF16)
+    near_scores = (near_probability * (products_ref[...] - delta) * SCALE).astype(BF16)
     grad_scores = (probability * (grad_weights - delta) * SCALE).astype(BF16)
-    dq_ref[...] = dot_nn(grad_scores, keys).astype(BF16)
-    key_terms = dot_tn(grad_scores, q)
-    value_terms = dot_tn(weights, grad)
-    for spans, ref in zip(pieces, sum_refs):
+    dq = dot_nn(grad_scores, keys)
+    dq = dq + dot_nn(near_scores[:, :BLK], block_refs[0][:, :HD])
+    dq = dq + dot_nn(near_scores[:, BLK:], block_refs[1][:, :HD])
+    dq_ref[...] = dq.astype(BF16)
+    key_terms = (dot_tn(near_scores, q), dot_tn(grad_scores, q))
+    value_terms = (dot_tn(near_weights, grad), dot_tn(weights, grad))
+    for spans, ref in zip(pieces, out_refs):
         row = 0
         for start, end in spans:
             rows = slice(row, row + end - start)
-            ref[rows, :HD] = key_terms[start:end].astype(ref.dtype)
-            ref[rows, HD:] = value_terms[start:end].astype(ref.dtype)
+            part = 0 if start < 2 * BLK else 1
+            source = slice(start - part * 2 * BLK, end - part * 2 * BLK)
+            ref[rows, :HD] = key_terms[part][source].astype(ref.dtype)
+            ref[rows, HD:] = value_terms[part][source].astype(ref.dtype)
             row += end - start
 
 
-def attend(mult, q, grad, blocks, pieces, wide):
+def attend(mult, q, grad, near, blocks, pieces, wide):
     def body(*refs):
         attend_kernel(len(blocks), pieces, *refs)
 
@@ -246,13 +283,13 @@
     return pl.pallas_call(
         body,
         out_shape=(shape(BLK, HD), shape(BLK, HD), *sums),
-        in_specs=[VMEM] * (3 + len(blocks)),
+        in_specs=[VMEM] * (7 + len(blocks)),
         out_specs=(VMEM,) * (2 + len(sums)),
-        scratch_shapes=[pltpu.VMEM((mult.shape[1], PAIR), BF16)],
+        scratch_shapes=[pltpu.VMEM((mult.shape[1] - 2 * BLK, PAIR), BF16)],
         compiler_params=PARAMS,
         cost_estimate=cost(ATTEND_COST),
         name="attend",
-    )(mult, q, grad, *blocks)
+    )(mult, q, grad, *near, *blocks)
 
 
 def half_rows():
@@ -294,8 +331,8 @@
     )(own, first, second, plus, minus, whole, half, att)
 
 
-def pack_kernel(first_ref, slices_ref, after_ref, out_ref):
-    del after_ref
+def pack_kernel(first_ref, slices_ref, *refs):
+    out_ref = refs[-1]
     out_ref[:BLK] = first_ref[...]
     out_ref[BLK:] = slices_ref[...]
 
@@ -304,12 +341,12 @@
     return pl.pallas_call(
         pack_kernel,
         out_shape=shape(BLK + slices.shape[0], PAIR),
-        in_specs=[VMEM] * 3,
+        in_specs=[VMEM] * (2 + len(after)),
         out_specs=VMEM,
         compiler_params=PARAMS,
         cost_estimate=cost(PACK_COST),
         name="pack",
-    )(first, slices, after)
+    )(first, slices, *after)
 
 
 def project_kernel(att_ref, two_ref, three_ref, mine_ref, whole_ref, out_ref):
@@ -465,7 +502,7 @@
         mine, whole, half = slices
         half = swap(half, 1)
         near, pair, whole = leads(own, first, mult, whole)
-        grad = prepare(cotangent, weight, pair)
+        grad, *terms = prepare(cotangent, weight, pair, mult, queries, own, first)
         whole = spread_slice(whole)
         near = trade(near, -1)
         blocks = (own, first, near, trade(pair, 3), trade(pair, 4))
@@ -474,7 +511,7 @@
         pieces = [[(i * BLK, (i + 1) * BLK)] for i in range(3)]
         pieces += [[(places[1], places[4])], [(places[4], places[5]), (places[0], places[1])]]
         att, dq, own_sum, first_sum, second_sum, to_plus, to_minus = attend(
-            mult, queries, grad, blocks, pieces, 3
+            mult, queries, grad, terms, blocks, pieces, 3
         )
         far = [swap(att, 2), swap(att, 3)]
         own_sum, to_first, to_second, out_slices, last = combine(
@@ -482,7 +519,7 @@
             att,
         )
         from_second = trade(to_second, -1)
-        packed = trade(pack(to_first, out_slices, far[1]), 1)
+        packed = trade(pack(to_first, out_slices, far), 1)
         partial = project(att, *far, mine, whole)
         one = gather(swap(last, 1), from_second, partial)
         mixed, dq, dk, dv = finish_ring(
@@ -490,13 +527,13 @@
         )
     else:
         second = trade(own, -1)
-        grad = prepare(cotangent, weight, own)
+        grad, *terms = prepare(cotangent, weight, own, mult, queries, own, first)
         slices = [slices[0]] + [swap(slices[r], r) for r in range(1, heads)]
         spread = jnp.broadcast_to(own[None, :n], (seq, n, PAIR))
         side = lax.all_to_all(spread, "seq", 0, 0).reshape(side_rows, PAIR)
         pieces = [[(i * BLK, (i + 1) * BLK)] for i in range(3)] + [[(3 * BLK, columns)]]
         att, dq, own_sum, to_first, to_second, to_side = attend(
-            mult, queries, grad, (own, first, second, side), pieces, 1
+            mult, queries, grad, terms, (own, first, second, side), pieces, 1
         )
         from_side = lax.all_to_all(to_side.reshape(seq, n, PAIR), "seq", 0, 0)
         mixed, dk, dv = finish(

time: 25.6 us -> 26.1 us (1.020)
  waiting for transfers between devices: 2.66 us -> 3.21 us
  starting transfers between devices: 17 us -> 16.7 us
    ppermute x4, starting transfers between devices: 5.74 us -> 4.9 us  [swap(): return lax.ppermute(array, 'head', [(i, i ^ mask) for i in range(count)])]
    ppermute x8, starting transfers between devices: 8.79 us -> 9.36 us  [trade(): lax.ppermute(array, 'seq', [(i, (i + (step if i % 2 == 0 else -step)) % c...]
    ppermute x8, waiting for transfers between devices: 0.02 us -> 0.57 us  [trade(): lax.ppermute(array, 'seq', [(i, (i + (step if i % 2 == 0 else -step)) % c...]
    pallas_call x1, Pallas kernels: 0.3 us -> 0.58 us  [prepare(): pl.pallas_call(prepare_kernel, out_shape=(shape(BLK, HD), shape(BLK, 2 *...]
  transfers between devices with their start and end apart: 13 -> 13, of which waited for: 3 -> 4; matrix products, arithmetic and copies ran while one was open for 0% -> 0% of each run, Pallas kernels for 11% -> 12%
where the time goes in v17:
time: 26.1 us; the launch traced here: 25.8 us
  starting transfers between devices  16.7 us (64%)
  Pallas kernels  4.14 us (16%)
  waiting for transfers between devices  3.21 us (12%)
  local copies, waits for them, and re-layouts  1 us (4%)
  between operations  0.75 us (3%)
    ppermute x8, starting transfers between devices, trade(): lax.ppermute(array, 'seq', [(i, (i + (step if i % 2 == 0 else -step)) % c...  9.36 us
    ppermute x4, starting transfers between devices, swap(): return lax.ppermute(array, 'head', [(i, i ^ mask) for i in range(count)])  4.9 us
    ppermute x4, waiting for transfers between devices, swap(): return lax.ppermute(array, 'head', [(i, i ^ mask) for i in range(count)])  2.64 us
    ppermute x1, starting transfers between devices, spread_slice(): return lax.ppermute(array, ('seq', 'head'), pairs)  2.47 us
    pallas_call x1, Pallas kernels, weight_slices(): pl.pallas_call(body, out_shape=(shape(8, columns, kind=F32), shape(BLK, H...  1.23 us
    pallas_call x1, Pallas kernels, finish_ring(): pl.pallas_call(finish_ring_kernel, out_shape=(shape(BLK, width),) + (shap...  1.05 us
    unnamed x9, local copies, waits for them, and re-layouts  0.99 us
    pallas_call x1, Pallas kernels, attend(): pl.pallas_call(body, out_shape=(shape(BLK, HD), shape(BLK, HD), *sums), i...  0.98 us
  transfers between devices with their start and end apart: 13, of which 4 were waited for; matrix products, arithmetic and copies ran while one was open for 0% of the time, Pallas kernels for 12%

profile of v17, /device:TPU:0, one launch (start us, length us, event | category | flops | bytes accessed | tf_op | source)
XLA Modules:
  0.0 25.8 jit_solution(15062928726072497309)
XLA Ops:
  0.6 0.8 %constant_dynamic-update-slice_fusion.1 = bf16[128,256]{1,0:T(8,128)(2,1)S(1)} fusion(bf16[128,128]{1,0:T(8,128)(2,1)} %param.7), kind=kLoop, calls=%fused_computation.1 | loop fusion | bytes 65536
  1.4 0.0 copy-start.1
  1.4 0.0 copy-start.2
  1.5 0.5 %collective-permute-start = (bf16[128,256]{1,0:T(8,128)(2,1)S(1)}, bf16[128,256]{1,0:T(8,128)(2,1)S(1)}, u32[]{:S(2)}, u32[]{:S(2)}) collective-permute-start(bf16[128,256]{1,0:T(8,128)(2,1)S(1)} %constant_dynamic-update-slice_fusion.refs_3_.own_ref.refs_7_), channel_id=1, source_target_pairs={{0,4},{4,0},{8,12},{12,8},{16,20},{20,16},{24,28},{28,24},{1,5},{5... | collective-permute-start | bytes 196616 | tf_op jit(solution)/shard_map/ppermute | solution.py:48
  2.0 0.2 copy-done.1
  2.2 1.2 %slices.1 = (f32[8,640]{1,0:T(8,128)S(1)}, bf16[128,128]{1,0:T(8,128)(2,1)S(1)}, bf16[128,2048]{1,0:T(8,128)(2,1)S(1)}, bf16[128,512]{1,0:T(8,128)(2,1)S(1)}, bf...) custom-call(s32[1,8]{1,0:T(1,128)S(1)} %copy-done.2, bf16[128,128]{1,0:T(8,128)(2,1)S(1)} %copy-done.1, ...), custom_call_target="tpu_custom_call" | custom-call | flops 10000000000 | tf_op jit(solution)/shard_map/slices/pallas_call | solution.py:143
  3.4 0.0 collective-permute-done.first_ref.refs_8_
  3.5 3.4 %collective-permute-start.1 = (bf16[160,256]{1,0:T(8,128)(2,1)S(1)}, bf16[160,256]{1,0:T(8,128)(2,1)S(1)}, u32[]{:S(2)}, u32[]{:S(2)}) collective-permute-start(bf16[160,256]{1,0:T(8,128)(2,1)S(1)} %get-tuple-element.40), channel_id=1, source_target_pairs={{0,28},{4,8},{8,4},{12,16},{16,12},{20,24},{24,20},{28,0},{1,29},{... | collective-permute-start | bytes 245768 | tf_op jit(solution)/shard_map/ppermute | solution.py:48
  6.9 0.5 %collective-permute-start.3 = (bf16[64,256]{1,0:T(8,128)(2,1)S(1)}, bf16[64,256]{1,0:T(8,128)(2,1)S(1)}, u32[]{:S(2)}, u32[]{:S(2)}) collective-permute-start(bf16[64,256]{1,0:T(8,128)(2,1)S(1)} %get-tuple-element.34.after_ref), channel_id=1, source_target_pairs={{0,16},{4,20},{8,24},{12,28},{16,0},{20,4},{24,8},{28,12},{1,17},{... | collective-permute-start | bytes 98312 | tf_op jit(solution)/shard_map/ppermute | solution.py:48
  7.4 0.3 %collective-permute-start.2 = (bf16[64,256]{1,0:T(8,128)(2,1)S(1)}, bf16[64,256]{1,0:T(8,128)(2,1)S(1)}, u32[]{:S(2)}, u32[]{:S(2)}) collective-permute-start(bf16[64,256]{1,0:T(8,128)(2,1)S(1)} %get-tuple-element.34.after_ref), channel_id=1, source_target_pairs={{0,12},{4,24},{8,20},{12,0},{16,28},{20,8},{24,4},{28,16},{1,13},{... | collective-permute-start | bytes 98312 | tf_op jit(solution)/shard_map/ppermute | solution.py:48
  7.7 1.8 %collective-permute-start.9 = (bf16[80,512]{1,0:T(8,128)(2,1)S(1)}, bf16[80,512]{1,0:T(8,128)(2,1)S(1)}, u32[]{:S(2)}, u32[]{:S(2)}) collective-permute-start(bf16[80,512]{1,0:T(8,128)(2,1)S(1)} %get-tuple-element.49), channel_id=1, source_target_pairs={{0,1},{1,0},{2,3},{3,2},{4,5},{5,4},{6,7},{7,6},{8,9},{9,8},{10,11... | collective-permute-start | bytes 245768 | tf_op jit(solution)/shard_map/ppermute | solution.py:55
  9.5 2.5 %collective-permute-start.6 = (bf16[128,512]{1,0:T(8,128)(2,1)S(1)}, bf16[128,512]{1,0:T(8,128)(2,1)S(1)}, u32[]{:S(2)}, u32[]{:S(2)}) collective-permute-start(bf16[128,512]{1,0:T(8,128)(2,1)S(1)} %get-tuple-element.43), channel_id=1, source_target_pairs={{0,3},{1,2},{2,1},{3,0},{4,6},{5,7},{6,4},{7,5},{8,11},{9,10},{10,... | collective-permute-start | bytes 393224 | tf_op jit(solution)/shard_map/ppermute | solution.py:486
  12.0 0.6 %prepare.1 = (bf16[128,128]{1,0:T(8,128)(2,1)S(1)}, f32[128,256]{1,0:T(8,128)S(1)}, f32[128,256]{1,0:T(8,128)S(1)}, f32[128,128]{1,0:T(8,128)S(1)}, f32[3,128,128]{2,1,0:T(8,128)S(1)}) custom-call(bf16[128,2048]{1,0:T(8,128)(2,1)S(1)} %copy-done, bf16[128,2048]{1,0:T(8,128)(2,1)S(1)} %get-tuple-element.32.w_ref, ...), custom_call_target="tpu_custom_call" | custom-call | tf_op jit(solution)/shard_map/prepare/pallas_call | solution.py:167
  12.5 0.0 collective-permute-done.3.refs_11_
  12.5 0.0 collective-permute-done.2.refs_10_
  12.5 0.0 collective-permute-done.1.refs_9_
  12.6 1.0 %attend.1 = (bf16[128,128]{1,0:T(8,128)(2,1)S(1)}, bf16[128,128]{1,0:T(8,128)(2,1)S(1)}, f32[128,256]{1,0:T(8,128)S(1)}, f32[128,256]{1,0:T(8,128)S(1)}, f32[128...) custom-call(f32[8,640]{1,0:T(8,128)S(1)} %get-tuple-element.30.mult_ref.refs_0_, ...), custom_call_target="tpu_custom_call" | custom-call | flops 10000000000 | tf_op jit(solution)/shard_map/attend/pallas_call | solution.py:283
  13.5 0.9 %collective-permute-start.7 = (bf16[96,256]{1,0:T(8,128)(2,1)S(1)}, bf16[96,256]{1,0:T(8,128)(2,1)S(1)}, u32[]{:S(2)}, u32[]{:S(2)}) collective-permute-start(bf16[96,256]{1,0:T(8,128)(2,1)S(1)} %get-tuple-element.47), channel_id=1, source_target_pairs={{0,12},{4,24},{8,20},{12,0},{16,28},{20,8},{24,4},{28,16},{1,13},{... | collective-permute-start | bytes 147464 | tf_op jit(solution)/shard_map/ppermute | solution.py:48
  14.4 1.9 %collective-permute-start.8 = (bf16[64,256]{1,0:T(8,128)(2,1)S(1)}, bf16[64,256]{1,0:T(8,128)(2,1)S(1)}, u32[]{:S(2)}, u32[]{:S(2)}) collective-permute-start(bf16[64,256]{1,0:T(8,128)(2,1)S(1)} %get-tuple-element.48), channel_id=1, source_target_pairs={{0,20},{4,16},{8,28},{12,24},{16,4},{20,0},{24,12},{28,8},{1,21},{... | collective-permute-start | bytes 98312 | tf_op jit(solution)/shard_map/ppermute | solution.py:48
  16.3 2.1 %collective-permute-start.5 = (bf16[128,128]{1,0:T(8,128)(2,1)S(1)}, bf16[128,128]{1,0:T(8,128)(2,1)S(1)}, u32[]{:S(2)}, u32[]{:S(2)}) collective-permute-start(bf16[128,128]{1,0:T(8,128)(2,1)S(1)} %get-tuple-element.41.att_ref), channel_id=1, source_target_pairs={{0,3},{1,2},{2,1},{3,0},{4,7},{5,6},{6,5},{7,4},{8,11},{9,10},{10,... | collective-permute-start | bytes 98312 | tf_op jit(solution)/shard_map/ppermute | solution.py:55
  18.3 0.0 collective-permute-done.9.half_ref
  18.3 0.1 collective-permute-start.4
  18.4 0.1 combine.1
  18.5 1.8 %collective-permute-start.11 = (bf16[128,256]{1,0:T(8,128)(2,1)S(1)}, bf16[128,256]{1,0:T(8,128)(2,1)S(1)}, u32[]{:S(2)}, u32[]{:S(2)}) collective-permute-start(bf16[128,256]{1,0:T(8,128)(2,1)S(1)} %get-tuple-element.51), channel_id=1, source_target_pairs={{0,28},{4,8},{8,4},{12,16},{16,12},{20,24},{24,20},{28,0},{1,29},{... | collective-permute-start | bytes 196616 | tf_op jit(solution)/shard_map/ppermute | solution.py:48
  20.3 1.0 %collective-permute-start.10 = (bf16[128,128]{1,0:T(8,128)(2,1)S(1)}, bf16[128,128]{1,0:T(8,128)(2,1)S(1)}, u32[]{:S(2)}, u32[]{:S(2)}) collective-permute-start(bf16[128,128]{1,0:T(8,128)(2,1)S(1)} %get-tuple-element.50), channel_id=1, source_target_pairs={{0,1},{1,0},{2,3},{3,2},{4,5},{5,4},{6,7},{7,6},{8,9},{9,8},{10,11... | collective-permute-start | bytes 98312 | tf_op jit(solution)/shard_map/ppermute | solution.py:55
  21.3 0.7 %collective-permute-done.5.three_ref.refs_1_ = bf16[128,128]{1,0:T(8,128)(2,1)S(1)} collective-permute-done((bf16[128,128]{1,0:T(8,128)(2,1)S(1)}, bf16[128,128]{1,0:T(8,128)(2,1)S(1)}, u32[]{:S(2)}, u32[]{:S(2)}) %collective-permute-start.5) | collective-permute-done | bytes 32800 | tf_op jit(solution)/shard_map/ppermute | solution.py:55
  22.0 1.2 %collective-permute-done.4.two_ref.refs_0_ = bf16[128,128]{1,0:T(8,128)(2,1)S(1)} collective-permute-done((bf16[128,128]{1,0:T(8,128)(2,1)S(1)}, bf16[128,128]{1,0:T(8,128)(2,1)S(1)}, u32[]{:S(2)}, u32[]{:S(2)}) %collective-permute-start.4) | collective-permute-done | bytes 32800 | tf_op jit(solution)/shard_map/ppermute | solution.py:55
  23.2 0.1 collective-permute-start.12
  23.3 0.2 project.1.partial_ref
  23.5 0.7 %collective-permute-done.10.one_ref = bf16[128,128]{1,0:T(8,128)(2,1)S(1)} collective-permute-done((bf16[128,128]{1,0:T(8,128)(2,1)S(1)}, bf16[128,128]{1,0:T(8,128)(2,1)S(1)}, u32[]{:S(2)}, u32[]{:S(2)}) %collective-permute-start.10) | collective-permute-done | bytes 32800 | tf_op jit(solution)/shard_map/ppermute | solution.py:55
  24.2 0.6 %collective-permute-done.12.first_ref = bf16[512,256]{1,0:T(8,128)(2,1)S(1)} collective-permute-done((bf16[512,256]{1,0:T(8,128)(2,1)S(1)}, bf16[512,256]{1,0:T(8,128)(2,1)S(1)}, u32[]{:S(2)}, u32[]{:S(2)}) %collective-permute-start.12) | collective-permute-done | bytes 262176 | tf_op jit(solution)/shard_map/ppermute | solution.py:48
  24.8 1.0 %finish.1 = (bf16[128,512]{1,0:T(8,128)(2,1)}, bf16[128,128]{1,0:T(8,128)(2,1)}, bf16[128,128]{1,0:T(8,128)(2,1)}, bf16[128,128]{1,0:T(8,128)(2,1)}) custom-call(f32[128,512]{1,0:T(8,128)S(1)} %project.1.partial_ref, bf16[128,128]{1,0:T(8,128)(2,1)S(1)} %gather.1.one_ref, bf16[128,128]{1,0:T(8,128)(2,1)S(1)} %collective-permute-done.4.two_ref.refs_0_, ...), custom_call_target="tpu_custom_call" | custom-call | tf_op jit(solution)/shard_map/finish/pallas_call | solution.py:432
  (13 shorter events, 0.1 us)
Async XLA Ops:
  0.6 0.8 %copy-start.3 = (bf16[128,128]{1,0:T(8,128)(2,1)S(1)}, bf16[128,128]{1,0:T(8,128)(2,1)}, u32[]{:S(2)}) copy-start(bf16[128,128]{1,0:T(8,128)(2,1)} %param.8) | copy-start | bytes 98308
  1.4 0.8 %copy-start.1 = (bf16[128,128]{1,0:T(8,128)(2,1)S(1)}, bf16[128,128]{1,0:T(8,128)(2,1)}, u32[]{:S(2)}) copy-start(bf16[128,128]{1,0:T(8,128)(2,1)} %refs_1_.1) | copy-start | bytes 98308
  1.4 0.8 %copy-start.2 = (s32[1,8]{1,0:T(1,128)S(1)}, s32[1,8]{1,0:T(1,128)}, u32[]{:S(2)}) copy-start(s32[1,8]{1,0:T(1,128)} %refs_0_.1) | copy-start | bytes 100
  1.5 2.0 %collective-permute-start = (bf16[128,256]{1,0:T(8,128)(2,1)S(1)}, bf16[128,256]{1,0:T(8,128)(2,1)S(1)}, u32[]{:S(2)}, u32[]{:S(2)}) collective-permute-start(bf16[128,256]{1,0:T(8,128)(2,1)S(1)} %constant_dynamic-update-slice_fusion.refs_3_.own_ref.refs_7_), channel_id=1, source_target_pairs={{0,4},{4,0},{8,12},{12,8},{16,20},{20,16},{24,28},{28,24},{1,5},{5... | collective-permute-start | bytes 196616 | tf_op jit(solution)/shard_map/ppermute | solution.py:48
  2.2 9.8 %copy-start = (bf16[128,2048]{1,0:T(8,128)(2,1)S(1)}, bf16[128,2048]{1,0:T(8,128)(2,1)}, u32[]{:S(2)}) copy-start(bf16[128,2048]{1,0:T(8,128)(2,1)} %cot_ref.1) | copy-start | bytes 1572868
  3.5 9.1 %collective-permute-start.1 = (bf16[160,256]{1,0:T(8,128)(2,1)S(1)}, bf16[160,256]{1,0:T(8,128)(2,1)S(1)}, u32[]{:S(2)}, u32[]{:S(2)}) collective-permute-start(bf16[160,256]{1,0:T(8,128)(2,1)S(1)} %get-tuple-element.40), channel_id=1, source_target_pairs={{0,28},{4,8},{8,4},{12,16},{16,12},{20,24},{24,20},{28,0},{1,29},{... | collective-permute-start | bytes 245768 | tf_op jit(solution)/shard_map/ppermute | solution.py:48
  6.9 5.7 %collective-permute-start.3 = (bf16[64,256]{1,0:T(8,128)(2,1)S(1)}, bf16[64,256]{1,0:T(8,128)(2,1)S(1)}, u32[]{:S(2)}, u32[]{:S(2)}) collective-permute-start(bf16[64,256]{1,0:T(8,128)(2,1)S(1)} %get-tuple-element.34.after_ref), channel_id=1, source_target_pairs={{0,16},{4,20},{8,24},{12,28},{16,0},{20,4},{24,8},{28,12},{1,17},{... | collective-permute-start | bytes 98312 | tf_op jit(solution)/shard_map/ppermute | solution.py:48
  7.4 5.2 %collective-permute-start.2 = (bf16[64,256]{1,0:T(8,128)(2,1)S(1)}, bf16[64,256]{1,0:T(8,128)(2,1)S(1)}, u32[]{:S(2)}, u32[]{:S(2)}) collective-permute-start(bf16[64,256]{1,0:T(8,128)(2,1)S(1)} %get-tuple-element.34.after_ref), channel_id=1, source_target_pairs={{0,12},{4,24},{8,20},{12,0},{16,28},{20,8},{24,4},{28,16},{1,13},{... | collective-permute-start | bytes 98312 | tf_op jit(solution)/shard_map/ppermute | solution.py:48
  7.7 10.7 %collective-permute-start.9 = (bf16[80,512]{1,0:T(8,128)(2,1)S(1)}, bf16[80,512]{1,0:T(8,128)(2,1)S(1)}, u32[]{:S(2)}, u32[]{:S(2)}) collective-permute-start(bf16[80,512]{1,0:T(8,128)(2,1)S(1)} %get-tuple-element.49), channel_id=1, source_target_pairs={{0,1},{1,0},{2,3},{3,2},{4,5},{5,4},{6,7},{7,6},{8,9},{9,8},{10,11... | collective-permute-start | bytes 245768 | tf_op jit(solution)/shard_map/ppermute | solution.py:55
  9.5 9.0 %collective-permute-start.6 = (bf16[128,512]{1,0:T(8,128)(2,1)S(1)}, bf16[128,512]{1,0:T(8,128)(2,1)S(1)}, u32[]{:S(2)}, u32[]{:S(2)}) collective-permute-start(bf16[128,512]{1,0:T(8,128)(2,1)S(1)} %get-tuple-element.43), channel_id=1, source_target_pairs={{0,3},{1,2},{2,1},{3,0},{4,6},{5,7},{6,4},{7,5},{8,11},{9,10},{10,... | collective-permute-start | bytes 393224 | tf_op jit(solution)/shard_map/ppermute | solution.py:486
  13.5 4.9 %collective-permute-start.7 = (bf16[96,256]{1,0:T(8,128)(2,1)S(1)}, bf16[96,256]{1,0:T(8,128)(2,1)S(1)}, u32[]{:S(2)}, u32[]{:S(2)}) collective-permute-start(bf16[96,256]{1,0:T(8,128)(2,1)S(1)} %get-tuple-element.47), channel_id=1, source_target_pairs={{0,12},{4,24},{8,20},{12,0},{16,28},{20,8},{24,4},{28,16},{1,13},{... | collective-permute-start | bytes 147464 | tf_op jit(solution)/shard_map/ppermute | solution.py:48
  14.4 4.0 %collective-permute-start.8 = (bf16[64,256]{1,0:T(8,128)(2,1)S(1)}, bf16[64,256]{1,0:T(8,128)(2,1)S(1)}, u32[]{:S(2)}, u32[]{:S(2)}) collective-permute-start(bf16[64,256]{1,0:T(8,128)(2,1)S(1)} %get-tuple-element.48), channel_id=1, source_target_pairs={{0,20},{4,16},{8,28},{12,24},{16,4},{20,0},{24,12},{28,8},{1,21},{... | collective-permute-start | bytes 98312 | tf_op jit(solution)/shard_map/ppermute | solution.py:48
  16.3 5.7 %collective-permute-start.5 = (bf16[128,128]{1,0:T(8,128)(2,1)S(1)}, bf16[128,128]{1,0:T(8,128)(2,1)S(1)}, u32[]{:S(2)}, u32[]{:S(2)}) collective-permute-start(bf16[128,128]{1,0:T(8,128)(2,1)S(1)} %get-tuple-element.41.att_ref), channel_id=1, source_target_pairs={{0,3},{1,2},{2,1},{3,0},{4,7},{5,6},{6,5},{7,4},{8,11},{9,10},{10,... | collective-permute-start | bytes 98312 | tf_op jit(solution)/shard_map/ppermute | solution.py:55
  18.3 4.8 %collective-permute-start.4 = (bf16[128,128]{1,0:T(8,128)(2,1)S(1)}, bf16[128,128]{1,0:T(8,128)(2,1)S(1)}, u32[]{:S(2)}, u32[]{:S(2)}) collective-permute-start(bf16[128,128]{1,0:T(8,128)(2,1)S(1)} %get-tuple-element.41.att_ref), channel_id=1, source_target_pairs={{0,2},{1,3},{2,0},{3,1},{4,6},{5,7},{6,4},{7,5},{8,10},{9,11},{10,... | collective-permute-start | bytes 98312 | tf_op jit(solution)/shard_map/ppermute | solution.py:55
  18.5 5.7 %collective-permute-start.11 = (bf16[128,256]{1,0:T(8,128)(2,1)S(1)}, bf16[128,256]{1,0:T(8,128)(2,1)S(1)}, u32[]{:S(2)}, u32[]{:S(2)}) collective-permute-start(bf16[128,256]{1,0:T(8,128)(2,1)S(1)} %get-tuple-element.51), channel_id=1, source_target_pairs={{0,28},{4,8},{8,4},{12,16},{16,12},{20,24},{24,20},{28,0},{1,29},{... | collective-permute-start | bytes 196616 | tf_op jit(solution)/shard_map/ppermute | solution.py:48
  20.3 3.9 %collective-permute-start.10 = (bf16[128,128]{1,0:T(8,128)(2,1)S(1)}, bf16[128,128]{1,0:T(8,128)(2,1)S(1)}, u32[]{:S(2)}, u32[]{:S(2)}) collective-permute-start(bf16[128,128]{1,0:T(8,128)(2,1)S(1)} %get-tuple-element.50), channel_id=1, source_target_pairs={{0,1},{1,0},{2,3},{3,2},{4,5},{5,4},{6,7},{7,6},{8,9},{9,8},{10,11... | collective-permute-start | bytes 98312 | tf_op jit(solution)/shard_map/ppermute | solution.py:55
  23.2 1.6 %collective-permute-start.12 = (bf16[512,256]{1,0:T(8,128)(2,1)S(1)}, bf16[512,256]{1,0:T(8,128)(2,1)S(1)}, u32[]{:S(2)}, u32[]{:S(2)}) collective-permute-start(bf16[512,256]{1,0:T(8,128)(2,1)S(1)} %pack.1), channel_id=1, source_target_pairs={{0,4},{4,0},{8,12},{12,8},{16,20},{20,16},{24,28},{28,24},{1,5},{5... | collective-permute-start | bytes 786440 | tf_op jit(solution)/shard_map/ppermute | solution.py:48

commit v18 on v16

--- a/solution.py
+++ b/solution.py
@@ -91,7 +91,7 @@
     return pl.CostEstimate(flops=flops, bytes_accessed=0, transcendentals=0)
 
 
-CHUNKS = 4
+CHUNKS = 8
 
 
 def row_copies(src, dst, sems, first):

time: 25.6 us -> 25.6 us (level)
  no operation moved by 1% of the time
where the time goes in v18:
time: 25.6 us; the launch traced here: 25.3 us
  starting transfers between devices  17 us (66%)
  Pallas kernels  3.9 us (15%)
  waiting for transfers between devices  2.66 us (10%)
  local copies, waits for them, and re-layouts  1 us (4%)
  between operations  0.78 us (3%)
    ppermute x8, starting transfers between devices, trade(): lax.ppermute(array, 'seq', [(i, (i + (step if i % 2 == 0 else -step)) % c...  8.8 us
    ppermute x4, starting transfers between devices, swap(): return lax.ppermute(array, 'head', [(i, i ^ mask) for i in range(count)])  5.73 us
    ppermute x4, waiting for transfers between devices, swap(): return lax.ppermute(array, 'head', [(i, i ^ mask) for i in range(count)])  2.64 us
    ppermute x1, starting transfers between devices, spread_slice(): return lax.ppermute(array, ('seq', 'head'), pairs)  2.47 us
    pallas_call x1, Pallas kernels, weight_slices(): pl.pallas_call(body, out_shape=(shape(8, columns, kind=F32), shape(BLK, H...  1.23 us
    pallas_call x1, Pallas kernels, finish_ring(): pl.pallas_call(finish_ring_kernel, out_shape=(shape(BLK, width),) + (shap...  1.05 us
    pallas_call x1, Pallas kernels, attend(): pl.pallas_call(body, out_shape=(shape(BLK, HD), shape(BLK, HD), *sums), i...  1.02 us
    unnamed x9, local copies, waits for them, and re-layouts  0.99 us
  transfers between devices with their start and end apart: 13, of which 3 were waited for; matrix products, arithmetic and copies ran while one was open for 0% of the time, Pallas kernels for 11%

profile of v18, /device:TPU:0, one launch (start us, length us, event | category | flops | bytes accessed | tf_op | source)
XLA Modules:
  0.0 25.3 jit_solution(16533380562872716859)
XLA Ops:
  0.6 0.8 %constant_dynamic-update-slice_fusion.1 = bf16[128,256]{1,0:T(8,128)(2,1)S(1)} fusion(bf16[128,128]{1,0:T(8,128)(2,1)} %param.7), kind=kLoop, calls=%fused_computation.1 | loop fusion | bytes 65536
  1.4 0.0 copy-start.1
  1.4 0.0 copy-start.2
  1.5 0.5 %collective-permute-start = (bf16[128,256]{1,0:T(8,128)(2,1)S(1)}, bf16[128,256]{1,0:T(8,128)(2,1)S(1)}, u32[]{:S(2)}, u32[]{:S(2)}) collective-permute-start(bf16[128,256]{1,0:T(8,128)(2,1)S(1)} %constant_dynamic-update-slice_fusion.refs_3_.own_ref), channel_id=1, source_target_pairs={{0,4},{4,0},{8,12},{12,8},{16,20},{20,16},{24,28},{28,24},{1,5},{5... | collective-permute-start | bytes 196616 | tf_op jit(solution)/shard_map/ppermute | solution.py:48
  2.0 0.2 copy-done.1
  2.2 1.2 %slices.1 = (f32[8,640]{1,0:T(8,128)S(1)}, bf16[128,128]{1,0:T(8,128)(2,1)S(1)}, bf16[128,2048]{1,0:T(8,128)(2,1)S(1)}, bf16[128,512]{1,0:T(8,128)(2,1)S(1)}, bf...) custom-call(s32[1,8]{1,0:T(1,128)S(1)} %copy-done.2, bf16[128,128]{1,0:T(8,128)(2,1)S(1)} %copy-done.1, ...), custom_call_target="tpu_custom_call" | custom-call | flops 10000000000 | tf_op jit(solution)/shard_map/slices/pallas_call | solution.py:143
  3.4 0.0 collective-permute-done.first_ref.refs_4_
  3.5 3.4 %collective-permute-start.1 = (bf16[160,256]{1,0:T(8,128)(2,1)S(1)}, bf16[160,256]{1,0:T(8,128)(2,1)S(1)}, u32[]{:S(2)}, u32[]{:S(2)}) collective-permute-start(bf16[160,256]{1,0:T(8,128)(2,1)S(1)} %get-tuple-element.30), channel_id=1, source_target_pairs={{0,28},{4,8},{8,4},{12,16},{16,12},{20,24},{24,20},{28,0},{1,29},{... | collective-permute-start | bytes 245768 | tf_op jit(solution)/shard_map/ppermute | solution.py:48
  6.9 0.8 %collective-permute-start.2 = (bf16[64,256]{1,0:T(8,128)(2,1)S(1)}, bf16[64,256]{1,0:T(8,128)(2,1)S(1)}, u32[]{:S(2)}, u32[]{:S(2)}) collective-permute-start(bf16[64,256]{1,0:T(8,128)(2,1)S(1)} %get-tuple-element.29.after_ref), channel_id=1, source_target_pairs={{0,12},{4,24},{8,20},{12,0},{16,28},{20,8},{24,4},{28,16},{1,13},{... | collective-permute-start | bytes 98312 | tf_op jit(solution)/shard_map/ppermute | solution.py:48
  7.7 0.0 collective-permute-start.3
  7.7 2.1 %collective-permute-start.9 = (bf16[80,512]{1,0:T(8,128)(2,1)S(1)}, bf16[80,512]{1,0:T(8,128)(2,1)S(1)}, u32[]{:S(2)}, u32[]{:S(2)}) collective-permute-start(bf16[80,512]{1,0:T(8,128)(2,1)S(1)} %get-tuple-element.39), channel_id=1, source_target_pairs={{0,1},{1,0},{2,3},{3,2},{4,5},{5,4},{6,7},{7,6},{8,9},{9,8},{10,11... | collective-permute-start | bytes 245768 | tf_op jit(solution)/shard_map/ppermute | solution.py:55
  9.8 2.5 %collective-permute-start.6 = (bf16[128,512]{1,0:T(8,128)(2,1)S(1)}, bf16[128,512]{1,0:T(8,128)(2,1)S(1)}, u32[]{:S(2)}, u32[]{:S(2)}) collective-permute-start(bf16[128,512]{1,0:T(8,128)(2,1)S(1)} %get-tuple-element.33), channel_id=1, source_target_pairs={{0,3},{1,2},{2,1},{3,0},{4,6},{5,7},{6,4},{7,5},{8,11},{9,10},{10,... | collective-permute-start | bytes 393224 | tf_op jit(solution)/shard_map/ppermute | solution.py:449
  12.2 0.3 %prepare.1.refs_2_ = bf16[128,128]{1,0:T(8,128)(2,1)S(1)} custom-call(bf16[128,2048]{1,0:T(8,128)(2,1)S(1)} %copy-done, bf16[128,2048]{1,0:T(8,128)(2,1)S(1)} %get-tuple-element.27.w_ref, bf16[64,256]{1,0:T(8,128)(2,1)S(1)} %get-tuple-element.29.after_ref), custom_call_target="tpu_custom_call" | custom-call | tf_op jit(solution)/shard_map/prepare/pallas_call | solution.py:165
  12.5 0.0 collective-permute-done.2.refs_6_
  12.6 0.0 collective-permute-done.3.refs_7_
  12.6 0.0 collective-permute-done.1.refs_5_
  12.6 1.0 %attend.1 = (bf16[128,128]{1,0:T(8,128)(2,1)S(1)}, bf16[128,128]{1,0:T(8,128)(2,1)S(1)}, f32[128,256]{1,0:T(8,128)S(1)}, f32[128,256]{1,0:T(8,128)S(1)}, f32[128...) custom-call(f32[8,640]{1,0:T(8,128)S(1)} %get-tuple-element.25.mult_ref.refs_0_, ...), custom_call_target="tpu_custom_call" | custom-call | flops 10000000000 | tf_op jit(solution)/shard_map/attend/pallas_call | solution.py:246
  13.6 0.3 %collective-permute-start.7 = (bf16[96,256]{1,0:T(8,128)(2,1)S(1)}, bf16[96,256]{1,0:T(8,128)(2,1)S(1)}, u32[]{:S(2)}, u32[]{:S(2)}) collective-permute-start(bf16[96,256]{1,0:T(8,128)(2,1)S(1)} %get-tuple-element.37), channel_id=1, source_target_pairs={{0,12},{4,24},{8,20},{12,0},{16,28},{20,8},{24,4},{28,16},{1,13},{... | collective-permute-start | bytes 147464 | tf_op jit(solution)/shard_map/ppermute | solution.py:48
  13.9 2.4 %collective-permute-start.8 = (bf16[64,256]{1,0:T(8,128)(2,1)S(1)}, bf16[64,256]{1,0:T(8,128)(2,1)S(1)}, u32[]{:S(2)}, u32[]{:S(2)}) collective-permute-start(bf16[64,256]{1,0:T(8,128)(2,1)S(1)} %get-tuple-element.38), channel_id=1, source_target_pairs={{0,20},{4,16},{8,28},{12,24},{16,4},{20,0},{24,12},{28,8},{1,21},{... | collective-permute-start | bytes 98312 | tf_op jit(solution)/shard_map/ppermute | solution.py:48
  16.3 2.7 %collective-permute-start.5 = (bf16[128,128]{1,0:T(8,128)(2,1)S(1)}, bf16[128,128]{1,0:T(8,128)(2,1)S(1)}, u32[]{:S(2)}, u32[]{:S(2)}) collective-permute-start(bf16[128,128]{1,0:T(8,128)(2,1)S(1)} %get-tuple-element.31.att_ref), channel_id=1, source_target_pairs={{0,3},{1,2},{2,1},{3,0},{4,7},{5,6},{6,5},{7,4},{8,11},{9,10},{10,... | collective-permute-start | bytes 98312 | tf_op jit(solution)/shard_map/ppermute | solution.py:55
  19.0 0.0 collective-permute-done.9.half_ref
  19.0 0.0 collective-permute-start.4
  19.0 0.0 collective-permute-done.7.plus_ref
  19.0 0.0 collective-permute-done.6.whole_ref
  19.1 1.3 %collective-permute-start.11 = (bf16[128,256]{1,0:T(8,128)(2,1)S(1)}, bf16[128,256]{1,0:T(8,128)(2,1)S(1)}, u32[]{:S(2)}, u32[]{:S(2)}) collective-permute-start(bf16[128,256]{1,0:T(8,128)(2,1)S(1)} %get-tuple-element.41), channel_id=1, source_target_pairs={{0,28},{4,8},{8,4},{12,16},{16,12},{20,24},{24,20},{28,0},{1,29},{... | collective-permute-start | bytes 196616 | tf_op jit(solution)/shard_map/ppermute | solution.py:48
  20.4 1.0 %collective-permute-start.10 = (bf16[128,128]{1,0:T(8,128)(2,1)S(1)}, bf16[128,128]{1,0:T(8,128)(2,1)S(1)}, u32[]{:S(2)}, u32[]{:S(2)}) collective-permute-start(bf16[128,128]{1,0:T(8,128)(2,1)S(1)} %get-tuple-element.40), channel_id=1, source_target_pairs={{0,1},{1,0},{2,3},{3,2},{4,5},{5,4},{6,7},{7,6},{8,9},{9,8},{10,11... | collective-permute-start | bytes 98312 | tf_op jit(solution)/shard_map/ppermute | solution.py:55
  21.3 0.8 %collective-permute-done.5.three_ref.after_ref = bf16[128,128]{1,0:T(8,128)(2,1)S(1)} collective-permute-done((bf16[128,128]{1,0:T(8,128)(2,1)S(1)}, bf16[128,128]{1,0:T(8,128)(2,1)S(1)}, u32[]{:S(2)}, u32[]{:S(2)}) %collective-permute-start.5) | collective-permute-done | bytes 32800 | tf_op jit(solution)/shard_map/ppermute | solution.py:55
  22.2 0.1 collective-permute-start.12
  22.3 1.6 %collective-permute-done.4.two_ref = bf16[128,128]{1,0:T(8,128)(2,1)S(1)} collective-permute-done((bf16[128,128]{1,0:T(8,128)(2,1)S(1)}, bf16[128,128]{1,0:T(8,128)(2,1)S(1)}, u32[]{:S(2)}, u32[]{:S(2)}) %collective-permute-start.4) | collective-permute-done | bytes 32800 | tf_op jit(solution)/shard_map/ppermute | solution.py:55
  23.8 0.2 project.1.partial_ref
  24.1 0.2 collective-permute-done.10.one_ref
  24.3 1.1 %finish.1 = (bf16[128,512]{1,0:T(8,128)(2,1)}, bf16[128,128]{1,0:T(8,128)(2,1)}, bf16[128,128]{1,0:T(8,128)(2,1)}, bf16[128,128]{1,0:T(8,128)(2,1)}) custom-call(f32[128,512]{1,0:T(8,128)S(1)} %project.1.partial_ref, bf16[128,128]{1,0:T(8,128)(2,1)S(1)} %gather.1.one_ref, bf16[128,128]{1,0:T(8,128)(2,1)S(1)} %collective-permute-done.4.two_ref, ...), custom_call_target="tpu_custom_call" | custom-call | tf_op jit(solution)/shard_map/finish/pallas_call | solution.py:395
  (13 shorter events, 0.1 us)
Async XLA Ops:
  0.6 0.8 %copy-start.3 = (bf16[128,128]{1,0:T(8,128)(2,1)S(1)}, bf16[128,128]{1,0:T(8,128)(2,1)}, u32[]{:S(2)}) copy-start(bf16[128,128]{1,0:T(8,128)(2,1)} %param.8) | copy-start | bytes 98308
  1.4 0.8 %copy-start.1 = (bf16[128,128]{1,0:T(8,128)(2,1)S(1)}, bf16[128,128]{1,0:T(8,128)(2,1)}, u32[]{:S(2)}) copy-start(bf16[128,128]{1,0:T(8,128)(2,1)} %refs_1_.1) | copy-start | bytes 98308
  1.4 0.8 %copy-start.2 = (s32[1,8]{1,0:T(1,128)S(1)}, s32[1,8]{1,0:T(1,128)}, u32[]{:S(2)}) copy-start(s32[1,8]{1,0:T(1,128)} %refs_0_.1) | copy-start | bytes 100
  1.5 2.0 %collective-permute-start = (bf16[128,256]{1,0:T(8,128)(2,1)S(1)}, bf16[128,256]{1,0:T(8,128)(2,1)S(1)}, u32[]{:S(2)}, u32[]{:S(2)}) collective-permute-start(bf16[128,256]{1,0:T(8,128)(2,1)S(1)} %constant_dynamic-update-slice_fusion.refs_3_.own_ref), channel_id=1, source_target_pairs={{0,4},{4,0},{8,12},{12,8},{16,20},{20,16},{24,28},{28,24},{1,5},{5... | collective-permute-start | bytes 196616 | tf_op jit(solution)/shard_map/ppermute | solution.py:48
  2.2 10.1 %copy-start = (bf16[128,2048]{1,0:T(8,128)(2,1)S(1)}, bf16[128,2048]{1,0:T(8,128)(2,1)}, u32[]{:S(2)}) copy-start(bf16[128,2048]{1,0:T(8,128)(2,1)} %cot_ref.1) | copy-start | bytes 1572868
  3.5 9.1 %collective-permute-start.1 = (bf16[160,256]{1,0:T(8,128)(2,1)S(1)}, bf16[160,256]{1,0:T(8,128)(2,1)S(1)}, u32[]{:S(2)}, u32[]{:S(2)}) collective-permute-start(bf16[160,256]{1,0:T(8,128)(2,1)S(1)} %get-tuple-element.30), channel_id=1, source_target_pairs={{0,28},{4,8},{8,4},{12,16},{16,12},{20,24},{24,20},{28,0},{1,29},{... | collective-permute-start | bytes 245768 | tf_op jit(solution)/shard_map/ppermute | solution.py:48
  6.9 5.7 %collective-permute-start.2 = (bf16[64,256]{1,0:T(8,128)(2,1)S(1)}, bf16[64,256]{1,0:T(8,128)(2,1)S(1)}, u32[]{:S(2)}, u32[]{:S(2)}) collective-permute-start(bf16[64,256]{1,0:T(8,128)(2,1)S(1)} %get-tuple-element.29.after_ref), channel_id=1, source_target_pairs={{0,12},{4,24},{8,20},{12,0},{16,28},{20,8},{24,4},{28,16},{1,13},{... | collective-permute-start | bytes 98312 | tf_op jit(solution)/shard_map/ppermute | solution.py:48
  7.7 4.9 %collective-permute-start.3 = (bf16[64,256]{1,0:T(8,128)(2,1)S(1)}, bf16[64,256]{1,0:T(8,128)(2,1)S(1)}, u32[]{:S(2)}, u32[]{:S(2)}) collective-permute-start(bf16[64,256]{1,0:T(8,128)(2,1)S(1)} %get-tuple-element.29.after_ref), channel_id=1, source_target_pairs={{0,16},{4,20},{8,24},{12,28},{16,0},{20,4},{24,8},{28,12},{1,17},{... | collective-permute-start | bytes 98312 | tf_op jit(solution)/shard_map/ppermute | solution.py:48
  7.7 11.4 %collective-permute-start.9 = (bf16[80,512]{1,0:T(8,128)(2,1)S(1)}, bf16[80,512]{1,0:T(8,128)(2,1)S(1)}, u32[]{:S(2)}, u32[]{:S(2)}) collective-permute-start(bf16[80,512]{1,0:T(8,128)(2,1)S(1)} %get-tuple-element.39), channel_id=1, source_target_pairs={{0,1},{1,0},{2,3},{3,2},{4,5},{5,4},{6,7},{7,6},{8,9},{9,8},{10,11... | collective-permute-start | bytes 245768 | tf_op jit(solution)/shard_map/ppermute | solution.py:55
  9.8 9.3 %collective-permute-start.6 = (bf16[128,512]{1,0:T(8,128)(2,1)S(1)}, bf16[128,512]{1,0:T(8,128)(2,1)S(1)}, u32[]{:S(2)}, u32[]{:S(2)}) collective-permute-start(bf16[128,512]{1,0:T(8,128)(2,1)S(1)} %get-tuple-element.33), channel_id=1, source_target_pairs={{0,3},{1,2},{2,1},{3,0},{4,6},{5,7},{6,4},{7,5},{8,11},{9,10},{10,... | collective-permute-start | bytes 393224 | tf_op jit(solution)/shard_map/ppermute | solution.py:449
  13.6 5.4 %collective-permute-start.7 = (bf16[96,256]{1,0:T(8,128)(2,1)S(1)}, bf16[96,256]{1,0:T(8,128)(2,1)S(1)}, u32[]{:S(2)}, u32[]{:S(2)}) collective-permute-start(bf16[96,256]{1,0:T(8,128)(2,1)S(1)} %get-tuple-element.37), channel_id=1, source_target_pairs={{0,12},{4,24},{8,20},{12,0},{16,28},{20,8},{24,4},{28,16},{1,13},{... | collective-permute-start | bytes 147464 | tf_op jit(solution)/shard_map/ppermute | solution.py:48
  13.9 5.1 %collective-permute-start.8 = (bf16[64,256]{1,0:T(8,128)(2,1)S(1)}, bf16[64,256]{1,0:T(8,128)(2,1)S(1)}, u32[]{:S(2)}, u32[]{:S(2)}) collective-permute-start(bf16[64,256]{1,0:T(8,128)(2,1)S(1)} %get-tuple-element.38), channel_id=1, source_target_pairs={{0,20},{4,16},{8,28},{12,24},{16,4},{20,0},{24,12},{28,8},{1,21},{... | collective-permute-start | bytes 98312 | tf_op jit(solution)/shard_map/ppermute | solution.py:48
  16.3 5.8 %collective-permute-start.5 = (bf16[128,128]{1,0:T(8,128)(2,1)S(1)}, bf16[128,128]{1,0:T(8,128)(2,1)S(1)}, u32[]{:S(2)}, u32[]{:S(2)}) collective-permute-start(bf16[128,128]{1,0:T(8,128)(2,1)S(1)} %get-tuple-element.31.att_ref), channel_id=1, source_target_pairs={{0,3},{1,2},{2,1},{3,0},{4,7},{5,6},{6,5},{7,4},{8,11},{9,10},{10,... | collective-permute-start | bytes 98312 | tf_op jit(solution)/shard_map/ppermute | solution.py:55
  19.0 4.8 %collective-permute-start.4 = (bf16[128,128]{1,0:T(8,128)(2,1)S(1)}, bf16[128,128]{1,0:T(8,128)(2,1)S(1)}, u32[]{:S(2)}, u32[]{:S(2)}) collective-permute-start(bf16[128,128]{1,0:T(8,128)(2,1)S(1)} %get-tuple-element.31.att_ref), channel_id=1, source_target_pairs={{0,2},{1,3},{2,0},{3,1},{4,6},{5,7},{6,4},{7,5},{8,10},{9,11},{10,... | collective-permute-start | bytes 98312 | tf_op jit(solution)/shard_map/ppermute | solution.py:55
  19.1 5.2 %collective-permute-start.11 = (bf16[128,256]{1,0:T(8,128)(2,1)S(1)}, bf16[128,256]{1,0:T(8,128)(2,1)S(1)}, u32[]{:S(2)}, u32[]{:S(2)}) collective-permute-start(bf16[128,256]{1,0:T(8,128)(2,1)S(1)} %get-tuple-element.41), channel_id=1, source_target_pairs={{0,28},{4,8},{8,4},{12,16},{16,12},{20,24},{24,20},{28,0},{1,29},{... | collective-permute-start | bytes 196616 | tf_op jit(solution)/shard_map/ppermute | solution.py:48
  20.4 3.9 %collective-permute-start.10 = (bf16[128,128]{1,0:T(8,128)(2,1)S(1)}, bf16[128,128]{1,0:T(8,128)(2,1)S(1)}, u32[]{:S(2)}, u32[]{:S(2)}) collective-permute-start(bf16[128,128]{1,0:T(8,128)(2,1)S(1)} %get-tuple-element.40), channel_id=1, source_target_pairs={{0,1},{1,0},{2,3},{3,2},{4,5},{5,4},{6,7},{7,6},{8,9},{9,8},{10,11... | collective-permute-start | bytes 98312 | tf_op jit(solution)/shard_map/ppermute | solution.py:55
  22.2 2.1 %collective-permute-start.12 = (bf16[512,256]{1,0:T(8,128)(2,1)S(1)}, bf16[512,256]{1,0:T(8,128)(2,1)S(1)}, u32[]{:S(2)}, u32[]{:S(2)}) collective-permute-start(bf16[512,256]{1,0:T(8,128)(2,1)S(1)} %pack.1), channel_id=1, source_target_pairs={{0,4},{4,0},{8,12},{12,8},{16,20},{20,16},{24,28},{28,24},{1,5},{5... | collective-permute-start | bytes 786440 | tf_op jit(solution)/shard_map/ppermute | solution.py:48
